TPU v7x, 32 devices: a whole 2x2x4 slice. The times are simulated.
32 devices in a mesh: ctx: 8 (over y, x, core), ch: 4 (over z).
Axes of the slice: x: 2, y: 2, z: 4, core: 2. Of those that a mesh axis runs over, the one named last changes fastest.
Arguments:
- grad_out: bfloat16 [8, 2, 256, 4096], P('ctx', None, None, 'ch'), may hold values from -6 to 6
- out_weight: bfloat16 [4096, 4096], P('ch'), may hold values from -0.09375 to 0.09375
- gate: bfloat16 [8, 2, 256, 4096], P('ctx', None, None, 'ch'), may hold values from -6 to 6
- filter_taps: float32 [768, 4096], P(None, 'ch'), may hold values from -0.21875 to 0.21875
- doc_starts: int32 [32], replicated, may hold values from 0 to 4096, as said below
Outputs:
- grad_input: float32 [8, 2, 256, 4096], P('ctx', None, None, 'ch')
Inputs may be any that keep to these rules, and one draw needn't show every extreme that they name: `doc_starts`: Non-decreasing; the first is 0; offsets below 4096 start documents, the others equal 4096. Every document is at most 768 tokens long and every one but the last at least 128; one has exactly 768 tokens and one exactly 128.
All inputs are finite; a program needn't handle non-finite values.
Results may differ from a plain program's by a relative error of at most 0.0029.
Values may be sent and summed in bfloat16 or wider, within the bound.
No kernel may reach another device: no remote copies, remote signals or barrier semaphores. Data moves between devices by JAX's collectives and lax.ppermute only.
A program may use at most 192 MiB of HBM per device.

v0:
```python
import functools
import math

import jax
import jax.numpy as jnp
import ml_dtypes
import numpy as np
from jax import lax
from jax.experimental import pallas as pl
from jax.experimental.pallas import tpu as pltpu
from jax.sharding import PartitionSpec as P

REACH = 3
LANES = 256
MIB = 1024 * 1024
F32 = jnp.float32
BF16 = jnp.bfloat16


def parts_of(table):
    high = table.astype(np.float32).astype(ml_dtypes.bfloat16)
    low = (table - high.astype(np.float64)).astype(np.float32).astype(ml_dtypes.bfloat16)
    return high, low


@functools.lru_cache(maxsize=None)
def tables(length):
    angle = np.outer(2 * np.arange(length) + 1, np.arange(length)) % (4 * length)
    angle = angle.astype(np.float64) * (math.pi / (2 * length))
    forward = np.concatenate([np.cos(angle), -np.sin(angle)], axis=0)
    high, low = parts_of(forward)
    stacked = np.concatenate([high, low], axis=0)
    back_high, back_low = parts_of(forward.T / length)
    return stacked, np.concatenate([back_high, back_low], axis=0)


def nn(a, b):
    return lax.dot_general(a, b, (((1,), (0,)), ((), ())), preferred_element_type=F32)


def nt(a, b):
    return lax.dot_general(a, b, (((1,), (1,)), ((), ())), preferred_element_type=F32)


def project_kernel(g_ref, w_ref, gate_ref, out_ref):
    total = nt(g_ref[...], w_ref[...])
    out_ref[...] = (total * gate_ref[...].astype(F32)).astype(BF16)


def project(gathered, weight, gate):
    rows, depth = gathered.shape
    width = weight.shape[0]
    tile = LANES
    return pl.pallas_call(
        project_kernel,
        grid=(width // tile,),
        out_shape=jax.ShapeDtypeStruct((rows, width), BF16),
        in_specs=[
            pl.BlockSpec((rows, depth), lambda c: (0, 0)),
            pl.BlockSpec((tile, depth), lambda c: (c, 0)),
            pl.BlockSpec((rows, tile), lambda c: (0, c)),
        ],
        out_specs=pl.BlockSpec((rows, tile), lambda c: (0, c)),
        compiler_params=pltpu.CompilerParams(vmem_limit_bytes=40 * MIB),
        cost_estimate=pl.CostEstimate(
            flops=2 * rows * depth * width,
            bytes_accessed=2 * (rows * depth + width * depth + 2 * rows * width),
            transcendentals=0,
        ),
    )(gathered, weight, gate)


def spectrum_kernel(table_ref, taps_ref, out_ref):
    length = table_ref.shape[1]
    table_high = table_ref[: 2 * length, :]
    table = table_ref[...]
    freq = lax.broadcasted_iota(jnp.int32, (length, 1), 0)
    sign = jnp.where(freq % 2 == 0, 1.0, -1.0).astype(F32)
    before = None
    for part in range(REACH + 1):
        if part < REACH:
            values = taps_ref[part * length : (part + 1) * length, :]
            high = values.astype(BF16)
            low = (values - high.astype(F32)).astype(BF16)
            both = nn(table, high)
            full = both[: 2 * length] + (both[2 * length :] + nn(table_high, low))
            real, imag = full[:length], -full[length:]
        else:
            real, imag = None, None
        if before is None:
            out_real, out_imag = real, imag
        else:
            turned_real, turned_imag = sign * before[1], -sign * before[0]
            if real is None:
                out_real, out_imag = turned_real, turned_imag
            else:
                out_real, out_imag = real + turned_real, imag + turned_imag
        out_ref[part, :length, :] = out_real
        out_ref[part, length:, :] = out_imag
        before = (real, imag)


def tap_spectra(table, taps):
    count, width = taps.shape
    length = count // REACH
    return pl.pallas_call(
        spectrum_kernel,
        grid=(width // LANES,),
        out_shape=jax.ShapeDtypeStruct((REACH + 1, 2 * length, width), F32),
        in_specs=[
            pl.BlockSpec((4 * length, length), lambda c: (0, 0)),
            pl.BlockSpec((count, LANES), lambda c: (0, c)),
        ],
        out_specs=pl.BlockSpec((REACH + 1, 2 * length, LANES), lambda c: (0, 0, c)),
        compiler_params=pltpu.CompilerParams(vmem_limit_bytes=40 * MIB),
        cost_estimate=pl.CostEstimate(
            flops=2 * 3 * 2 * count * length * width,
            bytes_accessed=4 * (count * width + 8 * length * width),
            transcendentals=0,
        ),
    )(table, taps)


def conv_kernel(pieces, with_alt, aliased, *refs):
    facts_ref, table_ref, back_ref, spec_ref = refs[:4]
    refs = refs[4:]
    own_refs, refs = refs[:pieces], refs[pieces:]
    halo_refs, refs = refs[: REACH * pieces], refs[REACH * pieces :]
    if with_alt:
        alt_refs, refs = refs[:REACH], refs[REACH:]
    if aliased:
        refs = refs[1:]
    out_ref, acc_ref = refs
    length = table_ref.shape[1]
    row = lax.broadcasted_iota(jnp.int32, (length, LANES), 0)

    def joined(some):
        if len(some) == 1:
            return some[0][...]
        return jnp.concatenate([one[...] for one in some], axis=0)

    def term(values, low, high, distance):
        kept = jnp.where((row >= low) & (row < high), values.astype(F32), 0.0).astype(BF16)
        both = nn(table_ref[...], kept)
        full = both[: 2 * length] + both[2 * length :]
        real, imag = full[:length], full[length:]
        k_real = spec_ref[distance, :length, :]
        k_imag = spec_ref[distance, length:, :]
        return k_real * real - k_imag * imag, k_real * imag + k_imag * real

    def back(real, imag):
        total = jnp.concatenate([real.astype(BF16), imag.astype(BF16)], axis=0)
        both = nn(back_ref[...], total)
        return both[:length] + both[length:]

    first_end, last_start = facts_ref[0], facts_ref[1]
    own = joined(own_refs)
    real, imag = term(own, last_start, length, 0)
    acc_ref[:length, :] = real
    acc_ref[length:, :] = imag
    for distance in range(1, REACH + 1):
        reach = facts_ref[1 + distance]

        @pl.when(reach > 0)
        def _(distance=distance, reach=reach):
            values = joined(halo_refs[(distance - 1) * pieces : distance * pieces])
            if with_alt:
                values = values.astype(F32) + alt_refs[distance - 1][...].astype(F32)
            real, imag = term(values, 0, reach, distance)
            acc_ref[:length, :] += real
            acc_ref[length:, :] += imag

    out_ref[0, 0] = back(acc_ref[:length, :], acc_ref[length:, :])

    @pl.when(last_start > 0)
    def _():
        signal = back(*term(own, 0, first_end, 0))
        out_ref[0, 0] = jnp.where(row < first_end, signal, out_ref[0, 0])

    @pl.when(last_start > first_end)
    def _():
        signal = back(*term(own, first_end, last_start, 0))
        keep = (row >= first_end) & (row < last_start)
        out_ref[0, 0] = jnp.where(keep, signal, out_ref[0, 0])


def convolve(slot, facts, table, back, spectra, own, halos, alts=None, result=None):
    length = table.shape[1]
    width = own[0].shape[1]
    pieces = len(own)
    piece_spec = pl.BlockSpec((length // pieces, LANES), lambda c: (0, c))
    operands = [facts, table, back, spectra, *own]
    for halo in halos:
        operands.extend(halo)
    specs = [
        pl.BlockSpec(memory_space=pltpu.SMEM),
        pl.BlockSpec((4 * length, length), lambda c: (0, 0)),
        pl.BlockSpec((2 * length, 2 * length), lambda c: (0, 0)),
        pl.BlockSpec((REACH + 1, 2 * length, LANES), lambda c: (0, 0, c)),
    ]
    specs += [piece_spec] * (pieces * (1 + REACH))
    if alts is not None:
        operands.extend(alts)
        specs += [pl.BlockSpec((length, LANES), lambda c: (0, c))] * REACH
    aliases = {}
    if result is not None:
        aliases = {len(operands): 0}
        operands.append(result)
        specs.append(pl.BlockSpec(memory_space=pl.ANY))
    return pl.pallas_call(
        functools.partial(conv_kernel, pieces, alts is not None, result is not None),
        grid=(width // LANES,),
        out_shape=jax.ShapeDtypeStruct((1, 2, length, width), F32),
        in_specs=specs,
        out_specs=pl.BlockSpec((1, 1, length, LANES), lambda c: (0, slot, 0, c)),
        scratch_shapes=[pltpu.VMEM((2 * length, LANES), F32)],
        input_output_aliases=aliases,
        compiler_params=pltpu.CompilerParams(vmem_limit_bytes=40 * MIB),
        cost_estimate=pl.CostEstimate(
            flops=2 * 10 * 2 * length * length * width,
            bytes_accessed=4 * (8 * length * width + 3 * length * width),
            transcendentals=0,
        ),
    )(*operands)


def shifted(value, steps):
    count = lax.axis_size("ctx")
    initial, last = (max(0, -steps), min(count, count - steps))
    return lax.ppermute(value, "ctx", [(source, source + steps) for source in range(initial, last)])


def block_facts(doc_starts, block, length, end):
    start = block * length

    def after(where):
        return jnp.min(jnp.where(doc_starts > where, doc_starts, end))

    first_end = jnp.clip(after(start) - start, 0, length)
    last_start = jnp.max(jnp.where(doc_starts <= start + length - 1, doc_starts, 0)) - start
    last_start = jnp.clip(last_start, 0, length)
    reaches = after(start + length - 1) - start
    facts = [first_end, last_start]
    facts += [jnp.clip(reaches - distance * length, 0, length) for distance in range(1, REACH + 1)]
    return jnp.stack(facts).astype(jnp.int32)


def on_device(grad_out, out_weight, gate, filter_taps, doc_starts):
    pairs = lax.axis_size("ctx")
    place = lax.axis_index("ctx")
    length = grad_out.shape[2]
    blocks = 2 * pairs
    table_np, back_np = tables(length)
    table, back = jnp.asarray(table_np), jnp.asarray(back_np)
    half = length // 2

    def gather(piece):
        return lax.all_gather(piece, "ch", axis=1, tiled=True)

    upper_in = gather(grad_out[0, 1])
    first_in = gather(grad_out[0, 0, :half])
    second_in = gather(grad_out[0, 0, half:])

    spectra = tap_spectra(table, filter_taps)
    lower_facts = block_facts(doc_starts, place, length, blocks * length)
    upper_facts = block_facts(doc_starts, blocks - 1 - place, length, blocks * length)

    upper = project(upper_in, out_weight, gate[0, 1])
    upper_halo = [shifted(upper, distance) for distance in range(1, REACH + 1)]
    fold_one = lax.ppermute(upper, "ctx", [(pairs - 1, pairs - 2)])
    fold_two = lax.ppermute(fold_one, "ctx", [(pairs - 2, pairs - 3)])
    result = convolve(
        1, upper_facts, table, back, spectra, [upper], [[halo] for halo in upper_halo]
    )
    last = place == pairs - 1
    alts = [
        jnp.where(last, upper, jnp.zeros_like(upper)),
        jnp.where(last, upper_halo[0], fold_one),
        jnp.where(last, upper_halo[1], jnp.where(place == pairs - 2, upper, fold_two)),
    ]

    first = project(first_in, out_weight, gate[0, 0, :half])
    first_halo = [shifted(first, -distance) for distance in range(1, REACH + 1)]
    second = project(second_in, out_weight, gate[0, 0, half:])
    second_halo = [shifted(second, -distance) for distance in range(1, REACH + 1)]
    halos = [list(both) for both in zip(first_halo, second_halo)]
    return convolve(
        0, lower_facts, table, back, spectra, [first, second], halos, alts, result
    )


def solution(mesh):
    in_specs = (
        P("ctx", None, None, "ch"),
        P("ch", None),
        P("ctx", None, None, "ch"),
        P(None, "ch"),
        P(),
    )
    out_specs = P("ctx", None, None, "ch")
    return jax.shard_map(
        on_device, mesh=mesh, in_specs=in_specs, out_specs=out_specs, check_vma=False
    )
```

profile of v0, /device:TPU:3, one launch (start us, length us, event | category | flops | bytes accessed | tf_op | source)
XLA Modules:
  0.0 173.8 jit_solution(13298069280389054695)
XLA Ops:
  6.5 2.0 %slice.22 = bf16[1,1,256,1024]{3,2,1,0:T(8,128)(2,1)} slice(bf16[1,2,256,1024]{3,2,1,0:T(8,128)(2,1)} %param.7), slice={[0:1], [1:2], [0:256], [0:1024]} | slice | bytes 1048576 | tf_op jit(solution)/shard_map/slice | solution.py:260
  8.6 1.8 %fusion.6 = (bf16[1,1,128,1024]{3,2,1,0:T(8,128)(2,1)}, bf16[1,1,128,1024]{3,2,1,0:T(8,128)(2,1)}) fusion(bf16[1,2,256,1024]{3,2,1,0:T(8,128)(2,1)} %param.7), kind=kLoop, calls=%fused_computation.18 | loop fusion | bytes 1048576 | tf_op jit(solution)/shard_map/slice | solution.py:262
  11.2 44.9 %all-gather.11.cloned.1.call-done = bf16[1,1,256,4096]{3,2,1,0:T(8,128)(2,1)} async-done(((bf16[1,1,256,1024]{3,2,1,0:T(8,128)(2,1)}), bf16[1,1,256,4096]{3,2,1,0:T(8,128)(2,1)}) %all-gather.11.cloned.1.call-update) | async-done | bytes 2097168 | tf_op jit(solution)/shard_map/all_gather | solution.py:258
  56.1 3.4 %copy-done.2 = bf16[1024,4096]{1,0:T(8,128)(2,1)S(1)} copy-done((bf16[1024,4096]{1,0:T(8,128)(2,1)S(1)}, bf16[1024,4096]{1,0:T(8,128)(2,1)}, u32[]{:S(2)}) %copy-start.2) | copy-done | bytes 8388632
  59.5 1.6 copy-done.7
  61.1 3.1 %shard_map.76.refs_4_ = bf16[256,1024]{1,0:T(8,128)(2,1)S(1)} custom-call(bf16[256,4096]{1,0:T(8,128)(2,1)S(1)} %bitcast.19, bf16[1024,4096]{1,0:T(8,128)(2,1)S(1)} %copy-done.2, bf16[256,1024]{1,0:T(8,128)(2,1)S(1)} %slice_bitcast_fusion.gate_ref), custom_call_target="tpu_custom_call" | custom-call | flops 2147483648 | bytes 11534336 | tf_op jit(solution)/shard_map/pallas_call | solution.py:54
  64.2 1.5 collective-permute-start.7
  65.7 4.2 %shard_map.73.refs_3_ = f32[4,512,1024]{2,1,0:T(8,128)S(1)} custom-call(bf16[1024,256]{1,0:T(8,128)(2,1)S(1)} %copy-done.5, f32[768,1024]{1,0:T(8,128)S(1)} %copy-done.6), custom_call_target="tpu_custom_call" | custom-call | flops 2415919104 | bytes 11534336 | tf_op jit(solution)/shard_map/pallas_call | solution.py:106
  69.9 3.2 %copy-done = f32[4,512,1024]{2,1,0:T(8,128)} copy-done((f32[4,512,1024]{2,1,0:T(8,128)}, f32[4,512,1024]{2,1,0:T(8,128)S(1)}, u32[]{:S(2)}) %copy-start) | copy-done | bytes 8388632
  73.1 3.7 %collective-permute-start.6 = (bf16[256,1024]{1,0:T(8,128)(2,1)S(1)}, bf16[256,1024]{1,0:T(8,128)(2,1)S(1)}, u32[]{:S(2)}, u32[]{:S(2)}) collective-permute-start(bf16[256,1024]{1,0:T(8,128)(2,1)S(1)} %shard_map.76.refs_4_), channel_id=1, source_target_pairs={{0,4},{4,8},{8,12},{12,16},{16,20},{20,24},{24,28},{1,5},{5,9},{9,... | collective-permute-start | bytes 1572872 | tf_op jit(solution)/shard_map/ppermute | solution.py:230
  76.8 2.9 %collective-permute-start.8 = (bf16[256,1024]{1,0:T(8,128)(2,1)S(1)}, bf16[256,1024]{1,0:T(8,128)(2,1)S(1)}, u32[]{:S(2)}, u32[]{:S(2)}) collective-permute-start(bf16[256,1024]{1,0:T(8,128)(2,1)S(1)} %shard_map.76.refs_4_), channel_id=1, source_target_pairs={{0,8},{4,12},{8,16},{12,20},{16,24},{20,28},{1,9},{5,13},{9,17},{1... | collective-permute-start | bytes 1572872 | tf_op jit(solution)/shard_map/ppermute | solution.py:230
  79.8 2.0 %collective-permute-start.10 = (bf16[256,1024]{1,0:T(8,128)(2,1)S(1)}, bf16[256,1024]{1,0:T(8,128)(2,1)S(1)}, u32[]{:S(2)}, u32[]{:S(2)}) collective-permute-start(bf16[256,1024]{1,0:T(8,128)(2,1)S(1)} %shard_map.76.refs_4_), channel_id=1, source_target_pairs={{0,12},{4,16},{8,20},{12,24},{16,28},{1,13},{5,17},{9,21},{13,25},... | collective-permute-start | bytes 1572872 | tf_op jit(solution)/shard_map/ppermute | solution.py:230
  87.5 3.4 %copy-done.3 = bf16[1024,4096]{1,0:T(8,128)(2,1)S(1)} copy-done((bf16[1024,4096]{1,0:T(8,128)(2,1)S(1)}, bf16[1024,4096]{1,0:T(8,128)(2,1)}, u32[]{:S(2)}) %copy-start.3) | copy-done | bytes 8388632
  90.9 1.2 copy-done.10
  92.1 3.4 %shard_map.74.refs_4_ = bf16[128,1024]{1,0:T(8,128)(2,1)S(1)} custom-call(bf16[128,4096]{1,0:T(8,128)(2,1)S(1)} %bitcast.21, bf16[1024,4096]{1,0:T(8,128)(2,1)S(1)} %copy-done.3, bf16[128,1024]{1,0:T(8,128)(2,1)S(1)} %get-tuple-element.12.gate_ref), custom_call_target="tpu_custom_call" | custom-call | flops 1073741824 | bytes 9961472 | tf_op jit(solution)/shard_map/pallas_call | solution.py:54
  95.6 3.2 %collective-permute-start = (bf16[128,1024]{1,0:T(8,128)(2,1)S(1)}, bf16[128,1024]{1,0:T(8,128)(2,1)S(1)}, u32[]{:S(2)}, u32[]{:S(2)}) collective-permute-start(bf16[128,1024]{1,0:T(8,128)(2,1)S(1)} %shard_map.74.refs_4_), channel_id=1, source_target_pairs={{4,0},{8,4},{12,8},{16,12},{20,16},{24,20},{28,24},{5,1},{9,5},{13... | collective-permute-start | bytes 786440 | tf_op jit(solution)/shard_map/ppermute | solution.py:230
  98.7 1.5 collective-permute-start.9
  100.2 13.1 %all-gather.9.cloned.1.call-done = bf16[1,1,128,4096]{3,2,1,0:T(8,128)(2,1)} async-done(((bf16[1,1,128,1024]{3,2,1,0:T(8,128)(2,1)}), bf16[1,1,128,4096]{3,2,1,0:T(8,128)(2,1)}) %all-gather.9.cloned.1.call-update) | async-done | bytes 1048592 | tf_op jit(solution)/shard_map/all_gather | solution.py:258
  113.3 3.4 %copy-done.4 = bf16[1024,4096]{1,0:T(8,128)(2,1)S(1)} copy-done((bf16[1024,4096]{1,0:T(8,128)(2,1)S(1)}, bf16[1024,4096]{1,0:T(8,128)(2,1)}, u32[]{:S(2)}) %copy-start.4) | copy-done | bytes 8388632
  116.7 1.2 copy-done.9
  117.9 3.4 %shard_map.75.refs_5_ = bf16[128,1024]{1,0:T(8,128)(2,1)S(1)} custom-call(bf16[128,4096]{1,0:T(8,128)(2,1)S(1)} %bitcast.20, bf16[1024,4096]{1,0:T(8,128)(2,1)S(1)} %copy-done.4, bf16[128,1024]{1,0:T(8,128)(2,1)S(1)} %get-tuple-element.11.gate_ref), custom_call_target="tpu_custom_call" | custom-call | flops 1073741824 | bytes 9961472 | tf_op jit(solution)/shard_map/pallas_call | solution.py:54
  121.3 2.2 %collective-permute-start.2 = (bf16[128,1024]{1,0:T(8,128)(2,1)S(1)}, bf16[128,1024]{1,0:T(8,128)(2,1)S(1)}, u32[]{:S(2)}, u32[]{:S(2)}) collective-permute-start(bf16[128,1024]{1,0:T(8,128)(2,1)S(1)} %shard_map.74.refs_4_), channel_id=1, source_target_pairs={{8,0},{12,4},{16,8},{20,12},{24,16},{28,20},{9,1},{13,5},{17,9},{2... | collective-permute-start | bytes 786440 | tf_op jit(solution)/shard_map/ppermute | solution.py:230
  123.5 3.0 %collective-permute-start.1 = (bf16[128,1024]{1,0:T(8,128)(2,1)S(1)}, bf16[128,1024]{1,0:T(8,128)(2,1)S(1)}, u32[]{:S(2)}, u32[]{:S(2)}) collective-permute-start(bf16[128,1024]{1,0:T(8,128)(2,1)S(1)} %shard_map.75.refs_5_), channel_id=1, source_target_pairs={{4,0},{8,4},{12,8},{16,12},{20,16},{24,20},{28,24},{5,1},{9,5},{13... | collective-permute-start | bytes 786440 | tf_op jit(solution)/shard_map/ppermute | solution.py:230
  126.6 1.9 %collective-permute-start.3 = (bf16[128,1024]{1,0:T(8,128)(2,1)S(1)}, bf16[128,1024]{1,0:T(8,128)(2,1)S(1)}, u32[]{:S(2)}, u32[]{:S(2)}) collective-permute-start(bf16[128,1024]{1,0:T(8,128)(2,1)S(1)} %shard_map.75.refs_5_), channel_id=1, source_target_pairs={{8,0},{12,4},{16,8},{20,12},{24,16},{28,20},{9,1},{13,5},{17,9},{2... | collective-permute-start | bytes 786440 | tf_op jit(solution)/shard_map/ppermute | solution.py:230
  128.5 3.4 %copy-done.1 = f32[4,512,1024]{2,1,0:T(8,128)S(1)} copy-done((f32[4,512,1024]{2,1,0:T(8,128)S(1)}, f32[4,512,1024]{2,1,0:T(8,128)}, u32[]{:S(2)}) %copy-start.1) | copy-done | bytes 8388632
  131.9 10.4 %shard_map.77.refs_15_ = f32[1,2,256,1024]{3,2,1,0:T(8,128)} custom-call(s32[5]{0:T(128)S(1)} %stack.47.refs_0_, bf16[1024,256]{1,0:T(8,128)(2,1)S(1)} %copy-done.5, bf16[512,512]{1,0:T(8,128)(2,1)S(1)} %copy-done.8, f32[4,512,1024]{2,1,0:T(8,128)S(1)} %copy-done.1, bf16[256,1024]{1,0:T(8,128)(2,1)S(1)} %shard_map.76.refs_4_, ...), custom_call_target="tpu_custom_call" | custom-call | flops 2684354560 | bytes 11534336 | tf_op jit(solution)/shard_map/pallas_call | solution.py:210
  143.4 1.9 %collective-permute-start.4 = (bf16[128,1024]{1,0:T(8,128)(2,1)S(1)}, bf16[128,1024]{1,0:T(8,128)(2,1)S(1)}, u32[]{:S(2)}, u32[]{:S(2)}) collective-permute-start(bf16[128,1024]{1,0:T(8,128)(2,1)S(1)} %shard_map.74.refs_4_), channel_id=1, source_target_pairs={{12,0},{16,4},{20,8},{24,12},{28,16},{13,1},{17,5},{21,9},{25,13},... | collective-permute-start | bytes 786440 | tf_op jit(solution)/shard_map/ppermute | solution.py:230
  145.3 1.9 %collective-permute-start.5 = (bf16[128,1024]{1,0:T(8,128)(2,1)S(1)}, bf16[128,1024]{1,0:T(8,128)(2,1)S(1)}, u32[]{:S(2)}, u32[]{:S(2)}) collective-permute-start(bf16[128,1024]{1,0:T(8,128)(2,1)S(1)} %shard_map.75.refs_5_), channel_id=1, source_target_pairs={{12,0},{16,4},{20,8},{24,12},{28,16},{13,1},{17,5},{21,9},{25,13},... | collective-permute-start | bytes 786440 | tf_op jit(solution)/shard_map/ppermute | solution.py:230
  147.2 1.1 select_select_fusion
  148.4 4.0 %collective-permute-done.4.refs_10_ = bf16[128,1024]{1,0:T(8,128)(2,1)S(1)} collective-permute-done((bf16[128,1024]{1,0:T(8,128)(2,1)S(1)}, bf16[128,1024]{1,0:T(8,128)(2,1)S(1)}, u32[]{:S(2)}, u32[]{:S(2)}) %collective-permute-start.4) | collective-permute-done | bytes 262176 | tf_op jit(solution)/shard_map/ppermute | solution.py:230
  152.3 2.8 %collective-permute-done.5.refs_11_ = bf16[128,1024]{1,0:T(8,128)(2,1)S(1)} collective-permute-done((bf16[128,1024]{1,0:T(8,128)(2,1)S(1)}, bf16[128,1024]{1,0:T(8,128)(2,1)S(1)}, u32[]{:S(2)}, u32[]{:S(2)}) %collective-permute-start.5) | collective-permute-done | bytes 262176 | tf_op jit(solution)/shard_map/ppermute | solution.py:230
  155.2 12.1 %shard_map.78 = f32[1,2,256,1024]{3,2,1,0:T(8,128)} custom-call(s32[5]{0:T(128)S(1)} %stack.41.refs_0_, bf16[1024,256]{1,0:T(8,128)(2,1)S(1)} %copy-done.5, bf16[512,512]{1,0:T(8,128)(2,1)S(1)} %copy-done.8, f32[4,512,1024]{2,1,0:T(8,128)S(1)} %copy-done.1, bf16[128,1024]{1,0:T(8,128)(2,1)S(1)} %shard_map.74.refs_4_, ...), custom_call_target="tpu_custom_call", output_to_operand_aliasing={{}: (15, {})} | custom-call | flops 2684354560 | bytes 11534336 | tf_op jit(solution)/shard_map/pallas_call | solution.py:210
  (40 shorter events, 4.0 us)
Async XLA Ops:
  6.5 4.6 %copy-start.11 = (bf16[1,2,256,1024]{3,2,1,0:T(8,128)(2,1)S(1)}, bf16[1,2,256,1024]{3,2,1,0:T(8,128)(2,1)}, u32[]{:S(2)}) copy-start(bf16[1,2,256,1024]{3,2,1,0:T(8,128)(2,1)} %param.9) | copy-start | bytes 3145732
  6.5 49.6 %all-gather.11.cloned.1.call-start = ((), (), s32[]{:S(2)}) async-start(), calls=%async_computation.2 | async-start | bytes 2621440 | tf_op jit(solution)/shard_map/all_gather | solution.py:258
  8.5 79.0 %all-gather.7.cloned.1.call-start = ((), (), s32[]{:S(2)}) async-start(), calls=%async_computation | async-start | bytes 1310720 | tf_op jit(solution)/shard_map/all_gather | solution.py:258
  10.4 102.8 %all-gather.9.cloned.1.call-start = ((), (), s32[]{:S(2)}) async-start(), calls=%async_computation.1 | async-start | bytes 1310720 | tf_op jit(solution)/shard_map/all_gather | solution.py:258
  56.1 3.4 %copy-start.2 = (bf16[1024,4096]{1,0:T(8,128)(2,1)S(1)}, bf16[1024,4096]{1,0:T(8,128)(2,1)}, u32[]{:S(2)}) copy-start(bf16[1024,4096]{1,0:T(8,128)(2,1)} %w_ref.5) | copy-start | bytes 25165828
  59.5 1.6 copy-start.7
  61.1 4.6 %copy-start.5 = (bf16[1024,256]{1,0:T(8,128)(2,1)S(1)}, bf16[1024,256]{1,0:T(8,128)(2,1)}, u32[]{:S(2)}) copy-start(bf16[1024,256]{1,0:T(8,128)(2,1)} %constant.45.clone.table_ref.refs_1_) | copy-start | bytes 1572868
  61.1 4.6 %copy-start.6 = (f32[768,1024]{1,0:T(8,128)S(1)}, f32[768,1024]{1,0:T(8,128)}, u32[]{:S(2)}) copy-start(f32[768,1024]{1,0:T(8,128)} %taps_ref.1) | copy-start | bytes 9437188
  64.2 17.5 %copy-start.12 = (s32[32]{0:T(128)S(1)}, s32[32]{0:T(128)}, u32[]{:S(2)}) copy-start(s32[32]{0:T(128)} %param.11) | copy-start | bytes 388
  64.2 34.5 %collective-permute-start.7 = (bf16[256,1024]{1,0:T(8,128)(2,1)S(1)}, bf16[256,1024]{1,0:T(8,128)(2,1)}, u32[]{:S(2)}, u32[]{:S(2)}) collective-permute-start(bf16[256,1024]{1,0:T(8,128)(2,1)S(1)} %shard_map.76.refs_4_), channel_id=1, source_target_pairs={{28,24},{29,25},{30,26},{31,27}} | collective-permute-start | bytes 1572872 | tf_op jit(solution)/shard_map/ppermute | solution.py:270
  69.9 3.2 %copy-start = (f32[4,512,1024]{2,1,0:T(8,128)}, f32[4,512,1024]{2,1,0:T(8,128)S(1)}, u32[]{:S(2)}) copy-start(f32[4,512,1024]{2,1,0:T(8,128)S(1)} %shard_map.73.refs_3_) | copy-start | bytes 25165828
  73.1 48.2 %collective-permute-start.6 = (bf16[256,1024]{1,0:T(8,128)(2,1)S(1)}, bf16[256,1024]{1,0:T(8,128)(2,1)S(1)}, u32[]{:S(2)}, u32[]{:S(2)}) collective-permute-start(bf16[256,1024]{1,0:T(8,128)(2,1)S(1)} %shard_map.76.refs_4_), channel_id=1, source_target_pairs={{0,4},{4,8},{8,12},{12,16},{16,20},{20,24},{24,28},{1,5},{5,9},{9,... | collective-permute-start | bytes 1572872 | tf_op jit(solution)/shard_map/ppermute | solution.py:230
  76.8 46.7 %collective-permute-start.8 = (bf16[256,1024]{1,0:T(8,128)(2,1)S(1)}, bf16[256,1024]{1,0:T(8,128)(2,1)S(1)}, u32[]{:S(2)}, u32[]{:S(2)}) collective-permute-start(bf16[256,1024]{1,0:T(8,128)(2,1)S(1)} %shard_map.76.refs_4_), channel_id=1, source_target_pairs={{0,8},{4,12},{8,16},{12,20},{16,24},{20,28},{1,9},{5,13},{9,17},{1... | collective-permute-start | bytes 1572872 | tf_op jit(solution)/shard_map/ppermute | solution.py:230
  79.8 46.8 %collective-permute-start.10 = (bf16[256,1024]{1,0:T(8,128)(2,1)S(1)}, bf16[256,1024]{1,0:T(8,128)(2,1)S(1)}, u32[]{:S(2)}, u32[]{:S(2)}) collective-permute-start(bf16[256,1024]{1,0:T(8,128)(2,1)S(1)} %shard_map.76.refs_4_), channel_id=1, source_target_pairs={{0,12},{4,16},{8,20},{12,24},{16,28},{1,13},{5,17},{9,21},{13,25},... | collective-permute-start | bytes 1572872 | tf_op jit(solution)/shard_map/ppermute | solution.py:230
  87.5 3.4 %copy-start.3 = (bf16[1024,4096]{1,0:T(8,128)(2,1)S(1)}, bf16[1024,4096]{1,0:T(8,128)(2,1)}, u32[]{:S(2)}) copy-start(bf16[1024,4096]{1,0:T(8,128)(2,1)} %w_ref.5) | copy-start | bytes 25165828
  90.9 1.2 copy-start.10
  95.6 47.8 %collective-permute-start = (bf16[128,1024]{1,0:T(8,128)(2,1)S(1)}, bf16[128,1024]{1,0:T(8,128)(2,1)S(1)}, u32[]{:S(2)}, u32[]{:S(2)}) collective-permute-start(bf16[128,1024]{1,0:T(8,128)(2,1)S(1)} %shard_map.74.refs_4_), channel_id=1, source_target_pairs={{4,0},{8,4},{12,8},{16,12},{20,16},{24,20},{28,24},{5,1},{9,5},{13... | collective-permute-start | bytes 786440 | tf_op jit(solution)/shard_map/ppermute | solution.py:230
  98.7 46.5 %collective-permute-start.9 = (bf16[256,1024]{1,0:T(8,128)(2,1)}, bf16[256,1024]{1,0:T(8,128)(2,1)}, u32[]{:S(2)}, u32[]{:S(2)}) collective-permute-start(bf16[256,1024]{1,0:T(8,128)(2,1)} %collective-permute-done.7), channel_id=1, source_target_pairs={{24,20},{25,21},{26,22},{27,23}} | collective-permute-start | bytes 1572872 | tf_op jit(solution)/shard_map/ppermute | solution.py:271
  113.3 3.4 %copy-start.4 = (bf16[1024,4096]{1,0:T(8,128)(2,1)S(1)}, bf16[1024,4096]{1,0:T(8,128)(2,1)}, u32[]{:S(2)}) copy-start(bf16[1024,4096]{1,0:T(8,128)(2,1)} %w_ref.5) | copy-start | bytes 25165828
  116.7 1.2 copy-start.9
  117.9 10.6 %copy-start.8 = (bf16[512,512]{1,0:T(8,128)(2,1)S(1)}, bf16[512,512]{1,0:T(8,128)(2,1)}, u32[]{:S(2)}) copy-start(bf16[512,512]{1,0:T(8,128)(2,1)} %constant.46.clone.refs_2_) | copy-start | bytes 1572868
  121.3 27.0 %collective-permute-start.2 = (bf16[128,1024]{1,0:T(8,128)(2,1)S(1)}, bf16[128,1024]{1,0:T(8,128)(2,1)S(1)}, u32[]{:S(2)}, u32[]{:S(2)}) collective-permute-start(bf16[128,1024]{1,0:T(8,128)(2,1)S(1)} %shard_map.74.refs_4_), channel_id=1, source_target_pairs={{8,0},{12,4},{16,8},{20,12},{24,16},{28,20},{9,1},{13,5},{17,9},{2... | collective-permute-start | bytes 786440 | tf_op jit(solution)/shard_map/ppermute | solution.py:230
  123.5 24.8 %collective-permute-start.1 = (bf16[128,1024]{1,0:T(8,128)(2,1)S(1)}, bf16[128,1024]{1,0:T(8,128)(2,1)S(1)}, u32[]{:S(2)}, u32[]{:S(2)}) collective-permute-start(bf16[128,1024]{1,0:T(8,128)(2,1)S(1)} %shard_map.75.refs_5_), channel_id=1, source_target_pairs={{4,0},{8,4},{12,8},{16,12},{20,16},{24,20},{28,24},{5,1},{9,5},{13... | collective-permute-start | bytes 786440 | tf_op jit(solution)/shard_map/ppermute | solution.py:230
  126.6 21.8 %collective-permute-start.3 = (bf16[128,1024]{1,0:T(8,128)(2,1)S(1)}, bf16[128,1024]{1,0:T(8,128)(2,1)S(1)}, u32[]{:S(2)}, u32[]{:S(2)}) collective-permute-start(bf16[128,1024]{1,0:T(8,128)(2,1)S(1)} %shard_map.75.refs_5_), channel_id=1, source_target_pairs={{8,0},{12,4},{16,8},{20,12},{24,16},{28,20},{9,1},{13,5},{17,9},{2... | collective-permute-start | bytes 786440 | tf_op jit(solution)/shard_map/ppermute | solution.py:230
  128.5 3.4 %copy-start.1 = (f32[4,512,1024]{2,1,0:T(8,128)S(1)}, f32[4,512,1024]{2,1,0:T(8,128)}, u32[]{:S(2)}) copy-start(f32[4,512,1024]{2,1,0:T(8,128)} %copy-done) | copy-start | bytes 25165828
  143.4 9.0 %collective-permute-start.4 = (bf16[128,1024]{1,0:T(8,128)(2,1)S(1)}, bf16[128,1024]{1,0:T(8,128)(2,1)S(1)}, u32[]{:S(2)}, u32[]{:S(2)}) collective-permute-start(bf16[128,1024]{1,0:T(8,128)(2,1)S(1)} %shard_map.74.refs_4_), channel_id=1, source_target_pairs={{12,0},{16,4},{20,8},{24,12},{28,16},{13,1},{17,5},{21,9},{25,13},... | collective-permute-start | bytes 786440 | tf_op jit(solution)/shard_map/ppermute | solution.py:230
  145.3 9.9 %collective-permute-start.5 = (bf16[128,1024]{1,0:T(8,128)(2,1)S(1)}, bf16[128,1024]{1,0:T(8,128)(2,1)S(1)}, u32[]{:S(2)}, u32[]{:S(2)}) collective-permute-start(bf16[128,1024]{1,0:T(8,128)(2,1)S(1)} %shard_map.75.refs_5_), channel_id=1, source_target_pairs={{12,0},{16,4},{20,8},{24,12},{28,16},{13,1},{17,5},{21,9},{25,13},... | collective-permute-start | bytes 786440 | tf_op jit(solution)/shard_map/ppermute | solution.py:230
Sparse Core Ops, SparseCore 0:
  8.9 47.1 all-gather.10
  57.7 26.5 all-gather.6
  85.8 27.4 all-gather.8
where the time goes:
time: 175 us; the launch traced here: 174 us
  waiting for transfers between devices  65.4 us (37%)
  Pallas kernels  36.6 us (21%)
  local copies, waits for them, and re-layouts  25.9 us (15%)
  starting transfers between devices  25.7 us (15%)
  between operations  17.1 us (10%)
  other arithmetic  2.98 us (2%)
    all_gather x3, waiting for transfers between devices, gather(): return lax.all_gather(piece, 'ch', axis=1, tiled=True)  57.9 us
    ppermute x9, starting transfers between devices, shifted(): lax.ppermute(value, 'ctx', [(source, source + steps) for source in range(...  22.7 us
    pallas_call x2, Pallas kernels, convolve(): pl.pallas_call(functools.partial(conv_kernel, pieces, alts is not None, r...  22.4 us
    unnamed x26, local copies, waits for them, and re-layouts  20.8 us
    pallas_call x3, Pallas kernels, project(): pl.pallas_call(project_kernel, grid=(width // tile,), out_shape=jax.Shape...  10 us
    ppermute x9, waiting for transfers between devices, shifted(): lax.ppermute(value, 'ctx', [(source, source + steps) for source in range(...  6.78 us
    pallas_call x1, Pallas kernels, tap_spectra(): pl.pallas_call(spectrum_kernel, grid=(width // LANES,), out_shape=jax.Sha...  4.17 us
  transfers between devices with their start and end apart: 14, of which 4 were waited for; matrix products, arithmetic and copies ran while one was open for 4% of the time, Pallas kernels for 14%

commit v1 on v0

--- a/solution.py
+++ b/solution.py
@@ -12,7 +12,7 @@
 
 REACH = 3
 LANES = 256
-MIB = 1024 * 1024
+VMEM = 60 * 1024 * 1024
 F32 = jnp.float32
 BF16 = jnp.bfloat16
 
@@ -42,32 +42,42 @@
     return lax.dot_general(a, b, (((1,), (1,)), ((), ())), preferred_element_type=F32)
 
 
-def project_kernel(g_ref, w_ref, gate_ref, out_ref):
-    total = nt(g_ref[...], w_ref[...])
+def project_kernel(place_ref, *refs):
+    count = (len(refs) - 2) // 2
+    gate_ref, out_ref = refs[-2:]
+    total = nt(refs[0][...], refs[count][...])
+    for step in range(1, count):
+        total = total + nt(refs[step][...], refs[count + step][...])
     out_ref[...] = (total * gate_ref[...].astype(F32)).astype(BF16)
 
 
-def project(gathered, weight, gate):
-    rows, depth = gathered.shape
+def project(place, shards, weight, gate):
+    count = len(shards)
+    rows, depth = shards[0].shape
     width = weight.shape[0]
     tile = LANES
+
+    def weight_spec(step):
+        return pl.BlockSpec((tile, depth), lambda c, at: (c, lax.rem(at[0] + count - step, count)))
+
     return pl.pallas_call(
         project_kernel,
-        grid=(width // tile,),
+        grid_spec=pltpu.PrefetchScalarGridSpec(
+            num_scalar_prefetch=1,
+            grid=(width // tile,),
+            in_specs=[pl.BlockSpec((rows, depth), lambda c, at: (0, 0))] * count
+            + [weight_spec(step) for step in range(count)]
+            + [pl.BlockSpec((rows, tile), lambda c, at: (0, c))],
+            out_specs=pl.BlockSpec((rows, tile), lambda c, at: (0, c)),
+        ),
         out_shape=jax.ShapeDtypeStruct((rows, width), BF16),
-        in_specs=[
-            pl.BlockSpec((rows, depth), lambda c: (0, 0)),
-            pl.BlockSpec((tile, depth), lambda c: (c, 0)),
-            pl.BlockSpec((rows, tile), lambda c: (0, c)),
-        ],
-        out_specs=pl.BlockSpec((rows, tile), lambda c: (0, c)),
-        compiler_params=pltpu.CompilerParams(vmem_limit_bytes=40 * MIB),
+        compiler_params=pltpu.CompilerParams(vmem_limit_bytes=VMEM),
         cost_estimate=pl.CostEstimate(
-            flops=2 * rows * depth * width,
-            bytes_accessed=2 * (rows * depth + width * depth + 2 * rows * width),
+            flops=2 * rows * depth * count * width,
+            bytes_accessed=2 * (rows * depth * count + width * depth * count + 2 * rows * width),
             transcendentals=0,
         ),
-    )(gathered, weight, gate)
+    )(place, *shards, *([weight] * count), gate)
 
 
 def spectrum_kernel(table_ref, taps_ref, out_ref):
@@ -112,7 +122,7 @@
             pl.BlockSpec((count, LANES), lambda c: (0, c)),
         ],
         out_specs=pl.BlockSpec((REACH + 1, 2 * length, LANES), lambda c: (0, 0, c)),
-        compiler_params=pltpu.CompilerParams(vmem_limit_bytes=40 * MIB),
+        compiler_params=pltpu.CompilerParams(vmem_limit_bytes=VMEM),
         cost_estimate=pl.CostEstimate(
             flops=2 * 3 * 2 * count * length * width,
             bytes_accessed=4 * (count * width + 8 * length * width),
@@ -125,7 +135,7 @@
     facts_ref, table_ref, back_ref, spec_ref = refs[:4]
     refs = refs[4:]
     own_refs, refs = refs[:pieces], refs[pieces:]
-    halo_refs, refs = refs[: REACH * pieces], refs[REACH * pieces :]
+    halo_refs, refs = refs[: 4 * pieces], refs[4 * pieces :]
     if with_alt:
         alt_refs, refs = refs[:REACH], refs[REACH:]
     if aliased:
@@ -138,6 +148,17 @@
         if len(some) == 1:
             return some[0][...]
         return jnp.concatenate([one[...] for one in some], axis=0)
+
+    def halo(distance):
+        two, swapped, mate, far = (
+            halo_refs[at * pieces : (at + 1) * pieces] for at in range(4)
+        )
+        if distance == 2:
+            return joined(two)
+        inner = facts_ref[5] == 1
+        if distance == 1:
+            return jnp.where(inner, joined(mate), joined(swapped))
+        return jnp.where(inner, joined(swapped), joined(far))
 
     def term(values, low, high, distance):
         kept = jnp.where((row >= low) & (row < high), values.astype(F32), 0.0).astype(BF16)
@@ -163,7 +184,7 @@
 
         @pl.when(reach > 0)
         def _(distance=distance, reach=reach):
-            values = joined(halo_refs[(distance - 1) * pieces : distance * pieces])
+            values = halo(distance)
             if with_alt:
                 values = values.astype(F32) + alt_refs[distance - 1][...].astype(F32)
             real, imag = term(values, 0, reach, distance)
@@ -198,7 +219,7 @@
         pl.BlockSpec((2 * length, 2 * length), lambda c: (0, 0)),
         pl.BlockSpec((REACH + 1, 2 * length, LANES), lambda c: (0, 0, c)),
     ]
-    specs += [piece_spec] * (pieces * (1 + REACH))
+    specs += [piece_spec] * (pieces * 5)
     if alts is not None:
         operands.extend(alts)
         specs += [pl.BlockSpec((length, LANES), lambda c: (0, c))] * REACH
@@ -215,7 +236,7 @@
         out_specs=pl.BlockSpec((1, 1, length, LANES), lambda c: (0, slot, 0, c)),
         scratch_shapes=[pltpu.VMEM((2 * length, LANES), F32)],
         input_output_aliases=aliases,
-        compiler_params=pltpu.CompilerParams(vmem_limit_bytes=40 * MIB),
+        compiler_params=pltpu.CompilerParams(vmem_limit_bytes=VMEM),
         cost_estimate=pl.CostEstimate(
             flops=2 * 10 * 2 * length * length * width,
             bytes_accessed=4 * (8 * length * width + 3 * length * width),
@@ -230,7 +251,24 @@
     return lax.ppermute(value, "ctx", [(source, source + steps) for source in range(initial, last)])
 
 
-def block_facts(doc_starts, block, length, end):
+def core_swapped(value):
+    count = lax.axis_size("ctx")
+    return lax.ppermute(value, "ctx", [(source, source ^ 1) for source in range(count)])
+
+
+def halo_of(value, way):
+    count = lax.axis_size("ctx")
+    two = shifted(value, 2 * way)
+    outer = 1 if way > 0 else 0
+    far = [
+        (source, source + 3 * way)
+        for source in range(outer, count, 2)
+        if 0 <= source + 3 * way < count
+    ]
+    return [two, core_swapped(two), core_swapped(value), lax.ppermute(value, "ctx", far)]
+
+
+def block_facts(doc_starts, block, length, end, inner):
     start = block * length
 
     def after(where):
@@ -242,6 +280,7 @@
     reaches = after(start + length - 1) - start
     facts = [first_end, last_start]
     facts += [jnp.clip(reaches - distance * length, 0, length) for distance in range(1, REACH + 1)]
+    facts.append(inner)
     return jnp.stack(facts).astype(jnp.int32)
 
 
@@ -253,36 +292,44 @@
     table_np, back_np = tables(length)
     table, back = jnp.asarray(table_np), jnp.asarray(back_np)
     half = length // 2
-
-    def gather(piece):
-        return lax.all_gather(piece, "ch", axis=1, tiled=True)
-
-    upper_in = gather(grad_out[0, 1])
-    first_in = gather(grad_out[0, 0, :half])
-    second_in = gather(grad_out[0, 0, half:])
+    count = lax.axis_size("ch")
+    lane = lax.axis_index("ch").astype(jnp.int32)[None]
+    around = [(source, (source + 1) % count) for source in range(count)]
+
+    def ring(piece):
+        shards = [piece]
+        for _ in range(1, count):
+            shards.append(lax.ppermute(shards[-1], "ch", around))
+        return shards
+
+    upper_in = ring(grad_out[0, 1])
+    first_in = ring(grad_out[0, 0, :half])
+    second_in = ring(grad_out[0, 0, half:])
 
     spectra = tap_spectra(table, filter_taps)
-    lower_facts = block_facts(doc_starts, place, length, blocks * length)
-    upper_facts = block_facts(doc_starts, blocks - 1 - place, length, blocks * length)
-
-    upper = project(upper_in, out_weight, gate[0, 1])
-    upper_halo = [shifted(upper, distance) for distance in range(1, REACH + 1)]
-    fold_one = lax.ppermute(upper, "ctx", [(pairs - 1, pairs - 2)])
-    fold_two = lax.ppermute(fold_one, "ctx", [(pairs - 2, pairs - 3)])
+    odd = place % 2
+    lower_facts = block_facts(doc_starts, place, length, blocks * length, 1 - odd)
+    upper_facts = block_facts(doc_starts, blocks - 1 - place, length, blocks * length, odd)
+
+    upper = project(lane, upper_in, out_weight, gate[0, 1])
+    upper_halo = halo_of(upper, 1)
     result = convolve(
         1, upper_facts, table, back, spectra, [upper], [[halo] for halo in upper_halo]
     )
-    last = place == pairs - 1
+    last, near = place == pairs - 1, place == pairs - 2
+    fold = lax.ppermute(upper, "ctx", [(pairs - 1, pairs - 3)])
+    two, _, mate, _ = upper_halo
+    nothing = jnp.zeros_like(upper)
     alts = [
-        jnp.where(last, upper, jnp.zeros_like(upper)),
-        jnp.where(last, upper_halo[0], fold_one),
-        jnp.where(last, upper_halo[1], jnp.where(place == pairs - 2, upper, fold_two)),
+        jnp.where(last, upper, nothing),
+        jnp.where(last | near, mate, nothing),
+        jnp.where(last, two, jnp.where(near, upper, fold)),
     ]
 
-    first = project(first_in, out_weight, gate[0, 0, :half])
-    first_halo = [shifted(first, -distance) for distance in range(1, REACH + 1)]
-    second = project(second_in, out_weight, gate[0, 0, half:])
-    second_halo = [shifted(second, -distance) for distance in range(1, REACH + 1)]
+    first = project(lane, first_in, out_weight, gate[0, 0, :half])
+    first_halo = halo_of(first, -1)
+    second = project(lane, second_in, out_weight, gate[0, 0, half:])
+    second_halo = halo_of(second, -1)
     halos = [list(both) for both in zip(first_halo, second_halo)]
     return convolve(
         0, lower_facts, table, back, spectra, [first, second], halos, alts, result

time: 175 us -> 154 us (0.88)
  the two profiles are of different devices: /device:TPU:3 before, /device:TPU:14 now
where the time goes in v1:
time: 154 us; the launch traced here: 157 us
  Pallas kernels  56.6 us (37%)
  waiting for transfers between devices  46.5 us (30%)
  starting transfers between devices  38.1 us (25%)
  local copies, waits for them, and re-layouts  8.78 us (6%)
  between operations  4.05 us (3%)
  other arithmetic  2.67 us (2%)
    ppermute x9, waiting for transfers between devices, ring(): shards.append(lax.ppermute(shards[-1], 'ch', around))  42.1 us
    pallas_call x2, Pallas kernels, convolve(): pl.pallas_call(functools.partial(conv_kernel, pieces, alts is not None, r...  27.7 us
    pallas_call x3, Pallas kernels, project(): pl.pallas_call(project_kernel, grid_spec=pltpu.PrefetchScalarGridSpec(num...  21.7 us
    ppermute x9, starting transfers between devices, ring(): shards.append(lax.ppermute(shards[-1], 'ch', around))  16.5 us
    ppermute x3, starting transfers between devices, halo_of(): lax.ppermute(value, 'ctx', far)  9.94 us
    ppermute x3, starting transfers between devices, shifted(): lax.ppermute(value, 'ctx', [(source, source + steps) for source in range(...  9.86 us
    pallas_call x1, Pallas kernels, tap_spectra(): pl.pallas_call(spectrum_kernel, grid=(width // LANES,), out_shape=jax.Sha...  7.28 us
    ppermute x3, waiting for transfers between devices, shifted(): lax.ppermute(value, 'ctx', [(source, source + steps) for source in range(...  4.42 us
  transfers between devices with their start and end apart: 22, of which 5 were waited for; matrix products, arithmetic and copies ran while one was open for 5% of the time, Pallas kernels for 26%

profile of v1, /device:TPU:14, one launch (start us, length us, event | category | flops | bytes accessed | tf_op | source)
XLA Modules:
  0.0 156.7 jit_solution(3317731416149201693)
XLA Ops:
  0.0 1.1 slice_bitcast_fusion.1.refs_0_
  1.1 1.6 %collective-permute-start.14 = (bf16[256,1024]{1,0:T(8,128)(2,1)S(1)}, bf16[256,1024]{1,0:T(8,128)(2,1)S(1)}, u32[]{:S(2)}, u32[]{:S(2)}) collective-permute-start(bf16[256,1024]{1,0:T(8,128)(2,1)S(1)} %slice_bitcast_fusion.1.refs_0_), channel_id=1, source_target_pairs={{0,1},{1,2},{2,3},{3,0},{4,5},{5,6},{6,7},{7,4},{8,9},{9,10},{10,1... | collective-permute-start | bytes 1572872 | tf_op jit(solution)/shard_map/ppermute | solution.py:302
  2.7 12.1 %collective-permute-done.14.refs_1_ = bf16[256,1024]{1,0:T(8,128)(2,1)S(1)} collective-permute-done((bf16[256,1024]{1,0:T(8,128)(2,1)S(1)}, bf16[256,1024]{1,0:T(8,128)(2,1)S(1)}, u32[]{:S(2)}, u32[]{:S(2)}) %collective-permute-start.14) | collective-permute-done | bytes 524320 | tf_op jit(solution)/shard_map/ppermute | solution.py:302
  14.8 1.6 %collective-permute-start.15 = (bf16[256,1024]{1,0:T(8,128)(2,1)S(1)}, bf16[256,1024]{1,0:T(8,128)(2,1)S(1)}, u32[]{:S(2)}, u32[]{:S(2)}) collective-permute-start(bf16[256,1024]{1,0:T(8,128)(2,1)S(1)} %collective-permute-done.14.refs_1_), channel_id=1, source_target_pairs={{0,1},{1,2},{2,3},{3,0},{4,5},{5,6},{6,7},{7,4},{8,9},{9,10},{10,1... | collective-permute-start | bytes 1572872 | tf_op jit(solution)/shard_map/ppermute | solution.py:302
  16.4 11.9 %collective-permute-done.15.refs_2_ = bf16[256,1024]{1,0:T(8,128)(2,1)S(1)} collective-permute-done((bf16[256,1024]{1,0:T(8,128)(2,1)S(1)}, bf16[256,1024]{1,0:T(8,128)(2,1)S(1)}, u32[]{:S(2)}, u32[]{:S(2)}) %collective-permute-start.15) | collective-permute-done | bytes 524320 | tf_op jit(solution)/shard_map/ppermute | solution.py:302
  28.2 0.9 collective-permute-start.16
  29.2 1.1 slice_bitcast_fusion.3
  30.3 1.6 %collective-permute-start = (bf16[128,1024]{1,0:T(8,128)(2,1)S(1)}, bf16[128,1024]{1,0:T(8,128)(2,1)}, u32[]{:S(2)}, u32[]{:S(2)}) collective-permute-start(bf16[128,1024]{1,0:T(8,128)(2,1)S(1)} %get-tuple-element.14.refs_0_), channel_id=1, source_target_pairs={{0,1},{1,2},{2,3},{3,0},{4,5},{5,6},{6,7},{7,4},{8,9},{9,10},{10,1... | collective-permute-start | bytes 786440 | tf_op jit(solution)/shard_map/ppermute | solution.py:302
  31.9 4.0 %collective-permute-start.3 = (bf16[128,1024]{1,0:T(8,128)(2,1)S(1)}, bf16[128,1024]{1,0:T(8,128)(2,1)S(1)}, u32[]{:S(2)}, u32[]{:S(2)}) collective-permute-start(bf16[128,1024]{1,0:T(8,128)(2,1)S(1)} %get-tuple-element.13.refs_0_), channel_id=1, source_target_pairs={{0,1},{1,2},{2,3},{3,0},{4,5},{5,6},{6,7},{7,4},{8,9},{9,10},{10,1... | collective-permute-start | bytes 786440 | tf_op jit(solution)/shard_map/ppermute | solution.py:302
  35.9 1.9 %slice_bitcast_fusion.refs_8_ = bf16[256,1024]{1,0:T(8,128)(2,1)} fusion(bf16[1,2,256,1024]{3,2,1,0:T(8,128)(2,1)} %param.9), kind=kLoop, calls=%fused_computation.1 | loop fusion | bytes 1048576 | tf_op jit(solution)/shard_map/squeeze | solution.py:314
  37.7 12.6 %collective-permute-done.refs_1_ = bf16[128,1024]{1,0:T(8,128)(2,1)} collective-permute-done((bf16[128,1024]{1,0:T(8,128)(2,1)S(1)}, bf16[128,1024]{1,0:T(8,128)(2,1)}, u32[]{:S(2)}, u32[]{:S(2)}) %collective-permute-start) | collective-permute-done | bytes 262176 | tf_op jit(solution)/shard_map/ppermute | solution.py:302
  50.3 5.5 %collective-permute-done.3.refs_1_ = bf16[128,1024]{1,0:T(8,128)(2,1)S(1)} collective-permute-done((bf16[128,1024]{1,0:T(8,128)(2,1)S(1)}, bf16[128,1024]{1,0:T(8,128)(2,1)S(1)}, u32[]{:S(2)}, u32[]{:S(2)}) %collective-permute-start.3) | collective-permute-done | bytes 262176 | tf_op jit(solution)/shard_map/ppermute | solution.py:302
  55.9 0.8 copy-done.10
  56.7 7.4 %shard_map.76.refs_4_ = bf16[256,1024]{1,0:T(8,128)(2,1)} custom-call(s32[1]{0:T(128)} %bitcast.6.place_ref, bf16[256,1024]{1,0:T(8,128)(2,1)} %copy-done.1, bf16[256,1024]{1,0:T(8,128)(2,1)} %copy-done.8, bf16[256,1024]{1,0:T(8,128)(2,1)} %copy-done.9, bf16[256,1024]{1,0:T(8,128)(2,1)} %copy-done.10, bf16[1024,4096]{1,0:T(8,128)(2,1)} %refs_7_.5, ...), custom_call_target="tpu_custom_call" | custom-call | flops 2147483648 | bytes 11534336 | tf_op jit(solution)/shard_map/pallas_call | solution.py:63
  64.1 1.3 collective-permute-start.18
  65.4 2.5 %collective-permute-start.2 = (bf16[128,1024]{1,0:T(8,128)(2,1)}, bf16[128,1024]{1,0:T(8,128)(2,1)S(1)}, u32[]{:S(2)}, u32[]{:S(2)}) collective-permute-start(bf16[128,1024]{1,0:T(8,128)(2,1)} %collective-permute-done.1.refs_2_), channel_id=1, source_target_pairs={{0,1},{1,2},{2,3},{3,0},{4,5},{5,6},{6,7},{7,4},{8,9},{9,10},{10,1... | collective-permute-start | bytes 786440 | tf_op jit(solution)/shard_map/ppermute | solution.py:302
  67.9 4.3 %collective-permute-start.5 = (bf16[128,1024]{1,0:T(8,128)(2,1)}, bf16[128,1024]{1,0:T(8,128)(2,1)S(1)}, u32[]{:S(2)}, u32[]{:S(2)}) collective-permute-start(bf16[128,1024]{1,0:T(8,128)(2,1)} %collective-permute-done.4.refs_2_), channel_id=1, source_target_pairs={{0,1},{1,2},{2,3},{3,0},{4,5},{5,6},{6,7},{7,4},{8,9},{9,10},{10,1... | collective-permute-start | bytes 786440 | tf_op jit(solution)/shard_map/ppermute | solution.py:302
  72.2 0.9 slice_bitcast_fusion.2
  73.7 0.8 fusion.5
  80.3 7.1 %shard_map.74.refs_4_ = bf16[128,1024]{1,0:T(8,128)(2,1)} custom-call(s32[1]{0:T(128)} %bitcast.6.place_ref, bf16[128,1024]{1,0:T(8,128)(2,1)} %copy-done.6, bf16[128,1024]{1,0:T(8,128)(2,1)} %collective-permute-done.refs_1_, bf16[128,1024]{1,0:T(8,128)(2,1)} %collective-permute-done.1.refs_2_, bf16[128,1024]{1,0:T(8,128)(2,1)} %copy-done.15, ...), custom_call_target="tpu_custom_call" | custom-call | flops 1073741824 | bytes 9961472 | tf_op jit(solution)/shard_map/pallas_call | solution.py:63
  87.4 4.6 %collective-permute-start.6 = (bf16[128,1024]{1,0:T(8,128)(2,1)}, bf16[128,1024]{1,0:T(8,128)(2,1)S(1)}, u32[]{:S(2)}, u32[]{:S(2)}) collective-permute-start(bf16[128,1024]{1,0:T(8,128)(2,1)} %shard_map.74.refs_4_), channel_id=1, source_target_pairs={{8,0},{12,4},{16,8},{20,12},{24,16},{28,20},{9,1},{13,5},{17,9},{2... | collective-permute-start | bytes 786440 | tf_op jit(solution)/shard_map/ppermute | solution.py:251
  92.1 1.3 collective-permute-start.21
  93.5 7.3 %shard_map.73.refs_3_ = f32[4,512,1024]{2,1,0:T(8,128)} custom-call(bf16[1024,256]{1,0:T(8,128)(2,1)} %constant.60.clone.table_ref.refs_1_, f32[768,1024]{1,0:T(8,128)} %taps_ref.1), custom_call_target="tpu_custom_call" | custom-call | flops 2415919104 | bytes 11534336 | tf_op jit(solution)/shard_map/pallas_call | solution.py:116
  100.8 7.2 %shard_map.75.refs_5_ = bf16[128,1024]{1,0:T(8,128)(2,1)} custom-call(s32[1]{0:T(128)} %bitcast.6.place_ref, bf16[128,1024]{1,0:T(8,128)(2,1)} %copy-done.5, bf16[128,1024]{1,0:T(8,128)(2,1)} %copy-done.13, bf16[128,1024]{1,0:T(8,128)(2,1)} %collective-permute-done.4.refs_2_, bf16[128,1024]{1,0:T(8,128)(2,1)} %copy-done.14, bf16[1024,4096]{1,0:T(8,128)(2,1)} %refs_7_.5, ...), custom_call_target="tpu_custom_call" | custom-call | flops 1073741824 | bytes 9961472 | tf_op jit(solution)/shard_map/pallas_call | solution.py:63
  108.4 4.0 %collective-permute-start.7 = (bf16[128,1024]{1,0:T(8,128)(2,1)}, bf16[128,1024]{1,0:T(8,128)(2,1)}, u32[]{:S(2)}, u32[]{:S(2)}) collective-permute-start(bf16[128,1024]{1,0:T(8,128)(2,1)} %shard_map.75.refs_5_), channel_id=1, source_target_pairs={{8,0},{12,4},{16,8},{20,12},{24,16},{28,20},{9,1},{13,5},{17,9},{2... | collective-permute-start | bytes 786440 | tf_op jit(solution)/shard_map/ppermute | solution.py:251
  112.4 1.0 select_select_fusion
  113.5 4.4 %collective-permute-done.7.refs_7_ = bf16[128,1024]{1,0:T(8,128)(2,1)} collective-permute-done((bf16[128,1024]{1,0:T(8,128)(2,1)}, bf16[128,1024]{1,0:T(8,128)(2,1)}, u32[]{:S(2)}, u32[]{:S(2)}) %collective-permute-start.7) | collective-permute-done | bytes 262176 | tf_op jit(solution)/shard_map/ppermute | solution.py:251
  117.9 6.6 %collective-permute-start.12 = (bf16[128,1024]{1,0:T(8,128)(2,1)S(1)}, bf16[128,1024]{1,0:T(8,128)(2,1)S(1)}, u32[]{:S(2)}, u32[]{:S(2)}) collective-permute-start(bf16[128,1024]{1,0:T(8,128)(2,1)S(1)} %copy-done.4), channel_id=1, source_target_pairs={{16,4},{24,12},{17,5},{25,13},{18,6},{26,14},{19,7},{27,15}} | collective-permute-start | bytes 786440 | tf_op jit(solution)/shard_map/ppermute | solution.py:268
  124.6 2.0 %collective-permute-start.13 = (bf16[128,1024]{1,0:T(8,128)(2,1)}, bf16[128,1024]{1,0:T(8,128)(2,1)}, u32[]{:S(2)}, u32[]{:S(2)}) collective-permute-start(bf16[128,1024]{1,0:T(8,128)(2,1)} %shard_map.75.refs_5_), channel_id=1, source_target_pairs={{16,4},{24,12},{17,5},{25,13},{18,6},{26,14},{19,7},{27,15}} | collective-permute-start | bytes 786440 | tf_op jit(solution)/shard_map/ppermute | solution.py:268
  127.1 0.9 broadcast_select_fusion.refs_15_
  128.0 11.4 %shard_map.77.refs_17_ = f32[1,2,256,1024]{3,2,1,0:T(8,128)} custom-call(s32[6]{0:T(128)} %stack.55.refs_0_, bf16[1024,256]{1,0:T(8,128)(2,1)} %constant.60.clone.table_ref.refs_1_, bf16[512,512]{1,0:T(8,128)(2,1)} %constant.61.clone.refs_2_, f32[4,512,1024]{2,1,0:T(8,128)} %shard_map.73.refs_3_, bf16[256,1024]{1,0:T(8,128)(2,1)} %shard_map.76.refs_4_, ...), custom_call_target="tpu_custom_call" | custom-call | flops 2684354560 | bytes 11534336 | tf_op jit(solution)/shard_map/pallas_call | solution.py:231
  140.5 16.2 %shard_map.78 = f32[1,2,256,1024]{3,2,1,0:T(8,128)} custom-call(s32[6]{0:T(128)} %stack.48.refs_0_, bf16[1024,256]{1,0:T(8,128)(2,1)} %constant.60.clone.table_ref.refs_1_, bf16[512,512]{1,0:T(8,128)(2,1)} %constant.61.clone.refs_2_, f32[4,512,1024]{2,1,0:T(8,128)} %shard_map.73.refs_3_, ...), custom_call_target="tpu_custom_call", output_to_operand_aliasing={{}: (17, {})} | custom-call | flops 2684354560 | bytes 11534336 | tf_op jit(solution)/shard_map/pallas_call | solution.py:231
  (73 shorter events, 4.9 us)
Async XLA Ops:
  1.1 54.8 %copy-start.1 = (bf16[256,1024]{1,0:T(8,128)(2,1)}, bf16[256,1024]{1,0:T(8,128)(2,1)S(1)}, u32[]{:S(2)}) copy-start(bf16[256,1024]{1,0:T(8,128)(2,1)S(1)} %slice_bitcast_fusion.1.refs_0_) | copy-start | bytes 1572868
  1.1 13.7 %collective-permute-start.14 = (bf16[256,1024]{1,0:T(8,128)(2,1)S(1)}, bf16[256,1024]{1,0:T(8,128)(2,1)S(1)}, u32[]{:S(2)}, u32[]{:S(2)}) collective-permute-start(bf16[256,1024]{1,0:T(8,128)(2,1)S(1)} %slice_bitcast_fusion.1.refs_0_), channel_id=1, source_target_pairs={{0,1},{1,2},{2,3},{3,0},{4,5},{5,6},{6,7},{7,4},{8,9},{9,10},{10,1... | collective-permute-start | bytes 1572872 | tf_op jit(solution)/shard_map/ppermute | solution.py:302
  14.8 41.1 %copy-start.8 = (bf16[256,1024]{1,0:T(8,128)(2,1)}, bf16[256,1024]{1,0:T(8,128)(2,1)S(1)}, u32[]{:S(2)}) copy-start(bf16[256,1024]{1,0:T(8,128)(2,1)S(1)} %collective-permute-done.14.refs_1_) | copy-start | bytes 1572868
  14.8 13.4 %collective-permute-start.15 = (bf16[256,1024]{1,0:T(8,128)(2,1)S(1)}, bf16[256,1024]{1,0:T(8,128)(2,1)S(1)}, u32[]{:S(2)}, u32[]{:S(2)}) collective-permute-start(bf16[256,1024]{1,0:T(8,128)(2,1)S(1)} %collective-permute-done.14.refs_1_), channel_id=1, source_target_pairs={{0,1},{1,2},{2,3},{3,0},{4,5},{5,6},{6,7},{7,4},{8,9},{9,10},{10,1... | collective-permute-start | bytes 1572872 | tf_op jit(solution)/shard_map/ppermute | solution.py:302
  28.2 27.7 %copy-start.9 = (bf16[256,1024]{1,0:T(8,128)(2,1)}, bf16[256,1024]{1,0:T(8,128)(2,1)S(1)}, u32[]{:S(2)}) copy-start(bf16[256,1024]{1,0:T(8,128)(2,1)S(1)} %collective-permute-done.15.refs_2_) | copy-start | bytes 1572868
  28.2 27.6 %collective-permute-start.16 = (bf16[256,1024]{1,0:T(8,128)(2,1)S(1)}, bf16[256,1024]{1,0:T(8,128)(2,1)S(1)}, u32[]{:S(2)}, u32[]{:S(2)}) collective-permute-start(bf16[256,1024]{1,0:T(8,128)(2,1)S(1)} %collective-permute-done.15.refs_2_), channel_id=1, source_target_pairs={{0,1},{1,2},{2,3},{3,0},{4,5},{5,6},{6,7},{7,4},{8,9},{9,10},{10,1... | collective-permute-start | bytes 1572872 | tf_op jit(solution)/shard_map/ppermute | solution.py:302
  30.2 33.8 %copy-start.5 = (bf16[128,1024]{1,0:T(8,128)(2,1)}, bf16[128,1024]{1,0:T(8,128)(2,1)S(1)}, u32[]{:S(2)}) copy-start(bf16[128,1024]{1,0:T(8,128)(2,1)S(1)} %get-tuple-element.13.refs_0_) | copy-start | bytes 786436
  30.3 33.8 %copy-start.6 = (bf16[128,1024]{1,0:T(8,128)(2,1)}, bf16[128,1024]{1,0:T(8,128)(2,1)S(1)}, u32[]{:S(2)}) copy-start(bf16[128,1024]{1,0:T(8,128)(2,1)S(1)} %get-tuple-element.14.refs_0_) | copy-start | bytes 786436
  30.3 20.1 %collective-permute-start = (bf16[128,1024]{1,0:T(8,128)(2,1)S(1)}, bf16[128,1024]{1,0:T(8,128)(2,1)}, u32[]{:S(2)}, u32[]{:S(2)}) collective-permute-start(bf16[128,1024]{1,0:T(8,128)(2,1)S(1)} %get-tuple-element.14.refs_0_), channel_id=1, source_target_pairs={{0,1},{1,2},{2,3},{3,0},{4,5},{5,6},{6,7},{7,4},{8,9},{9,10},{10,1... | collective-permute-start | bytes 786440 | tf_op jit(solution)/shard_map/ppermute | solution.py:302
  31.9 24.0 %collective-permute-start.3 = (bf16[128,1024]{1,0:T(8,128)(2,1)S(1)}, bf16[128,1024]{1,0:T(8,128)(2,1)S(1)}, u32[]{:S(2)}, u32[]{:S(2)}) collective-permute-start(bf16[128,1024]{1,0:T(8,128)(2,1)S(1)} %get-tuple-element.13.refs_0_), channel_id=1, source_target_pairs={{0,1},{1,2},{2,3},{3,0},{4,5},{5,6},{6,7},{7,4},{8,9},{9,10},{10,1... | collective-permute-start | bytes 786440 | tf_op jit(solution)/shard_map/ppermute | solution.py:302
  50.3 15.1 %collective-permute-start.1 = (bf16[128,1024]{1,0:T(8,128)(2,1)}, bf16[128,1024]{1,0:T(8,128)(2,1)}, u32[]{:S(2)}, u32[]{:S(2)}) collective-permute-start(bf16[128,1024]{1,0:T(8,128)(2,1)} %collective-permute-done.refs_1_), channel_id=1, source_target_pairs={{0,1},{1,2},{2,3},{3,0},{4,5},{5,6},{6,7},{7,4},{8,9},{9,10},{10,1... | collective-permute-start | bytes 786440 | tf_op jit(solution)/shard_map/ppermute | solution.py:302
  55.9 12.0 %collective-permute-start.4 = (bf16[128,1024]{1,0:T(8,128)(2,1)S(1)}, bf16[128,1024]{1,0:T(8,128)(2,1)}, u32[]{:S(2)}, u32[]{:S(2)}) collective-permute-start(bf16[128,1024]{1,0:T(8,128)(2,1)S(1)} %collective-permute-done.3.refs_1_), channel_id=1, source_target_pairs={{0,1},{1,2},{2,3},{3,0},{4,5},{5,6},{6,7},{7,4},{8,9},{9,10},{10,1... | collective-permute-start | bytes 786440 | tf_op jit(solution)/shard_map/ppermute | solution.py:302
  56.7 15.5 %copy-start.7 = (bf16[1,2,256,1024]{3,2,1,0:T(8,128)(2,1)S(1)}, bf16[1,2,256,1024]{3,2,1,0:T(8,128)(2,1)}, u32[]{:S(2)}) copy-start(bf16[1,2,256,1024]{3,2,1,0:T(8,128)(2,1)} %param.9) | copy-start | bytes 3145732
  56.7 17.0 %copy-start.22 = (s32[32]{0:T(128)S(1)}, s32[32]{0:T(128)}, u32[]{:S(2)}) copy-start(s32[32]{0:T(128)} %param.11) | copy-start | bytes 388
  64.1 29.3 %collective-permute-start.18 = (bf16[256,1024]{1,0:T(8,128)(2,1)}, bf16[256,1024]{1,0:T(8,128)(2,1)S(1)}, u32[]{:S(2)}, u32[]{:S(2)}) collective-permute-start(bf16[256,1024]{1,0:T(8,128)(2,1)} %shard_map.76.refs_4_), channel_id=1, source_target_pairs={{0,8},{4,12},{8,16},{12,20},{16,24},{20,28},{1,9},{5,13},{9,17},{1... | collective-permute-start | bytes 1572872 | tf_op jit(solution)/shard_map/ppermute | solution.py:251
  65.4 14.1 %collective-permute-start.2 = (bf16[128,1024]{1,0:T(8,128)(2,1)}, bf16[128,1024]{1,0:T(8,128)(2,1)S(1)}, u32[]{:S(2)}, u32[]{:S(2)}) collective-permute-start(bf16[128,1024]{1,0:T(8,128)(2,1)} %collective-permute-done.1.refs_2_), channel_id=1, source_target_pairs={{0,1},{1,2},{2,3},{3,0},{4,5},{5,6},{6,7},{7,4},{8,9},{9,10},{10,1... | collective-permute-start | bytes 786440 | tf_op jit(solution)/shard_map/ppermute | solution.py:302
  67.9 24.2 %collective-permute-start.5 = (bf16[128,1024]{1,0:T(8,128)(2,1)}, bf16[128,1024]{1,0:T(8,128)(2,1)S(1)}, u32[]{:S(2)}, u32[]{:S(2)}) collective-permute-start(bf16[128,1024]{1,0:T(8,128)(2,1)} %collective-permute-done.4.refs_2_), channel_id=1, source_target_pairs={{0,1},{1,2},{2,3},{3,0},{4,5},{5,6},{6,7},{7,4},{8,9},{9,10},{10,1... | collective-permute-start | bytes 786440 | tf_op jit(solution)/shard_map/ppermute | solution.py:302
  73.0 35.4 %collective-permute-start.19 = (bf16[256,1024]{1,0:T(8,128)(2,1)}, bf16[256,1024]{1,0:T(8,128)(2,1)S(1)}, u32[]{:S(2)}, u32[]{:S(2)}) collective-permute-start(bf16[256,1024]{1,0:T(8,128)(2,1)} %shard_map.76.refs_4_), channel_id=1, source_target_pairs={{28,20},{29,21},{30,22},{31,23}} | collective-permute-start | bytes 1572872 | tf_op jit(solution)/shard_map/ppermute | solution.py:320
  87.4 20.5 %collective-permute-start.6 = (bf16[128,1024]{1,0:T(8,128)(2,1)}, bf16[128,1024]{1,0:T(8,128)(2,1)S(1)}, u32[]{:S(2)}, u32[]{:S(2)}) collective-permute-start(bf16[128,1024]{1,0:T(8,128)(2,1)} %shard_map.74.refs_4_), channel_id=1, source_target_pairs={{8,0},{12,4},{16,8},{20,12},{24,16},{28,20},{9,1},{13,5},{17,9},{2... | collective-permute-start | bytes 786440 | tf_op jit(solution)/shard_map/ppermute | solution.py:251
  92.0 32.6 %collective-permute-start.17 = (bf16[256,1024]{1,0:T(8,128)(2,1)S(1)}, bf16[256,1024]{1,0:T(8,128)(2,1)S(1)}, u32[]{:S(2)}, u32[]{:S(2)}) collective-permute-start(bf16[256,1024]{1,0:T(8,128)(2,1)S(1)} %copy-done), channel_id=1, source_target_pairs={{0,4},{4,0},{8,12},{12,8},{16,20},{20,16},{24,28},{28,24},{1,5},{5... | collective-permute-start | bytes 1572872 | tf_op jit(solution)/shard_map/ppermute | solution.py:256
  92.1 34.5 %collective-permute-start.21 = (bf16[256,1024]{1,0:T(8,128)(2,1)S(1)}, bf16[256,1024]{1,0:T(8,128)(2,1)S(1)}, u32[]{:S(2)}, u32[]{:S(2)}) collective-permute-start(bf16[256,1024]{1,0:T(8,128)(2,1)S(1)} %copy-done), channel_id=1, source_target_pairs={{4,16},{12,24},{5,17},{13,25},{6,18},{14,26},{7,19},{15,27}} | collective-permute-start | bytes 1572872 | tf_op jit(solution)/shard_map/ppermute | solution.py:268
  93.4 19.0 %copy-start.2 = (bf16[256,1024]{1,0:T(8,128)(2,1)}, bf16[256,1024]{1,0:T(8,128)(2,1)S(1)}, u32[]{:S(2)}) copy-start(bf16[256,1024]{1,0:T(8,128)(2,1)S(1)} %collective-permute-done.18.refs_5_) | copy-start | bytes 1572868
  93.4 33.2 %collective-permute-start.20 = (bf16[256,1024]{1,0:T(8,128)(2,1)S(1)}, bf16[256,1024]{1,0:T(8,128)(2,1)S(1)}, u32[]{:S(2)}, u32[]{:S(2)}) collective-permute-start(bf16[256,1024]{1,0:T(8,128)(2,1)S(1)} %collective-permute-done.18.refs_5_), channel_id=1, source_target_pairs={{0,4},{4,0},{8,12},{12,8},{16,20},{20,16},{24,28},{28,24},{1,5},{5... | collective-permute-start | bytes 1572872 | tf_op jit(solution)/shard_map/ppermute | solution.py:256
  107.9 31.5 %copy-start.16 = (bf16[128,1024]{1,0:T(8,128)(2,1)}, bf16[128,1024]{1,0:T(8,128)(2,1)S(1)}, u32[]{:S(2)}) copy-start(bf16[128,1024]{1,0:T(8,128)(2,1)S(1)} %collective-permute-done.6.refs_6_) | copy-start | bytes 786436
  108.0 9.9 %collective-permute-start.10 = (bf16[128,1024]{1,0:T(8,128)(2,1)S(1)}, bf16[128,1024]{1,0:T(8,128)(2,1)S(1)}, u32[]{:S(2)}, u32[]{:S(2)}) collective-permute-start(bf16[128,1024]{1,0:T(8,128)(2,1)S(1)} %copy-done.4), channel_id=1, source_target_pairs={{0,4},{4,0},{8,12},{12,8},{16,20},{20,16},{24,28},{28,24},{1,5},{5... | collective-permute-start | bytes 786440 | tf_op jit(solution)/shard_map/ppermute | solution.py:256
  108.4 9.5 %collective-permute-start.7 = (bf16[128,1024]{1,0:T(8,128)(2,1)}, bf16[128,1024]{1,0:T(8,128)(2,1)}, u32[]{:S(2)}, u32[]{:S(2)}) collective-permute-start(bf16[128,1024]{1,0:T(8,128)(2,1)} %shard_map.75.refs_5_), channel_id=1, source_target_pairs={{8,0},{12,4},{16,8},{20,12},{24,16},{28,20},{9,1},{13,5},{17,9},{2... | collective-permute-start | bytes 786440 | tf_op jit(solution)/shard_map/ppermute | solution.py:251
  117.9 21.5 %collective-permute-start.11 = (bf16[128,1024]{1,0:T(8,128)(2,1)}, bf16[128,1024]{1,0:T(8,128)(2,1)S(1)}, u32[]{:S(2)}, u32[]{:S(2)}) collective-permute-start(bf16[128,1024]{1,0:T(8,128)(2,1)} %shard_map.75.refs_5_), channel_id=1, source_target_pairs={{0,4},{4,0},{8,12},{12,8},{16,20},{20,16},{24,28},{28,24},{1,5},{5... | collective-permute-start | bytes 786440 | tf_op jit(solution)/shard_map/ppermute | solution.py:256
  117.9 21.6 %copy-start.17 = (bf16[128,1024]{1,0:T(8,128)(2,1)}, bf16[128,1024]{1,0:T(8,128)(2,1)S(1)}, u32[]{:S(2)}) copy-start(bf16[128,1024]{1,0:T(8,128)(2,1)S(1)} %collective-permute-done.10.refs_10_) | copy-start | bytes 786436
  117.9 21.5 %collective-permute-start.12 = (bf16[128,1024]{1,0:T(8,128)(2,1)S(1)}, bf16[128,1024]{1,0:T(8,128)(2,1)S(1)}, u32[]{:S(2)}, u32[]{:S(2)}) collective-permute-start(bf16[128,1024]{1,0:T(8,128)(2,1)S(1)} %copy-done.4), channel_id=1, source_target_pairs={{16,4},{24,12},{17,5},{25,13},{18,6},{26,14},{19,7},{27,15}} | collective-permute-start | bytes 786440 | tf_op jit(solution)/shard_map/ppermute | solution.py:268
  124.6 14.9 %collective-permute-start.13 = (bf16[128,1024]{1,0:T(8,128)(2,1)}, bf16[128,1024]{1,0:T(8,128)(2,1)}, u32[]{:S(2)}, u32[]{:S(2)}) collective-permute-start(bf16[128,1024]{1,0:T(8,128)(2,1)} %shard_map.75.refs_5_), channel_id=1, source_target_pairs={{16,4},{24,12},{17,5},{25,13},{18,6},{26,14},{19,7},{27,15}} | collective-permute-start | bytes 786440 | tf_op jit(solution)/shard_map/ppermute | solution.py:268
  126.6 12.9 %collective-permute-start.8 = (bf16[128,1024]{1,0:T(8,128)(2,1)S(1)}, bf16[128,1024]{1,0:T(8,128)(2,1)S(1)}, u32[]{:S(2)}, u32[]{:S(2)}) collective-permute-start(bf16[128,1024]{1,0:T(8,128)(2,1)S(1)} %collective-permute-done.6.refs_6_), channel_id=1, source_target_pairs={{0,4},{4,0},{8,12},{12,8},{16,20},{20,16},{24,28},{28,24},{1,5},{5... | collective-permute-start | bytes 786440 | tf_op jit(solution)/shard_map/ppermute | solution.py:256
  126.6 12.9 %collective-permute-start.9 = (bf16[128,1024]{1,0:T(8,128)(2,1)}, bf16[128,1024]{1,0:T(8,128)(2,1)S(1)}, u32[]{:S(2)}, u32[]{:S(2)}) collective-permute-start(bf16[128,1024]{1,0:T(8,128)(2,1)} %collective-permute-done.7.refs_7_), channel_id=1, source_target_pairs={{0,4},{4,0},{8,12},{12,8},{16,20},{20,16},{24,28},{28,24},{1,5},{5... | collective-permute-start | bytes 786440 | tf_op jit(solution)/shard_map/ppermute | solution.py:256
  (13 other events, 46.9 us)

commit v2 on v1

v2 whole, which is shorter than its diff:
```python
import functools
import math

import jax
import jax.numpy as jnp
import ml_dtypes
import numpy as np
from jax import lax
from jax.experimental import pallas as pl
from jax.experimental.pallas import tpu as pltpu
from jax.sharding import PartitionSpec as P

REACH = 3
LANES = 256
VMEM = 20 * 1024 * 1024
F32 = jnp.float32
BF16 = jnp.bfloat16
WHOLE = pl.BlockSpec(memory_space=pltpu.VMEM)
ANYWHERE = pl.BlockSpec(memory_space=pl.ANY)
SCALARS = pl.BlockSpec(memory_space=pltpu.SMEM)


def parts_of(table):
    high = table.astype(np.float32).astype(ml_dtypes.bfloat16)
    low = (table - high.astype(np.float64)).astype(np.float32).astype(ml_dtypes.bfloat16)
    return high, low


@functools.lru_cache(maxsize=None)
def tables(length):
    angle = np.outer(2 * np.arange(length) + 1, np.arange(length)) % (4 * length)
    angle = angle.astype(np.float64) * (math.pi / (2 * length))
    forward = np.concatenate([np.cos(angle), -np.sin(angle)], axis=0)
    high, low = parts_of(forward)
    stacked = np.concatenate([high, low], axis=0)
    back_high, back_low = parts_of(forward.T / length)
    return stacked, np.concatenate([back_high, back_low], axis=0)


def nn(a, b):
    return lax.dot_general(a, b, (((1,), (0,)), ((), ())), preferred_element_type=F32)


def nt(a, b):
    return lax.dot_general(a, b, (((1,), (1,)), ((), ())), preferred_element_type=F32)


def params():
    return pltpu.CompilerParams(vmem_limit_bytes=VMEM)


def lanes_at(tile):
    return pl.ds(pl.multiple_of(tile * LANES, LANES), LANES)


def prepare_kernel(*refs):
    table_ref, back_ref, taps_ref, weight_ref, gate_ref = refs[:5]
    spec_out, weight_out, gate_out, table_out, back_out, sems = refs[-6:]
    copies = [
        pltpu.make_async_copy(source, target, sems.at[at])
        for at, (source, target) in enumerate(
            [(weight_ref, weight_out), (gate_ref, gate_out), (back_ref, back_out)]
        )
    ]
    step = pl.program_id(0)

    @pl.when(step == 0)
    def _():
        for copy in copies:
            copy.start()
        table_out[...] = table_ref[...]

    length = table_ref.shape[1]
    freq = lax.broadcasted_iota(jnp.int32, (length, 1), 0)
    sign = jnp.where(freq % 2 == 0, 1.0, -1.0).astype(F32)
    lanes = lanes_at(step)
    before = None
    for part in range(REACH + 1):
        if part < REACH:
            values = taps_ref[part * length : (part + 1) * length, :]
            high = values.astype(BF16)
            low = (values - high.astype(F32)).astype(BF16)
            both = nn(table_ref[...], high)
            full = both[: 2 * length] + (both[2 * length :] + nn(table_ref[: 2 * length, :], low))
            now = (full[:length], -full[length:])
        else:
            now = None
        if before is None:
            real, imag = now
        else:
            real, imag = sign * before[1], -sign * before[0]
            if now is not None:
                real, imag = now[0] + real, now[1] + imag
        spec_out[part, :length, lanes] = real
        spec_out[part, length:, lanes] = imag
        before = now

    @pl.when(step == pl.num_programs(0) - 1)
    def _():
        for copy in copies:
            copy.wait()


def prepare(table, back, taps, weight, gate, after):
    count, width = taps.shape
    length = count // REACH
    return pl.pallas_call(
        prepare_kernel,
        grid=(width // LANES,),
        out_shape=(
            pltpu.VMEM((REACH + 1, 2 * length, width), F32),
            pltpu.VMEM(weight.shape, BF16),
            pltpu.VMEM(gate.shape, BF16),
            pltpu.VMEM(table.shape, BF16),
            pltpu.VMEM(back.shape, BF16),
        ),
        in_specs=[
            pl.BlockSpec((4 * length, length), lambda c: (0, 0)),
            ANYWHERE,
            pl.BlockSpec((count, LANES), lambda c: (0, c)),
            ANYWHERE,
            ANYWHERE,
        ]
        + [ANYWHERE] * len(after),
        out_specs=(WHOLE,) * 5,
        scratch_shapes=[pltpu.SemaphoreType.DMA((3,))],
        compiler_params=params(),
        cost_estimate=pl.CostEstimate(
            flops=2 * 3 * 2 * count * length * width,
            bytes_accessed=4 * (count * width + 8 * length * width),
            transcendentals=0,
        ),
    )(table, back, taps, weight, gate, *after)


def project_kernel(steps, slot, start, first, last, place_ref, *refs):
    shards, refs = refs[: len(steps)], refs[len(steps) :]
    weight_ref, gate_ref, out_ref = refs[0], refs[1], refs[-1]
    before_ref = None if first else refs[2]
    rows, depth = shards[0].shape
    count = weight_ref.shape[1] // depth
    for tile in range(weight_ref.shape[0] // LANES):
        lanes = pl.ds(tile * LANES, LANES)
        total = None if first else before_ref[:, lanes]
        for shard, step in zip(shards, steps):
            at = lax.rem(place_ref[0] + count - step, count)
            features = pl.ds(pl.multiple_of(at * depth, depth), depth)
            part = nt(shard[...], weight_ref[lanes, features])
            total = part if total is None else total + part
        if last:
            gate = gate_ref[0, slot, start : start + rows, lanes].astype(F32)
            out_ref[:, lanes] = (total * gate).astype(BF16)
        else:
            out_ref[:, lanes] = total


def project(place, shards, steps, weight, gate, slot, start, before=None, last=True, after=()):
    rows, depth = shards[0].shape
    width = weight.shape[0]
    operands = [place, *shards, weight, gate]
    if before is not None:
        operands.append(before)
    body = functools.partial(project_kernel, steps, slot, start, before is None, last)
    return pl.pallas_call(
        body,
        out_shape=pltpu.VMEM((rows, width), BF16 if last else F32),
        in_specs=[SCALARS] + [WHOLE] * (len(operands) - 1) + [ANYWHERE] * len(after),
        out_specs=WHOLE,
        compiler_params=params(),
        cost_estimate=pl.CostEstimate(
            flops=2 * rows * depth * len(shards) * width,
            bytes_accessed=2 * (rows + width) * depth * len(shards),
            transcendentals=0,
        ),
    )(*operands, *after)


class Conv:
    def __init__(self, facts, table, back, spectra):
        self.facts, self.table, self.back, self.spectra = facts, table, back, spectra
        self.length = table.shape[1]
        self.lanes = lanes_at(pl.program_id(0))
        self.row = lax.broadcasted_iota(jnp.int32, (self.length, LANES), 0)

    def joined(self, pieces):
        tiles = [piece[:, self.lanes] for piece in pieces]
        return tiles[0] if len(tiles) == 1 else jnp.concatenate(tiles, axis=0)

    def within(self, low, high):
        return (self.row >= low) & (self.row < high)

    def term(self, values, low, high, distance):
        length = self.length
        kept = jnp.where(self.within(low, high), values.astype(F32), 0.0).astype(BF16)
        both = nn(self.table[...], kept)
        full = both[: 2 * length] + both[2 * length :]
        real, imag = full[:length], full[length:]
        k_real = self.spectra[distance, :length, self.lanes]
        k_imag = self.spectra[distance, length:, self.lanes]
        return k_real * real - k_imag * imag, k_real * imag + k_imag * real

    def signal(self, real, imag):
        total = jnp.concatenate([real.astype(BF16), imag.astype(BF16)], axis=0)
        both = nn(self.back[...], total)
        return both[: self.length] + both[self.length :]

    def far_terms(self, acc, values_of):
        for distance in range(1, REACH + 1):
            reach = self.facts[1 + distance]

            @pl.when(reach > 0)
            def _(distance=distance, reach=reach):
                real, imag = self.term(values_of(distance), 0, reach, distance)
                acc[: self.length, :] += real
                acc[self.length :, :] += imag

    def inner_documents(self, own, read, write):
        first_end, last_start = self.facts[0], self.facts[1]

        @pl.when(last_start > 0)
        def _():
            signal = self.signal(*self.term(own, 0, first_end, 0))
            write(jnp.where(self.row < first_end, signal, read()))

        @pl.when(last_start > first_end)
        def _():
            signal = self.signal(*self.term(own, first_end, last_start, 0))
            write(jnp.where(self.within(first_end, last_start), signal, read()))

    def halo(self, pieces, distance):
        count = len(pieces) // 4
        two, swapped, mate, far = (pieces[at * count : (at + 1) * count] for at in range(4))
        if distance == 2:
            return self.joined(two)
        inner = self.facts[5] == 1
        if distance == 1:
            return jnp.where(inner, self.joined(mate), self.joined(swapped))
        return jnp.where(inner, self.joined(swapped), self.joined(far))


def upper_kernel(facts_ref, table_ref, back_ref, spec_ref, own_ref, *refs):
    halos, (out_ref, acc_ref) = refs[:4], refs[-2:]
    conv = Conv(facts_ref, table_ref, back_ref, spec_ref)
    own = conv.joined([own_ref])
    real, imag = conv.term(own, facts_ref[1], conv.length, 0)
    acc_ref[: conv.length, :] = real
    acc_ref[conv.length :, :] = imag
    conv.far_terms(acc_ref, lambda distance: conv.halo(halos, distance))
    out_ref[0, 0] = conv.signal(acc_ref[: conv.length, :], acc_ref[conv.length :, :])

    def write(value):
        out_ref[0, 0] = value

    conv.inner_documents(own, lambda: out_ref[0, 0], write)


def own_kernel(pieces, facts_ref, table_ref, back_ref, spec_ref, *refs):
    own_refs, out_ref = refs[:pieces], refs[-1]
    conv = Conv(facts_ref, table_ref, back_ref, spec_ref)
    own = conv.joined(own_refs)
    out_ref[:, conv.lanes] = conv.signal(*conv.term(own, facts_ref[1], conv.length, 0))

    def write(value):
        out_ref[:, conv.lanes] = value

    conv.inner_documents(own, lambda: out_ref[:, conv.lanes], write)


def far_kernel(pieces, facts_ref, table_ref, back_ref, spec_ref, *refs):
    near_ref, upper_ref, mate_ref, two_ref, fold_ref = refs[:5]
    halos = refs[5 : 5 + 4 * pieces]
    out_ref, acc_ref = refs[-2:]
    conv = Conv(facts_ref, table_ref, back_ref, spec_ref)
    role = facts_ref[6]

    def values_of(distance):
        value = conv.halo(halos, distance)
        if distance == 1:
            return jnp.where(role == 1, conv.joined([upper_ref]), value)
        if distance == 2:
            return jnp.where((role == 1) | (role == 2), conv.joined([mate_ref]), value)
        value = jnp.where(role == 1, conv.joined([two_ref]), value)
        value = jnp.where(role == 2, conv.joined([upper_ref]), value)
        return jnp.where(role == 3, conv.joined([fold_ref]), value)

    reaches = facts_ref[2] > 0

    @pl.when(reaches)
    def _():
        acc_ref[...] = jnp.zeros_like(acc_ref)
        conv.far_terms(acc_ref, values_of)
        signal = conv.signal(acc_ref[: conv.length, :], acc_ref[conv.length :, :])
        kept = jnp.where(conv.row >= facts_ref[1], signal, 0.0)
        out_ref[0, 0] = near_ref[:, conv.lanes] + kept

    @pl.when(jnp.logical_not(reaches))
    def _():
        out_ref[0, 0] = near_ref[:, conv.lanes]


def conv_call(body, tabs, facts, arrays, out_shape, out_spec, scratch, terms, after=(), result=None):
    table, back, spectra = tabs
    length = table.shape[1]
    width = spectra.shape[2]
    operands = [facts, table, back, spectra, *arrays]
    specs = [SCALARS] + [WHOLE] * (len(operands) - 1)
    operands.extend(after)
    specs += [ANYWHERE] * len(after)
    aliases = {}
    if result is not None:
        aliases = {len(operands): 0}
        operands.append(result)
        specs.append(ANYWHERE)
    return pl.pallas_call(
        body,
        grid=(width // LANES,),
        out_shape=out_shape,
        in_specs=specs,
        out_specs=out_spec,
        scratch_shapes=[pltpu.VMEM((2 * length, LANES), F32)] * scratch,
        input_output_aliases=aliases,
        compiler_params=params(),
        cost_estimate=pl.CostEstimate(
            flops=8 * terms * length * length * width,
            bytes_accessed=4 * length * width,
            transcendentals=0,
        ),
    )(*operands)


def shifted(value, steps):
    count = lax.axis_size("ctx")
    initial, last = (max(0, -steps), min(count, count - steps))
    return lax.ppermute(value, "ctx", [(source, source + steps) for source in range(initial, last)])


def core_swapped(value):
    count = lax.axis_size("ctx")
    return lax.ppermute(value, "ctx", [(source, source ^ 1) for source in range(count)])


def halo_of(value, way):
    count = lax.axis_size("ctx")
    two = shifted(value, 2 * way)
    outer = 1 if way > 0 else 0
    far = [
        (source, source + 3 * way)
        for source in range(outer, count, 2)
        if 0 <= source + 3 * way < count
    ]
    return [two, core_swapped(two), core_swapped(value), lax.ppermute(value, "ctx", far)]


def block_facts(doc_starts, block, length, end, inner, role):
    start = block * length

    def after(where):
        return jnp.min(jnp.where(doc_starts > where, doc_starts, end))

    first_end = jnp.clip(after(start) - start, 0, length)
    last_start = jnp.max(jnp.where(doc_starts <= start + length - 1, doc_starts, 0)) - start
    last_start = jnp.clip(last_start, 0, length)
    reaches = after(start + length - 1) - start
    facts = [first_end, last_start]
    facts += [jnp.clip(reaches - distance * length, 0, length) for distance in range(1, REACH + 1)]
    facts += [inner, role]
    return jnp.stack(facts).astype(jnp.int32)


def on_device(grad_out, out_weight, gate, filter_taps, doc_starts):
    pairs = lax.axis_size("ctx")
    place = lax.axis_index("ctx")
    length = grad_out.shape[2]
    width = out_weight.shape[0]
    blocks = 2 * pairs
    half = length // 2
    count = lax.axis_size("ch")
    lane = lax.axis_index("ch").astype(jnp.int32)[None]
    around = [(source, (source + 1) % count) for source in range(count)]
    everything = tuple(range(count))

    def ring(piece):
        shards = [piece]
        for _ in range(1, count):
            shards.append(lax.ppermute(shards[-1], "ch", around))
        return shards

    upper_in = ring(grad_out[0, 1])
    first_in = ring(grad_out[0, 0, :half])
    second_in = ring(grad_out[0, 0, half:])

    odd = place % 2
    role = jnp.where(place >= pairs - 3, pairs - place, 0)
    end = blocks * length
    lower_facts = block_facts(doc_starts, place, length, end, 1 - odd, role)
    upper_facts = block_facts(doc_starts, blocks - 1 - place, length, end, odd, role)
    table, back = (jnp.asarray(one) for one in tables(length))
    spectra, weight, gates, table, back = prepare(
        table, back, filter_taps, out_weight, gate, [lower_facts, upper_facts]
    )
    tabs = (table, back, spectra)

    upper = project(lane, upper_in, everything, weight, gates, 1, 0)
    upper_halo = halo_of(upper, 1)
    fold = lax.ppermute(upper, "ctx", [(pairs - 1, pairs - 3)])
    out_shape = jax.ShapeDtypeStruct((1, 2, length, width), F32)
    result = conv_call(
        upper_kernel,
        tabs,
        upper_facts,
        [upper, *upper_halo],
        out_shape,
        pl.BlockSpec((1, 1, length, LANES), lambda c: (0, 1, 0, c)),
        1,
        6,
    )

    first = project(lane, first_in, everything, weight, gates, 0, 0)
    first_halo = halo_of(first, -1)
    partial = project(
        lane, second_in[:-1], everything[:-1], weight, gates, 0, half, last=False
    )
    second = project(
        lane, second_in[-1:], everything[-1:], weight, gates, 0, half, partial, after=[result]
    )
    second_halo = halo_of(second, -1)
    near = conv_call(
        functools.partial(own_kernel, 2),
        tabs,
        lower_facts,
        [first, second],
        pltpu.VMEM((length, width), F32),
        WHOLE,
        0,
        4,
    )
    two, _, mate, _ = upper_halo
    halos = [piece for both in zip(first_halo, second_halo) for piece in both]
    return conv_call(
        functools.partial(far_kernel, 2),
        tabs,
        lower_facts,
        [near, upper, mate, two, fold, *halos],
        out_shape,
        pl.BlockSpec((1, 1, length, LANES), lambda c: (0, 0, 0, c)),
        1,
        4,
        result=result,
    )


def solution(mesh):
    in_specs = (
        P("ctx", None, None, "ch"),
        P("ch", None),
        P("ctx", None, None, "ch"),
        P(None, "ch"),
        P(),
    )
    out_specs = P("ctx", None, None, "ch")
    return jax.shard_map(
        on_device, mesh=mesh, in_specs=in_specs, out_specs=out_specs, check_vma=False
    )
```

time: 154 us -> 132 us (0.86)
  the two profiles are of different devices: /device:TPU:14 before, /device:TPU:3 now
where the time goes in v2:
time: 132 us; the launch traced here: 131 us
  waiting for transfers between devices  52.3 us (40%)
  Pallas kernels  35.2 us (27%)
  starting transfers between devices  26.8 us (20%)
  local copies, waits for them, and re-layouts  11.5 us (9%)
  between operations  4.09 us (3%)
  other arithmetic  1.44 us (1%)
    ppermute x9, waiting for transfers between devices, ring(): shards.append(lax.ppermute(shards[-1], 'ch', around))  46.5 us
    pallas_call x3, Pallas kernels, conv_call(): pl.pallas_call(body, grid=(width // LANES,), out_shape=out_shape, in_spec...  22.5 us
    ppermute x6, starting transfers between devices, core_swapped(): lax.ppermute(value, 'ctx', [(source, source ^ 1) for source in range(coun...  12.6 us
    unnamed x14, local copies, waits for them, and re-layouts  10.2 us
    pallas_call x4, Pallas kernels, project(): pl.pallas_call(body, out_shape=pltpu.VMEM((rows, width), BF16 if last els...  8.31 us
    ppermute x3, starting transfers between devices, shifted(): lax.ppermute(value, 'ctx', [(source, source + steps) for source in range(...  7.64 us
    ppermute x3, waiting for transfers between devices, shifted(): lax.ppermute(value, 'ctx', [(source, source + steps) for source in range(...  5.72 us
    pallas_call x1, Pallas kernels, prepare(): pl.pallas_call(prepare_kernel, grid=(width // LANES,), out_shape=(pltpu.V...  4.36 us
  transfers between devices with their start and end apart: 22, of which 7 were waited for; matrix products, arithmetic and copies ran while one was open for 1% of the time, Pallas kernels for 21%

profile of v2, /device:TPU:3, one launch (start us, length us, event | category | flops | bytes accessed | tf_op | source)
XLA Modules:
  0.0 131.2 jit_solution(16086118229625722902)
XLA Ops:
  0.0 1.1 slice_bitcast_fusion.refs_0_
  1.1 1.3 %collective-permute-start.6 = (bf16[256,1024]{1,0:T(8,128)(2,1)S(1)}, bf16[256,1024]{1,0:T(8,128)(2,1)S(1)}, u32[]{:S(2)}, u32[]{:S(2)}) collective-permute-start(bf16[256,1024]{1,0:T(8,128)(2,1)S(1)} %slice_bitcast_fusion.refs_0_), channel_id=1, source_target_pairs={{0,1},{1,2},{2,3},{3,0},{4,5},{5,6},{6,7},{7,4},{8,9},{9,10},{10,1... | collective-permute-start | bytes 1572872 | tf_op jit(solution)/shard_map/ppermute | solution.py:385
  2.4 13.4 %collective-permute-done.6.refs_1_ = bf16[256,1024]{1,0:T(8,128)(2,1)S(1)} collective-permute-done((bf16[256,1024]{1,0:T(8,128)(2,1)S(1)}, bf16[256,1024]{1,0:T(8,128)(2,1)S(1)}, u32[]{:S(2)}, u32[]{:S(2)}) %collective-permute-start.6) | collective-permute-done | bytes 524320 | tf_op jit(solution)/shard_map/ppermute | solution.py:385
  15.9 13.7 %collective-permute-done.7.refs_2_ = bf16[256,1024]{1,0:T(8,128)(2,1)S(1)} collective-permute-done((bf16[256,1024]{1,0:T(8,128)(2,1)S(1)}, bf16[256,1024]{1,0:T(8,128)(2,1)S(1)}, u32[]{:S(2)}, u32[]{:S(2)}) %collective-permute-start.7) | collective-permute-done | bytes 524320 | tf_op jit(solution)/shard_map/ppermute | solution.py:385
  29.6 1.4 %fusion.5 = (s32[]{:T(128)}, s32[]{:T(128)}, s32[]{:T(128)}, s32[]{:T(128)}, s32[]{:T(128)}, /*index=5*/s32[]{:T(128)}) fusion(s32[32]{0:T(128)} %param.11, s32[]{:T(128)S(6)} %sub.64, s32[]{:T(128)S(6)} %sub.54, s32[]{:T(128)S(6)} %mul.6, s32[]{:T(128)S(6)} %mul.7), kind=kLoop, calls=%fused_computation.14 | loop fusion | flops 570 | bytes 168 | tf_op jit(solution)/shard_map/reduce_min | solution.py:358
  35.0 3.4 %copy-done.1 = bf16[1024,4096]{1,0:T(8,128)(2,1)S(1)} copy-done((bf16[1024,4096]{1,0:T(8,128)(2,1)S(1)}, bf16[1024,4096]{1,0:T(8,128)(2,1)}, u32[]{:S(2)}) %copy-start.1) | copy-done | bytes 8388632
  38.4 1.9 %copy-done.2 = f32[768,1024]{1,0:T(8,128)S(1)} copy-done((f32[768,1024]{1,0:T(8,128)S(1)}, f32[768,1024]{1,0:T(8,128)}, u32[]{:S(2)}) %copy-start.2) | copy-done | bytes 3145752
  40.3 1.2 copy-done.3
  41.5 1.0 copy-done.4
  42.6 1.0 copy-done.5
  43.6 4.4 %shard_map.73 = (f32[4,512,1024]{2,1,0:T(8,128)S(1)}, bf16[1024,4096]{1,0:T(8,128)(2,1)S(1)}, bf16[1,2,256,1024]{3,2,1,0:T(8,128)(2,1)S(1)}, bf16[1024,256]{1,0:T(8,128)(2,1)S(1)}, bf16[512,512]{1,0:T(8,128)(2,1)S(1)}) custom-call(bf16[1024,256]{1,0:T(8,128)(2,1)S(1)} %copy-done.4, bf16[512,512]{1,0:T(8,128)(2,1)S(1)} %copy-done.5, ...), custom_call_target="tpu_custom_call" | custom-call | flops 2415919104 | bytes 11534336 | tf_op jit(solution)/shard_map/pallas_call | solution.py:107
  48.0 2.4 %shard_map.76.own_ref.refs_1_ = bf16[256,1024]{1,0:T(8,128)(2,1)S(1)} custom-call(s32[1]{0:T(128)} %bitcast.13.place_ref, bf16[256,1024]{1,0:T(8,128)(2,1)S(1)} %slice_bitcast_fusion.refs_0_, bf16[256,1024]{1,0:T(8,128)(2,1)S(1)} %collective-permute-done.6.refs_1_, bf16[256,1024]{1,0:T(8,128)(2,1)S(1)} %collective-permute-done.7.refs_2_, ...), custom_call_target="tpu_custom_call" | custom-call | flops 2147483648 | bytes 10485760 | tf_op jit(solution)/shard_map/pallas_call | solution.py:164
  50.4 3.1 %collective-permute-start.9 = (bf16[256,1024]{1,0:T(8,128)(2,1)S(1)}, bf16[256,1024]{1,0:T(8,128)(2,1)S(1)}, u32[]{:S(2)}, u32[]{:S(2)}) collective-permute-start(bf16[256,1024]{1,0:T(8,128)(2,1)S(1)} %shard_map.76.own_ref.refs_1_), channel_id=1, source_target_pairs={{0,8},{4,12},{8,16},{12,20},{16,24},{20,28},{1,9},{5,13},{9,17},{1... | collective-permute-start | bytes 1572872 | tf_op jit(solution)/shard_map/ppermute | solution.py:334
  53.7 6.9 %collective-permute-done.refs_1_ = bf16[128,1024]{1,0:T(8,128)(2,1)S(1)} collective-permute-done((bf16[128,1024]{1,0:T(8,128)(2,1)S(1)}, bf16[128,1024]{1,0:T(8,128)(2,1)S(1)}, u32[]{:S(2)}, u32[]{:S(2)}) %collective-permute-start) | collective-permute-done | bytes 262176 | tf_op jit(solution)/shard_map/ppermute | solution.py:385
  60.6 6.7 %collective-permute-start.11 = (bf16[256,1024]{1,0:T(8,128)(2,1)S(1)}, bf16[256,1024]{1,0:T(8,128)(2,1)S(1)}, u32[]{:S(2)}, u32[]{:S(2)}) collective-permute-start(bf16[256,1024]{1,0:T(8,128)(2,1)S(1)} %shard_map.76.own_ref.refs_1_), channel_id=1, source_target_pairs={{0,4},{4,0},{8,12},{12,8},{16,20},{20,16},{24,28},{28,24},{1,5},{5... | collective-permute-start | bytes 1572872 | tf_op jit(solution)/shard_map/ppermute | solution.py:339
  67.3 1.3 collective-permute-start.12
  69.2 2.6 %collective-permute-done.1.refs_2_ = bf16[128,1024]{1,0:T(8,128)(2,1)S(1)} collective-permute-done((bf16[128,1024]{1,0:T(8,128)(2,1)S(1)}, bf16[128,1024]{1,0:T(8,128)(2,1)S(1)}, u32[]{:S(2)}, u32[]{:S(2)}) %collective-permute-start.1) | collective-permute-done | bytes 262176 | tf_op jit(solution)/shard_map/ppermute | solution.py:385
  71.8 6.5 %collective-permute-done.4.refs_2_ = bf16[128,1024]{1,0:T(8,128)(2,1)S(1)} collective-permute-done((bf16[128,1024]{1,0:T(8,128)(2,1)S(1)}, bf16[128,1024]{1,0:T(8,128)(2,1)S(1)}, u32[]{:S(2)}, u32[]{:S(2)}) %collective-permute-start.4) | collective-permute-done | bytes 262176 | tf_op jit(solution)/shard_map/ppermute | solution.py:385
  78.2 2.2 %shard_map.75.refs_3_ = f32[128,1024]{1,0:T(8,128)S(1)} custom-call(s32[1]{0:T(128)} %bitcast.13.place_ref, bf16[128,1024]{1,0:T(8,128)(2,1)S(1)} %get-tuple-element.21.refs_0_, bf16[128,1024]{1,0:T(8,128)(2,1)S(1)} %collective-permute-done.3.refs_1_, bf16[128,1024]{1,0:T(8,128)(2,1)S(1)} %collective-permute-done.4.refs_2_, ...), custom_call_target="tpu_custom_call" | custom-call | flops 805306368 | bytes 7077888 | tf_op jit(solution)/shard_map/pallas_call | solution.py:164
  80.5 3.4 %collective-permute-done.2.refs_3_ = bf16[128,1024]{1,0:T(8,128)(2,1)S(1)} collective-permute-done((bf16[128,1024]{1,0:T(8,128)(2,1)S(1)}, bf16[128,1024]{1,0:T(8,128)(2,1)S(1)}, u32[]{:S(2)}, u32[]{:S(2)}) %collective-permute-start.2) | collective-permute-done | bytes 262176 | tf_op jit(solution)/shard_map/ppermute | solution.py:385
  83.9 2.9 %shard_map.74.refs_0_ = bf16[128,1024]{1,0:T(8,128)(2,1)S(1)} custom-call(s32[1]{0:T(128)} %bitcast.13.place_ref, bf16[128,1024]{1,0:T(8,128)(2,1)S(1)} %get-tuple-element.22.refs_0_, bf16[128,1024]{1,0:T(8,128)(2,1)S(1)} %collective-permute-done.refs_1_, bf16[128,1024]{1,0:T(8,128)(2,1)S(1)} %collective-permute-done.1.refs_2_, ...), custom_call_target="tpu_custom_call" | custom-call | flops 1073741824 | bytes 9437184 | tf_op jit(solution)/shard_map/pallas_call | solution.py:164
  86.8 2.6 %collective-permute-start.14 = (bf16[128,1024]{1,0:T(8,128)(2,1)S(1)}, bf16[128,1024]{1,0:T(8,128)(2,1)S(1)}, u32[]{:S(2)}, u32[]{:S(2)}) collective-permute-start(bf16[128,1024]{1,0:T(8,128)(2,1)S(1)} %shard_map.74.refs_0_), channel_id=1, source_target_pairs={{8,0},{12,4},{16,8},{20,12},{24,16},{28,20},{9,1},{13,5},{17,9},{2... | collective-permute-start | bytes 786440 | tf_op jit(solution)/shard_map/ppermute | solution.py:334
  89.4 5.3 %collective-permute-start.18 = (bf16[128,1024]{1,0:T(8,128)(2,1)S(1)}, bf16[128,1024]{1,0:T(8,128)(2,1)S(1)}, u32[]{:S(2)}, u32[]{:S(2)}) collective-permute-start(bf16[128,1024]{1,0:T(8,128)(2,1)S(1)} %shard_map.74.refs_0_), channel_id=1, source_target_pairs={{0,4},{4,0},{8,12},{12,8},{16,20},{20,16},{24,28},{28,24},{1,5},{5... | collective-permute-start | bytes 786440 | tf_op jit(solution)/shard_map/ppermute | solution.py:339
  94.7 1.3 collective-permute-start.20
  96.7 9.8 %shard_map.77.refs_4_.refs_13_ = f32[1,2,256,1024]{3,2,1,0:T(8,128)} custom-call(s32[7]{0:T(128)S(1)} %stack.60.refs_6_.facts_ref, bf16[1024,256]{1,0:T(8,128)(2,1)S(1)} %get-tuple-element.10.table_ref, bf16[512,512]{1,0:T(8,128)(2,1)S(1)} %get-tuple-element.11.back_ref, f32[4,512,1024]{2,1,0:T(8,128)S(1)} %get-tuple-element.12.spec_ref, ...), custom_call_target="tpu_custom_call" | custom-call | flops 3221225472 | bytes 1048576 | tf_op jit(solution)/shard_map/pallas_call | solution.py:314
  106.5 1.6 %copy-done = f32[1,2,256,1024]{3,2,1,0:T(8,128)S(1)} copy-done((f32[1,2,256,1024]{3,2,1,0:T(8,128)S(1)}, f32[1,2,256,1024]{3,2,1,0:T(8,128)}, u32[]{:S(2)}) %copy-start) | copy-done | bytes 2097176
  108.1 0.8 shard_map.78.refs_1_
  108.9 1.9 %collective-permute-start.15 = (bf16[128,1024]{1,0:T(8,128)(2,1)S(1)}, bf16[128,1024]{1,0:T(8,128)(2,1)S(1)}, u32[]{:S(2)}, u32[]{:S(2)}) collective-permute-start(bf16[128,1024]{1,0:T(8,128)(2,1)S(1)} %shard_map.78.refs_1_), channel_id=1, source_target_pairs={{8,0},{12,4},{16,8},{20,12},{24,16},{28,20},{9,1},{13,5},{17,9},{2... | collective-permute-start | bytes 786440 | tf_op jit(solution)/shard_map/ppermute | solution.py:334
  111.4 1.3 collective-permute-start.21
  112.7 5.7 %collective-permute-done.15.refs_6_ = bf16[128,1024]{1,0:T(8,128)(2,1)S(1)} collective-permute-done((bf16[128,1024]{1,0:T(8,128)(2,1)S(1)}, bf16[128,1024]{1,0:T(8,128)(2,1)S(1)}, u32[]{:S(2)}, u32[]{:S(2)}) %collective-permute-start.15) | collective-permute-done | bytes 262176 | tf_op jit(solution)/shard_map/ppermute | solution.py:334
  118.5 7.1 %shard_map.79.refs_0_ = f32[256,1024]{1,0:T(8,128)S(1)} custom-call(s32[7]{0:T(128)S(1)} %stack.53.refs_5_.facts_ref, bf16[1024,256]{1,0:T(8,128)(2,1)S(1)} %get-tuple-element.10.table_ref, bf16[512,512]{1,0:T(8,128)(2,1)S(1)} %get-tuple-element.11.back_ref, f32[4,512,1024]{2,1,0:T(8,128)S(1)} %get-tuple-element.12.spec_ref, ...), custom_call_target="tpu_custom_call" | custom-call | flops 2147483648 | bytes 1048576 | tf_op jit(solution)/shard_map/pallas_call | solution.py:314
  125.6 5.6 %shard_map.80 = f32[1,2,256,1024]{3,2,1,0:T(8,128)} custom-call(s32[7]{0:T(128)S(1)} %stack.53.refs_5_.facts_ref, bf16[1024,256]{1,0:T(8,128)(2,1)S(1)} %get-tuple-element.10.table_ref, bf16[512,512]{1,0:T(8,128)(2,1)S(1)} %get-tuple-element.11.back_ref, f32[4,512,1024]{2,1,0:T(8,128)S(1)} %get-tuple-element.12.spec_ref, ...), custom_call_target="tpu_custom_call", output_to_operand_aliasing={{}: (17, {})} | custom-call | flops 2147483648 | bytes 1048576 | tf_op jit(solution)/shard_map/pallas_call | solution.py:314
  (39 shorter events, 2.2 us)
Async XLA Ops:
  1.1 14.8 %collective-permute-start.6 = (bf16[256,1024]{1,0:T(8,128)(2,1)S(1)}, bf16[256,1024]{1,0:T(8,128)(2,1)S(1)}, u32[]{:S(2)}, u32[]{:S(2)}) collective-permute-start(bf16[256,1024]{1,0:T(8,128)(2,1)S(1)} %slice_bitcast_fusion.refs_0_), channel_id=1, source_target_pairs={{0,1},{1,2},{2,3},{3,0},{4,5},{5,6},{6,7},{7,4},{8,9},{9,10},{10,1... | collective-permute-start | bytes 1572872 | tf_op jit(solution)/shard_map/ppermute | solution.py:385
  15.9 13.7 %collective-permute-start.7 = (bf16[256,1024]{1,0:T(8,128)(2,1)S(1)}, bf16[256,1024]{1,0:T(8,128)(2,1)S(1)}, u32[]{:S(2)}, u32[]{:S(2)}) collective-permute-start(bf16[256,1024]{1,0:T(8,128)(2,1)S(1)} %collective-permute-done.6.refs_1_), channel_id=1, source_target_pairs={{0,1},{1,2},{2,3},{3,0},{4,5},{5,6},{6,7},{7,4},{8,9},{9,10},{10,1... | collective-permute-start | bytes 1572872 | tf_op jit(solution)/shard_map/ppermute | solution.py:385
  29.6 18.4 %collective-permute-start.8 = (bf16[256,1024]{1,0:T(8,128)(2,1)S(1)}, bf16[256,1024]{1,0:T(8,128)(2,1)S(1)}, u32[]{:S(2)}, u32[]{:S(2)}) collective-permute-start(bf16[256,1024]{1,0:T(8,128)(2,1)S(1)} %collective-permute-done.7.refs_2_), channel_id=1, source_target_pairs={{0,1},{1,2},{2,3},{3,0},{4,5},{5,6},{6,7},{7,4},{8,9},{9,10},{10,1... | collective-permute-start | bytes 1572872 | tf_op jit(solution)/shard_map/ppermute | solution.py:385
  35.0 3.4 %copy-start.1 = (bf16[1024,4096]{1,0:T(8,128)(2,1)S(1)}, bf16[1024,4096]{1,0:T(8,128)(2,1)}, u32[]{:S(2)}) copy-start(bf16[1024,4096]{1,0:T(8,128)(2,1)} %refs_3_.1) | copy-start | bytes 25165828
  38.4 1.9 %copy-start.2 = (f32[768,1024]{1,0:T(8,128)S(1)}, f32[768,1024]{1,0:T(8,128)}, u32[]{:S(2)}) copy-start(f32[768,1024]{1,0:T(8,128)} %refs_2_.1) | copy-start | bytes 9437188
  40.3 1.2 copy-start.3
  41.5 1.0 copy-start.4
  42.6 1.0 copy-start.5
  48.0 5.5 %copy-start.6 = (bf16[1,2,256,1024]{3,2,1,0:T(8,128)(2,1)S(1)}, bf16[1,2,256,1024]{3,2,1,0:T(8,128)(2,1)}, u32[]{:S(2)}) copy-start(bf16[1,2,256,1024]{3,2,1,0:T(8,128)(2,1)} %param.7) | copy-start | bytes 3145732
  50.4 18.3 %collective-permute-start.9 = (bf16[256,1024]{1,0:T(8,128)(2,1)S(1)}, bf16[256,1024]{1,0:T(8,128)(2,1)S(1)}, u32[]{:S(2)}, u32[]{:S(2)}) collective-permute-start(bf16[256,1024]{1,0:T(8,128)(2,1)S(1)} %shard_map.76.own_ref.refs_1_), channel_id=1, source_target_pairs={{0,8},{4,12},{8,16},{12,20},{16,24},{20,28},{1,9},{5,13},{9,17},{1... | collective-permute-start | bytes 1572872 | tf_op jit(solution)/shard_map/ppermute | solution.py:334
  53.6 7.1 %collective-permute-start = (bf16[128,1024]{1,0:T(8,128)(2,1)S(1)}, bf16[128,1024]{1,0:T(8,128)(2,1)S(1)}, u32[]{:S(2)}, u32[]{:S(2)}) collective-permute-start(bf16[128,1024]{1,0:T(8,128)(2,1)S(1)} %get-tuple-element.22.refs_0_), channel_id=1, source_target_pairs={{0,1},{1,2},{2,3},{3,0},{4,5},{5,6},{6,7},{7,4},{8,9},{9,10},{10,1... | collective-permute-start | bytes 786440 | tf_op jit(solution)/shard_map/ppermute | solution.py:385
  53.6 15.1 %collective-permute-start.3 = (bf16[128,1024]{1,0:T(8,128)(2,1)S(1)}, bf16[128,1024]{1,0:T(8,128)(2,1)S(1)}, u32[]{:S(2)}, u32[]{:S(2)}) collective-permute-start(bf16[128,1024]{1,0:T(8,128)(2,1)S(1)} %get-tuple-element.21.refs_0_), channel_id=1, source_target_pairs={{0,1},{1,2},{2,3},{3,0},{4,5},{5,6},{6,7},{7,4},{8,9},{9,10},{10,1... | collective-permute-start | bytes 786440 | tf_op jit(solution)/shard_map/ppermute | solution.py:385
  60.6 11.1 %collective-permute-start.1 = (bf16[128,1024]{1,0:T(8,128)(2,1)S(1)}, bf16[128,1024]{1,0:T(8,128)(2,1)S(1)}, u32[]{:S(2)}, u32[]{:S(2)}) collective-permute-start(bf16[128,1024]{1,0:T(8,128)(2,1)S(1)} %collective-permute-done.refs_1_), channel_id=1, source_target_pairs={{0,1},{1,2},{2,3},{3,0},{4,5},{5,6},{6,7},{7,4},{8,9},{9,10},{10,1... | collective-permute-start | bytes 786440 | tf_op jit(solution)/shard_map/ppermute | solution.py:385
  60.6 28.7 %collective-permute-start.11 = (bf16[256,1024]{1,0:T(8,128)(2,1)S(1)}, bf16[256,1024]{1,0:T(8,128)(2,1)S(1)}, u32[]{:S(2)}, u32[]{:S(2)}) collective-permute-start(bf16[256,1024]{1,0:T(8,128)(2,1)S(1)} %shard_map.76.own_ref.refs_1_), channel_id=1, source_target_pairs={{0,4},{4,0},{8,12},{12,8},{16,20},{20,16},{24,28},{28,24},{1,5},{5... | collective-permute-start | bytes 1572872 | tf_op jit(solution)/shard_map/ppermute | solution.py:339
  67.3 27.3 %collective-permute-start.12 = (bf16[256,1024]{1,0:T(8,128)(2,1)S(1)}, bf16[256,1024]{1,0:T(8,128)(2,1)S(1)}, u32[]{:S(2)}, u32[]{:S(2)}) collective-permute-start(bf16[256,1024]{1,0:T(8,128)(2,1)S(1)} %shard_map.76.own_ref.refs_1_), channel_id=1, source_target_pairs={{4,16},{12,24},{5,17},{13,25},{6,18},{14,26},{7,19},{15,27}} | collective-permute-start | bytes 1572872 | tf_op jit(solution)/shard_map/ppermute | solution.py:351
  68.7 27.3 %collective-permute-start.10 = (bf16[256,1024]{1,0:T(8,128)(2,1)S(1)}, bf16[256,1024]{1,0:T(8,128)(2,1)S(1)}, u32[]{:S(2)}, u32[]{:S(2)}) collective-permute-start(bf16[256,1024]{1,0:T(8,128)(2,1)S(1)} %collective-permute-done.9.refs_0_.refs_3_), channel_id=1, source_target_pairs={{0,4},{4,0},{8,12},{12,8},{16,20},{20,16},{24,28},{28,24},{1,5},{5... | collective-permute-start | bytes 1572872 | tf_op jit(solution)/shard_map/ppermute | solution.py:339
  68.8 9.5 %collective-permute-start.4 = (bf16[128,1024]{1,0:T(8,128)(2,1)S(1)}, bf16[128,1024]{1,0:T(8,128)(2,1)S(1)}, u32[]{:S(2)}, u32[]{:S(2)}) collective-permute-start(bf16[128,1024]{1,0:T(8,128)(2,1)S(1)} %collective-permute-done.3.refs_1_), channel_id=1, source_target_pairs={{0,1},{1,2},{2,3},{3,0},{4,5},{5,6},{6,7},{7,4},{8,9},{9,10},{10,1... | collective-permute-start | bytes 786440 | tf_op jit(solution)/shard_map/ppermute | solution.py:385
  71.8 12.1 %collective-permute-start.2 = (bf16[128,1024]{1,0:T(8,128)(2,1)S(1)}, bf16[128,1024]{1,0:T(8,128)(2,1)S(1)}, u32[]{:S(2)}, u32[]{:S(2)}) collective-permute-start(bf16[128,1024]{1,0:T(8,128)(2,1)S(1)} %collective-permute-done.1.refs_2_), channel_id=1, source_target_pairs={{0,1},{1,2},{2,3},{3,0},{4,5},{5,6},{6,7},{7,4},{8,9},{9,10},{10,1... | collective-permute-start | bytes 786440 | tf_op jit(solution)/shard_map/ppermute | solution.py:385
  78.2 28.2 %collective-permute-start.5 = (bf16[128,1024]{1,0:T(8,128)(2,1)S(1)}, bf16[128,1024]{1,0:T(8,128)(2,1)S(1)}, u32[]{:S(2)}, u32[]{:S(2)}) collective-permute-start(bf16[128,1024]{1,0:T(8,128)(2,1)S(1)} %collective-permute-done.4.refs_2_), channel_id=1, source_target_pairs={{0,1},{1,2},{2,3},{3,0},{4,5},{5,6},{6,7},{7,4},{8,9},{9,10},{10,1... | collective-permute-start | bytes 786440 | tf_op jit(solution)/shard_map/ppermute | solution.py:385
  86.8 24.1 %collective-permute-start.14 = (bf16[128,1024]{1,0:T(8,128)(2,1)S(1)}, bf16[128,1024]{1,0:T(8,128)(2,1)S(1)}, u32[]{:S(2)}, u32[]{:S(2)}) collective-permute-start(bf16[128,1024]{1,0:T(8,128)(2,1)S(1)} %shard_map.74.refs_0_), channel_id=1, source_target_pairs={{8,0},{12,4},{16,8},{20,12},{24,16},{28,20},{9,1},{13,5},{17,9},{2... | collective-permute-start | bytes 786440 | tf_op jit(solution)/shard_map/ppermute | solution.py:334
  89.4 21.6 %collective-permute-start.18 = (bf16[128,1024]{1,0:T(8,128)(2,1)S(1)}, bf16[128,1024]{1,0:T(8,128)(2,1)S(1)}, u32[]{:S(2)}, u32[]{:S(2)}) collective-permute-start(bf16[128,1024]{1,0:T(8,128)(2,1)S(1)} %shard_map.74.refs_0_), channel_id=1, source_target_pairs={{0,4},{4,0},{8,12},{12,8},{16,20},{20,16},{24,28},{28,24},{1,5},{5... | collective-permute-start | bytes 786440 | tf_op jit(solution)/shard_map/ppermute | solution.py:339
  94.7 16.8 %collective-permute-start.20 = (bf16[128,1024]{1,0:T(8,128)(2,1)S(1)}, bf16[128,1024]{1,0:T(8,128)(2,1)S(1)}, u32[]{:S(2)}, u32[]{:S(2)}) collective-permute-start(bf16[128,1024]{1,0:T(8,128)(2,1)S(1)} %shard_map.74.refs_0_), channel_id=1, source_target_pairs={{16,4},{24,12},{17,5},{25,13},{18,6},{26,14},{19,7},{27,15}} | collective-permute-start | bytes 786440 | tf_op jit(solution)/shard_map/ppermute | solution.py:351
  96.0 29.6 %collective-permute-start.13 = (bf16[256,1024]{1,0:T(8,128)(2,1)S(1)}, bf16[256,1024]{1,0:T(8,128)(2,1)S(1)}, u32[]{:S(2)}, u32[]{:S(2)}) collective-permute-start(bf16[256,1024]{1,0:T(8,128)(2,1)S(1)} %shard_map.76.own_ref.refs_1_), channel_id=1, source_target_pairs={{28,20},{29,21},{30,22},{31,23}} | collective-permute-start | bytes 1572872 | tf_op jit(solution)/shard_map/ppermute | solution.py:405
  106.5 1.6 %copy-start = (f32[1,2,256,1024]{3,2,1,0:T(8,128)S(1)}, f32[1,2,256,1024]{3,2,1,0:T(8,128)}, u32[]{:S(2)}) copy-start(f32[1,2,256,1024]{3,2,1,0:T(8,128)} %shard_map.77.refs_4_.refs_13_) | copy-start | bytes 6291460
  108.9 9.5 %collective-permute-start.15 = (bf16[128,1024]{1,0:T(8,128)(2,1)S(1)}, bf16[128,1024]{1,0:T(8,128)(2,1)S(1)}, u32[]{:S(2)}, u32[]{:S(2)}) collective-permute-start(bf16[128,1024]{1,0:T(8,128)(2,1)S(1)} %shard_map.78.refs_1_), channel_id=1, source_target_pairs={{8,0},{12,4},{16,8},{20,12},{24,16},{28,20},{9,1},{13,5},{17,9},{2... | collective-permute-start | bytes 786440 | tf_op jit(solution)/shard_map/ppermute | solution.py:334
  110.9 14.7 %collective-permute-start.16 = (bf16[128,1024]{1,0:T(8,128)(2,1)S(1)}, bf16[128,1024]{1,0:T(8,128)(2,1)S(1)}, u32[]{:S(2)}, u32[]{:S(2)}) collective-permute-start(bf16[128,1024]{1,0:T(8,128)(2,1)S(1)} %collective-permute-done.14.refs_5_), channel_id=1, source_target_pairs={{0,4},{4,0},{8,12},{12,8},{16,20},{20,16},{24,28},{28,24},{1,5},{5... | collective-permute-start | bytes 786440 | tf_op jit(solution)/shard_map/ppermute | solution.py:339
  110.9 14.6 %collective-permute-start.19 = (bf16[128,1024]{1,0:T(8,128)(2,1)S(1)}, bf16[128,1024]{1,0:T(8,128)(2,1)S(1)}, u32[]{:S(2)}, u32[]{:S(2)}) collective-permute-start(bf16[128,1024]{1,0:T(8,128)(2,1)S(1)} %shard_map.78.refs_1_), channel_id=1, source_target_pairs={{0,4},{4,0},{8,12},{12,8},{16,20},{20,16},{24,28},{28,24},{1,5},{5... | collective-permute-start | bytes 786440 | tf_op jit(solution)/shard_map/ppermute | solution.py:339
  111.4 14.2 %collective-permute-start.21 = (bf16[128,1024]{1,0:T(8,128)(2,1)S(1)}, bf16[128,1024]{1,0:T(8,128)(2,1)S(1)}, u32[]{:S(2)}, u32[]{:S(2)}) collective-permute-start(bf16[128,1024]{1,0:T(8,128)(2,1)S(1)} %shard_map.78.refs_1_), channel_id=1, source_target_pairs={{16,4},{24,12},{17,5},{25,13},{18,6},{26,14},{19,7},{27,15}} | collective-permute-start | bytes 786440 | tf_op jit(solution)/shard_map/ppermute | solution.py:351
  118.4 7.2 %collective-permute-start.17 = (bf16[128,1024]{1,0:T(8,128)(2,1)S(1)}, bf16[128,1024]{1,0:T(8,128)(2,1)S(1)}, u32[]{:S(2)}, u32[]{:S(2)}) collective-permute-start(bf16[128,1024]{1,0:T(8,128)(2,1)S(1)} %collective-permute-done.15.refs_6_), channel_id=1, source_target_pairs={{0,4},{4,0},{8,12},{12,8},{16,20},{20,16},{24,28},{28,24},{1,5},{5... | collective-permute-start | bytes 786440 | tf_op jit(solution)/shard_map/ppermute | solution.py:339

commit v3 on v2

--- a/solution.py
+++ b/solution.py
@@ -17,6 +17,8 @@
 BF16 = jnp.bfloat16
 WHOLE = pl.BlockSpec(memory_space=pltpu.VMEM)
 ANYWHERE = pl.BlockSpec(memory_space=pl.ANY)
+OUTSIDE = pl.BlockSpec(memory_space=pltpu.HBM)
+TOKEN = pl.BlockSpec((8, 128), lambda *at: (0, 0))
 SCALARS = pl.BlockSpec(memory_space=pltpu.SMEM)
 
 
@@ -32,9 +34,8 @@
     angle = angle.astype(np.float64) * (math.pi / (2 * length))
     forward = np.concatenate([np.cos(angle), -np.sin(angle)], axis=0)
     high, low = parts_of(forward)
-    stacked = np.concatenate([high, low], axis=0)
     back_high, back_low = parts_of(forward.T / length)
-    return stacked, np.concatenate([back_high, back_low], axis=0)
+    return np.concatenate([high, low], axis=1), np.concatenate([back_high, back_low], axis=1)
 
 
 def nn(a, b):
@@ -45,8 +46,8 @@
     return lax.dot_general(a, b, (((1,), (1,)), ((), ())), preferred_element_type=F32)
 
 
-def params():
-    return pltpu.CompilerParams(vmem_limit_bytes=VMEM)
+def params(limit=VMEM):
+    return pltpu.CompilerParams(vmem_limit_bytes=limit)
 
 
 def lanes_at(tile):
@@ -55,7 +56,8 @@
 
 def prepare_kernel(*refs):
     table_ref, back_ref, taps_ref, weight_ref, gate_ref = refs[:5]
-    spec_out, weight_out, gate_out, table_out, back_out, sems = refs[-6:]
+    spec_out, weight_out, gate_out, table_out, back_out, token_out, sems = refs[-7:]
+    token_out[...] = jnp.zeros_like(token_out)
     copies = [
         pltpu.make_async_copy(source, target, sems.at[at])
         for at, (source, target) in enumerate(
@@ -70,7 +72,7 @@
             copy.start()
         table_out[...] = table_ref[...]
 
-    length = table_ref.shape[1]
+    length = table_ref.shape[1] // 2
     freq = lax.broadcasted_iota(jnp.int32, (length, 1), 0)
     sign = jnp.where(freq % 2 == 0, 1.0, -1.0).astype(F32)
     lanes = lanes_at(step)
@@ -80,8 +82,8 @@
             values = taps_ref[part * length : (part + 1) * length, :]
             high = values.astype(BF16)
             low = (values - high.astype(F32)).astype(BF16)
-            both = nn(table_ref[...], high)
-            full = both[: 2 * length] + (both[2 * length :] + nn(table_ref[: 2 * length, :], low))
+            full = nn(table_ref[...], jnp.concatenate([high, high], axis=0))
+            full = full + nn(table_ref[:, :length], low)
             now = (full[:length], -full[length:])
         else:
             now = None
@@ -113,18 +115,19 @@
             pltpu.VMEM(gate.shape, BF16),
             pltpu.VMEM(table.shape, BF16),
             pltpu.VMEM(back.shape, BF16),
+            jax.ShapeDtypeStruct((8, 128), F32),
         ),
         in_specs=[
-            pl.BlockSpec((4 * length, length), lambda c: (0, 0)),
-            ANYWHERE,
+            pl.BlockSpec((2 * length, 2 * length), lambda c: (0, 0)),
+            OUTSIDE,
             pl.BlockSpec((count, LANES), lambda c: (0, c)),
-            ANYWHERE,
-            ANYWHERE,
+            OUTSIDE,
+            OUTSIDE,
         ]
         + [ANYWHERE] * len(after),
-        out_specs=(WHOLE,) * 5,
+        out_specs=(WHOLE,) * 5 + (TOKEN,),
         scratch_shapes=[pltpu.SemaphoreType.DMA((3,))],
-        compiler_params=params(),
+        compiler_params=params(2 * VMEM),
         cost_estimate=pl.CostEstimate(
             flops=2 * 3 * 2 * count * length * width,
             bytes_accessed=4 * (count * width + 8 * length * width),
@@ -178,7 +181,7 @@
 class Conv:
     def __init__(self, facts, table, back, spectra):
         self.facts, self.table, self.back, self.spectra = facts, table, back, spectra
-        self.length = table.shape[1]
+        self.length = table.shape[0] // 2
         self.lanes = lanes_at(pl.program_id(0))
         self.row = lax.broadcasted_iota(jnp.int32, (self.length, LANES), 0)
 
@@ -192,17 +195,15 @@
     def term(self, values, low, high, distance):
         length = self.length
         kept = jnp.where(self.within(low, high), values.astype(F32), 0.0).astype(BF16)
-        both = nn(self.table[...], kept)
-        full = both[: 2 * length] + both[2 * length :]
+        full = nn(self.table[...], jnp.concatenate([kept, kept], axis=0))
         real, imag = full[:length], full[length:]
         k_real = self.spectra[distance, :length, self.lanes]
         k_imag = self.spectra[distance, length:, self.lanes]
         return k_real * real - k_imag * imag, k_real * imag + k_imag * real
 
     def signal(self, real, imag):
-        total = jnp.concatenate([real.astype(BF16), imag.astype(BF16)], axis=0)
-        both = nn(self.back[...], total)
-        return both[: self.length] + both[self.length :]
+        real, imag = real.astype(BF16), imag.astype(BF16)
+        return nn(self.back[...], jnp.concatenate([real, imag, real, imag], axis=0))
 
     def far_terms(self, acc, values_of):
         for distance in range(1, REACH + 1):
@@ -227,9 +228,11 @@
             signal = self.signal(*self.term(own, first_end, last_start, 0))
             write(jnp.where(self.within(first_end, last_start), signal, read()))
 
-    def halo(self, pieces, distance):
-        count = len(pieces) // 4
-        two, swapped, mate, far = (pieces[at * count : (at + 1) * count] for at in range(4))
+    def halo(self, pieces, distance, mixed):
+        sets = 3 if mixed else 4
+        count = len(pieces) // sets
+        kinds = [pieces[at * count : (at + 1) * count] for at in range(sets)]
+        two, swapped, mate, far = kinds[0], kinds[1], kinds[2], kinds[-1]
         if distance == 2:
             return self.joined(two)
         inner = self.facts[5] == 1
@@ -239,13 +242,14 @@
 
 
 def upper_kernel(facts_ref, table_ref, back_ref, spec_ref, own_ref, *refs):
-    halos, (out_ref, acc_ref) = refs[:4], refs[-2:]
+    halos, (out_ref, token_ref, acc_ref) = refs[:4], refs[-3:]
+    token_ref[...] = jnp.zeros_like(token_ref)
     conv = Conv(facts_ref, table_ref, back_ref, spec_ref)
     own = conv.joined([own_ref])
     real, imag = conv.term(own, facts_ref[1], conv.length, 0)
     acc_ref[: conv.length, :] = real
     acc_ref[conv.length :, :] = imag
-    conv.far_terms(acc_ref, lambda distance: conv.halo(halos, distance))
+    conv.far_terms(acc_ref, lambda distance: conv.halo(halos, distance, False))
     out_ref[0, 0] = conv.signal(acc_ref[: conv.length, :], acc_ref[conv.length :, :])
 
     def write(value):
@@ -268,13 +272,13 @@
 
 def far_kernel(pieces, facts_ref, table_ref, back_ref, spec_ref, *refs):
     near_ref, upper_ref, mate_ref, two_ref, fold_ref = refs[:5]
-    halos = refs[5 : 5 + 4 * pieces]
+    halos = refs[5 : 5 + 3 * pieces]
     out_ref, acc_ref = refs[-2:]
     conv = Conv(facts_ref, table_ref, back_ref, spec_ref)
     role = facts_ref[6]
 
     def values_of(distance):
-        value = conv.halo(halos, distance)
+        value = conv.halo(halos, distance, True)
         if distance == 1:
             return jnp.where(role == 1, conv.joined([upper_ref]), value)
         if distance == 2:
@@ -300,7 +304,7 @@
 
 def conv_call(body, tabs, facts, arrays, out_shape, out_spec, scratch, terms, after=(), result=None):
     table, back, spectra = tabs
-    length = table.shape[1]
+    length = table.shape[0] // 2
     width = spectra.shape[2]
     operands = [facts, table, back, spectra, *arrays]
     specs = [SCALARS] + [WHOLE] * (len(operands) - 1)
@@ -328,6 +332,16 @@
     )(*operands)
 
 
+def ordered(value, *earlier):
+    return pl.pallas_call(
+        lambda *refs: None,
+        out_shape=jax.ShapeDtypeStruct(value.shape, value.dtype),
+        in_specs=[ANYWHERE] * (1 + len(earlier)),
+        out_specs=ANYWHERE,
+        input_output_aliases={0: 0},
+    )(value, *earlier)
+
+
 def shifted(value, steps):
     count = lax.axis_size("ctx")
     initial, last = (max(0, -steps), min(count, count - steps))
@@ -339,16 +353,21 @@
     return lax.ppermute(value, "ctx", [(source, source ^ 1) for source in range(count)])
 
 
-def halo_of(value, way):
+def upper_halo_of(value):
     count = lax.axis_size("ctx")
-    two = shifted(value, 2 * way)
-    outer = 1 if way > 0 else 0
-    far = [
-        (source, source + 3 * way)
-        for source in range(outer, count, 2)
-        if 0 <= source + 3 * way < count
-    ]
-    return [two, core_swapped(two), core_swapped(value), lax.ppermute(value, "ctx", far)]
+    far = [(source, source + 3) for source in range(1, count - 3, 2)] + [(count - 1, count - 3)]
+    two = shifted(value, 2)
+    mate, far = core_swapped(value), lax.ppermute(value, "ctx", far)
+    return [two, core_swapped(two), mate, far]
+
+
+def lower_halo_of(value):
+    count = lax.axis_size("ctx")
+    mixed = [(source, source - 1) for source in range(1, count, 2)]
+    mixed += [(source, source - 3) for source in range(4, count, 2)]
+    two = shifted(value, -2)
+    mixed = lax.ppermute(value, "ctx", mixed)
+    return [two, core_swapped(two), mixed]
 
 
 def block_facts(doc_starts, block, length, end, inner, role):
@@ -379,15 +398,18 @@
     around = [(source, (source + 1) % count) for source in range(count)]
     everything = tuple(range(count))
 
+    def turned(piece):
+        return lax.ppermute(piece, "ch", around)
+
     def ring(piece):
         shards = [piece]
         for _ in range(1, count):
-            shards.append(lax.ppermute(shards[-1], "ch", around))
+            shards.append(turned(shards[-1]))
         return shards
 
-    upper_in = ring(grad_out[0, 1])
-    first_in = ring(grad_out[0, 0, :half])
-    second_in = ring(grad_out[0, 0, half:])
+    slices = [grad_out[0, 0, :half], grad_out[0, 0, half:]]
+    upper_in = [grad_out[0, 1]]
+    upper_in.append(turned(upper_in[0]))
 
     odd = place % 2
     role = jnp.where(place >= pairs - 3, pairs - place, 0)
@@ -395,35 +417,40 @@
     lower_facts = block_facts(doc_starts, place, length, end, 1 - odd, role)
     upper_facts = block_facts(doc_starts, blocks - 1 - place, length, end, odd, role)
     table, back = (jnp.asarray(one) for one in tables(length))
-    spectra, weight, gates, table, back = prepare(
-        table, back, filter_taps, out_weight, gate, [lower_facts, upper_facts]
+    spectra, weight, gates, table, back, prepared = prepare(
+        table, back, filter_taps, out_weight, gate, [lower_facts, upper_facts, *slices]
     )
     tabs = (table, back, spectra)
 
-    upper = project(lane, upper_in, everything, weight, gates, 1, 0)
-    upper_halo = halo_of(upper, 1)
-    fold = lax.ppermute(upper, "ctx", [(pairs - 1, pairs - 3)])
+    upper_in[1] = ordered(upper_in[1], prepared)
+    for step in range(2, count):
+        upper_in.append(turned(upper_in[-1]))
+    first_in = ring(ordered(slices[0], upper_in[-2]))
+    second_in = ring(ordered(slices[1], upper_in[-1]))
+
+    upper = project(lane, upper_in, everything, weight, gates, 1, 0, after=[first_in[1]])
+    upper_halo = upper_halo_of(upper)
     out_shape = jax.ShapeDtypeStruct((1, 2, length, width), F32)
-    result = conv_call(
+    result, convolved = conv_call(
         upper_kernel,
         tabs,
         upper_facts,
         [upper, *upper_halo],
-        out_shape,
-        pl.BlockSpec((1, 1, length, LANES), lambda c: (0, 1, 0, c)),
+        (out_shape, jax.ShapeDtypeStruct((8, 128), F32)),
+        (pl.BlockSpec((1, 1, length, LANES), lambda c: (0, 1, 0, c)), TOKEN),
         1,
         6,
     )
 
     first = project(lane, first_in, everything, weight, gates, 0, 0)
-    first_halo = halo_of(first, -1)
+    first_halo = lower_halo_of(first)
     partial = project(
         lane, second_in[:-1], everything[:-1], weight, gates, 0, half, last=False
     )
     second = project(
-        lane, second_in[-1:], everything[-1:], weight, gates, 0, half, partial, after=[result]
-    )
-    second_halo = halo_of(second, -1)
+        lane, second_in[-1:], everything[-1:], weight, gates, 0, half, partial, after=[convolved]
+    )
+    second_halo = lower_halo_of(second)
     near = conv_call(
         functools.partial(own_kernel, 2),
         tabs,
@@ -434,7 +461,7 @@
         0,
         4,
     )
-    two, _, mate, _ = upper_halo
+    two, _, mate, fold = upper_halo
     halos = [piece for both in zip(first_halo, second_halo) for piece in both]
     return conv_call(
         functools.partial(far_kernel, 2),

time: 132 us -> 149 us (1.13)
  the two profiles are of different devices: /device:TPU:3 before, /device:TPU:29 now
where the time goes in v3:
time: 149 us
  starting transfers between devices  44.7 us (30%)
  Pallas kernels  42.2 us (28%)
  waiting for transfers between devices  33.6 us (23%)
  local copies, waits for them, and re-layouts  22.8 us (15%)
  between operations  4.19 us (3%)
    ppermute x9, waiting for transfers between devices, turned(): return lax.ppermute(piece, 'ch', around)  32 us
    pallas_call x3, Pallas kernels, conv_call(): pl.pallas_call(body, grid=(width // LANES,), out_shape=out_shape, in_spec...  24 us
    unnamed x36, local copies, waits for them, and re-layouts  18.6 us
    ppermute x9, starting transfers between devices, turned(): return lax.ppermute(piece, 'ch', around)  16.4 us
    pallas_call x4, Pallas kernels, project(): pl.pallas_call(body, out_shape=pltpu.VMEM((rows, width), BF16 if last els...  10.5 us
    ppermute x3, starting transfers between devices, shifted(): lax.ppermute(value, 'ctx', [(source, source + steps) for source in range(...  10.2 us
    ppermute x2, starting transfers between devices, lower_halo_of(): mixed = lax.ppermute(value, 'ctx', mixed)  9.57 us
    pallas_call x1, Pallas kernels, prepare(): pl.pallas_call(prepare_kernel, grid=(width // LANES,), out_shape=(pltpu.V...  7.72 us
  transfers between devices with their start and end apart: 19, of which 4 were waited for; matrix products, arithmetic and copies ran while one was open for 3% of the time, Pallas kernels for 21%

profile of v3, /device:TPU:29, one launch (start us, length us, event | category | flops | bytes accessed | tf_op | source)
XLA Modules:
  0.0 149.0 jit_solution(284031259640039384)
XLA Ops:
  0.0 1.1 slice_bitcast_fusion.refs_0_
  1.2 1.4 fusion.5
  7.7 1.9 %slice_bitcast_fusion.1 = (bf16[128,1024]{1,0:T(8,128)(2,1)}, bf16[128,1024]{1,0:T(8,128)(2,1)}) fusion(bf16[1,2,256,1024]{3,2,1,0:T(8,128)(2,1)} %param.7), kind=kLoop, calls=%fused_computation.1 | loop fusion | bytes 1048576 | tf_op jit(solution)/shard_map/squeeze | solution.py:410
  9.6 7.7 %shard_map.73 = (f32[4,512,1024]{2,1,0:T(8,128)S(1)}, bf16[1024,4096]{1,0:T(8,128)(2,1)S(1)}, bf16[1,2,256,1024]{3,2,1,0:T(8,128)(2,1)S(1)}, bf16[512,512]{1,0:T...) custom-call(bf16[512,512]{1,0:T(8,128)(2,1)} %constant.58.clone.refs_0_, ...), custom_call_target="tpu_custom_call" | custom-call | flops 2415919104 | bytes 11534336 | tf_op jit(solution)/shard_map/pallas_call | solution.py:109
  17.3 3.3 %copy-done = bf16[1024,4096]{1,0:T(8,128)(2,1)} copy-done((bf16[1024,4096]{1,0:T(8,128)(2,1)}, bf16[1024,4096]{1,0:T(8,128)(2,1)S(1)}, u32[]{:S(2)}) %copy-start) | copy-done | bytes 8388632
  20.6 3.2 %copy-done.3 = f32[4,512,1024]{2,1,0:T(8,128)} copy-done((f32[4,512,1024]{2,1,0:T(8,128)}, f32[4,512,1024]{2,1,0:T(8,128)S(1)}, u32[]{:S(2)}) %copy-start.3) | copy-done | bytes 8388632
  24.6 1.2 collective-permute-start.1
  25.8 11.7 %collective-permute-done.1.refs_1_.refs_2_ = bf16[256,1024]{1,0:T(8,128)(2,1)} collective-permute-done((bf16[256,1024]{1,0:T(8,128)(2,1)}, bf16[256,1024]{1,0:T(8,128)(2,1)}, u32[]{:S(2)}, u32[]{:S(2)}) %collective-permute-start.1) | collective-permute-done | bytes 524320 | tf_op jit(solution)/shard_map/ppermute | solution.py:402
  37.5 2.9 %collective-permute-start.5 = (bf16[256,1024]{1,0:T(8,128)(2,1)}, bf16[256,1024]{1,0:T(8,128)(2,1)S(1)}, u32[]{:S(2)}, u32[]{:S(2)}) collective-permute-start(bf16[256,1024]{1,0:T(8,128)(2,1)} %collective-permute-done.1.refs_1_.refs_2_), channel_id=1, source_target_pairs={{0,1},{1,2},{2,3},{3,0},{4,5},{5,6},{6,7},{7,4},{8,9},{9,10},{10,1... | collective-permute-start | bytes 1572872 | tf_op jit(solution)/shard_map/ppermute | solution.py:402
  40.4 15.3 %collective-permute-done.2.refs_1_.refs_6_ = bf16[128,1024]{1,0:T(8,128)(2,1)} collective-permute-done((bf16[128,1024]{1,0:T(8,128)(2,1)}, bf16[128,1024]{1,0:T(8,128)(2,1)}, u32[]{:S(2)}, u32[]{:S(2)}) %collective-permute-start.2) | collective-permute-done | bytes 262176 | tf_op jit(solution)/shard_map/ppermute | solution.py:402
  56.5 3.4 %copy-done.1 = bf16[1024,4096]{1,0:T(8,128)(2,1)S(1)} copy-done((bf16[1024,4096]{1,0:T(8,128)(2,1)S(1)}, bf16[1024,4096]{1,0:T(8,128)(2,1)}, u32[]{:S(2)}) %copy-start.1) | copy-done | bytes 8388632
  59.9 1.0 copy-done.7
  61.9 3.4 %shard_map.79.own_ref.refs_1_ = bf16[256,1024]{1,0:T(8,128)(2,1)S(1)} custom-call(s32[1]{0:T(128)} %bitcast.15.place_ref, bf16[256,1024]{1,0:T(8,128)(2,1)S(1)} %slice_bitcast_fusion.refs_0_, bf16[256,1024]{1,0:T(8,128)(2,1)S(1)} %copy-done.7, bf16[256,1024]{1,0:T(8,128)(2,1)} %collective-permute-done.1.refs_1_.refs_2_, bf16[256,1024]{1,0:T(8,128)(2,1)S(1)} %copy-done.9, ...), custom_call_target="tpu_custom_call" | custom-call | flops 2147483648 | bytes 10485760 | tf_op jit(solution)/shard_map/pallas_call | solution.py:167
  65.4 3.1 %collective-permute-start.9 = (bf16[256,1024]{1,0:T(8,128)(2,1)S(1)}, bf16[256,1024]{1,0:T(8,128)(2,1)}, u32[]{:S(2)}, u32[]{:S(2)}) collective-permute-start(bf16[256,1024]{1,0:T(8,128)(2,1)S(1)} %shard_map.79.own_ref.refs_1_), channel_id=1, source_target_pairs={{0,8},{4,12},{8,16},{12,20},{16,24},{20,28},{1,9},{5,13},{9,17},{1... | collective-permute-start | bytes 1572872 | tf_op jit(solution)/shard_map/ppermute | solution.py:348
  68.5 4.1 %collective-permute-start.3 = (bf16[128,1024]{1,0:T(8,128)(2,1)}, bf16[128,1024]{1,0:T(8,128)(2,1)S(1)}, u32[]{:S(2)}, u32[]{:S(2)}) collective-permute-start(bf16[128,1024]{1,0:T(8,128)(2,1)} %collective-permute-done.2.refs_1_.refs_6_), channel_id=1, source_target_pairs={{0,1},{1,2},{2,3},{3,0},{4,5},{5,6},{6,7},{7,4},{8,9},{9,10},{10,1... | collective-permute-start | bytes 786440 | tf_op jit(solution)/shard_map/ppermute | solution.py:402
  72.7 3.4 %collective-permute-start.11 = (bf16[256,1024]{1,0:T(8,128)(2,1)S(1)}, bf16[256,1024]{1,0:T(8,128)(2,1)S(1)}, u32[]{:S(2)}, u32[]{:S(2)}) collective-permute-start(bf16[256,1024]{1,0:T(8,128)(2,1)S(1)} %shard_map.79.own_ref.refs_1_), channel_id=1, source_target_pairs={{0,4},{4,0},{8,12},{12,8},{16,20},{20,16},{24,28},{28,24},{1,5},{5... | collective-permute-start | bytes 1572872 | tf_op jit(solution)/shard_map/ppermute | solution.py:353
  76.0 1.3 collective-permute-start.12
  77.3 1.6 %collective-permute-done.9.refs_0_.refs_3_ = bf16[256,1024]{1,0:T(8,128)(2,1)} collective-permute-done((bf16[256,1024]{1,0:T(8,128)(2,1)S(1)}, bf16[256,1024]{1,0:T(8,128)(2,1)}, u32[]{:S(2)}, u32[]{:S(2)}) %collective-permute-start.9) | collective-permute-done | bytes 524320 | tf_op jit(solution)/shard_map/ppermute | solution.py:348
  78.9 3.8 %collective-permute-start.10 = (bf16[256,1024]{1,0:T(8,128)(2,1)}, bf16[256,1024]{1,0:T(8,128)(2,1)S(1)}, u32[]{:S(2)}, u32[]{:S(2)}) collective-permute-start(bf16[256,1024]{1,0:T(8,128)(2,1)} %collective-permute-done.9.refs_0_.refs_3_), channel_id=1, source_target_pairs={{0,4},{4,0},{8,12},{12,8},{16,20},{20,16},{24,28},{28,24},{1,5},{5... | collective-permute-start | bytes 1572872 | tf_op jit(solution)/shard_map/ppermute | solution.py:353
  82.7 4.0 %collective-permute-start.4 = (bf16[128,1024]{1,0:T(8,128)(2,1)S(1)}, bf16[128,1024]{1,0:T(8,128)(2,1)S(1)}, u32[]{:S(2)}, u32[]{:S(2)}) collective-permute-start(bf16[128,1024]{1,0:T(8,128)(2,1)S(1)} %collective-permute-done.3.refs_2_), channel_id=1, source_target_pairs={{0,1},{1,2},{2,3},{3,0},{4,5},{5,6},{6,7},{7,4},{8,9},{9,10},{10,1... | collective-permute-start | bytes 786440 | tf_op jit(solution)/shard_map/ppermute | solution.py:402
  87.5 5.0 %collective-permute-done.4.refs_3_ = bf16[128,1024]{1,0:T(8,128)(2,1)S(1)} collective-permute-done((bf16[128,1024]{1,0:T(8,128)(2,1)S(1)}, bf16[128,1024]{1,0:T(8,128)(2,1)S(1)}, u32[]{:S(2)}, u32[]{:S(2)}) %collective-permute-start.4) | collective-permute-done | bytes 262176 | tf_op jit(solution)/shard_map/ppermute | solution.py:402
  92.5 3.4 %copy-done.2 = bf16[1024,4096]{1,0:T(8,128)(2,1)S(1)} copy-done((bf16[1024,4096]{1,0:T(8,128)(2,1)S(1)}, bf16[1024,4096]{1,0:T(8,128)(2,1)}, u32[]{:S(2)}) %copy-start.2) | copy-done | bytes 8388632
  96.8 4.0 %shard_map.76.refs_0_ = bf16[128,1024]{1,0:T(8,128)(2,1)S(1)} custom-call(s32[1]{0:T(128)} %bitcast.15.place_ref, bf16[128,1024]{1,0:T(8,128)(2,1)S(1)} %copy-done.5, bf16[128,1024]{1,0:T(8,128)(2,1)} %collective-permute-done.2.refs_1_.refs_6_, bf16[128,1024]{1,0:T(8,128)(2,1)S(1)} %copy-done.11, bf16[128,1024]{1,0:T(8,128)(2,1)S(1)} %collective-permute-done.4.refs_3_, ...), custom_call_target="tpu_custom_call" | custom-call | flops 1073741824 | bytes 9437184 | tf_op jit(solution)/shard_map/pallas_call | solution.py:167
  100.8 2.2 %collective-permute-start.13 = (bf16[128,1024]{1,0:T(8,128)(2,1)S(1)}, bf16[128,1024]{1,0:T(8,128)(2,1)S(1)}, u32[]{:S(2)}, u32[]{:S(2)}) collective-permute-start(bf16[128,1024]{1,0:T(8,128)(2,1)S(1)} %shard_map.76.refs_0_), channel_id=1, source_target_pairs={{8,0},{12,4},{16,8},{20,12},{24,16},{28,20},{9,1},{13,5},{17,9},{2... | collective-permute-start | bytes 786440 | tf_op jit(solution)/shard_map/ppermute | solution.py:348
  103.0 4.1 %collective-permute-start.8 = (bf16[128,1024]{1,0:T(8,128)(2,1)S(1)}, bf16[128,1024]{1,0:T(8,128)(2,1)S(1)}, u32[]{:S(2)}, u32[]{:S(2)}) collective-permute-start(bf16[128,1024]{1,0:T(8,128)(2,1)S(1)} %collective-permute-done.7.refs_2_), channel_id=1, source_target_pairs={{0,1},{1,2},{2,3},{3,0},{4,5},{5,6},{6,7},{7,4},{8,9},{9,10},{10,1... | collective-permute-start | bytes 786440 | tf_op jit(solution)/shard_map/ppermute | solution.py:402
  107.1 2.2 %shard_map.78.refs_3_ = f32[128,1024]{1,0:T(8,128)S(1)} custom-call(s32[1]{0:T(128)} %bitcast.15.place_ref, bf16[128,1024]{1,0:T(8,128)(2,1)S(1)} %copy-done.4, bf16[128,1024]{1,0:T(8,128)(2,1)S(1)} %collective-permute-done.6.refs_1_, bf16[128,1024]{1,0:T(8,128)(2,1)S(1)} %collective-permute-done.7.refs_2_, bf16[1024,4096]{1,0:T(8,128)(2,1)S(1)} %copy-done.2, ...), custom_call_target="tpu_custom_call" | custom-call | flops 805306368 | bytes 7077888 | tf_op jit(solution)/shard_map/pallas_call | solution.py:167
  109.4 5.9 %shard_map.80 = (f32[1,2,256,1024]{3,2,1,0:T(8,128)}, f32[8,128]{1,0:T(8,128)S(1)}) custom-call(s32[7]{0:T(128)S(1)} %copy-done.13, bf16[512,512]{1,0:T(8,128)(2,1)S(1)} %get-tuple-element.13.table_ref, bf16[256,1024]{1,0:T(8,128)(2,1)S(1)} %get-tuple-element.14.back_ref, f32[4,512,1024]{2,1,0:T(8,128)S(1)} %bitcast.23, ...), custom_call_target="tpu_custom_call" | custom-call | flops 3221225472 | bytes 1048576 | tf_op jit(solution)/shard_map/pallas_call | solution.py:318
  116.2 4.9 %collective-permute-start.14 = (bf16[128,1024]{1,0:T(8,128)(2,1)S(1)}, bf16[128,1024]{1,0:T(8,128)(2,1)S(1)}, u32[]{:S(2)}, u32[]{:S(2)}) collective-permute-start(bf16[128,1024]{1,0:T(8,128)(2,1)S(1)} %shard_map.81.refs_1_), channel_id=1, source_target_pairs={{8,0},{12,4},{16,8},{20,12},{24,16},{28,20},{9,1},{13,5},{17,9},{2... | collective-permute-start | bytes 786440 | tf_op jit(solution)/shard_map/ppermute | solution.py:348
  121.1 7.2 %collective-permute-start.17 = (bf16[128,1024]{1,0:T(8,128)(2,1)S(1)}, bf16[128,1024]{1,0:T(8,128)(2,1)S(1)}, u32[]{:S(2)}, u32[]{:S(2)}) collective-permute-start(bf16[128,1024]{1,0:T(8,128)(2,1)S(1)} %shard_map.76.refs_0_), channel_id=1, source_target_pairs={{4,0},{12,8},{20,16},{28,24},{16,4},{24,12},{5,1},{13,9},{21,17},{... | collective-permute-start | bytes 786440 | tf_op jit(solution)/shard_map/ppermute | solution.py:369
  128.3 2.4 %collective-permute-start.18 = (bf16[128,1024]{1,0:T(8,128)(2,1)S(1)}, bf16[128,1024]{1,0:T(8,128)(2,1)S(1)}, u32[]{:S(2)}, u32[]{:S(2)}) collective-permute-start(bf16[128,1024]{1,0:T(8,128)(2,1)S(1)} %shard_map.81.refs_1_), channel_id=1, source_target_pairs={{4,0},{12,8},{20,16},{28,24},{16,4},{24,12},{5,1},{13,9},{21,17},{... | collective-permute-start | bytes 786440 | tf_op jit(solution)/shard_map/ppermute | solution.py:369
  130.8 10.4 %shard_map.82.refs_0_ = f32[256,1024]{1,0:T(8,128)S(1)} custom-call(s32[7]{0:T(128)S(1)} %copy-done.12, bf16[512,512]{1,0:T(8,128)(2,1)S(1)} %get-tuple-element.13.table_ref, bf16[256,1024]{1,0:T(8,128)(2,1)S(1)} %get-tuple-element.14.back_ref, f32[4,512,1024]{2,1,0:T(8,128)S(1)} %bitcast.23, bf16[128,1024]{1,0:T(8,128)(2,1)S(1)} %shard_map.76.refs_0_, ...), custom_call_target="tpu_custom_call" | custom-call | flops 2147483648 | bytes 1048576 | tf_op jit(solution)/shard_map/pallas_call | solution.py:318
  141.3 7.7 %shard_map.83 = f32[1,2,256,1024]{3,2,1,0:T(8,128)} custom-call(s32[7]{0:T(128)S(1)} %copy-done.12, bf16[512,512]{1,0:T(8,128)(2,1)S(1)} %get-tuple-element.13.table_ref, bf16[256,1024]{1,0:T(8,128)(2,1)S(1)} %get-tuple-element.14.back_ref, f32[4,512,1024]{2,1,0:T(8,128)S(1)} %bitcast.23, ...), custom_call_target="tpu_custom_call", output_to_operand_aliasing={{}: (15, {})} | custom-call | flops 2147483648 | bytes 1048576 | tf_op jit(solution)/shard_map/pallas_call | solution.py:318
  (60 shorter events, 6.8 us)
Async XLA Ops:
  1.1 22.7 %collective-permute-start = (bf16[256,1024]{1,0:T(8,128)(2,1)S(1)}, bf16[256,1024]{1,0:T(8,128)(2,1)S(1)}, u32[]{:S(2)}, u32[]{:S(2)}) collective-permute-start(bf16[256,1024]{1,0:T(8,128)(2,1)S(1)} %slice_bitcast_fusion.refs_0_), channel_id=1, source_target_pairs={{0,1},{1,2},{2,3},{3,0},{4,5},{5,6},{6,7},{7,4},{8,9},{9,10},{10,1... | collective-permute-start | bytes 1572872 | tf_op jit(solution)/shard_map/ppermute | solution.py:402
  17.3 3.3 %copy-start = (bf16[1024,4096]{1,0:T(8,128)(2,1)}, bf16[1024,4096]{1,0:T(8,128)(2,1)S(1)}, u32[]{:S(2)}) copy-start(bf16[1024,4096]{1,0:T(8,128)(2,1)S(1)} %get-tuple-element.17.refs_4_.refs_3_.refs_1_) | copy-start | bytes 25165828
  20.6 3.2 %copy-start.3 = (f32[4,512,1024]{2,1,0:T(8,128)}, f32[4,512,1024]{2,1,0:T(8,128)S(1)}, u32[]{:S(2)}) copy-start(f32[4,512,1024]{2,1,0:T(8,128)S(1)} %get-tuple-element.15.spec_ref) | copy-start | bytes 25165828
  24.6 12.9 %collective-permute-start.1 = (bf16[256,1024]{1,0:T(8,128)(2,1)}, bf16[256,1024]{1,0:T(8,128)(2,1)}, u32[]{:S(2)}, u32[]{:S(2)}) collective-permute-start(bf16[256,1024]{1,0:T(8,128)(2,1)} %shard_map.74.refs_1_), channel_id=1, source_target_pairs={{0,1},{1,2},{2,3},{3,0},{4,5},{5,6},{6,7},{7,4},{8,9},{9,10},{10,1... | collective-permute-start | bytes 1572872 | tf_op jit(solution)/shard_map/ppermute | solution.py:402
  37.5 18.2 %collective-permute-start.5 = (bf16[256,1024]{1,0:T(8,128)(2,1)}, bf16[256,1024]{1,0:T(8,128)(2,1)S(1)}, u32[]{:S(2)}, u32[]{:S(2)}) collective-permute-start(bf16[256,1024]{1,0:T(8,128)(2,1)} %collective-permute-done.1.refs_1_.refs_2_), channel_id=1, source_target_pairs={{0,1},{1,2},{2,3},{3,0},{4,5},{5,6},{6,7},{7,4},{8,9},{9,10},{10,1... | collective-permute-start | bytes 1572872 | tf_op jit(solution)/shard_map/ppermute | solution.py:402
  40.4 15.3 %collective-permute-start.2 = (bf16[128,1024]{1,0:T(8,128)(2,1)}, bf16[128,1024]{1,0:T(8,128)(2,1)}, u32[]{:S(2)}, u32[]{:S(2)}) collective-permute-start(bf16[128,1024]{1,0:T(8,128)(2,1)} %shard_map.75.refs_0_), channel_id=1, source_target_pairs={{0,1},{1,2},{2,3},{3,0},{4,5},{5,6},{6,7},{7,4},{8,9},{9,10},{10,1... | collective-permute-start | bytes 786440 | tf_op jit(solution)/shard_map/ppermute | solution.py:402
  56.5 3.4 %copy-start.1 = (bf16[1024,4096]{1,0:T(8,128)(2,1)S(1)}, bf16[1024,4096]{1,0:T(8,128)(2,1)}, u32[]{:S(2)}) copy-start(bf16[1024,4096]{1,0:T(8,128)(2,1)} %copy-done) | copy-start | bytes 25165828
  59.9 1.0 copy-start.7
  61.9 30.5 %copy-start.5 = (bf16[128,1024]{1,0:T(8,128)(2,1)S(1)}, bf16[128,1024]{1,0:T(8,128)(2,1)}, u32[]{:S(2)}) copy-start(bf16[128,1024]{1,0:T(8,128)(2,1)} %shard_map.75.refs_0_) | copy-start | bytes 786436
  65.4 13.5 %collective-permute-start.9 = (bf16[256,1024]{1,0:T(8,128)(2,1)S(1)}, bf16[256,1024]{1,0:T(8,128)(2,1)}, u32[]{:S(2)}, u32[]{:S(2)}) collective-permute-start(bf16[256,1024]{1,0:T(8,128)(2,1)S(1)} %shard_map.79.own_ref.refs_1_), channel_id=1, source_target_pairs={{0,8},{4,12},{8,16},{12,20},{16,24},{20,28},{1,9},{5,13},{9,17},{1... | collective-permute-start | bytes 1572872 | tf_op jit(solution)/shard_map/ppermute | solution.py:348
  68.5 14.2 %collective-permute-start.3 = (bf16[128,1024]{1,0:T(8,128)(2,1)}, bf16[128,1024]{1,0:T(8,128)(2,1)S(1)}, u32[]{:S(2)}, u32[]{:S(2)}) collective-permute-start(bf16[128,1024]{1,0:T(8,128)(2,1)} %collective-permute-done.2.refs_1_.refs_6_), channel_id=1, source_target_pairs={{0,1},{1,2},{2,3},{3,0},{4,5},{5,6},{6,7},{7,4},{8,9},{9,10},{10,1... | collective-permute-start | bytes 786440 | tf_op jit(solution)/shard_map/ppermute | solution.py:402
  72.6 36.8 %copy-start.13 = (s32[7]{0:T(128)S(1)}, s32[7]{0:T(128)}, u32[]{:S(2)}) copy-start(s32[7]{0:T(128)} %stack.60.refs_6_.facts_ref) | copy-start | bytes 88
  72.6 14.9 %collective-permute-start.6 = (bf16[128,1024]{1,0:T(8,128)(2,1)}, bf16[128,1024]{1,0:T(8,128)(2,1)S(1)}, u32[]{:S(2)}, u32[]{:S(2)}) collective-permute-start(bf16[128,1024]{1,0:T(8,128)(2,1)} %shard_map.77.refs_0_), channel_id=1, source_target_pairs={{0,1},{1,2},{2,3},{3,0},{4,5},{5,6},{6,7},{7,4},{8,9},{9,10},{10,1... | collective-permute-start | bytes 786440 | tf_op jit(solution)/shard_map/ppermute | solution.py:402
  72.7 36.7 %collective-permute-start.11 = (bf16[256,1024]{1,0:T(8,128)(2,1)S(1)}, bf16[256,1024]{1,0:T(8,128)(2,1)S(1)}, u32[]{:S(2)}, u32[]{:S(2)}) collective-permute-start(bf16[256,1024]{1,0:T(8,128)(2,1)S(1)} %shard_map.79.own_ref.refs_1_), channel_id=1, source_target_pairs={{0,4},{4,0},{8,12},{12,8},{16,20},{20,16},{24,28},{28,24},{1,5},{5... | collective-permute-start | bytes 1572872 | tf_op jit(solution)/shard_map/ppermute | solution.py:353
  76.0 33.3 %collective-permute-start.12 = (bf16[256,1024]{1,0:T(8,128)(2,1)S(1)}, bf16[256,1024]{1,0:T(8,128)(2,1)S(1)}, u32[]{:S(2)}, u32[]{:S(2)}) collective-permute-start(bf16[256,1024]{1,0:T(8,128)(2,1)S(1)} %shard_map.79.own_ref.refs_1_), channel_id=1, source_target_pairs={{4,16},{12,24},{28,20},{5,17},{13,25},{29,21},{6,18},{14,26},{30,2... | collective-permute-start | bytes 1572872 | tf_op jit(solution)/shard_map/ppermute | solution.py:360
  78.9 30.4 %collective-permute-start.10 = (bf16[256,1024]{1,0:T(8,128)(2,1)}, bf16[256,1024]{1,0:T(8,128)(2,1)S(1)}, u32[]{:S(2)}, u32[]{:S(2)}) collective-permute-start(bf16[256,1024]{1,0:T(8,128)(2,1)} %collective-permute-done.9.refs_0_.refs_3_), channel_id=1, source_target_pairs={{0,4},{4,0},{8,12},{12,8},{16,20},{20,16},{24,28},{28,24},{1,5},{5... | collective-permute-start | bytes 1572872 | tf_op jit(solution)/shard_map/ppermute | solution.py:353
  82.7 9.7 %collective-permute-start.4 = (bf16[128,1024]{1,0:T(8,128)(2,1)S(1)}, bf16[128,1024]{1,0:T(8,128)(2,1)S(1)}, u32[]{:S(2)}, u32[]{:S(2)}) collective-permute-start(bf16[128,1024]{1,0:T(8,128)(2,1)S(1)} %collective-permute-done.3.refs_2_), channel_id=1, source_target_pairs={{0,1},{1,2},{2,3},{3,0},{4,5},{5,6},{6,7},{7,4},{8,9},{9,10},{10,1... | collective-permute-start | bytes 786440 | tf_op jit(solution)/shard_map/ppermute | solution.py:402
  87.4 15.6 %collective-permute-start.7 = (bf16[128,1024]{1,0:T(8,128)(2,1)S(1)}, bf16[128,1024]{1,0:T(8,128)(2,1)S(1)}, u32[]{:S(2)}, u32[]{:S(2)}) collective-permute-start(bf16[128,1024]{1,0:T(8,128)(2,1)S(1)} %collective-permute-done.6.refs_1_), channel_id=1, source_target_pairs={{0,1},{1,2},{2,3},{3,0},{4,5},{5,6},{6,7},{7,4},{8,9},{9,10},{10,1... | collective-permute-start | bytes 786440 | tf_op jit(solution)/shard_map/ppermute | solution.py:402
  92.5 3.4 %copy-start.2 = (bf16[1024,4096]{1,0:T(8,128)(2,1)S(1)}, bf16[1024,4096]{1,0:T(8,128)(2,1)}, u32[]{:S(2)}) copy-start(bf16[1024,4096]{1,0:T(8,128)(2,1)} %copy-done) | copy-start | bytes 25165828
  96.8 10.3 %copy-start.4 = (bf16[128,1024]{1,0:T(8,128)(2,1)S(1)}, bf16[128,1024]{1,0:T(8,128)(2,1)}, u32[]{:S(2)}) copy-start(bf16[128,1024]{1,0:T(8,128)(2,1)} %shard_map.77.refs_0_) | copy-start | bytes 786436
  96.8 12.6 %slice-start.2 = ((s8[8388608]{0:T(1024)(128)(4,1)}), s8[4194304]{0:T(1024)(128)(4,1)S(1)}, s32[]{:S(2)}) async-start(s8[8388608]{0:T(1024)(128)(4,1)} %bitcast.22), calls=%async_computation.2 | async-start | bytes 8388608
  100.8 8.6 %slice-start.3 = ((s8[8388608]{0:T(1024)(128)(4,1)}), s8[4194304]{0:T(1024)(128)(4,1)S(1)}, s32[]{:S(2)}) async-start(s8[8388608]{0:T(1024)(128)(4,1)} %bitcast.22), calls=%async_computation.3 | async-start | bytes 8388608
  100.8 27.4 %collective-permute-start.13 = (bf16[128,1024]{1,0:T(8,128)(2,1)S(1)}, bf16[128,1024]{1,0:T(8,128)(2,1)S(1)}, u32[]{:S(2)}, u32[]{:S(2)}) collective-permute-start(bf16[128,1024]{1,0:T(8,128)(2,1)S(1)} %shard_map.76.refs_0_), channel_id=1, source_target_pairs={{8,0},{12,4},{16,8},{20,12},{24,16},{28,20},{9,1},{13,5},{17,9},{2... | collective-permute-start | bytes 786440 | tf_op jit(solution)/shard_map/ppermute | solution.py:348
  103.0 12.3 %collective-permute-start.8 = (bf16[128,1024]{1,0:T(8,128)(2,1)S(1)}, bf16[128,1024]{1,0:T(8,128)(2,1)S(1)}, u32[]{:S(2)}, u32[]{:S(2)}) collective-permute-start(bf16[128,1024]{1,0:T(8,128)(2,1)S(1)} %collective-permute-done.7.refs_2_), channel_id=1, source_target_pairs={{0,1},{1,2},{2,3},{3,0},{4,5},{5,6},{6,7},{7,4},{8,9},{9,10},{10,1... | collective-permute-start | bytes 786440 | tf_op jit(solution)/shard_map/ppermute | solution.py:402
  107.1 8.2 %slice-start = ((s8[8388608]{0:T(1024)(128)(4,1)}), s8[4194304]{0:T(1024)(128)(4,1)S(1)}, s32[]{:S(2)}) async-start(s8[8388608]{0:T(1024)(128)(4,1)} %bitcast.20), calls=%async_computation | async-start | bytes 8388608
  109.4 5.9 %slice-start.1 = ((s8[8388608]{0:T(1024)(128)(4,1)}), s8[4194304]{0:T(1024)(128)(4,1)S(1)}, s32[]{:S(2)}) async-start(s8[8388608]{0:T(1024)(128)(4,1)} %bitcast.20), calls=%async_computation.1 | async-start | bytes 8388608
  109.4 21.4 %copy-start.12 = (s32[7]{0:T(128)S(1)}, s32[7]{0:T(128)}, u32[]{:S(2)}) copy-start(s32[7]{0:T(128)} %stack.53.refs_5_.facts_ref) | copy-start | bytes 88
  116.2 14.6 %collective-permute-start.14 = (bf16[128,1024]{1,0:T(8,128)(2,1)S(1)}, bf16[128,1024]{1,0:T(8,128)(2,1)S(1)}, u32[]{:S(2)}, u32[]{:S(2)}) collective-permute-start(bf16[128,1024]{1,0:T(8,128)(2,1)S(1)} %shard_map.81.refs_1_), channel_id=1, source_target_pairs={{8,0},{12,4},{16,8},{20,12},{24,16},{28,20},{9,1},{13,5},{17,9},{2... | collective-permute-start | bytes 786440 | tf_op jit(solution)/shard_map/ppermute | solution.py:348
  121.1 20.2 %collective-permute-start.17 = (bf16[128,1024]{1,0:T(8,128)(2,1)S(1)}, bf16[128,1024]{1,0:T(8,128)(2,1)S(1)}, u32[]{:S(2)}, u32[]{:S(2)}) collective-permute-start(bf16[128,1024]{1,0:T(8,128)(2,1)S(1)} %shard_map.76.refs_0_), channel_id=1, source_target_pairs={{4,0},{12,8},{20,16},{28,24},{16,4},{24,12},{5,1},{13,9},{21,17},{... | collective-permute-start | bytes 786440 | tf_op jit(solution)/shard_map/ppermute | solution.py:369
  128.3 13.0 %collective-permute-start.15 = (bf16[128,1024]{1,0:T(8,128)(2,1)S(1)}, bf16[128,1024]{1,0:T(8,128)(2,1)S(1)}, u32[]{:S(2)}, u32[]{:S(2)}) collective-permute-start(bf16[128,1024]{1,0:T(8,128)(2,1)S(1)} %collective-permute-done.13.refs_5_), channel_id=1, source_target_pairs={{0,4},{4,0},{8,12},{12,8},{16,20},{20,16},{24,28},{28,24},{1,5},{5... | collective-permute-start | bytes 786440 | tf_op jit(solution)/shard_map/ppermute | solution.py:353
  128.3 12.9 %collective-permute-start.18 = (bf16[128,1024]{1,0:T(8,128)(2,1)S(1)}, bf16[128,1024]{1,0:T(8,128)(2,1)S(1)}, u32[]{:S(2)}, u32[]{:S(2)}) collective-permute-start(bf16[128,1024]{1,0:T(8,128)(2,1)S(1)} %shard_map.81.refs_1_), channel_id=1, source_target_pairs={{4,0},{12,8},{20,16},{28,24},{16,4},{24,12},{5,1},{13,9},{21,17},{... | collective-permute-start | bytes 786440 | tf_op jit(solution)/shard_map/ppermute | solution.py:369
  130.8 10.5 %collective-permute-start.16 = (bf16[128,1024]{1,0:T(8,128)(2,1)S(1)}, bf16[128,1024]{1,0:T(8,128)(2,1)S(1)}, u32[]{:S(2)}, u32[]{:S(2)}) collective-permute-start(bf16[128,1024]{1,0:T(8,128)(2,1)S(1)} %collective-permute-done.14.refs_6_), channel_id=1, source_target_pairs={{0,4},{4,0},{8,12},{12,8},{16,20},{20,16},{24,28},{28,24},{1,5},{5... | collective-permute-start | bytes 786440 | tf_op jit(solution)/shard_map/ppermute | solution.py:353
  (5 other events, 4.3 us)

commit v4 on v3

--- a/solution.py
+++ b/solution.py
@@ -46,17 +46,41 @@
     return lax.dot_general(a, b, (((1,), (1,)), ((), ())), preferred_element_type=F32)
 
 
-def params(limit=VMEM):
-    return pltpu.CompilerParams(vmem_limit_bytes=limit)
+def params():
+    return pltpu.CompilerParams(vmem_limit_bytes=VMEM)
 
 
 def lanes_at(tile):
     return pl.ds(pl.multiple_of(tile * LANES, LANES), LANES)
 
 
-def prepare_kernel(*refs):
-    table_ref, back_ref, taps_ref, weight_ref, gate_ref = refs[:5]
-    spec_out, weight_out, gate_out, table_out, back_out, token_out, sems = refs[-7:]
+def write_facts(facts_ref, slot, docs_ref, block, length, end, inner, role):
+    start = block * length
+    stop = start + length - 1
+
+    def visit(at, found):
+        first, following, last = found
+        here = docs_ref[at]
+        first = jnp.minimum(first, jnp.where(here > start, here, end))
+        following = jnp.minimum(following, jnp.where(here > stop, here, end))
+        last = jnp.maximum(last, jnp.where(here <= stop, here, 0))
+        return first, following, last
+
+    whole = jnp.int32(end)
+    first, following, last = lax.fori_loop(
+        0, docs_ref.shape[0], visit, (whole, whole, jnp.int32(0))
+    )
+    facts_ref[slot, 0] = jnp.clip(first - start, 0, length)
+    facts_ref[slot, 1] = jnp.clip(last - start, 0, length)
+    for distance in range(1, REACH + 1):
+        facts_ref[slot, 1 + distance] = jnp.clip(following - start - distance * length, 0, length)
+    facts_ref[slot, 2 + REACH] = inner
+    facts_ref[slot, 3 + REACH] = role
+
+
+def prepare_kernel(pairs, *refs):
+    place_ref, docs_ref, table_ref, back_ref, taps_ref, weight_ref, gate_ref = refs[:7]
+    spec_out, weight_out, gate_out, table_out, back_out, facts_out, token_out, sems = refs[-8:]
     token_out[...] = jnp.zeros_like(token_out)
     copies = [
         pltpu.make_async_copy(source, target, sems.at[at])
@@ -65,14 +89,20 @@
         )
     ]
     step = pl.program_id(0)
+    length = table_ref.shape[1] // 2
 
     @pl.when(step == 0)
     def _():
         for copy in copies:
             copy.start()
-        table_out[...] = table_ref[...]
-
-    length = table_ref.shape[1] // 2
+        table_out[...] = table_ref[:, :length]
+        place = place_ref[0]
+        odd = lax.rem(place, 2)
+        role = jnp.where(place >= pairs - 3, pairs - place, 0)
+        end = 2 * pairs * length
+        write_facts(facts_out, 0, docs_ref, place, length, end, 1 - odd, role)
+        write_facts(facts_out, 1, docs_ref, 2 * pairs - 1 - place, length, end, odd, role)
+
     freq = lax.broadcasted_iota(jnp.int32, (length, 1), 0)
     sign = jnp.where(freq % 2 == 0, 1.0, -1.0).astype(F32)
     lanes = lanes_at(step)
@@ -103,21 +133,24 @@
             copy.wait()
 
 
-def prepare(table, back, taps, weight, gate, after):
+def prepare(pairs, place, docs, table, back, taps, weight, gate, after):
     count, width = taps.shape
     length = count // REACH
     return pl.pallas_call(
-        prepare_kernel,
+        functools.partial(prepare_kernel, pairs),
         grid=(width // LANES,),
         out_shape=(
             pltpu.VMEM((REACH + 1, 2 * length, width), F32),
             pltpu.VMEM(weight.shape, BF16),
             pltpu.VMEM(gate.shape, BF16),
-            pltpu.VMEM(table.shape, BF16),
+            pltpu.VMEM((2 * length, length), BF16),
             pltpu.VMEM(back.shape, BF16),
+            jax.ShapeDtypeStruct((2, 8), jnp.int32),
             jax.ShapeDtypeStruct((8, 128), F32),
         ),
         in_specs=[
+            SCALARS,
+            SCALARS,
             pl.BlockSpec((2 * length, 2 * length), lambda c: (0, 0)),
             OUTSIDE,
             pl.BlockSpec((count, LANES), lambda c: (0, c)),
@@ -125,15 +158,15 @@
             OUTSIDE,
         ]
         + [ANYWHERE] * len(after),
-        out_specs=(WHOLE,) * 5 + (TOKEN,),
+        out_specs=(WHOLE,) * 5 + (SCALARS, TOKEN),
         scratch_shapes=[pltpu.SemaphoreType.DMA((3,))],
-        compiler_params=params(2 * VMEM),
+        compiler_params=params(),
         cost_estimate=pl.CostEstimate(
             flops=2 * 3 * 2 * count * length * width,
             bytes_accessed=4 * (count * width + 8 * length * width),
             transcendentals=0,
         ),
-    )(table, back, taps, weight, gate, *after)
+    )(place, docs, table, back, taps, weight, gate, *after)
 
 
 def project_kernel(steps, slot, start, first, last, place_ref, *refs):
@@ -179,8 +212,9 @@
 
 
 class Conv:
-    def __init__(self, facts, table, back, spectra):
-        self.facts, self.table, self.back, self.spectra = facts, table, back, spectra
+    def __init__(self, slot, facts, table, back, spectra):
+        self.facts = [facts[slot, at] for at in range(4 + REACH)]
+        self.table, self.back, self.spectra = table, back, spectra
         self.length = table.shape[0] // 2
         self.lanes = lanes_at(pl.program_id(0))
         self.row = lax.broadcasted_iota(jnp.int32, (self.length, LANES), 0)
@@ -195,7 +229,7 @@
     def term(self, values, low, high, distance):
         length = self.length
         kept = jnp.where(self.within(low, high), values.astype(F32), 0.0).astype(BF16)
-        full = nn(self.table[...], jnp.concatenate([kept, kept], axis=0))
+        full = nn(self.table[...], kept)
         real, imag = full[:length], full[length:]
         k_real = self.spectra[distance, :length, self.lanes]
         k_imag = self.spectra[distance, length:, self.lanes]
@@ -244,9 +278,9 @@
 def upper_kernel(facts_ref, table_ref, back_ref, spec_ref, own_ref, *refs):
     halos, (out_ref, token_ref, acc_ref) = refs[:4], refs[-3:]
     token_ref[...] = jnp.zeros_like(token_ref)
-    conv = Conv(facts_ref, table_ref, back_ref, spec_ref)
+    conv = Conv(1, facts_ref, table_ref, back_ref, spec_ref)
     own = conv.joined([own_ref])
-    real, imag = conv.term(own, facts_ref[1], conv.length, 0)
+    real, imag = conv.term(own, conv.facts[1], conv.length, 0)
     acc_ref[: conv.length, :] = real
     acc_ref[conv.length :, :] = imag
     conv.far_terms(acc_ref, lambda distance: conv.halo(halos, distance, False))
@@ -260,9 +294,9 @@
 
 def own_kernel(pieces, facts_ref, table_ref, back_ref, spec_ref, *refs):
     own_refs, out_ref = refs[:pieces], refs[-1]
-    conv = Conv(facts_ref, table_ref, back_ref, spec_ref)
+    conv = Conv(0, facts_ref, table_ref, back_ref, spec_ref)
     own = conv.joined(own_refs)
-    out_ref[:, conv.lanes] = conv.signal(*conv.term(own, facts_ref[1], conv.length, 0))
+    out_ref[:, conv.lanes] = conv.signal(*conv.term(own, conv.facts[1], conv.length, 0))
 
     def write(value):
         out_ref[:, conv.lanes] = value
@@ -274,8 +308,8 @@
     near_ref, upper_ref, mate_ref, two_ref, fold_ref = refs[:5]
     halos = refs[5 : 5 + 3 * pieces]
     out_ref, acc_ref = refs[-2:]
-    conv = Conv(facts_ref, table_ref, back_ref, spec_ref)
-    role = facts_ref[6]
+    conv = Conv(0, facts_ref, table_ref, back_ref, spec_ref)
+    role = conv.facts[6]
 
     def values_of(distance):
         value = conv.halo(halos, distance, True)
@@ -287,14 +321,14 @@
         value = jnp.where(role == 2, conv.joined([upper_ref]), value)
         return jnp.where(role == 3, conv.joined([fold_ref]), value)
 
-    reaches = facts_ref[2] > 0
+    reaches = conv.facts[2] > 0
 
     @pl.when(reaches)
     def _():
         acc_ref[...] = jnp.zeros_like(acc_ref)
         conv.far_terms(acc_ref, values_of)
         signal = conv.signal(acc_ref[: conv.length, :], acc_ref[conv.length :, :])
-        kept = jnp.where(conv.row >= facts_ref[1], signal, 0.0)
+        kept = jnp.where(conv.row >= conv.facts[1], signal, 0.0)
         out_ref[0, 0] = near_ref[:, conv.lanes] + kept
 
     @pl.when(jnp.logical_not(reaches))
@@ -370,29 +404,12 @@
     return [two, core_swapped(two), mixed]
 
 
-def block_facts(doc_starts, block, length, end, inner, role):
-    start = block * length
-
-    def after(where):
-        return jnp.min(jnp.where(doc_starts > where, doc_starts, end))
-
-    first_end = jnp.clip(after(start) - start, 0, length)
-    last_start = jnp.max(jnp.where(doc_starts <= start + length - 1, doc_starts, 0)) - start
-    last_start = jnp.clip(last_start, 0, length)
-    reaches = after(start + length - 1) - start
-    facts = [first_end, last_start]
-    facts += [jnp.clip(reaches - distance * length, 0, length) for distance in range(1, REACH + 1)]
-    facts += [inner, role]
-    return jnp.stack(facts).astype(jnp.int32)
-
-
 def on_device(grad_out, out_weight, gate, filter_taps, doc_starts):
     pairs = lax.axis_size("ctx")
     place = lax.axis_index("ctx")
     length = grad_out.shape[2]
     width = out_weight.shape[0]
-    blocks = 2 * pairs
-    half = length // 2
+    cut = length * 5 // 8
     count = lax.axis_size("ch")
     lane = lax.axis_index("ch").astype(jnp.int32)[None]
     around = [(source, (source + 1) % count) for source in range(count)]
@@ -401,32 +418,34 @@
     def turned(piece):
         return lax.ppermute(piece, "ch", around)
 
-    def ring(piece):
-        shards = [piece]
-        for _ in range(1, count):
-            shards.append(turned(shards[-1]))
-        return shards
-
-    slices = [grad_out[0, 0, :half], grad_out[0, 0, half:]]
+    slices = [grad_out[0, 0, :cut], grad_out[0, 0, cut:]]
     upper_in = [grad_out[0, 1]]
     upper_in.append(turned(upper_in[0]))
 
-    odd = place % 2
-    role = jnp.where(place >= pairs - 3, pairs - place, 0)
-    end = blocks * length
-    lower_facts = block_facts(doc_starts, place, length, end, 1 - odd, role)
-    upper_facts = block_facts(doc_starts, blocks - 1 - place, length, end, odd, role)
     table, back = (jnp.asarray(one) for one in tables(length))
-    spectra, weight, gates, table, back, prepared = prepare(
-        table, back, filter_taps, out_weight, gate, [lower_facts, upper_facts, *slices]
+    spectra, weight, gates, table, back, facts, prepared = prepare(
+        pairs,
+        place.astype(jnp.int32)[None],
+        doc_starts,
+        table,
+        back,
+        filter_taps,
+        out_weight,
+        gate,
+        slices,
     )
     tabs = (table, back, spectra)
 
     upper_in[1] = ordered(upper_in[1], prepared)
     for step in range(2, count):
         upper_in.append(turned(upper_in[-1]))
-    first_in = ring(ordered(slices[0], upper_in[-2]))
-    second_in = ring(ordered(slices[1], upper_in[-1]))
+    first_in = [ordered(slices[0], upper_in[-2])]
+    for step in range(1, count):
+        first_in.append(turned(first_in[-1]))
+    second_in = [ordered(slices[1], upper_in[-1])]
+    second_in.append(ordered(turned(second_in[0]), first_in[-1]))
+    for step in range(2, count):
+        second_in.append(turned(second_in[-1]))
 
     upper = project(lane, upper_in, everything, weight, gates, 1, 0, after=[first_in[1]])
     upper_halo = upper_halo_of(upper)
@@ -434,7 +453,7 @@
     result, convolved = conv_call(
         upper_kernel,
         tabs,
-        upper_facts,
+        facts,
         [upper, *upper_halo],
         (out_shape, jax.ShapeDtypeStruct((8, 128), F32)),
         (pl.BlockSpec((1, 1, length, LANES), lambda c: (0, 1, 0, c)), TOKEN),
@@ -445,16 +464,16 @@
     first = project(lane, first_in, everything, weight, gates, 0, 0)
     first_halo = lower_halo_of(first)
     partial = project(
-        lane, second_in[:-1], everything[:-1], weight, gates, 0, half, last=False
+        lane, second_in[:-1], everything[:-1], weight, gates, 0, cut, last=False
     )
     second = project(
-        lane, second_in[-1:], everything[-1:], weight, gates, 0, half, partial, after=[convolved]
+        lane, second_in[-1:], everything[-1:], weight, gates, 0, cut, partial, after=[convolved]
     )
     second_halo = lower_halo_of(second)
     near = conv_call(
         functools.partial(own_kernel, 2),
         tabs,
-        lower_facts,
+        facts,
         [first, second],
         pltpu.VMEM((length, width), F32),
         WHOLE,
@@ -466,7 +485,7 @@
     return conv_call(
         functools.partial(far_kernel, 2),
         tabs,
-        lower_facts,
+        facts,
         [near, upper, mate, two, fold, *halos],
         out_shape,
         pl.BlockSpec((1, 1, length, LANES), lambda c: (0, 0, 0, c)),

time: 149 us -> 147 us (0.987)
  the two profiles are of different devices: /device:TPU:29 before, /device:TPU:19 now
where the time goes in v4:
time: 147 us; the launch traced here: 145 us
  starting transfers between devices  43.5 us (30%)
  waiting for transfers between devices  37.9 us (26%)
  Pallas kernels  34.3 us (23%)
  local copies, waits for them, and re-layouts  29.4 us (20%)
    ppermute x9, waiting for transfers between devices, turned(): return lax.ppermute(piece, 'ch', around)  37.8 us
    unnamed x44, local copies, waits for them, and re-layouts  26.3 us
    ppermute x9, starting transfers between devices, turned(): return lax.ppermute(piece, 'ch', around)  17.4 us
    pallas_call x3, Pallas kernels, conv_call(): pl.pallas_call(body, grid=(width // LANES,), out_shape=out_shape, in_spec...  16.7 us
    pallas_call x4, Pallas kernels, project(): pl.pallas_call(body, out_shape=pltpu.VMEM((rows, width), BF16 if last els...  11.3 us
    ppermute x3, starting transfers between devices, shifted(): lax.ppermute(value, 'ctx', [(source, source + steps) for source in range(...  11.1 us
    ppermute x2, starting transfers between devices, lower_halo_of(): mixed = lax.ppermute(value, 'ctx', mixed)  6.6 us
    ppermute x4, starting transfers between devices, core_swapped(): lax.ppermute(value, 'ctx', [(source, source ^ 1) for source in range(coun...  6.39 us
  transfers between devices with their start and end apart: 19, of which 4 were waited for; matrix products, arithmetic and copies ran while one was open for 1% of the time, Pallas kernels for 17%

profile of v4, /device:TPU:19, one launch (start us, length us, event | category | flops | bytes accessed | tf_op | source)
XLA Modules:
  0.0 145.4 jit_solution(11928762633920456837)
XLA Ops:
  1.1 1.3 collective-permute-start
  4.5 3.5 %copy-done.6 = bf16[1024,4096]{1,0:T(8,128)(2,1)S(1)} copy-done((bf16[1024,4096]{1,0:T(8,128)(2,1)S(1)}, bf16[1024,4096]{1,0:T(8,128)(2,1)}, u32[]{:S(2)}) %copy-start.6) | copy-done | bytes 8388632
  8.0 1.9 %copy-done.9 = f32[768,1024]{1,0:T(8,128)S(1)} copy-done((f32[768,1024]{1,0:T(8,128)S(1)}, f32[768,1024]{1,0:T(8,128)}, u32[]{:S(2)}) %copy-start.9) | copy-done | bytes 3145752
  9.9 1.2 copy-done.17
  13.8 6.3 %shard_map.73 = (f32[4,512,1024]{2,1,0:T(8,128)S(1)}, bf16[1024,4096]{1,0:T(8,128)(2,1)S(1)}, bf16[1,2,256,1024]{3,2,1,0:T(8,128)(2,1)S(1)}, bf16[512,256]{1,0:T...) custom-call(s32[1]{0:T(128)} %bitcast.refs_0_, s32[32]{0:T(128)S(1)} %copy-done.21, ...), custom_call_target="tpu_custom_call" | custom-call | flops 2415919104 | bytes 11534336 | tf_op jit(solution)/shard_map/pallas_call | solution.py:139
  20.1 3.2 %copy-done = bf16[1024,4096]{1,0:T(8,128)(2,1)} copy-done((bf16[1024,4096]{1,0:T(8,128)(2,1)}, bf16[1024,4096]{1,0:T(8,128)(2,1)S(1)}, u32[]{:S(2)}) %copy-start) | copy-done | bytes 8388632
  23.4 3.3 %copy-done.4 = f32[4,512,1024]{2,1,0:T(8,128)} copy-done((f32[4,512,1024]{2,1,0:T(8,128)}, f32[4,512,1024]{2,1,0:T(8,128)S(1)}, u32[]{:S(2)}) %copy-start.4) | copy-done | bytes 8388632
  28.2 12.6 %collective-permute-done.1.refs_1_.refs_2_ = bf16[256,1024]{1,0:T(8,128)(2,1)} collective-permute-done((bf16[256,1024]{1,0:T(8,128)(2,1)}, bf16[256,1024]{1,0:T(8,128)(2,1)}, u32[]{:S(2)}, u32[]{:S(2)}) %collective-permute-start.1) | collective-permute-done | bytes 524320 | tf_op jit(solution)/shard_map/ppermute | solution.py:419
  41.2 2.7 %collective-permute-start.2 = (bf16[160,1024]{1,0:T(8,128)(2,1)}, bf16[160,1024]{1,0:T(8,128)(2,1)S(1)}, u32[]{:S(2)}, u32[]{:S(2)}) collective-permute-start(bf16[160,1024]{1,0:T(8,128)(2,1)} %shard_map.75.refs_0_), channel_id=1, source_target_pairs={{0,1},{1,2},{2,3},{3,0},{4,5},{5,6},{6,7},{7,4},{8,9},{9,10},{10,1... | collective-permute-start | bytes 983048 | tf_op jit(solution)/shard_map/ppermute | solution.py:419
  44.0 15.7 %collective-permute-done.2.refs_1_.refs_6_ = bf16[160,1024]{1,0:T(8,128)(2,1)S(1)} collective-permute-done((bf16[160,1024]{1,0:T(8,128)(2,1)}, bf16[160,1024]{1,0:T(8,128)(2,1)S(1)}, u32[]{:S(2)}, u32[]{:S(2)}) %collective-permute-start.2) | collective-permute-done | bytes 327712 | tf_op jit(solution)/shard_map/ppermute | solution.py:419
  59.6 3.6 %copy-done.1 = bf16[1024,4096]{1,0:T(8,128)(2,1)S(1)} copy-done((bf16[1024,4096]{1,0:T(8,128)(2,1)S(1)}, bf16[1024,4096]{1,0:T(8,128)(2,1)}, u32[]{:S(2)}) %copy-start.1) | copy-done | bytes 8388632
  65.3 3.4 %shard_map.80.own_ref.refs_1_ = bf16[256,1024]{1,0:T(8,128)(2,1)S(1)} custom-call(s32[1]{0:T(128)} %bitcast.3.place_ref, bf16[256,1024]{1,0:T(8,128)(2,1)S(1)} %copy-done.14, bf16[256,1024]{1,0:T(8,128)(2,1)S(1)} %copy-done.16, bf16[256,1024]{1,0:T(8,128)(2,1)} %collective-permute-done.1.refs_1_.refs_2_, ...), custom_call_target="tpu_custom_call" | custom-call | flops 2147483648 | bytes 10485760 | tf_op jit(solution)/shard_map/pallas_call | solution.py:200
  68.7 3.1 %collective-permute-start.9 = (bf16[256,1024]{1,0:T(8,128)(2,1)S(1)}, bf16[256,1024]{1,0:T(8,128)(2,1)}, u32[]{:S(2)}, u32[]{:S(2)}) collective-permute-start(bf16[256,1024]{1,0:T(8,128)(2,1)S(1)} %shard_map.80.own_ref.refs_1_), channel_id=1, source_target_pairs={{0,8},{4,12},{8,16},{12,20},{16,24},{20,28},{1,9},{5,13},{9,17},{1... | collective-permute-start | bytes 1572872 | tf_op jit(solution)/shard_map/ppermute | solution.py:382
  72.9 5.4 %collective-permute-done.3.refs_2_ = bf16[160,1024]{1,0:T(8,128)(2,1)} collective-permute-done((bf16[160,1024]{1,0:T(8,128)(2,1)S(1)}, bf16[160,1024]{1,0:T(8,128)(2,1)}, u32[]{:S(2)}, u32[]{:S(2)}) %collective-permute-start.3) | collective-permute-done | bytes 327712 | tf_op jit(solution)/shard_map/ppermute | solution.py:419
  78.2 2.6 %collective-permute-start.4 = (bf16[160,1024]{1,0:T(8,128)(2,1)}, bf16[160,1024]{1,0:T(8,128)(2,1)}, u32[]{:S(2)}, u32[]{:S(2)}) collective-permute-start(bf16[160,1024]{1,0:T(8,128)(2,1)} %collective-permute-done.3.refs_2_), channel_id=1, source_target_pairs={{0,1},{1,2},{2,3},{3,0},{4,5},{5,6},{6,7},{7,4},{8,9},{9,10},{10,1... | collective-permute-start | bytes 983048 | tf_op jit(solution)/shard_map/ppermute | solution.py:419
  80.8 4.2 %collective-permute-start.11 = (bf16[256,1024]{1,0:T(8,128)(2,1)S(1)}, bf16[256,1024]{1,0:T(8,128)(2,1)}, u32[]{:S(2)}, u32[]{:S(2)}) collective-permute-start(bf16[256,1024]{1,0:T(8,128)(2,1)S(1)} %shard_map.80.own_ref.refs_1_), channel_id=1, source_target_pairs={{0,4},{4,0},{8,12},{12,8},{16,20},{20,16},{24,28},{28,24},{1,5},{5... | collective-permute-start | bytes 1572872 | tf_op jit(solution)/shard_map/ppermute | solution.py:387
  85.0 2.1 %collective-permute-start.12 = (bf16[256,1024]{1,0:T(8,128)(2,1)S(1)}, bf16[256,1024]{1,0:T(8,128)(2,1)}, u32[]{:S(2)}, u32[]{:S(2)}) collective-permute-start(bf16[256,1024]{1,0:T(8,128)(2,1)S(1)} %shard_map.80.own_ref.refs_1_), channel_id=1, source_target_pairs={{4,16},{12,24},{28,20},{5,17},{13,25},{29,21},{6,18},{14,26},{30,2... | collective-permute-start | bytes 1572872 | tf_op jit(solution)/shard_map/ppermute | solution.py:394
  87.1 4.2 %collective-permute-start.6 = (bf16[96,1024]{1,0:T(8,128)(2,1)}, bf16[96,1024]{1,0:T(8,128)(2,1)}, u32[]{:S(2)}, u32[]{:S(2)}) collective-permute-start(bf16[96,1024]{1,0:T(8,128)(2,1)} %shard_map.77.refs_0_), channel_id=1, source_target_pairs={{0,1},{1,2},{2,3},{3,0},{4,5},{5,6},{6,7},{7,4},{8,9},{9,10},{10,1... | collective-permute-start | bytes 589832 | tf_op jit(solution)/shard_map/ppermute | solution.py:419
  91.3 4.2 %collective-permute-done.6.refs_0_ = bf16[96,1024]{1,0:T(8,128)(2,1)} collective-permute-done((bf16[96,1024]{1,0:T(8,128)(2,1)}, bf16[96,1024]{1,0:T(8,128)(2,1)}, u32[]{:S(2)}, u32[]{:S(2)}) %collective-permute-start.6) | collective-permute-done | bytes 196640 | tf_op jit(solution)/shard_map/ppermute | solution.py:419
  95.4 2.2 %collective-permute-start.7 = (bf16[96,1024]{1,0:T(8,128)(2,1)}, bf16[96,1024]{1,0:T(8,128)(2,1)S(1)}, u32[]{:S(2)}, u32[]{:S(2)}) collective-permute-start(bf16[96,1024]{1,0:T(8,128)(2,1)} %shard_map.78.refs_1_), channel_id=1, source_target_pairs={{0,1},{1,2},{2,3},{3,0},{4,5},{5,6},{6,7},{7,4},{8,9},{9,10},{10,1... | collective-permute-start | bytes 589832 | tf_op jit(solution)/shard_map/ppermute | solution.py:419
  97.6 3.4 %copy-done.2 = bf16[1024,4096]{1,0:T(8,128)(2,1)S(1)} copy-done((bf16[1024,4096]{1,0:T(8,128)(2,1)S(1)}, bf16[1024,4096]{1,0:T(8,128)(2,1)}, u32[]{:S(2)}) %copy-start.2) | copy-done | bytes 8388632
  101.0 4.1 %shard_map.76.refs_0_ = bf16[160,1024]{1,0:T(8,128)(2,1)S(1)} custom-call(s32[1]{0:T(128)} %bitcast.3.place_ref, bf16[160,1024]{1,0:T(8,128)(2,1)S(1)} %copy-done.8, bf16[160,1024]{1,0:T(8,128)(2,1)S(1)} %collective-permute-done.2.refs_1_.refs_6_, bf16[160,1024]{1,0:T(8,128)(2,1)} %collective-permute-done.3.refs_2_, ...), custom_call_target="tpu_custom_call" | custom-call | flops 1342177280 | bytes 9699328 | tf_op jit(solution)/shard_map/pallas_call | solution.py:200
  105.2 4.2 %collective-permute-start.13 = (bf16[160,1024]{1,0:T(8,128)(2,1)S(1)}, bf16[160,1024]{1,0:T(8,128)(2,1)S(1)}, u32[]{:S(2)}, u32[]{:S(2)}) collective-permute-start(bf16[160,1024]{1,0:T(8,128)(2,1)S(1)} %shard_map.76.refs_0_), channel_id=1, source_target_pairs={{8,0},{12,4},{16,8},{20,12},{24,16},{28,20},{9,1},{13,5},{17,9},{2... | collective-permute-start | bytes 983048 | tf_op jit(solution)/shard_map/ppermute | solution.py:382
  109.3 2.8 %collective-permute-start.8 = (bf16[96,1024]{1,0:T(8,128)(2,1)S(1)}, bf16[96,1024]{1,0:T(8,128)(2,1)S(1)}, u32[]{:S(2)}, u32[]{:S(2)}) collective-permute-start(bf16[96,1024]{1,0:T(8,128)(2,1)S(1)} %collective-permute-done.7.refs_2_), channel_id=1, source_target_pairs={{0,1},{1,2},{2,3},{3,0},{4,5},{5,6},{6,7},{7,4},{8,9},{9,10},{10,1... | collective-permute-start | bytes 589832 | tf_op jit(solution)/shard_map/ppermute | solution.py:419
  112.2 3.0 %shard_map.79.refs_3_ = f32[96,1024]{1,0:T(8,128)S(1)} custom-call(s32[1]{0:T(128)} %bitcast.3.place_ref, bf16[96,1024]{1,0:T(8,128)(2,1)S(1)} %copy-done.11, bf16[96,1024]{1,0:T(8,128)(2,1)} %shard_map.78.refs_1_, bf16[96,1024]{1,0:T(8,128)(2,1)S(1)} %collective-permute-done.7.refs_2_, bf16[1024,4096]{1,0:T(8,128)(2,1)S(1)} %copy-done.3, ...), custom_call_target="tpu_custom_call" | custom-call | flops 603979776 | bytes 6881280 | tf_op jit(solution)/shard_map/pallas_call | solution.py:200
  115.2 5.6 %shard_map.81 = (f32[1,2,256,1024]{3,2,1,0:T(8,128)}, f32[8,128]{1,0:T(8,128)S(1)}) custom-call(s32[2,8]{1,0:T(2,128)S(1)} %get-tuple-element.14.facts_ref, bf16[512,256]{1,0:T(8,128)(2,1)S(1)} %get-tuple-element.15.table_ref, bf16[256,1024]{1,0:T(8,128)(2,1)S(1)} %get-tuple-element.16.back_ref, f32[4,512,1024]{2,1,0:T(8,128)S(1)} %copy-done.5, ...), custom_call_target="tpu_custom_call" | custom-call | flops 3221225472 | bytes 1048576 | tf_op jit(solution)/shard_map/pallas_call | solution.py:352
  121.5 3.8 %collective-permute-start.14 = (bf16[96,1024]{1,0:T(8,128)(2,1)S(1)}, bf16[96,1024]{1,0:T(8,128)(2,1)S(1)}, u32[]{:S(2)}, u32[]{:S(2)}) collective-permute-start(bf16[96,1024]{1,0:T(8,128)(2,1)S(1)} %shard_map.82.refs_1_), channel_id=1, source_target_pairs={{8,0},{12,4},{16,8},{20,12},{24,16},{28,20},{9,1},{13,5},{17,9},{2... | collective-permute-start | bytes 589832 | tf_op jit(solution)/shard_map/ppermute | solution.py:382
  125.3 4.2 %collective-permute-start.17 = (bf16[160,1024]{1,0:T(8,128)(2,1)S(1)}, bf16[160,1024]{1,0:T(8,128)(2,1)S(1)}, u32[]{:S(2)}, u32[]{:S(2)}) collective-permute-start(bf16[160,1024]{1,0:T(8,128)(2,1)S(1)} %shard_map.76.refs_0_), channel_id=1, source_target_pairs={{4,0},{12,8},{20,16},{28,24},{16,4},{24,12},{5,1},{13,9},{21,17},{... | collective-permute-start | bytes 983048 | tf_op jit(solution)/shard_map/ppermute | solution.py:403
  129.6 2.4 %collective-permute-start.18 = (bf16[96,1024]{1,0:T(8,128)(2,1)S(1)}, bf16[96,1024]{1,0:T(8,128)(2,1)S(1)}, u32[]{:S(2)}, u32[]{:S(2)}) collective-permute-start(bf16[96,1024]{1,0:T(8,128)(2,1)S(1)} %shard_map.82.refs_1_), channel_id=1, source_target_pairs={{4,0},{12,8},{20,16},{28,24},{16,4},{24,12},{5,1},{13,9},{21,17},{... | collective-permute-start | bytes 589832 | tf_op jit(solution)/shard_map/ppermute | solution.py:403
  132.0 2.1 %collective-permute-start.16 = (bf16[96,1024]{1,0:T(8,128)(2,1)S(1)}, bf16[96,1024]{1,0:T(8,128)(2,1)S(1)}, u32[]{:S(2)}, u32[]{:S(2)}) collective-permute-start(bf16[96,1024]{1,0:T(8,128)(2,1)S(1)} %collective-permute-done.14.refs_6_), channel_id=1, source_target_pairs={{0,4},{4,0},{8,12},{12,8},{16,20},{20,16},{24,28},{28,24},{1,5},{5... | collective-permute-start | bytes 589832 | tf_op jit(solution)/shard_map/ppermute | solution.py:387
  134.2 5.6 %shard_map.83.refs_0_ = f32[256,1024]{1,0:T(8,128)S(1)} custom-call(s32[2,8]{1,0:T(2,128)S(1)} %get-tuple-element.14.facts_ref, bf16[512,256]{1,0:T(8,128)(2,1)S(1)} %get-tuple-element.15.table_ref, bf16[256,1024]{1,0:T(8,128)(2,1)S(1)} %get-tuple-element.16.back_ref, f32[4,512,1024]{2,1,0:T(8,128)S(1)} %copy-done.5, ...), custom_call_target="tpu_custom_call" | custom-call | flops 2147483648 | bytes 1048576 | tf_op jit(solution)/shard_map/pallas_call | solution.py:352
  139.8 5.5 %shard_map.84 = f32[1,2,256,1024]{3,2,1,0:T(8,128)} custom-call(s32[2,8]{1,0:T(2,128)S(1)} %get-tuple-element.14.facts_ref, bf16[512,256]{1,0:T(8,128)(2,1)S(1)} %get-tuple-element.15.table_ref, bf16[256,1024]{1,0:T(8,128)(2,1)S(1)} %get-tuple-element.16.back_ref, f32[4,512,1024]{2,1,0:T(8,128)S(1)} %copy-done.5, ...), custom_call_target="tpu_custom_call", output_to_operand_aliasing={{}: (15, {})} | custom-call | flops 2147483648 | bytes 1048576 | tf_op jit(solution)/shard_map/pallas_call | solution.py:352
  (65 shorter events, 11.8 us)
Async XLA Ops:
  1.1 40.1 %copy-start.13 = (bf16[256,1024]{1,0:T(8,128)(2,1)}, bf16[256,1024]{1,0:T(8,128)(2,1)S(1)}, u32[]{:S(2)}) copy-start(bf16[256,1024]{1,0:T(8,128)(2,1)S(1)} %slice_bitcast_fusion.refs_0_) | copy-start | bytes 1572868
  1.1 26.2 %collective-permute-start = (bf16[256,1024]{1,0:T(8,128)(2,1)S(1)}, bf16[256,1024]{1,0:T(8,128)(2,1)S(1)}, u32[]{:S(2)}, u32[]{:S(2)}) collective-permute-start(bf16[256,1024]{1,0:T(8,128)(2,1)S(1)} %slice_bitcast_fusion.refs_0_), channel_id=1, source_target_pairs={{0,1},{1,2},{2,3},{3,0},{4,5},{5,6},{6,7},{7,4},{8,9},{9,10},{10,1... | collective-permute-start | bytes 1572872 | tf_op jit(solution)/shard_map/ppermute | solution.py:419
  3.4 37.8 %copy-start.10 = (bf16[96,1024]{1,0:T(8,128)(2,1)}, bf16[96,1024]{1,0:T(8,128)(2,1)S(1)}, u32[]{:S(2)}) copy-start(bf16[96,1024]{1,0:T(8,128)(2,1)S(1)} %slice_bitcast_fusion.2.refs_8_.refs_0_) | copy-start | bytes 589828
  4.5 36.8 %copy-start.7 = (bf16[160,1024]{1,0:T(8,128)(2,1)}, bf16[160,1024]{1,0:T(8,128)(2,1)S(1)}, u32[]{:S(2)}) copy-start(bf16[160,1024]{1,0:T(8,128)(2,1)S(1)} %slice_bitcast_fusion.1.refs_7_.refs_0_) | copy-start | bytes 983044
  4.5 3.5 %copy-start.6 = (bf16[1024,4096]{1,0:T(8,128)(2,1)S(1)}, bf16[1024,4096]{1,0:T(8,128)(2,1)}, u32[]{:S(2)}) copy-start(bf16[1024,4096]{1,0:T(8,128)(2,1)} %refs_5_.1) | copy-start | bytes 25165828
  20.1 3.2 %copy-start = (bf16[1024,4096]{1,0:T(8,128)(2,1)}, bf16[1024,4096]{1,0:T(8,128)(2,1)S(1)}, u32[]{:S(2)}) copy-start(bf16[1024,4096]{1,0:T(8,128)(2,1)S(1)} %get-tuple-element.19.refs_4_.refs_3_.refs_1_) | copy-start | bytes 25165828
  23.4 3.3 %copy-start.4 = (f32[4,512,1024]{2,1,0:T(8,128)}, f32[4,512,1024]{2,1,0:T(8,128)S(1)}, u32[]{:S(2)}) copy-start(f32[4,512,1024]{2,1,0:T(8,128)S(1)} %get-tuple-element.17.spec_ref) | copy-start | bytes 25165828
  28.0 12.8 %collective-permute-start.1 = (bf16[256,1024]{1,0:T(8,128)(2,1)}, bf16[256,1024]{1,0:T(8,128)(2,1)}, u32[]{:S(2)}, u32[]{:S(2)}) collective-permute-start(bf16[256,1024]{1,0:T(8,128)(2,1)} %shard_map.74.refs_1_), channel_id=1, source_target_pairs={{0,1},{1,2},{2,3},{3,0},{4,5},{5,6},{6,7},{7,4},{8,9},{9,10},{10,1... | collective-permute-start | bytes 1572872 | tf_op jit(solution)/shard_map/ppermute | solution.py:419
  40.8 18.8 %collective-permute-start.5 = (bf16[256,1024]{1,0:T(8,128)(2,1)}, bf16[256,1024]{1,0:T(8,128)(2,1)S(1)}, u32[]{:S(2)}, u32[]{:S(2)}) collective-permute-start(bf16[256,1024]{1,0:T(8,128)(2,1)} %collective-permute-done.1.refs_1_.refs_2_), channel_id=1, source_target_pairs={{0,1},{1,2},{2,3},{3,0},{4,5},{5,6},{6,7},{7,4},{8,9},{9,10},{10,1... | collective-permute-start | bytes 1572872 | tf_op jit(solution)/shard_map/ppermute | solution.py:419
  41.2 18.4 %collective-permute-start.2 = (bf16[160,1024]{1,0:T(8,128)(2,1)}, bf16[160,1024]{1,0:T(8,128)(2,1)S(1)}, u32[]{:S(2)}, u32[]{:S(2)}) collective-permute-start(bf16[160,1024]{1,0:T(8,128)(2,1)} %shard_map.75.refs_0_), channel_id=1, source_target_pairs={{0,1},{1,2},{2,3},{3,0},{4,5},{5,6},{6,7},{7,4},{8,9},{9,10},{10,1... | collective-permute-start | bytes 983048 | tf_op jit(solution)/shard_map/ppermute | solution.py:419
  59.6 27.5 %copy-start.12 = (bf16[256,1024]{1,0:T(8,128)(2,1)}, bf16[256,1024]{1,0:T(8,128)(2,1)S(1)}, u32[]{:S(2)}) copy-start(bf16[256,1024]{1,0:T(8,128)(2,1)S(1)} %collective-permute-done.5.refs_1_.refs_3_) | copy-start | bytes 1572868
  59.6 3.6 %copy-start.1 = (bf16[1024,4096]{1,0:T(8,128)(2,1)S(1)}, bf16[1024,4096]{1,0:T(8,128)(2,1)}, u32[]{:S(2)}) copy-start(bf16[1024,4096]{1,0:T(8,128)(2,1)} %copy-done) | copy-start | bytes 25165828
  65.3 32.3 %copy-start.8 = (bf16[160,1024]{1,0:T(8,128)(2,1)S(1)}, bf16[160,1024]{1,0:T(8,128)(2,1)}, u32[]{:S(2)}) copy-start(bf16[160,1024]{1,0:T(8,128)(2,1)} %shard_map.75.refs_0_) | copy-start | bytes 983044
  68.7 18.3 %collective-permute-start.9 = (bf16[256,1024]{1,0:T(8,128)(2,1)S(1)}, bf16[256,1024]{1,0:T(8,128)(2,1)}, u32[]{:S(2)}, u32[]{:S(2)}) collective-permute-start(bf16[256,1024]{1,0:T(8,128)(2,1)S(1)} %shard_map.80.own_ref.refs_1_), channel_id=1, source_target_pairs={{0,8},{4,12},{8,16},{12,20},{16,24},{20,28},{1,9},{5,13},{9,17},{1... | collective-permute-start | bytes 1572872 | tf_op jit(solution)/shard_map/ppermute | solution.py:382
  71.9 6.4 %collective-permute-start.3 = (bf16[160,1024]{1,0:T(8,128)(2,1)S(1)}, bf16[160,1024]{1,0:T(8,128)(2,1)}, u32[]{:S(2)}, u32[]{:S(2)}) collective-permute-start(bf16[160,1024]{1,0:T(8,128)(2,1)S(1)} %collective-permute-done.2.refs_1_.refs_6_), channel_id=1, source_target_pairs={{0,1},{1,2},{2,3},{3,0},{4,5},{5,6},{6,7},{7,4},{8,9},{9,10},{10,1... | collective-permute-start | bytes 983048 | tf_op jit(solution)/shard_map/ppermute | solution.py:419
  78.2 17.2 %collective-permute-start.4 = (bf16[160,1024]{1,0:T(8,128)(2,1)}, bf16[160,1024]{1,0:T(8,128)(2,1)}, u32[]{:S(2)}, u32[]{:S(2)}) collective-permute-start(bf16[160,1024]{1,0:T(8,128)(2,1)} %collective-permute-done.3.refs_2_), channel_id=1, source_target_pairs={{0,1},{1,2},{2,3},{3,0},{4,5},{5,6},{6,7},{7,4},{8,9},{9,10},{10,1... | collective-permute-start | bytes 983048 | tf_op jit(solution)/shard_map/ppermute | solution.py:419
  80.8 34.3 %collective-permute-start.11 = (bf16[256,1024]{1,0:T(8,128)(2,1)S(1)}, bf16[256,1024]{1,0:T(8,128)(2,1)}, u32[]{:S(2)}, u32[]{:S(2)}) collective-permute-start(bf16[256,1024]{1,0:T(8,128)(2,1)S(1)} %shard_map.80.own_ref.refs_1_), channel_id=1, source_target_pairs={{0,4},{4,0},{8,12},{12,8},{16,20},{20,16},{24,28},{28,24},{1,5},{5... | collective-permute-start | bytes 1572872 | tf_op jit(solution)/shard_map/ppermute | solution.py:387
  85.0 30.1 %collective-permute-start.12 = (bf16[256,1024]{1,0:T(8,128)(2,1)S(1)}, bf16[256,1024]{1,0:T(8,128)(2,1)}, u32[]{:S(2)}, u32[]{:S(2)}) collective-permute-start(bf16[256,1024]{1,0:T(8,128)(2,1)S(1)} %shard_map.80.own_ref.refs_1_), channel_id=1, source_target_pairs={{4,16},{12,24},{28,20},{5,17},{13,25},{29,21},{6,18},{14,26},{30,2... | collective-permute-start | bytes 1572872 | tf_op jit(solution)/shard_map/ppermute | solution.py:394
  87.1 28.1 %collective-permute-start.10 = (bf16[256,1024]{1,0:T(8,128)(2,1)}, bf16[256,1024]{1,0:T(8,128)(2,1)}, u32[]{:S(2)}, u32[]{:S(2)}) collective-permute-start(bf16[256,1024]{1,0:T(8,128)(2,1)} %collective-permute-done.9.refs_0_.refs_3_), channel_id=1, source_target_pairs={{0,4},{4,0},{8,12},{12,8},{16,20},{20,16},{24,28},{28,24},{1,5},{5... | collective-permute-start | bytes 1572872 | tf_op jit(solution)/shard_map/ppermute | solution.py:387
  87.1 25.1 %copy-start.11 = (bf16[96,1024]{1,0:T(8,128)(2,1)S(1)}, bf16[96,1024]{1,0:T(8,128)(2,1)}, u32[]{:S(2)}) copy-start(bf16[96,1024]{1,0:T(8,128)(2,1)} %shard_map.77.refs_0_) | copy-start | bytes 589828
  87.1 8.3 %collective-permute-start.6 = (bf16[96,1024]{1,0:T(8,128)(2,1)}, bf16[96,1024]{1,0:T(8,128)(2,1)}, u32[]{:S(2)}, u32[]{:S(2)}) collective-permute-start(bf16[96,1024]{1,0:T(8,128)(2,1)} %shard_map.77.refs_0_), channel_id=1, source_target_pairs={{0,1},{1,2},{2,3},{3,0},{4,5},{5,6},{6,7},{7,4},{8,9},{9,10},{10,1... | collective-permute-start | bytes 589832 | tf_op jit(solution)/shard_map/ppermute | solution.py:419
  95.4 13.9 %collective-permute-start.7 = (bf16[96,1024]{1,0:T(8,128)(2,1)}, bf16[96,1024]{1,0:T(8,128)(2,1)S(1)}, u32[]{:S(2)}, u32[]{:S(2)}) collective-permute-start(bf16[96,1024]{1,0:T(8,128)(2,1)} %shard_map.78.refs_1_), channel_id=1, source_target_pairs={{0,1},{1,2},{2,3},{3,0},{4,5},{5,6},{6,7},{7,4},{8,9},{9,10},{10,1... | collective-permute-start | bytes 589832 | tf_op jit(solution)/shard_map/ppermute | solution.py:419
  97.6 3.4 %copy-start.2 = (bf16[1024,4096]{1,0:T(8,128)(2,1)S(1)}, bf16[1024,4096]{1,0:T(8,128)(2,1)}, u32[]{:S(2)}) copy-start(bf16[1024,4096]{1,0:T(8,128)(2,1)} %copy-done) | copy-start | bytes 25165828
  101.0 11.2 %copy-start.3 = (bf16[1024,4096]{1,0:T(8,128)(2,1)S(1)}, bf16[1024,4096]{1,0:T(8,128)(2,1)}, u32[]{:S(2)}) copy-start(bf16[1024,4096]{1,0:T(8,128)(2,1)} %copy-done) | copy-start | bytes 25165828
  101.0 14.1 %copy-start.5 = (f32[4,512,1024]{2,1,0:T(8,128)S(1)}, f32[4,512,1024]{2,1,0:T(8,128)}, u32[]{:S(2)}) copy-start(f32[4,512,1024]{2,1,0:T(8,128)} %copy-done.4) | copy-start | bytes 25165828
  105.2 24.4 %collective-permute-start.13 = (bf16[160,1024]{1,0:T(8,128)(2,1)S(1)}, bf16[160,1024]{1,0:T(8,128)(2,1)S(1)}, u32[]{:S(2)}, u32[]{:S(2)}) collective-permute-start(bf16[160,1024]{1,0:T(8,128)(2,1)S(1)} %shard_map.76.refs_0_), channel_id=1, source_target_pairs={{8,0},{12,4},{16,8},{20,12},{24,16},{28,20},{9,1},{13,5},{17,9},{2... | collective-permute-start | bytes 983048 | tf_op jit(solution)/shard_map/ppermute | solution.py:382
  109.3 11.4 %collective-permute-start.8 = (bf16[96,1024]{1,0:T(8,128)(2,1)S(1)}, bf16[96,1024]{1,0:T(8,128)(2,1)S(1)}, u32[]{:S(2)}, u32[]{:S(2)}) collective-permute-start(bf16[96,1024]{1,0:T(8,128)(2,1)S(1)} %collective-permute-done.7.refs_2_), channel_id=1, source_target_pairs={{0,1},{1,2},{2,3},{3,0},{4,5},{5,6},{6,7},{7,4},{8,9},{9,10},{10,1... | collective-permute-start | bytes 589832 | tf_op jit(solution)/shard_map/ppermute | solution.py:419
  121.5 10.5 %collective-permute-start.14 = (bf16[96,1024]{1,0:T(8,128)(2,1)S(1)}, bf16[96,1024]{1,0:T(8,128)(2,1)S(1)}, u32[]{:S(2)}, u32[]{:S(2)}) collective-permute-start(bf16[96,1024]{1,0:T(8,128)(2,1)S(1)} %shard_map.82.refs_1_), channel_id=1, source_target_pairs={{8,0},{12,4},{16,8},{20,12},{24,16},{28,20},{9,1},{13,5},{17,9},{2... | collective-permute-start | bytes 589832 | tf_op jit(solution)/shard_map/ppermute | solution.py:382
  125.3 14.5 %collective-permute-start.17 = (bf16[160,1024]{1,0:T(8,128)(2,1)S(1)}, bf16[160,1024]{1,0:T(8,128)(2,1)S(1)}, u32[]{:S(2)}, u32[]{:S(2)}) collective-permute-start(bf16[160,1024]{1,0:T(8,128)(2,1)S(1)} %shard_map.76.refs_0_), channel_id=1, source_target_pairs={{4,0},{12,8},{20,16},{28,24},{16,4},{24,12},{5,1},{13,9},{21,17},{... | collective-permute-start | bytes 983048 | tf_op jit(solution)/shard_map/ppermute | solution.py:403
  129.6 10.3 %collective-permute-start.15 = (bf16[160,1024]{1,0:T(8,128)(2,1)S(1)}, bf16[160,1024]{1,0:T(8,128)(2,1)S(1)}, u32[]{:S(2)}, u32[]{:S(2)}) collective-permute-start(bf16[160,1024]{1,0:T(8,128)(2,1)S(1)} %collective-permute-done.13.refs_5_), channel_id=1, source_target_pairs={{0,4},{4,0},{8,12},{12,8},{16,20},{20,16},{24,28},{28,24},{1,5},{5... | collective-permute-start | bytes 983048 | tf_op jit(solution)/shard_map/ppermute | solution.py:387
  129.6 10.2 %collective-permute-start.18 = (bf16[96,1024]{1,0:T(8,128)(2,1)S(1)}, bf16[96,1024]{1,0:T(8,128)(2,1)S(1)}, u32[]{:S(2)}, u32[]{:S(2)}) collective-permute-start(bf16[96,1024]{1,0:T(8,128)(2,1)S(1)} %shard_map.82.refs_1_), channel_id=1, source_target_pairs={{4,0},{12,8},{20,16},{28,24},{16,4},{24,12},{5,1},{13,9},{21,17},{... | collective-permute-start | bytes 589832 | tf_op jit(solution)/shard_map/ppermute | solution.py:403
  132.0 7.8 %collective-permute-start.16 = (bf16[96,1024]{1,0:T(8,128)(2,1)S(1)}, bf16[96,1024]{1,0:T(8,128)(2,1)S(1)}, u32[]{:S(2)}, u32[]{:S(2)}) collective-permute-start(bf16[96,1024]{1,0:T(8,128)(2,1)S(1)} %collective-permute-done.14.refs_6_), channel_id=1, source_target_pairs={{0,4},{4,0},{8,12},{12,8},{16,20},{20,16},{24,28},{28,24},{1,5},{5... | collective-permute-start | bytes 589832 | tf_op jit(solution)/shard_map/ppermute | solution.py:387
  (9 other events, 9.3 us)

commit v5 on v4

--- a/solution.py
+++ b/solution.py
@@ -46,8 +46,8 @@
     return lax.dot_general(a, b, (((1,), (1,)), ((), ())), preferred_element_type=F32)
 
 
-def params():
-    return pltpu.CompilerParams(vmem_limit_bytes=VMEM)
+def params(limit=VMEM):
+    return pltpu.CompilerParams(vmem_limit_bytes=limit)
 
 
 def lanes_at(tile):
@@ -160,7 +160,7 @@
         + [ANYWHERE] * len(after),
         out_specs=(WHOLE,) * 5 + (SCALARS, TOKEN),
         scratch_shapes=[pltpu.SemaphoreType.DMA((3,))],
-        compiler_params=params(),
+        compiler_params=params(2 * VMEM),
         cost_estimate=pl.CostEstimate(
             flops=2 * 3 * 2 * count * length * width,
             bytes_accessed=4 * (count * width + 8 * length * width),
@@ -239,13 +239,19 @@
         real, imag = real.astype(BF16), imag.astype(BF16)
         return nn(self.back[...], jnp.concatenate([real, imag, real, imag], axis=0))
 
-    def far_terms(self, acc, values_of):
+    def far_terms(self, acc, chosen, choices):
         for distance in range(1, REACH + 1):
             reach = self.facts[1 + distance]
 
             @pl.when(reach > 0)
             def _(distance=distance, reach=reach):
-                real, imag = self.term(values_of(distance), 0, reach, distance)
+                for pieces, holds in choices(distance):
+
+                    @pl.when(holds)
+                    def _(pieces=pieces):
+                        chosen[...] = self.joined(pieces)
+
+                real, imag = self.term(chosen[...], 0, reach, distance)
                 acc[: self.length, :] += real
                 acc[self.length :, :] += imag
 
@@ -267,34 +273,17 @@
         count = len(pieces) // sets
         kinds = [pieces[at * count : (at + 1) * count] for at in range(sets)]
         two, swapped, mate, far = kinds[0], kinds[1], kinds[2], kinds[-1]
+        inner = self.facts[5]
         if distance == 2:
-            return self.joined(two)
-        inner = self.facts[5] == 1
+            return [(two, inner >= 0)]
         if distance == 1:
-            return jnp.where(inner, self.joined(mate), self.joined(swapped))
-        return jnp.where(inner, self.joined(swapped), self.joined(far))
-
-
-def upper_kernel(facts_ref, table_ref, back_ref, spec_ref, own_ref, *refs):
-    halos, (out_ref, token_ref, acc_ref) = refs[:4], refs[-3:]
-    token_ref[...] = jnp.zeros_like(token_ref)
-    conv = Conv(1, facts_ref, table_ref, back_ref, spec_ref)
-    own = conv.joined([own_ref])
-    real, imag = conv.term(own, conv.facts[1], conv.length, 0)
-    acc_ref[: conv.length, :] = real
-    acc_ref[conv.length :, :] = imag
-    conv.far_terms(acc_ref, lambda distance: conv.halo(halos, distance, False))
-    out_ref[0, 0] = conv.signal(acc_ref[: conv.length, :], acc_ref[conv.length :, :])
-
-    def write(value):
-        out_ref[0, 0] = value
-
-    conv.inner_documents(own, lambda: out_ref[0, 0], write)
-
-
-def own_kernel(pieces, facts_ref, table_ref, back_ref, spec_ref, *refs):
+            return [(mate, inner == 1), (swapped, inner == 0)]
+        return [(swapped, inner == 1), (far, inner == 0)]
+
+
+def own_kernel(slot, pieces, facts_ref, table_ref, back_ref, spec_ref, *refs):
     own_refs, out_ref = refs[:pieces], refs[-1]
-    conv = Conv(0, facts_ref, table_ref, back_ref, spec_ref)
+    conv = Conv(slot, facts_ref, table_ref, back_ref, spec_ref)
     own = conv.joined(own_refs)
     out_ref[:, conv.lanes] = conv.signal(*conv.term(own, conv.facts[1], conv.length, 0))
 
@@ -304,29 +293,34 @@
     conv.inner_documents(own, lambda: out_ref[:, conv.lanes], write)
 
 
-def far_kernel(pieces, facts_ref, table_ref, back_ref, spec_ref, *refs):
-    near_ref, upper_ref, mate_ref, two_ref, fold_ref = refs[:5]
-    halos = refs[5 : 5 + 3 * pieces]
-    out_ref, acc_ref = refs[-2:]
-    conv = Conv(0, facts_ref, table_ref, back_ref, spec_ref)
+def far_kernel(slot, pieces, facts_ref, table_ref, back_ref, spec_ref, *refs):
+    near_ref, refs = refs[0], refs[1:]
+    if slot == 0:
+        upper_ref, mate_ref, two_ref, fold_ref = refs[:4]
+        halos = refs[4 : 4 + 3 * pieces]
+    else:
+        halos = refs[: 4 * pieces]
+    out_ref, acc_ref, chosen_ref = refs[-3:]
+    conv = Conv(slot, facts_ref, table_ref, back_ref, spec_ref)
     role = conv.facts[6]
 
-    def values_of(distance):
-        value = conv.halo(halos, distance, True)
-        if distance == 1:
-            return jnp.where(role == 1, conv.joined([upper_ref]), value)
-        if distance == 2:
-            return jnp.where((role == 1) | (role == 2), conv.joined([mate_ref]), value)
-        value = jnp.where(role == 1, conv.joined([two_ref]), value)
-        value = jnp.where(role == 2, conv.joined([upper_ref]), value)
-        return jnp.where(role == 3, conv.joined([fold_ref]), value)
+    def choices(distance):
+        found = conv.halo(halos, distance, slot == 0)
+        if slot == 0:
+            folded = {
+                1: [([upper_ref], role == 1)],
+                2: [([mate_ref], (role == 1) | (role == 2))],
+                3: [([two_ref], role == 1), ([upper_ref], role == 2), ([fold_ref], role == 3)],
+            }
+            found = found + folded[distance]
+        return found
 
     reaches = conv.facts[2] > 0
 
     @pl.when(reaches)
     def _():
         acc_ref[...] = jnp.zeros_like(acc_ref)
-        conv.far_terms(acc_ref, values_of)
+        conv.far_terms(acc_ref, chosen_ref, choices)
         signal = conv.signal(acc_ref[: conv.length, :], acc_ref[conv.length :, :])
         kept = jnp.where(conv.row >= conv.facts[1], signal, 0.0)
         out_ref[0, 0] = near_ref[:, conv.lanes] + kept
@@ -336,14 +330,12 @@
         out_ref[0, 0] = near_ref[:, conv.lanes]
 
 
-def conv_call(body, tabs, facts, arrays, out_shape, out_spec, scratch, terms, after=(), result=None):
+def conv_call(body, tabs, facts, arrays, out_shape, out_spec, scratch, terms, result=None):
     table, back, spectra = tabs
     length = table.shape[0] // 2
     width = spectra.shape[2]
     operands = [facts, table, back, spectra, *arrays]
     specs = [SCALARS] + [WHOLE] * (len(operands) - 1)
-    operands.extend(after)
-    specs += [ANYWHERE] * len(after)
     aliases = {}
     if result is not None:
         aliases = {len(operands): 0}
@@ -355,15 +347,32 @@
         out_shape=out_shape,
         in_specs=specs,
         out_specs=out_spec,
-        scratch_shapes=[pltpu.VMEM((2 * length, LANES), F32)] * scratch,
+        scratch_shapes=scratch,
         input_output_aliases=aliases,
         compiler_params=params(),
         cost_estimate=pl.CostEstimate(
-            flops=8 * terms * length * length * width,
+            flops=4 * terms * length * length * width,
             bytes_accessed=4 * length * width,
             transcendentals=0,
         ),
     )(*operands)
+
+
+def own_terms(slot, tabs, facts, pieces):
+    _, back, spectra = tabs
+    shape = pltpu.VMEM((back.shape[0], spectra.shape[2]), F32)
+    body = functools.partial(own_kernel, slot, len(pieces))
+    return conv_call(body, tabs, facts, pieces, shape, WHOLE, [], 8)
+
+
+def far_terms(slot, count, tabs, facts, arrays, result=None):
+    _, back, spectra = tabs
+    length, width = back.shape[0], spectra.shape[2]
+    shape = jax.ShapeDtypeStruct((1, 2, length, width), F32)
+    spec = pl.BlockSpec((1, 1, length, LANES), lambda c: (0, slot, 0, c))
+    scratch = [pltpu.VMEM((2 * length, LANES), F32), pltpu.VMEM((length, LANES), BF16)]
+    body = functools.partial(far_kernel, slot, count)
+    return conv_call(body, tabs, facts, arrays, shape, spec, scratch, 8, result)
 
 
 def ordered(value, *earlier):
@@ -373,6 +382,7 @@
         in_specs=[ANYWHERE] * (1 + len(earlier)),
         out_specs=ANYWHERE,
         input_output_aliases={0: 0},
+        compiler_params=params(VMEM // 20),
     )(value, *earlier)
 
 
@@ -449,50 +459,18 @@
 
     upper = project(lane, upper_in, everything, weight, gates, 1, 0, after=[first_in[1]])
     upper_halo = upper_halo_of(upper)
-    out_shape = jax.ShapeDtypeStruct((1, 2, length, width), F32)
-    result, convolved = conv_call(
-        upper_kernel,
-        tabs,
-        facts,
-        [upper, *upper_halo],
-        (out_shape, jax.ShapeDtypeStruct((8, 128), F32)),
-        (pl.BlockSpec((1, 1, length, LANES), lambda c: (0, 1, 0, c)), TOKEN),
-        1,
-        6,
-    )
+    near = own_terms(1, tabs, facts, [upper])
+    result = far_terms(1, 1, tabs, facts, [near, *upper_halo])
 
     first = project(lane, first_in, everything, weight, gates, 0, 0)
     first_halo = lower_halo_of(first)
-    partial = project(
-        lane, second_in[:-1], everything[:-1], weight, gates, 0, cut, last=False
-    )
-    second = project(
-        lane, second_in[-1:], everything[-1:], weight, gates, 0, cut, partial, after=[convolved]
-    )
+    partial = project(lane, second_in[:-1], everything[:-1], weight, gates, 0, cut, last=False)
+    second = project(lane, second_in[-1:], everything[-1:], weight, gates, 0, cut, partial)
     second_halo = lower_halo_of(second)
-    near = conv_call(
-        functools.partial(own_kernel, 2),
-        tabs,
-        facts,
-        [first, second],
-        pltpu.VMEM((length, width), F32),
-        WHOLE,
-        0,
-        4,
-    )
+    near = own_terms(0, tabs, facts, [first, second])
     two, _, mate, fold = upper_halo
     halos = [piece for both in zip(first_halo, second_halo) for piece in both]
-    return conv_call(
-        functools.partial(far_kernel, 2),
-        tabs,
-        facts,
-        [near, upper, mate, two, fold, *halos],
-        out_shape,
-        pl.BlockSpec((1, 1, length, LANES), lambda c: (0, 0, 0, c)),
-        1,
-        4,
-        result=result,
-    )
+    return far_terms(0, 2, tabs, facts, [near, upper, mate, two, fold, *halos], result)
 
 
 def solution(mesh):

time: 147 us -> 130 us (0.88)
  the two profiles are of different devices: /device:TPU:19 before, /device:TPU:10 now
where the time goes in v5:
time: 130 us
  Pallas kernels  42.9 us (33%)
  waiting for transfers between devices  37.1 us (29%)
  starting transfers between devices  33 us (25%)
  local copies, waits for them, and re-layouts  16.9 us (13%)
    ppermute x9, waiting for transfers between devices, turned(): return lax.ppermute(piece, 'ch', around)  36.4 us
    pallas_call x4, Pallas kernels, conv_call(): pl.pallas_call(body, grid=(width // LANES,), out_shape=out_shape, in_spec...  24.7 us
    ppermute x9, starting transfers between devices, turned(): return lax.ppermute(piece, 'ch', around)  17.1 us
    unnamed x24, local copies, waits for them, and re-layouts  12.5 us
    pallas_call x4, Pallas kernels, project(): pl.pallas_call(body, out_shape=pltpu.VMEM((rows, width), BF16 if last els...  10.4 us
    ppermute x3, starting transfers between devices, shifted(): lax.ppermute(value, 'ctx', [(source, source + steps) for source in range(...  8.08 us
    pallas_call x1, Pallas kernels, prepare(): pl.pallas_call(functools.partial(prepare_kernel, pairs), grid=(width // L...  7.9 us
    ppermute x4, starting transfers between devices, core_swapped(): lax.ppermute(value, 'ctx', [(source, source ^ 1) for source in range(coun...  4.58 us
  transfers between devices with their start and end apart: 19, of which 4 were waited for; matrix products, arithmetic and copies ran while one was open for 3% of the time, Pallas kernels for 28%

profile of v5, /device:TPU:10, one launch (start us, length us, event | category | flops | bytes accessed | tf_op | source)
XLA Modules:
  0.0 130.2 jit_solution(6813751688957346782)
XLA Ops:
  0.0 1.1 slice_bitcast_fusion.refs_0_
  1.1 1.6 %collective-permute-start = (bf16[256,1024]{1,0:T(8,128)(2,1)S(1)}, bf16[256,1024]{1,0:T(8,128)(2,1)S(1)}, u32[]{:S(2)}, u32[]{:S(2)}) collective-permute-start(bf16[256,1024]{1,0:T(8,128)(2,1)S(1)} %slice_bitcast_fusion.refs_0_), channel_id=1, source_target_pairs={{0,1},{1,2},{2,3},{3,0},{4,5},{5,6},{6,7},{7,4},{8,9},{9,10},{10,1... | collective-permute-start | bytes 1572872 | tf_op jit(solution)/shard_map/ppermute | solution.py:429
  2.7 1.6 %slice_bitcast_fusion.2.refs_8_.refs_0_ = bf16[96,1024]{1,0:T(8,128)(2,1)} fusion(bf16[1,2,256,1024]{3,2,1,0:T(8,128)(2,1)} %param.7), kind=kLoop, calls=%fused_computation.2 | loop fusion | bytes 393216 | tf_op jit(solution)/shard_map/squeeze | solution.py:431
  4.3 1.7 %slice_bitcast_fusion.1.refs_7_.refs_0_ = bf16[160,1024]{1,0:T(8,128)(2,1)} fusion(bf16[1,2,256,1024]{3,2,1,0:T(8,128)(2,1)} %param.7), kind=kLoop, calls=%fused_computation.1 | loop fusion | bytes 655360 | tf_op jit(solution)/shard_map/squeeze | solution.py:431
  6.0 7.9 %shard_map.73 = (f32[4,512,1024]{2,1,0:T(8,128)S(1)}, bf16[1024,4096]{1,0:T(8,128)(2,1)S(1)}, bf16[1,2,256,1024]{3,2,1,0:T(8,128)(2,1)S(1)}, bf16[512,256]{1,0:T...) custom-call(s32[1]{0:T(128)} %bitcast.refs_0_, s32[32]{0:T(128)} %refs_1_.1, ...), custom_call_target="tpu_custom_call" | custom-call | flops 2415919104 | bytes 11534336 | tf_op jit(solution)/shard_map/pallas_call | solution.py:139
  13.9 3.3 %copy-done = f32[4,512,1024]{2,1,0:T(8,128)} copy-done((f32[4,512,1024]{2,1,0:T(8,128)}, f32[4,512,1024]{2,1,0:T(8,128)S(1)}, u32[]{:S(2)}) %copy-start) | copy-done | bytes 8388632
  17.2 3.2 %copy-done.1 = bf16[1024,4096]{1,0:T(8,128)(2,1)} copy-done((bf16[1024,4096]{1,0:T(8,128)(2,1)}, bf16[1024,4096]{1,0:T(8,128)(2,1)S(1)}, u32[]{:S(2)}) %copy-start.1) | copy-done | bytes 8388632
  21.2 1.6 %collective-permute-start.1 = (bf16[256,1024]{1,0:T(8,128)(2,1)S(1)}, bf16[256,1024]{1,0:T(8,128)(2,1)}, u32[]{:S(2)}, u32[]{:S(2)}) collective-permute-start(bf16[256,1024]{1,0:T(8,128)(2,1)S(1)} %shard_map.74.refs_1_), channel_id=1, source_target_pairs={{0,1},{1,2},{2,3},{3,0},{4,5},{5,6},{6,7},{7,4},{8,9},{9,10},{10,1... | collective-permute-start | bytes 1572872 | tf_op jit(solution)/shard_map/ppermute | solution.py:429
  23.6 11.1 %collective-permute-done.1.refs_1_.refs_2_ = bf16[256,1024]{1,0:T(8,128)(2,1)} collective-permute-done((bf16[256,1024]{1,0:T(8,128)(2,1)S(1)}, bf16[256,1024]{1,0:T(8,128)(2,1)}, u32[]{:S(2)}, u32[]{:S(2)}) %collective-permute-start.1) | collective-permute-done | bytes 524320 | tf_op jit(solution)/shard_map/ppermute | solution.py:429
  34.7 1.6 %collective-permute-start.5 = (bf16[256,1024]{1,0:T(8,128)(2,1)}, bf16[256,1024]{1,0:T(8,128)(2,1)S(1)}, u32[]{:S(2)}, u32[]{:S(2)}) collective-permute-start(bf16[256,1024]{1,0:T(8,128)(2,1)} %collective-permute-done.1.refs_1_.refs_2_), channel_id=1, source_target_pairs={{0,1},{1,2},{2,3},{3,0},{4,5},{5,6},{6,7},{7,4},{8,9},{9,10},{10,1... | collective-permute-start | bytes 1572872 | tf_op jit(solution)/shard_map/ppermute | solution.py:429
  36.6 18.5 %collective-permute-done.2.refs_1_.refs_6_ = bf16[160,1024]{1,0:T(8,128)(2,1)} collective-permute-done((bf16[160,1024]{1,0:T(8,128)(2,1)S(1)}, bf16[160,1024]{1,0:T(8,128)(2,1)}, u32[]{:S(2)}, u32[]{:S(2)}) %collective-permute-start.2) | collective-permute-done | bytes 327712 | tf_op jit(solution)/shard_map/ppermute | solution.py:429
  55.0 1.0 collective-permute-start.3
  56.1 3.4 %copy-done.2 = bf16[1024,4096]{1,0:T(8,128)(2,1)S(1)} copy-done((bf16[1024,4096]{1,0:T(8,128)(2,1)S(1)}, bf16[1024,4096]{1,0:T(8,128)(2,1)}, u32[]{:S(2)}) %copy-start.2) | copy-done | bytes 8388632
  60.5 3.6 %shard_map.82.refs_0_.refs_1_ = bf16[256,1024]{1,0:T(8,128)(2,1)S(1)} custom-call(s32[1]{0:T(128)} %bitcast.3.place_ref, bf16[256,1024]{1,0:T(8,128)(2,1)S(1)} %slice_bitcast_fusion.refs_0_, bf16[256,1024]{1,0:T(8,128)(2,1)S(1)} %copy-done.7, bf16[256,1024]{1,0:T(8,128)(2,1)} %collective-permute-done.1.refs_1_.refs_2_, ...), custom_call_target="tpu_custom_call" | custom-call | flops 2147483648 | bytes 10485760 | tf_op jit(solution)/shard_map/pallas_call | solution.py:200
  64.1 3.7 %collective-permute-start.10 = (bf16[256,1024]{1,0:T(8,128)(2,1)S(1)}, bf16[256,1024]{1,0:T(8,128)(2,1)S(1)}, u32[]{:S(2)}, u32[]{:S(2)}) collective-permute-start(bf16[256,1024]{1,0:T(8,128)(2,1)S(1)} %shard_map.82.refs_0_.refs_1_), channel_id=1, source_target_pairs={{0,8},{4,12},{8,16},{12,20},{16,24},{20,28},{1,9},{5,13},{9,17},{1... | collective-permute-start | bytes 1572872 | tf_op jit(solution)/shard_map/ppermute | solution.py:392
  67.7 1.1 collective-permute-start.4
  68.8 4.4 %collective-permute-start.6 = (bf16[96,1024]{1,0:T(8,128)(2,1)S(1)}, bf16[96,1024]{1,0:T(8,128)(2,1)S(1)}, u32[]{:S(2)}, u32[]{:S(2)}) collective-permute-start(bf16[96,1024]{1,0:T(8,128)(2,1)S(1)} %shard_map.77.refs_0_), channel_id=1, source_target_pairs={{0,1},{1,2},{2,3},{3,0},{4,5},{5,6},{6,7},{7,4},{8,9},{9,10},{10,1... | collective-permute-start | bytes 589832 | tf_op jit(solution)/shard_map/ppermute | solution.py:429
  73.2 6.8 %collective-permute-done.6.refs_0_ = bf16[96,1024]{1,0:T(8,128)(2,1)S(1)} collective-permute-done((bf16[96,1024]{1,0:T(8,128)(2,1)S(1)}, bf16[96,1024]{1,0:T(8,128)(2,1)S(1)}, u32[]{:S(2)}, u32[]{:S(2)}) %collective-permute-start.6) | collective-permute-done | bytes 196640 | tf_op jit(solution)/shard_map/ppermute | solution.py:429
  80.0 3.0 %collective-permute-start.7 = (bf16[96,1024]{1,0:T(8,128)(2,1)S(1)}, bf16[96,1024]{1,0:T(8,128)(2,1)S(1)}, u32[]{:S(2)}, u32[]{:S(2)}) collective-permute-start(bf16[96,1024]{1,0:T(8,128)(2,1)S(1)} %shard_map.78.refs_1_), channel_id=1, source_target_pairs={{0,1},{1,2},{2,3},{3,0},{4,5},{5,6},{6,7},{7,4},{8,9},{9,10},{10,1... | collective-permute-start | bytes 589832 | tf_op jit(solution)/shard_map/ppermute | solution.py:429
  83.0 4.0 %shard_map.76.refs_0_ = bf16[160,1024]{1,0:T(8,128)(2,1)S(1)} custom-call(s32[1]{0:T(128)} %bitcast.3.place_ref, bf16[160,1024]{1,0:T(8,128)(2,1)S(1)} %shard_map.75.refs_0_, bf16[160,1024]{1,0:T(8,128)(2,1)} %collective-permute-done.2.refs_1_.refs_6_, bf16[160,1024]{1,0:T(8,128)(2,1)} %collective-permute-done.3.refs_2_, ...), custom_call_target="tpu_custom_call" | custom-call | flops 1342177280 | bytes 9699328 | tf_op jit(solution)/shard_map/pallas_call | solution.py:200
  87.0 2.5 %collective-permute-start.12 = (bf16[160,1024]{1,0:T(8,128)(2,1)S(1)}, bf16[160,1024]{1,0:T(8,128)(2,1)S(1)}, u32[]{:S(2)}, u32[]{:S(2)}) collective-permute-start(bf16[160,1024]{1,0:T(8,128)(2,1)S(1)} %shard_map.76.refs_0_), channel_id=1, source_target_pairs={{8,0},{12,4},{16,8},{20,12},{24,16},{28,20},{9,1},{13,5},{17,9},{2... | collective-permute-start | bytes 983048 | tf_op jit(solution)/shard_map/ppermute | solution.py:392
  90.2 2.9 %collective-permute-start.18 = (bf16[256,1024]{1,0:T(8,128)(2,1)S(1)}, bf16[256,1024]{1,0:T(8,128)(2,1)S(1)}, u32[]{:S(2)}, u32[]{:S(2)}) collective-permute-start(bf16[256,1024]{1,0:T(8,128)(2,1)S(1)} %collective-permute-done.10.refs_1_.refs_3_), channel_id=1, source_target_pairs={{0,4},{4,0},{8,12},{12,8},{16,20},{20,16},{24,28},{28,24},{1,5},{5... | collective-permute-start | bytes 1572872 | tf_op jit(solution)/shard_map/ppermute | solution.py:397
  93.1 2.5 %collective-permute-start.8 = (bf16[96,1024]{1,0:T(8,128)(2,1)S(1)}, bf16[96,1024]{1,0:T(8,128)(2,1)S(1)}, u32[]{:S(2)}, u32[]{:S(2)}) collective-permute-start(bf16[96,1024]{1,0:T(8,128)(2,1)S(1)} %collective-permute-done.7.refs_2_), channel_id=1, source_target_pairs={{0,1},{1,2},{2,3},{3,0},{4,5},{5,6},{6,7},{7,4},{8,9},{9,10},{10,1... | collective-permute-start | bytes 589832 | tf_op jit(solution)/shard_map/ppermute | solution.py:429
  95.6 8.1 %shard_map.83.refs_0_ = f32[256,1024]{1,0:T(8,128)S(1)} custom-call(s32[2,8]{1,0:T(2,128)S(1)} %copy-done.8, bf16[512,256]{1,0:T(8,128)(2,1)S(1)} %get-tuple-element.13.table_ref, bf16[256,1024]{1,0:T(8,128)(2,1)S(1)} %get-tuple-element.14.back_ref, f32[4,512,1024]{2,1,0:T(8,128)S(1)} %bitcast.9, bf16[256,1024]{1,0:T(8,128)(2,1)S(1)} %shard_map.82.refs_0_.refs_1_), custom_call_target="tpu_custom_call" | custom-call | flops 2147483648 | bytes 1048576 | tf_op jit(solution)/shard_map/pallas_call | solution.py:344
  103.8 2.0 %shard_map.79.refs_3_ = f32[96,1024]{1,0:T(8,128)S(1)} custom-call(s32[1]{0:T(128)} %bitcast.3.place_ref, bf16[96,1024]{1,0:T(8,128)(2,1)S(1)} %shard_map.77.refs_0_, bf16[96,1024]{1,0:T(8,128)(2,1)S(1)} %shard_map.78.refs_1_, bf16[96,1024]{1,0:T(8,128)(2,1)S(1)} %collective-permute-done.7.refs_2_, bf16[1024,4096]{1,0:T(8,128)(2,1)S(1)} %copy-done.3, ...), custom_call_target="tpu_custom_call" | custom-call | flops 603979776 | bytes 6881280 | tf_op jit(solution)/shard_map/pallas_call | solution.py:200
  105.8 1.3 collective-permute-start.16
  107.2 1.2 collective-permute-start.14
  109.1 1.9 %collective-permute-start.13 = (bf16[96,1024]{1,0:T(8,128)(2,1)S(1)}, bf16[96,1024]{1,0:T(8,128)(2,1)S(1)}, u32[]{:S(2)}, u32[]{:S(2)}) collective-permute-start(bf16[96,1024]{1,0:T(8,128)(2,1)S(1)} %shard_map.80.refs_1_), channel_id=1, source_target_pairs={{8,0},{12,4},{16,8},{20,12},{24,16},{28,20},{9,1},{13,5},{17,9},{2... | collective-permute-start | bytes 589832 | tf_op jit(solution)/shard_map/ppermute | solution.py:392
  111.1 5.7 %shard_map.81.refs_0_ = f32[256,1024]{1,0:T(8,128)S(1)} custom-call(s32[2,8]{1,0:T(2,128)S(1)} %copy-done.8, bf16[512,256]{1,0:T(8,128)(2,1)S(1)} %get-tuple-element.13.table_ref, bf16[256,1024]{1,0:T(8,128)(2,1)S(1)} %get-tuple-element.14.back_ref, f32[4,512,1024]{2,1,0:T(8,128)S(1)} %bitcast.9, bf16[160,1024]{1,0:T(8,128)(2,1)S(1)} %shard_map.76.refs_0_, ...), custom_call_target="tpu_custom_call" | custom-call | flops 2147483648 | bytes 1048576 | tf_op jit(solution)/shard_map/pallas_call | solution.py:344
  116.7 1.3 collective-permute-start.17
  119.2 4.8 %shard_map.84.refs_11_ = f32[1,2,256,1024]{3,2,1,0:T(8,128)} custom-call(s32[2,8]{1,0:T(2,128)S(1)} %copy-done.8, bf16[512,256]{1,0:T(8,128)(2,1)S(1)} %get-tuple-element.13.table_ref, bf16[256,1024]{1,0:T(8,128)(2,1)S(1)} %get-tuple-element.14.back_ref, f32[4,512,1024]{2,1,0:T(8,128)S(1)} %bitcast.9, f32[256,1024]{1,0:T(8,128)S(1)} %shard_map.83.refs_0_, ...), custom_call_target="tpu_custom_call" | custom-call | flops 2147483648 | bytes 1048576 | tf_op jit(solution)/shard_map/pallas_call | solution.py:344
  124.1 6.0 %shard_map.85 = f32[1,2,256,1024]{3,2,1,0:T(8,128)} custom-call(s32[2,8]{1,0:T(2,128)S(1)} %copy-done.8, bf16[512,256]{1,0:T(8,128)(2,1)S(1)} %get-tuple-element.13.table_ref, bf16[256,1024]{1,0:T(8,128)(2,1)S(1)} %get-tuple-element.14.back_ref, f32[4,512,1024]{2,1,0:T(8,128)S(1)} %bitcast.9, ...), custom_call_target="tpu_custom_call", output_to_operand_aliasing={{}: (15, {})} | custom-call | flops 2147483648 | bytes 1048576 | tf_op jit(solution)/shard_map/pallas_call | solution.py:344
  (47 shorter events, 5.6 us)
Async XLA Ops:
  1.1 19.4 %collective-permute-start = (bf16[256,1024]{1,0:T(8,128)(2,1)S(1)}, bf16[256,1024]{1,0:T(8,128)(2,1)S(1)}, u32[]{:S(2)}, u32[]{:S(2)}) collective-permute-start(bf16[256,1024]{1,0:T(8,128)(2,1)S(1)} %slice_bitcast_fusion.refs_0_), channel_id=1, source_target_pairs={{0,1},{1,2},{2,3},{3,0},{4,5},{5,6},{6,7},{7,4},{8,9},{9,10},{10,1... | collective-permute-start | bytes 1572872 | tf_op jit(solution)/shard_map/ppermute | solution.py:429
  6.0 30.2 %copy-start.4 = (bf16[160,1024]{1,0:T(8,128)(2,1)S(1)}, bf16[160,1024]{1,0:T(8,128)(2,1)}, u32[]{:S(2)}) copy-start(bf16[160,1024]{1,0:T(8,128)(2,1)} %slice_bitcast_fusion.1.refs_7_.refs_0_) | copy-start | bytes 983044
  13.9 3.3 %copy-start = (f32[4,512,1024]{2,1,0:T(8,128)}, f32[4,512,1024]{2,1,0:T(8,128)S(1)}, u32[]{:S(2)}) copy-start(f32[4,512,1024]{2,1,0:T(8,128)S(1)} %get-tuple-element.15.spec_ref) | copy-start | bytes 25165828
  17.2 3.2 %copy-start.1 = (bf16[1024,4096]{1,0:T(8,128)(2,1)}, bf16[1024,4096]{1,0:T(8,128)(2,1)S(1)}, u32[]{:S(2)}) copy-start(bf16[1024,4096]{1,0:T(8,128)(2,1)S(1)} %get-tuple-element.17.refs_4_.refs_3_.refs_1_) | copy-start | bytes 25165828
  20.5 48.3 %copy-start.5 = (bf16[96,1024]{1,0:T(8,128)(2,1)S(1)}, bf16[96,1024]{1,0:T(8,128)(2,1)}, u32[]{:S(2)}) copy-start(bf16[96,1024]{1,0:T(8,128)(2,1)} %slice_bitcast_fusion.2.refs_8_.refs_0_) | copy-start | bytes 589828
  20.5 0.7 copy-start.9
  21.2 13.5 %collective-permute-start.1 = (bf16[256,1024]{1,0:T(8,128)(2,1)S(1)}, bf16[256,1024]{1,0:T(8,128)(2,1)}, u32[]{:S(2)}, u32[]{:S(2)}) collective-permute-start(bf16[256,1024]{1,0:T(8,128)(2,1)S(1)} %shard_map.74.refs_1_), channel_id=1, source_target_pairs={{0,1},{1,2},{2,3},{3,0},{4,5},{5,6},{6,7},{7,4},{8,9},{9,10},{10,1... | collective-permute-start | bytes 1572872 | tf_op jit(solution)/shard_map/ppermute | solution.py:429
  22.8 0.8 copy-start.6
  34.7 21.4 %collective-permute-start.5 = (bf16[256,1024]{1,0:T(8,128)(2,1)}, bf16[256,1024]{1,0:T(8,128)(2,1)S(1)}, u32[]{:S(2)}, u32[]{:S(2)}) collective-permute-start(bf16[256,1024]{1,0:T(8,128)(2,1)} %collective-permute-done.1.refs_1_.refs_2_), channel_id=1, source_target_pairs={{0,1},{1,2},{2,3},{3,0},{4,5},{5,6},{6,7},{7,4},{8,9},{9,10},{10,1... | collective-permute-start | bytes 1572872 | tf_op jit(solution)/shard_map/ppermute | solution.py:429
  36.3 18.8 %collective-permute-start.2 = (bf16[160,1024]{1,0:T(8,128)(2,1)S(1)}, bf16[160,1024]{1,0:T(8,128)(2,1)}, u32[]{:S(2)}, u32[]{:S(2)}) collective-permute-start(bf16[160,1024]{1,0:T(8,128)(2,1)S(1)} %shard_map.75.refs_0_), channel_id=1, source_target_pairs={{0,1},{1,2},{2,3},{3,0},{4,5},{5,6},{6,7},{7,4},{8,9},{9,10},{10,1... | collective-permute-start | bytes 983048 | tf_op jit(solution)/shard_map/ppermute | solution.py:429
  55.0 12.7 %collective-permute-start.3 = (bf16[160,1024]{1,0:T(8,128)(2,1)}, bf16[160,1024]{1,0:T(8,128)(2,1)}, u32[]{:S(2)}, u32[]{:S(2)}) collective-permute-start(bf16[160,1024]{1,0:T(8,128)(2,1)} %collective-permute-done.2.refs_1_.refs_6_), channel_id=1, source_target_pairs={{0,1},{1,2},{2,3},{3,0},{4,5},{5,6},{6,7},{7,4},{8,9},{9,10},{10,1... | collective-permute-start | bytes 983048 | tf_op jit(solution)/shard_map/ppermute | solution.py:429
  56.1 3.4 %copy-start.2 = (bf16[1024,4096]{1,0:T(8,128)(2,1)S(1)}, bf16[1024,4096]{1,0:T(8,128)(2,1)}, u32[]{:S(2)}) copy-start(bf16[1024,4096]{1,0:T(8,128)(2,1)} %copy-done.1) | copy-start | bytes 25165828
  59.4 1.0 copy-start.7
  60.5 22.5 %copy-start.3 = (bf16[1024,4096]{1,0:T(8,128)(2,1)S(1)}, bf16[1024,4096]{1,0:T(8,128)(2,1)}, u32[]{:S(2)}) copy-start(bf16[1024,4096]{1,0:T(8,128)(2,1)} %copy-done.1) | copy-start | bytes 25165828
  60.5 35.1 %slice-start = ((s8[8388608]{0:T(1024)(128)(4,1)}), s8[4194304]{0:T(1024)(128)(4,1)S(1)}, s32[]{:S(2)}) async-start(s8[8388608]{0:T(1024)(128)(4,1)} %bitcast.8), calls=%async_computation | async-start | bytes 8388608
  64.0 31.6 %slice-start.1 = ((s8[8388608]{0:T(1024)(128)(4,1)}), s8[4194304]{0:T(1024)(128)(4,1)S(1)}, s32[]{:S(2)}) async-start(s8[8388608]{0:T(1024)(128)(4,1)} %bitcast.8), calls=%async_computation.1 | async-start | bytes 8388608
  64.1 31.6 %copy-start.8 = (s32[2,8]{1,0:T(2,128)S(1)}, s32[2,8]{1,0:T(2,128)}, u32[]{:S(2)}) copy-start(s32[2,8]{1,0:T(2,128)} %get-tuple-element.12.facts_ref) | copy-start | bytes 196
  64.1 26.2 %collective-permute-start.10 = (bf16[256,1024]{1,0:T(8,128)(2,1)S(1)}, bf16[256,1024]{1,0:T(8,128)(2,1)S(1)}, u32[]{:S(2)}, u32[]{:S(2)}) collective-permute-start(bf16[256,1024]{1,0:T(8,128)(2,1)S(1)} %shard_map.82.refs_0_.refs_1_), channel_id=1, source_target_pairs={{0,8},{4,12},{8,16},{12,20},{16,24},{20,28},{1,9},{5,13},{9,17},{1... | collective-permute-start | bytes 1572872 | tf_op jit(solution)/shard_map/ppermute | solution.py:392
  67.7 12.3 %collective-permute-start.4 = (bf16[160,1024]{1,0:T(8,128)(2,1)}, bf16[160,1024]{1,0:T(8,128)(2,1)S(1)}, u32[]{:S(2)}, u32[]{:S(2)}) collective-permute-start(bf16[160,1024]{1,0:T(8,128)(2,1)} %collective-permute-done.3.refs_2_), channel_id=1, source_target_pairs={{0,1},{1,2},{2,3},{3,0},{4,5},{5,6},{6,7},{7,4},{8,9},{9,10},{10,1... | collective-permute-start | bytes 983048 | tf_op jit(solution)/shard_map/ppermute | solution.py:429
  68.8 11.2 %collective-permute-start.6 = (bf16[96,1024]{1,0:T(8,128)(2,1)S(1)}, bf16[96,1024]{1,0:T(8,128)(2,1)S(1)}, u32[]{:S(2)}, u32[]{:S(2)}) collective-permute-start(bf16[96,1024]{1,0:T(8,128)(2,1)S(1)} %shard_map.77.refs_0_), channel_id=1, source_target_pairs={{0,1},{1,2},{2,3},{3,0},{4,5},{5,6},{6,7},{7,4},{8,9},{9,10},{10,1... | collective-permute-start | bytes 589832 | tf_op jit(solution)/shard_map/ppermute | solution.py:429
  73.2 35.9 %collective-permute-start.9 = (bf16[256,1024]{1,0:T(8,128)(2,1)S(1)}, bf16[256,1024]{1,0:T(8,128)(2,1)S(1)}, u32[]{:S(2)}, u32[]{:S(2)}) collective-permute-start(bf16[256,1024]{1,0:T(8,128)(2,1)S(1)} %shard_map.82.refs_0_.refs_1_), channel_id=1, source_target_pairs={{0,4},{4,0},{8,12},{12,8},{16,20},{20,16},{24,28},{28,24},{1,5},{5... | collective-permute-start | bytes 1572872 | tf_op jit(solution)/shard_map/ppermute | solution.py:397
  80.0 13.1 %collective-permute-start.7 = (bf16[96,1024]{1,0:T(8,128)(2,1)S(1)}, bf16[96,1024]{1,0:T(8,128)(2,1)S(1)}, u32[]{:S(2)}, u32[]{:S(2)}) collective-permute-start(bf16[96,1024]{1,0:T(8,128)(2,1)S(1)} %shard_map.78.refs_1_), channel_id=1, source_target_pairs={{0,1},{1,2},{2,3},{3,0},{4,5},{5,6},{6,7},{7,4},{8,9},{9,10},{10,1... | collective-permute-start | bytes 589832 | tf_op jit(solution)/shard_map/ppermute | solution.py:429
  87.0 18.8 %collective-permute-start.12 = (bf16[160,1024]{1,0:T(8,128)(2,1)S(1)}, bf16[160,1024]{1,0:T(8,128)(2,1)S(1)}, u32[]{:S(2)}, u32[]{:S(2)}) collective-permute-start(bf16[160,1024]{1,0:T(8,128)(2,1)S(1)} %shard_map.76.refs_0_), channel_id=1, source_target_pairs={{8,0},{12,4},{16,8},{20,12},{24,16},{28,20},{9,1},{13,5},{17,9},{2... | collective-permute-start | bytes 983048 | tf_op jit(solution)/shard_map/ppermute | solution.py:392
  89.5 27.2 %collective-permute-start.11 = (bf16[256,1024]{1,0:T(8,128)(2,1)S(1)}, bf16[256,1024]{1,0:T(8,128)(2,1)S(1)}, u32[]{:S(2)}, u32[]{:S(2)}) collective-permute-start(bf16[256,1024]{1,0:T(8,128)(2,1)S(1)} %shard_map.82.refs_0_.refs_1_), channel_id=1, source_target_pairs={{4,16},{12,24},{28,20},{5,17},{13,25},{29,21},{6,18},{14,26},{30,2... | collective-permute-start | bytes 1572872 | tf_op jit(solution)/shard_map/ppermute | solution.py:404
  90.2 29.0 %collective-permute-start.18 = (bf16[256,1024]{1,0:T(8,128)(2,1)S(1)}, bf16[256,1024]{1,0:T(8,128)(2,1)S(1)}, u32[]{:S(2)}, u32[]{:S(2)}) collective-permute-start(bf16[256,1024]{1,0:T(8,128)(2,1)S(1)} %collective-permute-done.10.refs_1_.refs_3_), channel_id=1, source_target_pairs={{0,4},{4,0},{8,12},{12,8},{16,20},{20,16},{24,28},{28,24},{1,5},{5... | collective-permute-start | bytes 1572872 | tf_op jit(solution)/shard_map/ppermute | solution.py:397
  93.1 14.0 %collective-permute-start.8 = (bf16[96,1024]{1,0:T(8,128)(2,1)S(1)}, bf16[96,1024]{1,0:T(8,128)(2,1)S(1)}, u32[]{:S(2)}, u32[]{:S(2)}) collective-permute-start(bf16[96,1024]{1,0:T(8,128)(2,1)S(1)} %collective-permute-done.7.refs_2_), channel_id=1, source_target_pairs={{0,1},{1,2},{2,3},{3,0},{4,5},{5,6},{6,7},{7,4},{8,9},{9,10},{10,1... | collective-permute-start | bytes 589832 | tf_op jit(solution)/shard_map/ppermute | solution.py:429
  105.8 18.2 %collective-permute-start.16 = (bf16[160,1024]{1,0:T(8,128)(2,1)S(1)}, bf16[160,1024]{1,0:T(8,128)(2,1)S(1)}, u32[]{:S(2)}, u32[]{:S(2)}) collective-permute-start(bf16[160,1024]{1,0:T(8,128)(2,1)S(1)} %shard_map.76.refs_0_), channel_id=1, source_target_pairs={{4,0},{12,8},{20,16},{28,24},{16,4},{24,12},{5,1},{13,9},{21,17},{... | collective-permute-start | bytes 983048 | tf_op jit(solution)/shard_map/ppermute | solution.py:413
  107.2 16.9 %collective-permute-start.14 = (bf16[160,1024]{1,0:T(8,128)(2,1)S(1)}, bf16[160,1024]{1,0:T(8,128)(2,1)S(1)}, u32[]{:S(2)}, u32[]{:S(2)}) collective-permute-start(bf16[160,1024]{1,0:T(8,128)(2,1)S(1)} %collective-permute-done.12.refs_5_), channel_id=1, source_target_pairs={{0,4},{4,0},{8,12},{12,8},{16,20},{20,16},{24,28},{28,24},{1,5},{5... | collective-permute-start | bytes 983048 | tf_op jit(solution)/shard_map/ppermute | solution.py:397
  109.1 9.6 %collective-permute-start.13 = (bf16[96,1024]{1,0:T(8,128)(2,1)S(1)}, bf16[96,1024]{1,0:T(8,128)(2,1)S(1)}, u32[]{:S(2)}, u32[]{:S(2)}) collective-permute-start(bf16[96,1024]{1,0:T(8,128)(2,1)S(1)} %shard_map.80.refs_1_), channel_id=1, source_target_pairs={{8,0},{12,4},{16,8},{20,12},{24,16},{28,20},{9,1},{13,5},{17,9},{2... | collective-permute-start | bytes 589832 | tf_op jit(solution)/shard_map/ppermute | solution.py:392
  116.7 7.4 %collective-permute-start.17 = (bf16[96,1024]{1,0:T(8,128)(2,1)S(1)}, bf16[96,1024]{1,0:T(8,128)(2,1)S(1)}, u32[]{:S(2)}, u32[]{:S(2)}) collective-permute-start(bf16[96,1024]{1,0:T(8,128)(2,1)S(1)} %shard_map.80.refs_1_), channel_id=1, source_target_pairs={{4,0},{12,8},{20,16},{28,24},{16,4},{24,12},{5,1},{13,9},{21,17},{... | collective-permute-start | bytes 589832 | tf_op jit(solution)/shard_map/ppermute | solution.py:413
  118.8 5.3 %collective-permute-start.15 = (bf16[96,1024]{1,0:T(8,128)(2,1)S(1)}, bf16[96,1024]{1,0:T(8,128)(2,1)S(1)}, u32[]{:S(2)}, u32[]{:S(2)}) collective-permute-start(bf16[96,1024]{1,0:T(8,128)(2,1)S(1)} %collective-permute-done.13.refs_6_), channel_id=1, source_target_pairs={{0,4},{4,0},{8,12},{12,8},{16,20},{20,16},{24,28},{28,24},{1,5},{5... | collective-permute-start | bytes 589832 | tf_op jit(solution)/shard_map/ppermute | solution.py:397

commit v6 on v5

--- a/solution.py
+++ b/solution.py
@@ -160,7 +160,7 @@
         + [ANYWHERE] * len(after),
         out_specs=(WHOLE,) * 5 + (SCALARS, TOKEN),
         scratch_shapes=[pltpu.SemaphoreType.DMA((3,))],
-        compiler_params=params(2 * VMEM),
+        compiler_params=params(),
         cost_estimate=pl.CostEstimate(
             flops=2 * 3 * 2 * count * length * width,
             bytes_accessed=4 * (count * width + 8 * length * width),
@@ -446,9 +446,10 @@
     )
     tabs = (table, back, spectra)
 
-    upper_in[1] = ordered(upper_in[1], prepared)
     for step in range(2, count):
         upper_in.append(turned(upper_in[-1]))
+    upper_in[-2] = ordered(upper_in[-2], prepared)
+    upper_in[-1] = turned(upper_in[-2])
     first_in = [ordered(slices[0], upper_in[-2])]
     for step in range(1, count):
         first_in.append(turned(first_in[-1]))

time: 130 us -> 133 us (1.023)
  the two profiles are of different devices: /device:TPU:10 before, /device:TPU:12 now
where the time goes in v6:
time: 133 us; the launch traced here: 132 us
  Pallas kernels  36.5 us (27%)
  starting transfers between devices  36.1 us (27%)
  waiting for transfers between devices  34.5 us (26%)
  local copies, waits for them, and re-layouts  25 us (19%)
    ppermute x9, waiting for transfers between devices, turned(): return lax.ppermute(piece, 'ch', around)  34.5 us
    unnamed x32, local copies, waits for them, and re-layouts  22 us
    pallas_call x4, Pallas kernels, conv_call(): pl.pallas_call(body, grid=(width // LANES,), out_shape=out_shape, in_spec...  21 us
    ppermute x9, starting transfers between devices, turned(): return lax.ppermute(piece, 'ch', around)  18.1 us
    ppermute x3, starting transfers between devices, shifted(): lax.ppermute(value, 'ctx', [(source, source + steps) for source in range(...  11.7 us
    pallas_call x4, Pallas kernels, project(): pl.pallas_call(body, out_shape=pltpu.VMEM((rows, width), BF16 if last els...  9.18 us
    pallas_call x1, Pallas kernels, prepare(): pl.pallas_call(functools.partial(prepare_kernel, pairs), grid=(width // L...  6.27 us
    ppermute x2, starting transfers between devices, lower_halo_of(): mixed = lax.ppermute(value, 'ctx', mixed)  3.84 us
  transfers between devices with their start and end apart: 19, of which 3 were waited for; matrix products, arithmetic and copies ran while one was open for 1% of the time, Pallas kernels for 24%

profile of v6, /device:TPU:12, one launch (start us, length us, event | category | flops | bytes accessed | tf_op | source)
XLA Modules:
  0.0 132.4 jit_solution(818241599707856773)
XLA Ops:
  1.1 1.6 %collective-permute-start = (bf16[256,1024]{1,0:T(8,128)(2,1)S(1)}, bf16[256,1024]{1,0:T(8,128)(2,1)S(1)}, u32[]{:S(2)}, u32[]{:S(2)}) collective-permute-start(bf16[256,1024]{1,0:T(8,128)(2,1)S(1)} %slice_bitcast_fusion.refs_0_), channel_id=1, source_target_pairs={{0,1},{1,2},{2,3},{3,0},{4,5},{5,6},{6,7},{7,4},{8,9},{9,10},{10,1... | collective-permute-start | bytes 1572872 | tf_op jit(solution)/shard_map/ppermute | solution.py:429
  3.5 11.3 %collective-permute-done.refs_1_ = bf16[256,1024]{1,0:T(8,128)(2,1)S(1)} collective-permute-done((bf16[256,1024]{1,0:T(8,128)(2,1)S(1)}, bf16[256,1024]{1,0:T(8,128)(2,1)S(1)}, u32[]{:S(2)}, u32[]{:S(2)}) %collective-permute-start) | collective-permute-done | bytes 524320 | tf_op jit(solution)/shard_map/ppermute | solution.py:429
  14.8 1.6 %collective-permute-start.1 = (bf16[256,1024]{1,0:T(8,128)(2,1)S(1)}, bf16[256,1024]{1,0:T(8,128)(2,1)S(1)}, u32[]{:S(2)}, u32[]{:S(2)}) collective-permute-start(bf16[256,1024]{1,0:T(8,128)(2,1)S(1)} %collective-permute-done.refs_1_), channel_id=1, source_target_pairs={{0,1},{1,2},{2,3},{3,0},{4,5},{5,6},{6,7},{7,4},{8,9},{9,10},{10,1... | collective-permute-start | bytes 1572872 | tf_op jit(solution)/shard_map/ppermute | solution.py:429
  18.3 3.4 %copy-done.4 = bf16[1024,4096]{1,0:T(8,128)(2,1)S(1)} copy-done((bf16[1024,4096]{1,0:T(8,128)(2,1)S(1)}, bf16[1024,4096]{1,0:T(8,128)(2,1)}, u32[]{:S(2)}) %copy-start.4) | copy-done | bytes 8388632
  21.7 1.9 %copy-done.5 = f32[768,1024]{1,0:T(8,128)S(1)} copy-done((f32[768,1024]{1,0:T(8,128)S(1)}, f32[768,1024]{1,0:T(8,128)}, u32[]{:S(2)}) %copy-start.5) | copy-done | bytes 3145752
  23.6 1.2 copy-done.8
  27.6 6.3 %shard_map.73 = (f32[4,512,1024]{2,1,0:T(8,128)S(1)}, bf16[1024,4096]{1,0:T(8,128)(2,1)S(1)}, bf16[1,2,256,1024]{3,2,1,0:T(8,128)(2,1)S(1)}, bf16[512,256]{1,0:T...) custom-call(s32[1]{0:T(128)} %bitcast.refs_0_, s32[32]{0:T(128)S(1)} %copy-done.13, ...), custom_call_target="tpu_custom_call" | custom-call | flops 2415919104 | bytes 11534336 | tf_op jit(solution)/shard_map/pallas_call | solution.py:139
  33.9 3.3 %copy-done = f32[4,512,1024]{2,1,0:T(8,128)} copy-done((f32[4,512,1024]{2,1,0:T(8,128)}, f32[4,512,1024]{2,1,0:T(8,128)S(1)}, u32[]{:S(2)}) %copy-start) | copy-done | bytes 8388632
  37.1 3.3 %copy-done.1 = bf16[1024,4096]{1,0:T(8,128)(2,1)} copy-done((bf16[1024,4096]{1,0:T(8,128)(2,1)}, bf16[1024,4096]{1,0:T(8,128)(2,1)S(1)}, u32[]{:S(2)}) %copy-start.1) | copy-done | bytes 8388632
  40.4 1.6 %collective-permute-start.5 = (bf16[256,1024]{1,0:T(8,128)(2,1)S(1)}, bf16[256,1024]{1,0:T(8,128)(2,1)S(1)}, u32[]{:S(2)}, u32[]{:S(2)}) collective-permute-start(bf16[256,1024]{1,0:T(8,128)(2,1)S(1)} %shard_map.74.refs_1_.refs_2_), channel_id=1, source_target_pairs={{0,1},{1,2},{2,3},{3,0},{4,5},{5,6},{6,7},{7,4},{8,9},{9,10},{10,1... | collective-permute-start | bytes 1572872 | tf_op jit(solution)/shard_map/ppermute | solution.py:429
  42.0 2.1 %collective-permute-start.2 = (bf16[160,1024]{1,0:T(8,128)(2,1)S(1)}, bf16[160,1024]{1,0:T(8,128)(2,1)}, u32[]{:S(2)}, u32[]{:S(2)}) collective-permute-start(bf16[160,1024]{1,0:T(8,128)(2,1)S(1)} %shard_map.75.refs_0_), channel_id=1, source_target_pairs={{0,1},{1,2},{2,3},{3,0},{4,5},{5,6},{6,7},{7,4},{8,9},{9,10},{10,1... | collective-permute-start | bytes 983048 | tf_op jit(solution)/shard_map/ppermute | solution.py:429
  44.0 16.0 %collective-permute-done.2.refs_1_.refs_6_ = bf16[160,1024]{1,0:T(8,128)(2,1)} collective-permute-done((bf16[160,1024]{1,0:T(8,128)(2,1)S(1)}, bf16[160,1024]{1,0:T(8,128)(2,1)}, u32[]{:S(2)}, u32[]{:S(2)}) %collective-permute-start.2) | collective-permute-done | bytes 327712 | tf_op jit(solution)/shard_map/ppermute | solution.py:429
  60.0 1.6 %collective-permute-start.3 = (bf16[160,1024]{1,0:T(8,128)(2,1)}, bf16[160,1024]{1,0:T(8,128)(2,1)}, u32[]{:S(2)}, u32[]{:S(2)}) collective-permute-start(bf16[160,1024]{1,0:T(8,128)(2,1)} %collective-permute-done.2.refs_1_.refs_6_), channel_id=1, source_target_pairs={{0,1},{1,2},{2,3},{3,0},{4,5},{5,6},{6,7},{7,4},{8,9},{9,10},{10,1... | collective-permute-start | bytes 983048 | tf_op jit(solution)/shard_map/ppermute | solution.py:429
  61.6 3.4 %copy-done.2 = bf16[1024,4096]{1,0:T(8,128)(2,1)S(1)} copy-done((bf16[1024,4096]{1,0:T(8,128)(2,1)S(1)}, bf16[1024,4096]{1,0:T(8,128)(2,1)}, u32[]{:S(2)}) %copy-start.2) | copy-done | bytes 8388632
  67.1 2.4 %shard_map.82.refs_0_.refs_1_ = bf16[256,1024]{1,0:T(8,128)(2,1)S(1)} custom-call(s32[1]{0:T(128)} %bitcast.3.place_ref, bf16[256,1024]{1,0:T(8,128)(2,1)S(1)} %copy-done.7, bf16[256,1024]{1,0:T(8,128)(2,1)S(1)} %copy-done.12, bf16[256,1024]{1,0:T(8,128)(2,1)S(1)} %shard_map.74.refs_1_.refs_2_, bf16[256,1024]{1,0:T(8,128)(2,1)S(1)} %collective-permute-done.5.refs_1_.refs_3_, ...), custom_call_target="tpu_custom_call" | custom-call | flops 2147483648 | bytes 10485760 | tf_op jit(solution)/shard_map/pallas_call | solution.py:200
  69.5 3.7 %collective-permute-start.10 = (bf16[256,1024]{1,0:T(8,128)(2,1)S(1)}, bf16[256,1024]{1,0:T(8,128)(2,1)S(1)}, u32[]{:S(2)}, u32[]{:S(2)}) collective-permute-start(bf16[256,1024]{1,0:T(8,128)(2,1)S(1)} %shard_map.82.refs_0_.refs_1_), channel_id=1, source_target_pairs={{0,8},{4,12},{8,16},{12,20},{16,24},{20,28},{1,9},{5,13},{9,17},{1... | collective-permute-start | bytes 1572872 | tf_op jit(solution)/shard_map/ppermute | solution.py:392
  73.1 2.2 %collective-permute-start.4 = (bf16[160,1024]{1,0:T(8,128)(2,1)}, bf16[160,1024]{1,0:T(8,128)(2,1)S(1)}, u32[]{:S(2)}, u32[]{:S(2)}) collective-permute-start(bf16[160,1024]{1,0:T(8,128)(2,1)} %collective-permute-done.3.refs_2_), channel_id=1, source_target_pairs={{0,1},{1,2},{2,3},{3,0},{4,5},{5,6},{6,7},{7,4},{8,9},{9,10},{10,1... | collective-permute-start | bytes 983048 | tf_op jit(solution)/shard_map/ppermute | solution.py:429
  75.4 2.3 %collective-permute-start.6 = (bf16[96,1024]{1,0:T(8,128)(2,1)S(1)}, bf16[96,1024]{1,0:T(8,128)(2,1)S(1)}, u32[]{:S(2)}, u32[]{:S(2)}) collective-permute-start(bf16[96,1024]{1,0:T(8,128)(2,1)S(1)} %shard_map.77.refs_0_), channel_id=1, source_target_pairs={{0,1},{1,2},{2,3},{3,0},{4,5},{5,6},{6,7},{7,4},{8,9},{9,10},{10,1... | collective-permute-start | bytes 589832 | tf_op jit(solution)/shard_map/ppermute | solution.py:429
  77.6 7.2 %collective-permute-done.6.refs_0_ = bf16[96,1024]{1,0:T(8,128)(2,1)S(1)} collective-permute-done((bf16[96,1024]{1,0:T(8,128)(2,1)S(1)}, bf16[96,1024]{1,0:T(8,128)(2,1)S(1)}, u32[]{:S(2)}, u32[]{:S(2)}) %collective-permute-start.6) | collective-permute-done | bytes 196640 | tf_op jit(solution)/shard_map/ppermute | solution.py:429
  84.8 2.6 %collective-permute-start.7 = (bf16[96,1024]{1,0:T(8,128)(2,1)S(1)}, bf16[96,1024]{1,0:T(8,128)(2,1)S(1)}, u32[]{:S(2)}, u32[]{:S(2)}) collective-permute-start(bf16[96,1024]{1,0:T(8,128)(2,1)S(1)} %shard_map.78.refs_1_), channel_id=1, source_target_pairs={{0,1},{1,2},{2,3},{3,0},{4,5},{5,6},{6,7},{7,4},{8,9},{9,10},{10,1... | collective-permute-start | bytes 589832 | tf_op jit(solution)/shard_map/ppermute | solution.py:429
  87.4 4.0 %shard_map.76.refs_0_ = bf16[160,1024]{1,0:T(8,128)(2,1)S(1)} custom-call(s32[1]{0:T(128)} %bitcast.3.place_ref, bf16[160,1024]{1,0:T(8,128)(2,1)S(1)} %shard_map.75.refs_0_, bf16[160,1024]{1,0:T(8,128)(2,1)} %collective-permute-done.2.refs_1_.refs_6_, bf16[160,1024]{1,0:T(8,128)(2,1)} %collective-permute-done.3.refs_2_, ...), custom_call_target="tpu_custom_call" | custom-call | flops 1342177280 | bytes 9699328 | tf_op jit(solution)/shard_map/pallas_call | solution.py:200
  91.4 3.3 %collective-permute-start.12 = (bf16[160,1024]{1,0:T(8,128)(2,1)S(1)}, bf16[160,1024]{1,0:T(8,128)(2,1)S(1)}, u32[]{:S(2)}, u32[]{:S(2)}) collective-permute-start(bf16[160,1024]{1,0:T(8,128)(2,1)S(1)} %shard_map.76.refs_0_), channel_id=1, source_target_pairs={{8,0},{12,4},{16,8},{20,12},{24,16},{28,20},{9,1},{13,5},{17,9},{2... | collective-permute-start | bytes 983048 | tf_op jit(solution)/shard_map/ppermute | solution.py:392
  94.8 1.3 collective-permute-start.11
  96.2 2.5 %collective-permute-start.8 = (bf16[96,1024]{1,0:T(8,128)(2,1)S(1)}, bf16[96,1024]{1,0:T(8,128)(2,1)S(1)}, u32[]{:S(2)}, u32[]{:S(2)}) collective-permute-start(bf16[96,1024]{1,0:T(8,128)(2,1)S(1)} %collective-permute-done.7.refs_2_), channel_id=1, source_target_pairs={{0,1},{1,2},{2,3},{3,0},{4,5},{5,6},{6,7},{7,4},{8,9},{9,10},{10,1... | collective-permute-start | bytes 589832 | tf_op jit(solution)/shard_map/ppermute | solution.py:429
  98.7 5.6 %shard_map.83.refs_0_ = f32[256,1024]{1,0:T(8,128)S(1)} custom-call(s32[2,8]{1,0:T(2,128)S(1)} %get-tuple-element.12.facts_ref, bf16[512,256]{1,0:T(8,128)(2,1)S(1)} %get-tuple-element.13.table_ref, bf16[256,1024]{1,0:T(8,128)(2,1)S(1)} %get-tuple-element.14.back_ref, f32[4,512,1024]{2,1,0:T(8,128)S(1)} %bitcast.9, ...), custom_call_target="tpu_custom_call" | custom-call | flops 2147483648 | bytes 1048576 | tf_op jit(solution)/shard_map/pallas_call | solution.py:344
  104.4 2.0 %shard_map.79.refs_3_ = f32[96,1024]{1,0:T(8,128)S(1)} custom-call(s32[1]{0:T(128)} %bitcast.3.place_ref, bf16[96,1024]{1,0:T(8,128)(2,1)S(1)} %shard_map.77.refs_0_, bf16[96,1024]{1,0:T(8,128)(2,1)S(1)} %shard_map.78.refs_1_, bf16[96,1024]{1,0:T(8,128)(2,1)S(1)} %collective-permute-done.7.refs_2_, bf16[1024,4096]{1,0:T(8,128)(2,1)S(1)} %copy-done.3, ...), custom_call_target="tpu_custom_call" | custom-call | flops 603979776 | bytes 6881280 | tf_op jit(solution)/shard_map/pallas_call | solution.py:200
  106.4 1.9 %collective-permute-start.16 = (bf16[160,1024]{1,0:T(8,128)(2,1)S(1)}, bf16[160,1024]{1,0:T(8,128)(2,1)S(1)}, u32[]{:S(2)}, u32[]{:S(2)}) collective-permute-start(bf16[160,1024]{1,0:T(8,128)(2,1)S(1)} %shard_map.76.refs_0_), channel_id=1, source_target_pairs={{4,0},{12,8},{20,16},{28,24},{16,4},{24,12},{5,1},{13,9},{21,17},{... | collective-permute-start | bytes 983048 | tf_op jit(solution)/shard_map/ppermute | solution.py:413
  109.7 4.7 %collective-permute-start.13 = (bf16[96,1024]{1,0:T(8,128)(2,1)S(1)}, bf16[96,1024]{1,0:T(8,128)(2,1)S(1)}, u32[]{:S(2)}, u32[]{:S(2)}) collective-permute-start(bf16[96,1024]{1,0:T(8,128)(2,1)S(1)} %shard_map.80.refs_1_), channel_id=1, source_target_pairs={{8,0},{12,4},{16,8},{20,12},{24,16},{28,20},{9,1},{13,5},{17,9},{2... | collective-permute-start | bytes 589832 | tf_op jit(solution)/shard_map/ppermute | solution.py:392
  114.4 5.6 %shard_map.81.refs_0_ = f32[256,1024]{1,0:T(8,128)S(1)} custom-call(s32[2,8]{1,0:T(2,128)S(1)} %get-tuple-element.12.facts_ref, bf16[512,256]{1,0:T(8,128)(2,1)S(1)} %get-tuple-element.13.table_ref, bf16[256,1024]{1,0:T(8,128)(2,1)S(1)} %get-tuple-element.14.back_ref, f32[4,512,1024]{2,1,0:T(8,128)S(1)} %bitcast.9, bf16[160,1024]{1,0:T(8,128)(2,1)S(1)} %shard_map.76.refs_0_, ...), custom_call_target="tpu_custom_call" | custom-call | flops 2147483648 | bytes 1048576 | tf_op jit(solution)/shard_map/pallas_call | solution.py:344
  120.1 1.9 %collective-permute-start.17 = (bf16[96,1024]{1,0:T(8,128)(2,1)S(1)}, bf16[96,1024]{1,0:T(8,128)(2,1)S(1)}, u32[]{:S(2)}, u32[]{:S(2)}) collective-permute-start(bf16[96,1024]{1,0:T(8,128)(2,1)S(1)} %shard_map.80.refs_1_), channel_id=1, source_target_pairs={{4,0},{12,8},{20,16},{28,24},{16,4},{24,12},{5,1},{13,9},{21,17},{... | collective-permute-start | bytes 589832 | tf_op jit(solution)/shard_map/ppermute | solution.py:413
  122.6 4.8 %shard_map.84.refs_11_ = f32[1,2,256,1024]{3,2,1,0:T(8,128)} custom-call(s32[2,8]{1,0:T(2,128)S(1)} %get-tuple-element.12.facts_ref, bf16[512,256]{1,0:T(8,128)(2,1)S(1)} %get-tuple-element.13.table_ref, bf16[256,1024]{1,0:T(8,128)(2,1)S(1)} %get-tuple-element.14.back_ref, f32[4,512,1024]{2,1,0:T(8,128)S(1)} %bitcast.9, f32[256,1024]{1,0:T(8,128)S(1)} %shard_map.83.refs_0_, ...), custom_call_target="tpu_custom_call" | custom-call | flops 2147483648 | bytes 1048576 | tf_op jit(solution)/shard_map/pallas_call | solution.py:344
  127.4 4.9 %shard_map.85 = f32[1,2,256,1024]{3,2,1,0:T(8,128)} custom-call(s32[2,8]{1,0:T(2,128)S(1)} %get-tuple-element.12.facts_ref, bf16[512,256]{1,0:T(8,128)(2,1)S(1)} %get-tuple-element.13.table_ref, bf16[256,1024]{1,0:T(8,128)(2,1)S(1)} %get-tuple-element.14.back_ref, f32[4,512,1024]{2,1,0:T(8,128)S(1)} %bitcast.9, ...), custom_call_target="tpu_custom_call", output_to_operand_aliasing={{}: (15, {})} | custom-call | flops 2147483648 | bytes 1048576 | tf_op jit(solution)/shard_map/pallas_call | solution.py:344
  (55 shorter events, 10.7 us)
Async XLA Ops:
  1.1 13.7 %collective-permute-start = (bf16[256,1024]{1,0:T(8,128)(2,1)S(1)}, bf16[256,1024]{1,0:T(8,128)(2,1)S(1)}, u32[]{:S(2)}, u32[]{:S(2)}) collective-permute-start(bf16[256,1024]{1,0:T(8,128)(2,1)S(1)} %slice_bitcast_fusion.refs_0_), channel_id=1, source_target_pairs={{0,1},{1,2},{2,3},{3,0},{4,5},{5,6},{6,7},{7,4},{8,9},{9,10},{10,1... | collective-permute-start | bytes 1572872 | tf_op jit(solution)/shard_map/ppermute | solution.py:429
  14.8 25.6 %copy-start.11 = (bf16[256,1024]{1,0:T(8,128)(2,1)}, bf16[256,1024]{1,0:T(8,128)(2,1)S(1)}, u32[]{:S(2)}) copy-start(bf16[256,1024]{1,0:T(8,128)(2,1)S(1)} %collective-permute-done.refs_1_) | copy-start | bytes 1572868
  14.8 25.6 %collective-permute-start.1 = (bf16[256,1024]{1,0:T(8,128)(2,1)S(1)}, bf16[256,1024]{1,0:T(8,128)(2,1)S(1)}, u32[]{:S(2)}, u32[]{:S(2)}) collective-permute-start(bf16[256,1024]{1,0:T(8,128)(2,1)S(1)} %collective-permute-done.refs_1_), channel_id=1, source_target_pairs={{0,1},{1,2},{2,3},{3,0},{4,5},{5,6},{6,7},{7,4},{8,9},{9,10},{10,1... | collective-permute-start | bytes 1572872 | tf_op jit(solution)/shard_map/ppermute | solution.py:429
  18.3 3.4 %copy-start.4 = (bf16[1024,4096]{1,0:T(8,128)(2,1)S(1)}, bf16[1024,4096]{1,0:T(8,128)(2,1)}, u32[]{:S(2)}) copy-start(bf16[1024,4096]{1,0:T(8,128)(2,1)} %refs_5_.1) | copy-start | bytes 25165828
  21.7 1.9 %copy-start.5 = (f32[768,1024]{1,0:T(8,128)S(1)}, f32[768,1024]{1,0:T(8,128)}, u32[]{:S(2)}) copy-start(f32[768,1024]{1,0:T(8,128)} %refs_4_.1) | copy-start | bytes 9437188
  23.6 1.2 copy-start.8
  24.8 1.0 copy-start.9
  25.9 1.0 copy-start.10
  33.8 3.3 %copy-start = (f32[4,512,1024]{2,1,0:T(8,128)}, f32[4,512,1024]{2,1,0:T(8,128)S(1)}, u32[]{:S(2)}) copy-start(f32[4,512,1024]{2,1,0:T(8,128)S(1)} %get-tuple-element.15.spec_ref) | copy-start | bytes 25165828
  37.1 3.3 %copy-start.1 = (bf16[1024,4096]{1,0:T(8,128)(2,1)}, bf16[1024,4096]{1,0:T(8,128)(2,1)S(1)}, u32[]{:S(2)}) copy-start(bf16[1024,4096]{1,0:T(8,128)(2,1)S(1)} %get-tuple-element.17.refs_4_.refs_3_.refs_1_) | copy-start | bytes 25165828
  40.4 21.2 %collective-permute-start.5 = (bf16[256,1024]{1,0:T(8,128)(2,1)S(1)}, bf16[256,1024]{1,0:T(8,128)(2,1)S(1)}, u32[]{:S(2)}, u32[]{:S(2)}) collective-permute-start(bf16[256,1024]{1,0:T(8,128)(2,1)S(1)} %shard_map.74.refs_1_.refs_2_), channel_id=1, source_target_pairs={{0,1},{1,2},{2,3},{3,0},{4,5},{5,6},{6,7},{7,4},{8,9},{9,10},{10,1... | collective-permute-start | bytes 1572872 | tf_op jit(solution)/shard_map/ppermute | solution.py:429
  42.0 18.1 %collective-permute-start.2 = (bf16[160,1024]{1,0:T(8,128)(2,1)S(1)}, bf16[160,1024]{1,0:T(8,128)(2,1)}, u32[]{:S(2)}, u32[]{:S(2)}) collective-permute-start(bf16[160,1024]{1,0:T(8,128)(2,1)S(1)} %shard_map.75.refs_0_), channel_id=1, source_target_pairs={{0,1},{1,2},{2,3},{3,0},{4,5},{5,6},{6,7},{7,4},{8,9},{9,10},{10,1... | collective-permute-start | bytes 983048 | tf_op jit(solution)/shard_map/ppermute | solution.py:429
  60.0 13.1 %collective-permute-start.3 = (bf16[160,1024]{1,0:T(8,128)(2,1)}, bf16[160,1024]{1,0:T(8,128)(2,1)}, u32[]{:S(2)}, u32[]{:S(2)}) collective-permute-start(bf16[160,1024]{1,0:T(8,128)(2,1)} %collective-permute-done.2.refs_1_.refs_6_), channel_id=1, source_target_pairs={{0,1},{1,2},{2,3},{3,0},{4,5},{5,6},{6,7},{7,4},{8,9},{9,10},{10,1... | collective-permute-start | bytes 983048 | tf_op jit(solution)/shard_map/ppermute | solution.py:429
  61.6 3.4 %copy-start.2 = (bf16[1024,4096]{1,0:T(8,128)(2,1)S(1)}, bf16[1024,4096]{1,0:T(8,128)(2,1)}, u32[]{:S(2)}) copy-start(bf16[1024,4096]{1,0:T(8,128)(2,1)} %copy-done.1) | copy-start | bytes 25165828
  65.0 1.0 copy-start.7
  67.1 20.4 %copy-start.3 = (bf16[1024,4096]{1,0:T(8,128)(2,1)S(1)}, bf16[1024,4096]{1,0:T(8,128)(2,1)}, u32[]{:S(2)}) copy-start(bf16[1024,4096]{1,0:T(8,128)(2,1)} %copy-done.1) | copy-start | bytes 25165828
  67.1 31.7 %slice-start = ((s8[8388608]{0:T(1024)(128)(4,1)}), s8[4194304]{0:T(1024)(128)(4,1)S(1)}, s32[]{:S(2)}) async-start(s8[8388608]{0:T(1024)(128)(4,1)} %bitcast.8), calls=%async_computation | async-start | bytes 8388608
  69.5 29.3 %slice-start.1 = ((s8[8388608]{0:T(1024)(128)(4,1)}), s8[4194304]{0:T(1024)(128)(4,1)S(1)}, s32[]{:S(2)}) async-start(s8[8388608]{0:T(1024)(128)(4,1)} %bitcast.8), calls=%async_computation.1 | async-start | bytes 8388608
  69.5 26.6 %collective-permute-start.10 = (bf16[256,1024]{1,0:T(8,128)(2,1)S(1)}, bf16[256,1024]{1,0:T(8,128)(2,1)S(1)}, u32[]{:S(2)}, u32[]{:S(2)}) collective-permute-start(bf16[256,1024]{1,0:T(8,128)(2,1)S(1)} %shard_map.82.refs_0_.refs_1_), channel_id=1, source_target_pairs={{0,8},{4,12},{8,16},{12,20},{16,24},{20,28},{1,9},{5,13},{9,17},{1... | collective-permute-start | bytes 1572872 | tf_op jit(solution)/shard_map/ppermute | solution.py:392
  73.1 11.7 %collective-permute-start.4 = (bf16[160,1024]{1,0:T(8,128)(2,1)}, bf16[160,1024]{1,0:T(8,128)(2,1)S(1)}, u32[]{:S(2)}, u32[]{:S(2)}) collective-permute-start(bf16[160,1024]{1,0:T(8,128)(2,1)} %collective-permute-done.3.refs_2_), channel_id=1, source_target_pairs={{0,1},{1,2},{2,3},{3,0},{4,5},{5,6},{6,7},{7,4},{8,9},{9,10},{10,1... | collective-permute-start | bytes 983048 | tf_op jit(solution)/shard_map/ppermute | solution.py:429
  75.4 9.5 %collective-permute-start.6 = (bf16[96,1024]{1,0:T(8,128)(2,1)S(1)}, bf16[96,1024]{1,0:T(8,128)(2,1)S(1)}, u32[]{:S(2)}, u32[]{:S(2)}) collective-permute-start(bf16[96,1024]{1,0:T(8,128)(2,1)S(1)} %shard_map.77.refs_0_), channel_id=1, source_target_pairs={{0,1},{1,2},{2,3},{3,0},{4,5},{5,6},{6,7},{7,4},{8,9},{9,10},{10,1... | collective-permute-start | bytes 589832 | tf_op jit(solution)/shard_map/ppermute | solution.py:429
  77.6 32.1 %collective-permute-start.9 = (bf16[256,1024]{1,0:T(8,128)(2,1)S(1)}, bf16[256,1024]{1,0:T(8,128)(2,1)S(1)}, u32[]{:S(2)}, u32[]{:S(2)}) collective-permute-start(bf16[256,1024]{1,0:T(8,128)(2,1)S(1)} %shard_map.82.refs_0_.refs_1_), channel_id=1, source_target_pairs={{0,4},{4,0},{8,12},{12,8},{16,20},{20,16},{24,28},{28,24},{1,5},{5... | collective-permute-start | bytes 1572872 | tf_op jit(solution)/shard_map/ppermute | solution.py:397
  84.8 11.3 %collective-permute-start.7 = (bf16[96,1024]{1,0:T(8,128)(2,1)S(1)}, bf16[96,1024]{1,0:T(8,128)(2,1)S(1)}, u32[]{:S(2)}, u32[]{:S(2)}) collective-permute-start(bf16[96,1024]{1,0:T(8,128)(2,1)S(1)} %shard_map.78.refs_1_), channel_id=1, source_target_pairs={{0,1},{1,2},{2,3},{3,0},{4,5},{5,6},{6,7},{7,4},{8,9},{9,10},{10,1... | collective-permute-start | bytes 589832 | tf_op jit(solution)/shard_map/ppermute | solution.py:429
  91.4 15.0 %collective-permute-start.12 = (bf16[160,1024]{1,0:T(8,128)(2,1)S(1)}, bf16[160,1024]{1,0:T(8,128)(2,1)S(1)}, u32[]{:S(2)}, u32[]{:S(2)}) collective-permute-start(bf16[160,1024]{1,0:T(8,128)(2,1)S(1)} %shard_map.76.refs_0_), channel_id=1, source_target_pairs={{8,0},{12,4},{16,8},{20,12},{24,16},{28,20},{9,1},{13,5},{17,9},{2... | collective-permute-start | bytes 983048 | tf_op jit(solution)/shard_map/ppermute | solution.py:392
  94.8 25.3 %collective-permute-start.11 = (bf16[256,1024]{1,0:T(8,128)(2,1)S(1)}, bf16[256,1024]{1,0:T(8,128)(2,1)S(1)}, u32[]{:S(2)}, u32[]{:S(2)}) collective-permute-start(bf16[256,1024]{1,0:T(8,128)(2,1)S(1)} %shard_map.82.refs_0_.refs_1_), channel_id=1, source_target_pairs={{4,16},{12,24},{28,20},{5,17},{13,25},{29,21},{6,18},{14,26},{30,2... | collective-permute-start | bytes 1572872 | tf_op jit(solution)/shard_map/ppermute | solution.py:404
  96.1 26.5 %collective-permute-start.18 = (bf16[256,1024]{1,0:T(8,128)(2,1)S(1)}, bf16[256,1024]{1,0:T(8,128)(2,1)S(1)}, u32[]{:S(2)}, u32[]{:S(2)}) collective-permute-start(bf16[256,1024]{1,0:T(8,128)(2,1)S(1)} %collective-permute-done.10.refs_1_.refs_3_), channel_id=1, source_target_pairs={{0,4},{4,0},{8,12},{12,8},{16,20},{20,16},{24,28},{28,24},{1,5},{5... | collective-permute-start | bytes 1572872 | tf_op jit(solution)/shard_map/ppermute | solution.py:397
  96.2 12.2 %collective-permute-start.8 = (bf16[96,1024]{1,0:T(8,128)(2,1)S(1)}, bf16[96,1024]{1,0:T(8,128)(2,1)S(1)}, u32[]{:S(2)}, u32[]{:S(2)}) collective-permute-start(bf16[96,1024]{1,0:T(8,128)(2,1)S(1)} %collective-permute-done.7.refs_2_), channel_id=1, source_target_pairs={{0,1},{1,2},{2,3},{3,0},{4,5},{5,6},{6,7},{7,4},{8,9},{9,10},{10,1... | collective-permute-start | bytes 589832 | tf_op jit(solution)/shard_map/ppermute | solution.py:429
  106.4 21.0 %collective-permute-start.16 = (bf16[160,1024]{1,0:T(8,128)(2,1)S(1)}, bf16[160,1024]{1,0:T(8,128)(2,1)S(1)}, u32[]{:S(2)}, u32[]{:S(2)}) collective-permute-start(bf16[160,1024]{1,0:T(8,128)(2,1)S(1)} %shard_map.76.refs_0_), channel_id=1, source_target_pairs={{4,0},{12,8},{20,16},{28,24},{16,4},{24,12},{5,1},{13,9},{21,17},{... | collective-permute-start | bytes 983048 | tf_op jit(solution)/shard_map/ppermute | solution.py:413
  108.4 19.1 %collective-permute-start.14 = (bf16[160,1024]{1,0:T(8,128)(2,1)S(1)}, bf16[160,1024]{1,0:T(8,128)(2,1)S(1)}, u32[]{:S(2)}, u32[]{:S(2)}) collective-permute-start(bf16[160,1024]{1,0:T(8,128)(2,1)S(1)} %collective-permute-done.12.refs_5_), channel_id=1, source_target_pairs={{0,4},{4,0},{8,12},{12,8},{16,20},{20,16},{24,28},{28,24},{1,5},{5... | collective-permute-start | bytes 983048 | tf_op jit(solution)/shard_map/ppermute | solution.py:397
  109.7 12.3 %collective-permute-start.13 = (bf16[96,1024]{1,0:T(8,128)(2,1)S(1)}, bf16[96,1024]{1,0:T(8,128)(2,1)S(1)}, u32[]{:S(2)}, u32[]{:S(2)}) collective-permute-start(bf16[96,1024]{1,0:T(8,128)(2,1)S(1)} %shard_map.80.refs_1_), channel_id=1, source_target_pairs={{8,0},{12,4},{16,8},{20,12},{24,16},{28,20},{9,1},{13,5},{17,9},{2... | collective-permute-start | bytes 589832 | tf_op jit(solution)/shard_map/ppermute | solution.py:392
  120.1 7.4 %collective-permute-start.17 = (bf16[96,1024]{1,0:T(8,128)(2,1)S(1)}, bf16[96,1024]{1,0:T(8,128)(2,1)S(1)}, u32[]{:S(2)}, u32[]{:S(2)}) collective-permute-start(bf16[96,1024]{1,0:T(8,128)(2,1)S(1)} %shard_map.80.refs_1_), channel_id=1, source_target_pairs={{4,0},{12,8},{20,16},{28,24},{16,4},{24,12},{5,1},{13,9},{21,17},{... | collective-permute-start | bytes 589832 | tf_op jit(solution)/shard_map/ppermute | solution.py:413
  122.0 5.4 %collective-permute-start.15 = (bf16[96,1024]{1,0:T(8,128)(2,1)S(1)}, bf16[96,1024]{1,0:T(8,128)(2,1)S(1)}, u32[]{:S(2)}, u32[]{:S(2)}) collective-permute-start(bf16[96,1024]{1,0:T(8,128)(2,1)S(1)} %collective-permute-done.13.refs_6_), channel_id=1, source_target_pairs={{0,4},{4,0},{8,12},{12,8},{16,20},{20,16},{24,28},{28,24},{1,5},{5... | collective-permute-start | bytes 589832 | tf_op jit(solution)/shard_map/ppermute | solution.py:397
  (3 other events, 2.5 us)

commit v7 on v5

--- a/solution.py
+++ b/solution.py
@@ -79,7 +79,7 @@
 
 
 def prepare_kernel(pairs, *refs):
-    place_ref, docs_ref, table_ref, back_ref, taps_ref, weight_ref, gate_ref = refs[:7]
+    place_ref, lane_ref, docs_ref, table_ref, back_ref, taps_ref, weight_ref, gate_ref = refs[:8]
     spec_out, weight_out, gate_out, table_out, back_out, facts_out, token_out, sems = refs[-8:]
     token_out[...] = jnp.zeros_like(token_out)
     copies = [
@@ -100,6 +100,8 @@
         odd = lax.rem(place, 2)
         role = jnp.where(place >= pairs - 3, pairs - place, 0)
         end = 2 * pairs * length
+        for slot in range(2):
+            facts_out[slot, 4 + REACH] = lane_ref[0]
         write_facts(facts_out, 0, docs_ref, place, length, end, 1 - odd, role)
         write_facts(facts_out, 1, docs_ref, 2 * pairs - 1 - place, length, end, odd, role)
 
@@ -133,7 +135,7 @@
             copy.wait()
 
 
-def prepare(pairs, place, docs, table, back, taps, weight, gate, after):
+def prepare(pairs, place, lane, docs, table, back, taps, weight, gate, after):
     count, width = taps.shape
     length = count // REACH
     return pl.pallas_call(
@@ -151,6 +153,7 @@
         in_specs=[
             SCALARS,
             SCALARS,
+            SCALARS,
             pl.BlockSpec((2 * length, 2 * length), lambda c: (0, 0)),
             OUTSIDE,
             pl.BlockSpec((count, LANES), lambda c: (0, c)),
@@ -166,10 +169,10 @@
             bytes_accessed=4 * (count * width + 8 * length * width),
             transcendentals=0,
         ),
-    )(place, docs, table, back, taps, weight, gate, *after)
-
-
-def project_kernel(steps, slot, start, first, last, place_ref, *refs):
+    )(place, lane, docs, table, back, taps, weight, gate, *after)
+
+
+def project_kernel(steps, slot, start, first, last, facts_ref, *refs):
     shards, refs = refs[: len(steps)], refs[len(steps) :]
     weight_ref, gate_ref, out_ref = refs[0], refs[1], refs[-1]
     before_ref = None if first else refs[2]
@@ -179,7 +182,7 @@
         lanes = pl.ds(tile * LANES, LANES)
         total = None if first else before_ref[:, lanes]
         for shard, step in zip(shards, steps):
-            at = lax.rem(place_ref[0] + count - step, count)
+            at = lax.rem(facts_ref[0, 4 + REACH] + count - step, count)
             features = pl.ds(pl.multiple_of(at * depth, depth), depth)
             part = nt(shard[...], weight_ref[lanes, features])
             total = part if total is None else total + part
@@ -190,10 +193,10 @@
             out_ref[:, lanes] = total
 
 
-def project(place, shards, steps, weight, gate, slot, start, before=None, last=True, after=()):
+def project(facts, shards, steps, weight, gate, slot, start, before=None, last=True, after=()):
     rows, depth = shards[0].shape
     width = weight.shape[0]
-    operands = [place, *shards, weight, gate]
+    operands = [facts, *shards, weight, gate]
     if before is not None:
         operands.append(before)
     body = functools.partial(project_kernel, steps, slot, start, before is None, last)
@@ -436,6 +439,7 @@
     spectra, weight, gates, table, back, facts, prepared = prepare(
         pairs,
         place.astype(jnp.int32)[None],
+        lane,
         doc_starts,
         table,
         back,
@@ -457,15 +461,15 @@
     for step in range(2, count):
         second_in.append(turned(second_in[-1]))
 
-    upper = project(lane, upper_in, everything, weight, gates, 1, 0, after=[first_in[1]])
+    upper = project(facts, upper_in, everything, weight, gates, 1, 0, after=[first_in[1]])
     upper_halo = upper_halo_of(upper)
     near = own_terms(1, tabs, facts, [upper])
     result = far_terms(1, 1, tabs, facts, [near, *upper_halo])
 
-    first = project(lane, first_in, everything, weight, gates, 0, 0)
+    first = project(facts, first_in, everything, weight, gates, 0, 0)
     first_halo = lower_halo_of(first)
-    partial = project(lane, second_in[:-1], everything[:-1], weight, gates, 0, cut, last=False)
-    second = project(lane, second_in[-1:], everything[-1:], weight, gates, 0, cut, partial)
+    partial = project(facts, second_in[:-1], everything[:-1], weight, gates, 0, cut, last=False)
+    second = project(facts, second_in[-1:], everything[-1:], weight, gates, 0, cut, partial)
     second_halo = lower_halo_of(second)
     near = own_terms(0, tabs, facts, [first, second])
     two, _, mate, fold = upper_halo

time: 130 us -> 121 us (0.931)
  the two profiles are of different devices: /device:TPU:10 before, /device:TPU:3 now
where the time goes in v7:
time: 121 us; the launch traced here: 119 us
  waiting for transfers between devices  47.1 us (39%)
  Pallas kernels  34.2 us (28%)
  starting transfers between devices  31.7 us (26%)
  local copies, waits for them, and re-layouts  5.75 us (5%)
    ppermute x9, waiting for transfers between devices, turned(): return lax.ppermute(piece, 'ch', around)  43 us
    pallas_call x4, Pallas kernels, conv_call(): pl.pallas_call(body, grid=(width // LANES,), out_shape=out_shape, in_spec...  16 us
    ppermute x3, starting transfers between devices, shifted(): lax.ppermute(value, 'ctx', [(source, source + steps) for source in range(...  10.5 us
    pallas_call x4, Pallas kernels, project(): pl.pallas_call(body, out_shape=pltpu.VMEM((rows, width), BF16 if last els...  10.3 us
    ppermute x1, starting transfers between devices, upper_halo_of(): mate, far = (core_swapped(value), lax.ppermute(value, 'ctx', far))  8.17 us
    pallas_call x1, Pallas kernels, prepare(): pl.pallas_call(functools.partial(prepare_kernel, pairs), grid=(width // L...  7.9 us
    ppermute x4, starting transfers between devices, core_swapped(): lax.ppermute(value, 'ctx', [(source, source ^ 1) for source in range(coun...  5.86 us
    ppermute x2, starting transfers between devices, lower_halo_of(): mixed = lax.ppermute(value, 'ctx', mixed)  5.31 us
  transfers between devices with their start and end apart: 19, of which 7 were waited for; matrix products, arithmetic and copies ran while one was open for 3% of the time, Pallas kernels for 25%

profile of v7, /device:TPU:3, one launch (start us, length us, event | category | flops | bytes accessed | tf_op | source)
XLA Modules:
  0.0 119.0 jit_solution(18052309502054886764)
XLA Ops:
  0.0 1.1 slice_bitcast_fusion.refs_0_
  1.1 1.3 %collective-permute-start = (bf16[256,1024]{1,0:T(8,128)(2,1)S(1)}, bf16[256,1024]{1,0:T(8,128)(2,1)S(1)}, u32[]{:S(2)}, u32[]{:S(2)}) collective-permute-start(bf16[256,1024]{1,0:T(8,128)(2,1)S(1)} %slice_bitcast_fusion.refs_0_), channel_id=1, source_target_pairs={{0,1},{1,2},{2,3},{3,0},{4,5},{5,6},{6,7},{7,4},{8,9},{9,10},{10,1... | collective-permute-start | bytes 1572872 | tf_op jit(solution)/shard_map/ppermute | solution.py:432
  2.4 1.6 %slice_bitcast_fusion.2.refs_9_.refs_0_ = bf16[96,1024]{1,0:T(8,128)(2,1)} fusion(bf16[1,2,256,1024]{3,2,1,0:T(8,128)(2,1)} %param.7), kind=kLoop, calls=%fused_computation.2 | loop fusion | bytes 393216 | tf_op jit(solution)/shard_map/squeeze | solution.py:434
  4.0 1.7 %slice_bitcast_fusion.1.refs_8_.refs_0_ = bf16[160,1024]{1,0:T(8,128)(2,1)} fusion(bf16[1,2,256,1024]{3,2,1,0:T(8,128)(2,1)} %param.7), kind=kLoop, calls=%fused_computation.1 | loop fusion | bytes 655360 | tf_op jit(solution)/shard_map/squeeze | solution.py:434
  5.8 7.9 %shard_map.73 = (f32[4,512,1024]{2,1,0:T(8,128)S(1)}, bf16[1024,4096]{1,0:T(8,128)(2,1)S(1)}, bf16[1,2,256,1024]{3,2,1,0:T(8,128)(2,1)S(1)}, bf16[512,256]{1,0:T...) custom-call(s32[1]{0:T(128)} %bitcast.refs_0_, s32[1]{0:T(128)} %bitcast.1.refs_1_, ...), custom_call_target="tpu_custom_call" | custom-call | flops 2415919104 | bytes 11534336 | tf_op jit(solution)/shard_map/pallas_call | solution.py:141
  13.7 2.2 %collective-permute-done.refs_0_ = bf16[256,1024]{1,0:T(8,128)(2,1)S(1)} collective-permute-done((bf16[256,1024]{1,0:T(8,128)(2,1)S(1)}, bf16[256,1024]{1,0:T(8,128)(2,1)S(1)}, u32[]{:S(2)}, u32[]{:S(2)}) %collective-permute-start) | collective-permute-done | bytes 524320 | tf_op jit(solution)/shard_map/ppermute | solution.py:432
  15.9 0.7 copy-done.3
  16.5 13.7 %collective-permute-done.1.refs_1_.refs_2_ = bf16[256,1024]{1,0:T(8,128)(2,1)S(1)} collective-permute-done((bf16[256,1024]{1,0:T(8,128)(2,1)S(1)}, bf16[256,1024]{1,0:T(8,128)(2,1)S(1)}, u32[]{:S(2)}, u32[]{:S(2)}) %collective-permute-start.1) | collective-permute-done | bytes 524320 | tf_op jit(solution)/shard_map/ppermute | solution.py:432
  30.3 19.8 %collective-permute-done.2.refs_1_.refs_6_ = bf16[160,1024]{1,0:T(8,128)(2,1)S(1)} collective-permute-done((bf16[160,1024]{1,0:T(8,128)(2,1)S(1)}, bf16[160,1024]{1,0:T(8,128)(2,1)S(1)}, u32[]{:S(2)}, u32[]{:S(2)}) %collective-permute-start.2) | collective-permute-done | bytes 327712 | tf_op jit(solution)/shard_map/ppermute | solution.py:432
  50.1 0.7 copy-done.2
  50.8 2.9 %shard_map.82.refs_0_.refs_1_ = bf16[256,1024]{1,0:T(8,128)(2,1)S(1)} custom-call(s32[2,8]{1,0:T(2,128)S(1)} %copy-done.2, bf16[256,1024]{1,0:T(8,128)(2,1)S(1)} %slice_bitcast_fusion.refs_0_, bf16[256,1024]{1,0:T(8,128)(2,1)S(1)} %shard_map.74.refs_1_, bf16[256,1024]{1,0:T(8,128)(2,1)S(1)} %collective-permute-done.1.refs_1_.refs_2_, ...), custom_call_target="tpu_custom_call" | custom-call | flops 2147483648 | bytes 10485760 | tf_op jit(solution)/shard_map/pallas_call | solution.py:203
  53.7 3.1 %collective-permute-start.10 = (bf16[256,1024]{1,0:T(8,128)(2,1)S(1)}, bf16[256,1024]{1,0:T(8,128)(2,1)S(1)}, u32[]{:S(2)}, u32[]{:S(2)}) collective-permute-start(bf16[256,1024]{1,0:T(8,128)(2,1)S(1)} %shard_map.82.refs_0_.refs_1_), channel_id=1, source_target_pairs={{0,8},{4,12},{8,16},{12,20},{16,24},{20,28},{1,9},{5,13},{9,17},{1... | collective-permute-start | bytes 1572872 | tf_op jit(solution)/shard_map/ppermute | solution.py:395
  56.8 1.0 collective-permute-done.3.refs_2_
  57.9 4.5 %collective-permute-start.9 = (bf16[256,1024]{1,0:T(8,128)(2,1)S(1)}, bf16[256,1024]{1,0:T(8,128)(2,1)S(1)}, u32[]{:S(2)}, u32[]{:S(2)}) collective-permute-start(bf16[256,1024]{1,0:T(8,128)(2,1)S(1)} %shard_map.82.refs_0_.refs_1_), channel_id=1, source_target_pairs={{0,4},{4,0},{8,12},{12,8},{16,20},{20,16},{24,28},{28,24},{1,5},{5... | collective-permute-start | bytes 1572872 | tf_op jit(solution)/shard_map/ppermute | solution.py:400
  62.4 6.2 %collective-permute-done.6.refs_0_ = bf16[96,1024]{1,0:T(8,128)(2,1)S(1)} collective-permute-done((bf16[96,1024]{1,0:T(8,128)(2,1)S(1)}, bf16[96,1024]{1,0:T(8,128)(2,1)S(1)}, u32[]{:S(2)}, u32[]{:S(2)}) %collective-permute-start.6) | collective-permute-done | bytes 196640 | tf_op jit(solution)/shard_map/ppermute | solution.py:432
  68.6 3.5 %shard_map.76.refs_0_ = bf16[160,1024]{1,0:T(8,128)(2,1)S(1)} custom-call(s32[2,8]{1,0:T(2,128)S(1)} %copy-done.2, bf16[160,1024]{1,0:T(8,128)(2,1)S(1)} %shard_map.75.refs_0_, bf16[160,1024]{1,0:T(8,128)(2,1)S(1)} %collective-permute-done.2.refs_1_.refs_6_, bf16[160,1024]{1,0:T(8,128)(2,1)S(1)} %collective-permute-done.3.refs_2_, ...), custom_call_target="tpu_custom_call" | custom-call | flops 1342177280 | bytes 9699328 | tf_op jit(solution)/shard_map/pallas_call | solution.py:203
  72.1 3.2 %collective-permute-start.12 = (bf16[160,1024]{1,0:T(8,128)(2,1)S(1)}, bf16[160,1024]{1,0:T(8,128)(2,1)S(1)}, u32[]{:S(2)}, u32[]{:S(2)}) collective-permute-start(bf16[160,1024]{1,0:T(8,128)(2,1)S(1)} %shard_map.76.refs_0_), channel_id=1, source_target_pairs={{8,0},{12,4},{16,8},{20,12},{24,16},{28,20},{9,1},{13,5},{17,9},{2... | collective-permute-start | bytes 983048 | tf_op jit(solution)/shard_map/ppermute | solution.py:395
  75.3 8.2 %collective-permute-start.11 = (bf16[256,1024]{1,0:T(8,128)(2,1)S(1)}, bf16[256,1024]{1,0:T(8,128)(2,1)S(1)}, u32[]{:S(2)}, u32[]{:S(2)}) collective-permute-start(bf16[256,1024]{1,0:T(8,128)(2,1)S(1)} %shard_map.82.refs_0_.refs_1_), channel_id=1, source_target_pairs={{4,16},{12,24},{28,20},{5,17},{13,25},{29,21},{6,18},{14,26},{30,2... | collective-permute-start | bytes 1572872 | tf_op jit(solution)/shard_map/ppermute | solution.py:407
  83.5 0.4 collective-permute-start.8
  84.0 3.1 %shard_map.83.refs_0_ = f32[256,1024]{1,0:T(8,128)S(1)} custom-call(s32[2,8]{1,0:T(2,128)S(1)} %copy-done.2, bf16[512,256]{1,0:T(8,128)(2,1)S(1)} %get-tuple-element.13.table_ref, bf16[256,1024]{1,0:T(8,128)(2,1)S(1)} %get-tuple-element.14.back_ref, f32[4,512,1024]{2,1,0:T(8,128)S(1)} %get-tuple-element.15.spec_ref, ...), custom_call_target="tpu_custom_call" | custom-call | flops 2147483648 | bytes 1048576 | tf_op jit(solution)/shard_map/pallas_call | solution.py:347
  87.1 2.6 %shard_map.79.refs_3_ = f32[96,1024]{1,0:T(8,128)S(1)} custom-call(s32[2,8]{1,0:T(2,128)S(1)} %copy-done.2, bf16[96,1024]{1,0:T(8,128)(2,1)S(1)} %shard_map.77.refs_0_, bf16[96,1024]{1,0:T(8,128)(2,1)S(1)} %shard_map.78.refs_1_, bf16[96,1024]{1,0:T(8,128)(2,1)S(1)} %collective-permute-done.7.refs_2_, ...), custom_call_target="tpu_custom_call" | custom-call | flops 603979776 | bytes 6881280 | tf_op jit(solution)/shard_map/pallas_call | solution.py:203
  89.7 2.6 %collective-permute-start.16 = (bf16[160,1024]{1,0:T(8,128)(2,1)S(1)}, bf16[160,1024]{1,0:T(8,128)(2,1)S(1)}, u32[]{:S(2)}, u32[]{:S(2)}) collective-permute-start(bf16[160,1024]{1,0:T(8,128)(2,1)S(1)} %shard_map.76.refs_0_), channel_id=1, source_target_pairs={{4,0},{12,8},{20,16},{28,24},{16,4},{24,12},{5,1},{13,9},{21,17},{... | collective-permute-start | bytes 983048 | tf_op jit(solution)/shard_map/ppermute | solution.py:416
  92.3 0.7 collective-permute-start.14
  93.0 1.3 %shard_map.80.refs_1_ = bf16[96,1024]{1,0:T(8,128)(2,1)S(1)} custom-call(s32[2,8]{1,0:T(2,128)S(1)} %copy-done.2, bf16[96,1024]{1,0:T(8,128)(2,1)S(1)} %collective-permute-done.8.refs_0_, bf16[1024,4096]{1,0:T(8,128)(2,1)S(1)} %get-tuple-element.17.refs_4_.refs_3_.refs_1_, bf16[1,2,256,1024]{3,2,1,0:T(8,128)(2,1)S(1)} %get-tuple-element.18.refs_5_.refs_4_.refs_2_, ...), custom_call_target="tpu_custom_call" | custom-call | flops 201326592 | bytes 2293760 | tf_op jit(solution)/shard_map/pallas_call | solution.py:203
  94.4 4.3 %collective-permute-start.13 = (bf16[96,1024]{1,0:T(8,128)(2,1)S(1)}, bf16[96,1024]{1,0:T(8,128)(2,1)S(1)}, u32[]{:S(2)}, u32[]{:S(2)}) collective-permute-start(bf16[96,1024]{1,0:T(8,128)(2,1)S(1)} %shard_map.80.refs_1_), channel_id=1, source_target_pairs={{8,0},{12,4},{16,8},{20,12},{24,16},{28,20},{9,1},{13,5},{17,9},{2... | collective-permute-start | bytes 589832 | tf_op jit(solution)/shard_map/ppermute | solution.py:395
  98.6 3.1 %shard_map.81.refs_0_ = f32[256,1024]{1,0:T(8,128)S(1)} custom-call(s32[2,8]{1,0:T(2,128)S(1)} %copy-done.2, bf16[512,256]{1,0:T(8,128)(2,1)S(1)} %get-tuple-element.13.table_ref, bf16[256,1024]{1,0:T(8,128)(2,1)S(1)} %get-tuple-element.14.back_ref, f32[4,512,1024]{2,1,0:T(8,128)S(1)} %get-tuple-element.15.spec_ref, ...), custom_call_target="tpu_custom_call" | custom-call | flops 2147483648 | bytes 1048576 | tf_op jit(solution)/shard_map/pallas_call | solution.py:347
  101.8 2.7 %collective-permute-start.17 = (bf16[96,1024]{1,0:T(8,128)(2,1)S(1)}, bf16[96,1024]{1,0:T(8,128)(2,1)S(1)}, u32[]{:S(2)}, u32[]{:S(2)}) collective-permute-start(bf16[96,1024]{1,0:T(8,128)(2,1)S(1)} %shard_map.80.refs_1_), channel_id=1, source_target_pairs={{4,0},{12,8},{20,16},{28,24},{16,4},{24,12},{5,1},{13,9},{21,17},{... | collective-permute-start | bytes 589832 | tf_op jit(solution)/shard_map/ppermute | solution.py:416
  104.5 0.9 collective-permute-done.13.refs_6_
  105.4 0.6 collective-permute-start.15
  106.0 4.8 %shard_map.84.refs_11_ = f32[1,2,256,1024]{3,2,1,0:T(8,128)} custom-call(s32[2,8]{1,0:T(2,128)S(1)} %copy-done.2, bf16[512,256]{1,0:T(8,128)(2,1)S(1)} %get-tuple-element.13.table_ref, bf16[256,1024]{1,0:T(8,128)(2,1)S(1)} %get-tuple-element.14.back_ref, f32[4,512,1024]{2,1,0:T(8,128)S(1)} %get-tuple-element.15.spec_ref, f32[256,1024]{1,0:T(8,128)S(1)} %shard_map.83.refs_0_, ...), custom_call_target="tpu_custom_call" | custom-call | flops 2147483648 | bytes 1048576 | tf_op jit(solution)/shard_map/pallas_call | solution.py:347
  110.8 3.2 %collective-permute-done.17.refs_10_ = bf16[96,1024]{1,0:T(8,128)(2,1)S(1)} collective-permute-done((bf16[96,1024]{1,0:T(8,128)(2,1)S(1)}, bf16[96,1024]{1,0:T(8,128)(2,1)S(1)}, u32[]{:S(2)}, u32[]{:S(2)}) %collective-permute-start.17) | collective-permute-done | bytes 196640 | tf_op jit(solution)/shard_map/ppermute | solution.py:416
  114.1 4.9 %shard_map.85 = f32[1,2,256,1024]{3,2,1,0:T(8,128)} custom-call(s32[2,8]{1,0:T(2,128)S(1)} %copy-done.2, bf16[512,256]{1,0:T(8,128)(2,1)S(1)} %get-tuple-element.13.table_ref, bf16[256,1024]{1,0:T(8,128)(2,1)S(1)} %get-tuple-element.14.back_ref, f32[4,512,1024]{2,1,0:T(8,128)S(1)} %get-tuple-element.15.spec_ref, ...), custom_call_target="tpu_custom_call", output_to_operand_aliasing={{}: (15, {})} | custom-call | flops 2147483648 | bytes 1048576 | tf_op jit(solution)/shard_map/pallas_call | solution.py:347
  (30 shorter events, 0.1 us)
Async XLA Ops:
  1.1 14.8 %collective-permute-start = (bf16[256,1024]{1,0:T(8,128)(2,1)S(1)}, bf16[256,1024]{1,0:T(8,128)(2,1)S(1)}, u32[]{:S(2)}, u32[]{:S(2)}) collective-permute-start(bf16[256,1024]{1,0:T(8,128)(2,1)S(1)} %slice_bitcast_fusion.refs_0_), channel_id=1, source_target_pairs={{0,1},{1,2},{2,3},{3,0},{4,5},{5,6},{6,7},{7,4},{8,9},{9,10},{10,1... | collective-permute-start | bytes 1572872 | tf_op jit(solution)/shard_map/ppermute | solution.py:432
  5.8 24.5 %copy-start = (bf16[160,1024]{1,0:T(8,128)(2,1)S(1)}, bf16[160,1024]{1,0:T(8,128)(2,1)}, u32[]{:S(2)}) copy-start(bf16[160,1024]{1,0:T(8,128)(2,1)} %slice_bitcast_fusion.1.refs_8_.refs_0_) | copy-start | bytes 983044
  13.7 44.2 %copy-start.1 = (bf16[96,1024]{1,0:T(8,128)(2,1)S(1)}, bf16[96,1024]{1,0:T(8,128)(2,1)}, u32[]{:S(2)}) copy-start(bf16[96,1024]{1,0:T(8,128)(2,1)} %slice_bitcast_fusion.2.refs_9_.refs_0_) | copy-start | bytes 589828
  15.9 0.7 copy-start.3
  16.5 13.7 %collective-permute-start.1 = (bf16[256,1024]{1,0:T(8,128)(2,1)S(1)}, bf16[256,1024]{1,0:T(8,128)(2,1)S(1)}, u32[]{:S(2)}, u32[]{:S(2)}) collective-permute-start(bf16[256,1024]{1,0:T(8,128)(2,1)S(1)} %shard_map.74.refs_1_), channel_id=1, source_target_pairs={{0,1},{1,2},{2,3},{3,0},{4,5},{5,6},{6,7},{7,4},{8,9},{9,10},{10,1... | collective-permute-start | bytes 1572872 | tf_op jit(solution)/shard_map/ppermute | solution.py:432
  30.3 19.8 %collective-permute-start.5 = (bf16[256,1024]{1,0:T(8,128)(2,1)S(1)}, bf16[256,1024]{1,0:T(8,128)(2,1)S(1)}, u32[]{:S(2)}, u32[]{:S(2)}) collective-permute-start(bf16[256,1024]{1,0:T(8,128)(2,1)S(1)} %collective-permute-done.1.refs_1_.refs_2_), channel_id=1, source_target_pairs={{0,1},{1,2},{2,3},{3,0},{4,5},{5,6},{6,7},{7,4},{8,9},{9,10},{10,1... | collective-permute-start | bytes 1572872 | tf_op jit(solution)/shard_map/ppermute | solution.py:432
  30.3 19.8 %collective-permute-start.2 = (bf16[160,1024]{1,0:T(8,128)(2,1)S(1)}, bf16[160,1024]{1,0:T(8,128)(2,1)S(1)}, u32[]{:S(2)}, u32[]{:S(2)}) collective-permute-start(bf16[160,1024]{1,0:T(8,128)(2,1)S(1)} %shard_map.75.refs_0_), channel_id=1, source_target_pairs={{0,1},{1,2},{2,3},{3,0},{4,5},{5,6},{6,7},{7,4},{8,9},{9,10},{10,1... | collective-permute-start | bytes 983048 | tf_op jit(solution)/shard_map/ppermute | solution.py:432
  50.1 7.7 %collective-permute-start.3 = (bf16[160,1024]{1,0:T(8,128)(2,1)S(1)}, bf16[160,1024]{1,0:T(8,128)(2,1)S(1)}, u32[]{:S(2)}, u32[]{:S(2)}) collective-permute-start(bf16[160,1024]{1,0:T(8,128)(2,1)S(1)} %collective-permute-done.2.refs_1_.refs_6_), channel_id=1, source_target_pairs={{0,1},{1,2},{2,3},{3,0},{4,5},{5,6},{6,7},{7,4},{8,9},{9,10},{10,1... | collective-permute-start | bytes 983048 | tf_op jit(solution)/shard_map/ppermute | solution.py:432
  50.1 0.7 copy-start.2
  53.7 29.7 %collective-permute-start.10 = (bf16[256,1024]{1,0:T(8,128)(2,1)S(1)}, bf16[256,1024]{1,0:T(8,128)(2,1)S(1)}, u32[]{:S(2)}, u32[]{:S(2)}) collective-permute-start(bf16[256,1024]{1,0:T(8,128)(2,1)S(1)} %shard_map.82.refs_0_.refs_1_), channel_id=1, source_target_pairs={{0,8},{4,12},{8,16},{12,20},{16,24},{20,28},{1,9},{5,13},{9,17},{1... | collective-permute-start | bytes 1572872 | tf_op jit(solution)/shard_map/ppermute | solution.py:395
  57.8 10.7 %collective-permute-start.4 = (bf16[160,1024]{1,0:T(8,128)(2,1)S(1)}, bf16[160,1024]{1,0:T(8,128)(2,1)S(1)}, u32[]{:S(2)}, u32[]{:S(2)}) collective-permute-start(bf16[160,1024]{1,0:T(8,128)(2,1)S(1)} %collective-permute-done.3.refs_2_), channel_id=1, source_target_pairs={{0,1},{1,2},{2,3},{3,0},{4,5},{5,6},{6,7},{7,4},{8,9},{9,10},{10,1... | collective-permute-start | bytes 983048 | tf_op jit(solution)/shard_map/ppermute | solution.py:432
  57.9 10.7 %collective-permute-start.6 = (bf16[96,1024]{1,0:T(8,128)(2,1)S(1)}, bf16[96,1024]{1,0:T(8,128)(2,1)S(1)}, u32[]{:S(2)}, u32[]{:S(2)}) collective-permute-start(bf16[96,1024]{1,0:T(8,128)(2,1)S(1)} %shard_map.77.refs_0_), channel_id=1, source_target_pairs={{0,1},{1,2},{2,3},{3,0},{4,5},{5,6},{6,7},{7,4},{8,9},{9,10},{10,1... | collective-permute-start | bytes 589832 | tf_op jit(solution)/shard_map/ppermute | solution.py:432
  57.9 36.5 %collective-permute-start.9 = (bf16[256,1024]{1,0:T(8,128)(2,1)S(1)}, bf16[256,1024]{1,0:T(8,128)(2,1)S(1)}, u32[]{:S(2)}, u32[]{:S(2)}) collective-permute-start(bf16[256,1024]{1,0:T(8,128)(2,1)S(1)} %shard_map.82.refs_0_.refs_1_), channel_id=1, source_target_pairs={{0,4},{4,0},{8,12},{12,8},{16,20},{20,16},{24,28},{28,24},{1,5},{5... | collective-permute-start | bytes 1572872 | tf_op jit(solution)/shard_map/ppermute | solution.py:400
  68.6 14.9 %collective-permute-start.7 = (bf16[96,1024]{1,0:T(8,128)(2,1)S(1)}, bf16[96,1024]{1,0:T(8,128)(2,1)S(1)}, u32[]{:S(2)}, u32[]{:S(2)}) collective-permute-start(bf16[96,1024]{1,0:T(8,128)(2,1)S(1)} %shard_map.78.refs_1_), channel_id=1, source_target_pairs={{0,1},{1,2},{2,3},{3,0},{4,5},{5,6},{6,7},{7,4},{8,9},{9,10},{10,1... | collective-permute-start | bytes 589832 | tf_op jit(solution)/shard_map/ppermute | solution.py:432
  72.1 17.6 %collective-permute-start.12 = (bf16[160,1024]{1,0:T(8,128)(2,1)S(1)}, bf16[160,1024]{1,0:T(8,128)(2,1)S(1)}, u32[]{:S(2)}, u32[]{:S(2)}) collective-permute-start(bf16[160,1024]{1,0:T(8,128)(2,1)S(1)} %shard_map.76.refs_0_), channel_id=1, source_target_pairs={{8,0},{12,4},{16,8},{20,12},{24,16},{28,20},{9,1},{13,5},{17,9},{2... | collective-permute-start | bytes 983048 | tf_op jit(solution)/shard_map/ppermute | solution.py:395
  75.3 26.5 %collective-permute-start.11 = (bf16[256,1024]{1,0:T(8,128)(2,1)S(1)}, bf16[256,1024]{1,0:T(8,128)(2,1)S(1)}, u32[]{:S(2)}, u32[]{:S(2)}) collective-permute-start(bf16[256,1024]{1,0:T(8,128)(2,1)S(1)} %shard_map.82.refs_0_.refs_1_), channel_id=1, source_target_pairs={{4,16},{12,24},{28,20},{5,17},{13,25},{29,21},{6,18},{14,26},{30,2... | collective-permute-start | bytes 1572872 | tf_op jit(solution)/shard_map/ppermute | solution.py:407
  83.5 22.6 %collective-permute-start.18 = (bf16[256,1024]{1,0:T(8,128)(2,1)S(1)}, bf16[256,1024]{1,0:T(8,128)(2,1)S(1)}, u32[]{:S(2)}, u32[]{:S(2)}) collective-permute-start(bf16[256,1024]{1,0:T(8,128)(2,1)S(1)} %collective-permute-done.10.refs_1_.refs_3_), channel_id=1, source_target_pairs={{0,4},{4,0},{8,12},{12,8},{16,20},{20,16},{24,28},{28,24},{1,5},{5... | collective-permute-start | bytes 1572872 | tf_op jit(solution)/shard_map/ppermute | solution.py:400
  83.5 8.8 %collective-permute-start.8 = (bf16[96,1024]{1,0:T(8,128)(2,1)S(1)}, bf16[96,1024]{1,0:T(8,128)(2,1)S(1)}, u32[]{:S(2)}, u32[]{:S(2)}) collective-permute-start(bf16[96,1024]{1,0:T(8,128)(2,1)S(1)} %collective-permute-done.7.refs_2_), channel_id=1, source_target_pairs={{0,1},{1,2},{2,3},{3,0},{4,5},{5,6},{6,7},{7,4},{8,9},{9,10},{10,1... | collective-permute-start | bytes 589832 | tf_op jit(solution)/shard_map/ppermute | solution.py:432
  89.7 21.1 %collective-permute-start.16 = (bf16[160,1024]{1,0:T(8,128)(2,1)S(1)}, bf16[160,1024]{1,0:T(8,128)(2,1)S(1)}, u32[]{:S(2)}, u32[]{:S(2)}) collective-permute-start(bf16[160,1024]{1,0:T(8,128)(2,1)S(1)} %shard_map.76.refs_0_), channel_id=1, source_target_pairs={{4,0},{12,8},{20,16},{28,24},{16,4},{24,12},{5,1},{13,9},{21,17},{... | collective-permute-start | bytes 983048 | tf_op jit(solution)/shard_map/ppermute | solution.py:416
  92.3 21.7 %collective-permute-start.14 = (bf16[160,1024]{1,0:T(8,128)(2,1)S(1)}, bf16[160,1024]{1,0:T(8,128)(2,1)S(1)}, u32[]{:S(2)}, u32[]{:S(2)}) collective-permute-start(bf16[160,1024]{1,0:T(8,128)(2,1)S(1)} %collective-permute-done.12.refs_5_), channel_id=1, source_target_pairs={{0,4},{4,0},{8,12},{12,8},{16,20},{20,16},{24,28},{28,24},{1,5},{5... | collective-permute-start | bytes 983048 | tf_op jit(solution)/shard_map/ppermute | solution.py:400
  94.4 11.1 %collective-permute-start.13 = (bf16[96,1024]{1,0:T(8,128)(2,1)S(1)}, bf16[96,1024]{1,0:T(8,128)(2,1)S(1)}, u32[]{:S(2)}, u32[]{:S(2)}) collective-permute-start(bf16[96,1024]{1,0:T(8,128)(2,1)S(1)} %shard_map.80.refs_1_), channel_id=1, source_target_pairs={{8,0},{12,4},{16,8},{20,12},{24,16},{28,20},{9,1},{13,5},{17,9},{2... | collective-permute-start | bytes 589832 | tf_op jit(solution)/shard_map/ppermute | solution.py:395
  101.8 12.3 %collective-permute-start.17 = (bf16[96,1024]{1,0:T(8,128)(2,1)S(1)}, bf16[96,1024]{1,0:T(8,128)(2,1)S(1)}, u32[]{:S(2)}, u32[]{:S(2)}) collective-permute-start(bf16[96,1024]{1,0:T(8,128)(2,1)S(1)} %shard_map.80.refs_1_), channel_id=1, source_target_pairs={{4,0},{12,8},{20,16},{28,24},{16,4},{24,12},{5,1},{13,9},{21,17},{... | collective-permute-start | bytes 589832 | tf_op jit(solution)/shard_map/ppermute | solution.py:416
  105.4 8.6 %collective-permute-start.15 = (bf16[96,1024]{1,0:T(8,128)(2,1)S(1)}, bf16[96,1024]{1,0:T(8,128)(2,1)S(1)}, u32[]{:S(2)}, u32[]{:S(2)}) collective-permute-start(bf16[96,1024]{1,0:T(8,128)(2,1)S(1)} %collective-permute-done.13.refs_6_), channel_id=1, source_target_pairs={{0,4},{4,0},{8,12},{12,8},{16,20},{20,16},{24,28},{28,24},{1,5},{5... | collective-permute-start | bytes 589832 | tf_op jit(solution)/shard_map/ppermute | solution.py:400

commit v8 on v7

--- a/solution.py
+++ b/solution.py
@@ -18,7 +18,6 @@
 WHOLE = pl.BlockSpec(memory_space=pltpu.VMEM)
 ANYWHERE = pl.BlockSpec(memory_space=pl.ANY)
 OUTSIDE = pl.BlockSpec(memory_space=pltpu.HBM)
-TOKEN = pl.BlockSpec((8, 128), lambda *at: (0, 0))
 SCALARS = pl.BlockSpec(memory_space=pltpu.SMEM)
 
 
@@ -147,8 +146,8 @@
             pltpu.VMEM(gate.shape, BF16),
             pltpu.VMEM((2 * length, length), BF16),
             pltpu.VMEM(back.shape, BF16),
-            jax.ShapeDtypeStruct((2, 8), jnp.int32),
-            jax.ShapeDtypeStruct((8, 128), F32),
+            pltpu.SMEM((2, 8), jnp.int32),
+            pltpu.VMEM((8, 128), F32),
         ),
         in_specs=[
             SCALARS,
@@ -161,7 +160,7 @@
             OUTSIDE,
         ]
         + [ANYWHERE] * len(after),
-        out_specs=(WHOLE,) * 5 + (SCALARS, TOKEN),
+        out_specs=(WHOLE,) * 5 + (SCALARS, WHOLE),
         scratch_shapes=[pltpu.SemaphoreType.DMA((3,))],
         compiler_params=params(2 * VMEM),
         cost_estimate=pl.CostEstimate(
@@ -333,12 +332,13 @@
         out_ref[0, 0] = near_ref[:, conv.lanes]
 
 
-def conv_call(body, tabs, facts, arrays, out_shape, out_spec, scratch, terms, result=None):
+def conv_call(body, tabs, facts, arrays, out_shape, out_spec, scratch, after=(), result=None):
     table, back, spectra = tabs
     length = table.shape[0] // 2
     width = spectra.shape[2]
     operands = [facts, table, back, spectra, *arrays]
-    specs = [SCALARS] + [WHOLE] * (len(operands) - 1)
+    specs = [SCALARS] + [WHOLE] * (len(operands) - 1) + [ANYWHERE] * len(after)
+    operands.extend(after)
     aliases = {}
     if result is not None:
         aliases = {len(operands): 0}
@@ -354,18 +354,18 @@
         input_output_aliases=aliases,
         compiler_params=params(),
         cost_estimate=pl.CostEstimate(
-            flops=4 * terms * length * length * width,
+            flops=32 * length * length * width,
             bytes_accessed=4 * length * width,
             transcendentals=0,
         ),
     )(*operands)
 
 
-def own_terms(slot, tabs, facts, pieces):
+def own_terms(slot, tabs, facts, pieces, after=()):
     _, back, spectra = tabs
     shape = pltpu.VMEM((back.shape[0], spectra.shape[2]), F32)
     body = functools.partial(own_kernel, slot, len(pieces))
-    return conv_call(body, tabs, facts, pieces, shape, WHOLE, [], 8)
+    return conv_call(body, tabs, facts, pieces, shape, WHOLE, [], after)
 
 
 def far_terms(slot, count, tabs, facts, arrays, result=None):
@@ -375,7 +375,7 @@
     spec = pl.BlockSpec((1, 1, length, LANES), lambda c: (0, slot, 0, c))
     scratch = [pltpu.VMEM((2 * length, LANES), F32), pltpu.VMEM((length, LANES), BF16)]
     body = functools.partial(far_kernel, slot, count)
-    return conv_call(body, tabs, facts, arrays, shape, spec, scratch, 8, result)
+    return conv_call(body, tabs, facts, arrays, shape, spec, scratch, (), result)
 
 
 def ordered(value, *earlier):
@@ -461,17 +461,21 @@
     for step in range(2, count):
         second_in.append(turned(second_in[-1]))
 
-    upper = project(facts, upper_in, everything, weight, gates, 1, 0, after=[first_in[1]])
+    def projected(shards, slot, start, early=(), late=()):
+        args = (weight, gates, slot, start)
+        partial = project(facts, shards[:-1], everything[:-1], *args, last=False, after=early)
+        return project(facts, shards[-1:], everything[-1:], *args, partial, after=late)
+
+    upper = projected(upper_in, 1, 0, early=[first_in[0]], late=[first_in[1]])
     upper_halo = upper_halo_of(upper)
     near = own_terms(1, tabs, facts, [upper])
     result = far_terms(1, 1, tabs, facts, [near, *upper_halo])
 
-    first = project(facts, first_in, everything, weight, gates, 0, 0)
+    first = projected(first_in, 0, 0, late=[upper_halo[1], upper_halo[3]])
     first_halo = lower_halo_of(first)
-    partial = project(facts, second_in[:-1], everything[:-1], weight, gates, 0, cut, last=False)
-    second = project(facts, second_in[-1:], everything[-1:], weight, gates, 0, cut, partial)
+    second = projected(second_in, 0, cut)
     second_halo = lower_halo_of(second)
-    near = own_terms(0, tabs, facts, [first, second])
+    near = own_terms(0, tabs, facts, [first, second], after=second_halo[:1])
     two, _, mate, fold = upper_halo
     halos = [piece for both in zip(first_halo, second_halo) for piece in both]
     return far_terms(0, 2, tabs, facts, [near, upper, mate, two, fold, *halos], result)

time: 121 us -> 123 us (1.017)
  the two profiles are of different devices: /device:TPU:3 before, /device:TPU:4 now
where the time goes in v8:
time: 123 us; the launch traced here: 122 us
  waiting for transfers between devices  67.9 us (55%)
  Pallas kernels  33.3 us (27%)
  starting transfers between devices  16.3 us (13%)
  local copies, waits for them, and re-layouts  4.4 us (4%)
    ppermute x9, waiting for transfers between devices, turned(): return lax.ppermute(piece, 'ch', around)  58.2 us
    pallas_call x4, Pallas kernels, conv_call(): pl.pallas_call(body, grid=(width // LANES,), out_shape=out_shape, in_spec...  17.6 us
    ppermute x3, waiting for transfers between devices, shifted(): lax.ppermute(value, 'ctx', [(source, source + steps) for source in range(...  9.65 us
    pallas_call x6, Pallas kernels, project(): pl.pallas_call(body, out_shape=pltpu.VMEM((rows, width), BF16 if last els...  8.42 us
    ppermute x3, starting transfers between devices, shifted(): lax.ppermute(value, 'ctx', [(source, source + steps) for source in range(...  7.66 us
    pallas_call x1, Pallas kernels, prepare(): pl.pallas_call(functools.partial(prepare_kernel, pairs), grid=(width // L...  7.28 us
    ppermute x2, starting transfers between devices, lower_halo_of(): mixed = lax.ppermute(value, 'ctx', mixed)  3.84 us
    squeeze x2, local copies, waits for them, and re-layouts, on_device(): slices = [grad_out[0, 0, :cut], grad_out[0, 0, cut:]]  3.32 us
  transfers between devices with their start and end apart: 19, of which 8 were waited for; matrix products, arithmetic and copies ran while one was open for 3% of the time, Pallas kernels for 24%

profile of v8, /device:TPU:4, one launch (start us, length us, event | category | flops | bytes accessed | tf_op | source)
XLA Modules:
  0.0 122.1 jit_solution(18399678718130835583)
XLA Ops:
  0.0 1.1 slice_bitcast_fusion.refs_0_
  1.1 1.6 %collective-permute-start = (bf16[256,1024]{1,0:T(8,128)(2,1)S(1)}, bf16[256,1024]{1,0:T(8,128)(2,1)S(1)}, u32[]{:S(2)}, u32[]{:S(2)}) collective-permute-start(bf16[256,1024]{1,0:T(8,128)(2,1)S(1)} %slice_bitcast_fusion.refs_0_), channel_id=1, source_target_pairs={{0,1},{1,2},{2,3},{3,0},{4,5},{5,6},{6,7},{7,4},{8,9},{9,10},{10,1... | collective-permute-start | bytes 1572872 | tf_op jit(solution)/shard_map/ppermute | solution.py:432
  2.7 1.6 %slice_bitcast_fusion.2.refs_9_.refs_0_ = bf16[96,1024]{1,0:T(8,128)(2,1)} fusion(bf16[1,2,256,1024]{3,2,1,0:T(8,128)(2,1)} %param.7), kind=kLoop, calls=%fused_computation.2 | loop fusion | bytes 393216 | tf_op jit(solution)/shard_map/squeeze | solution.py:434
  4.3 1.7 %slice_bitcast_fusion.1.refs_8_.refs_0_ = bf16[160,1024]{1,0:T(8,128)(2,1)} fusion(bf16[1,2,256,1024]{3,2,1,0:T(8,128)(2,1)} %param.7), kind=kLoop, calls=%fused_computation.1 | loop fusion | bytes 655360 | tf_op jit(solution)/shard_map/squeeze | solution.py:434
  6.0 7.3 %shard_map.73 = (f32[4,512,1024]{2,1,0:T(8,128)S(1)}, bf16[1024,4096]{1,0:T(8,128)(2,1)S(1)}, bf16[1,2,256,1024]{3,2,1,0:T(8,128)(2,1)S(1)}, bf16[512,256]{1,0:T...) custom-call(s32[1]{0:T(128)} %bitcast.refs_0_, s32[1]{0:T(128)} %bitcast.1.refs_1_, ...), custom_call_target="tpu_custom_call" | custom-call | flops 2415919104 | bytes 11534336 | tf_op jit(solution)/shard_map/pallas_call | solution.py:140
  13.3 3.3 %collective-permute-done.refs_0_ = bf16[256,1024]{1,0:T(8,128)(2,1)S(1)} collective-permute-done((bf16[256,1024]{1,0:T(8,128)(2,1)S(1)}, bf16[256,1024]{1,0:T(8,128)(2,1)S(1)}, u32[]{:S(2)}, u32[]{:S(2)}) %collective-permute-start) | collective-permute-done | bytes 524320 | tf_op jit(solution)/shard_map/ppermute | solution.py:432
  16.7 14.7 %collective-permute-done.1.refs_1_.refs_2_ = bf16[256,1024]{1,0:T(8,128)(2,1)S(1)} collective-permute-done((bf16[256,1024]{1,0:T(8,128)(2,1)S(1)}, bf16[256,1024]{1,0:T(8,128)(2,1)S(1)}, u32[]{:S(2)}, u32[]{:S(2)}) %collective-permute-start.1) | collective-permute-done | bytes 524320 | tf_op jit(solution)/shard_map/ppermute | solution.py:432
  31.3 1.8 %shard_map.77.refs_3_ = f32[256,1024]{1,0:T(8,128)S(1)} custom-call(s32[2,8]{1,0:T(2,128)S(4)} %get-tuple-element.12.facts_ref, bf16[256,1024]{1,0:T(8,128)(2,1)S(1)} %slice_bitcast_fusion.refs_0_, bf16[256,1024]{1,0:T(8,128)(2,1)S(1)} %shard_map.74.refs_1_, bf16[256,1024]{1,0:T(8,128)(2,1)S(1)} %collective-permute-done.1.refs_1_.refs_2_, ...), custom_call_target="tpu_custom_call" | custom-call | flops 1610612736 | bytes 7864320 | tf_op jit(solution)/shard_map/pallas_call | solution.py:202
  33.2 18.9 %collective-permute-done.2.refs_1_.refs_4_ = bf16[160,1024]{1,0:T(8,128)(2,1)S(1)} collective-permute-done((bf16[160,1024]{1,0:T(8,128)(2,1)S(1)}, bf16[160,1024]{1,0:T(8,128)(2,1)S(1)}, u32[]{:S(2)}, u32[]{:S(2)}) %collective-permute-start.2) | collective-permute-done | bytes 327712 | tf_op jit(solution)/shard_map/ppermute | solution.py:432
  52.1 0.7 shard_map.78.refs_0_.refs_1_
  52.8 3.4 %collective-permute-start.6 = (bf16[256,1024]{1,0:T(8,128)(2,1)S(1)}, bf16[256,1024]{1,0:T(8,128)(2,1)S(1)}, u32[]{:S(2)}, u32[]{:S(2)}) collective-permute-start(bf16[256,1024]{1,0:T(8,128)(2,1)S(1)} %shard_map.78.refs_0_.refs_1_), channel_id=1, source_target_pairs={{0,8},{4,12},{8,16},{12,20},{16,24},{20,28},{1,9},{5,13},{9,17},{1... | collective-permute-start | bytes 1572872 | tf_op jit(solution)/shard_map/ppermute | solution.py:395
  56.3 1.3 %collective-permute-start.8 = (bf16[256,1024]{1,0:T(8,128)(2,1)S(1)}, bf16[256,1024]{1,0:T(8,128)(2,1)S(1)}, u32[]{:S(2)}, u32[]{:S(2)}) collective-permute-start(bf16[256,1024]{1,0:T(8,128)(2,1)S(1)} %shard_map.78.refs_0_.refs_1_), channel_id=1, source_target_pairs={{4,16},{12,24},{28,20},{5,17},{13,25},{29,21},{6,18},{14,26},{30,2... | collective-permute-start | bytes 1572872 | tf_op jit(solution)/shard_map/ppermute | solution.py:407
  57.6 9.1 %collective-permute-done.6.refs_1_.refs_3_ = bf16[256,1024]{1,0:T(8,128)(2,1)S(1)} collective-permute-done((bf16[256,1024]{1,0:T(8,128)(2,1)S(1)}, bf16[256,1024]{1,0:T(8,128)(2,1)S(1)}, u32[]{:S(2)}, u32[]{:S(2)}) %collective-permute-start.6) | collective-permute-done | bytes 524320 | tf_op jit(solution)/shard_map/ppermute | solution.py:395
  66.9 0.6 collective-permute-start.13
  67.4 15.5 %collective-permute-done.9.refs_0_ = bf16[96,1024]{1,0:T(8,128)(2,1)S(1)} collective-permute-done((bf16[96,1024]{1,0:T(8,128)(2,1)S(1)}, bf16[96,1024]{1,0:T(8,128)(2,1)S(1)}, u32[]{:S(2)}, u32[]{:S(2)}) %collective-permute-start.9) | collective-permute-done | bytes 196640 | tf_op jit(solution)/shard_map/ppermute | solution.py:432
  82.9 2.2 %shard_map.76.refs_3_ = f32[160,1024]{1,0:T(8,128)S(1)} custom-call(s32[2,8]{1,0:T(2,128)S(4)} %get-tuple-element.12.facts_ref, bf16[160,1024]{1,0:T(8,128)(2,1)S(1)} %shard_map.75.refs_0_.refs_5_, bf16[160,1024]{1,0:T(8,128)(2,1)S(1)} %collective-permute-done.2.refs_1_.refs_4_, bf16[160,1024]{1,0:T(8,128)(2,1)S(1)} %collective-permute-done.3.refs_2_, ...), custom_call_target="tpu_custom_call" | custom-call | flops 1006632960 | bytes 7274496 | tf_op jit(solution)/shard_map/pallas_call | solution.py:202
  85.2 0.8 shard_map.79.refs_0_
  86.0 2.3 %collective-permute-start.14 = (bf16[160,1024]{1,0:T(8,128)(2,1)S(1)}, bf16[160,1024]{1,0:T(8,128)(2,1)S(1)}, u32[]{:S(2)}, u32[]{:S(2)}) collective-permute-start(bf16[160,1024]{1,0:T(8,128)(2,1)S(1)} %shard_map.79.refs_0_), channel_id=1, source_target_pairs={{8,0},{12,4},{16,8},{20,12},{24,16},{28,20},{9,1},{13,5},{17,9},{2... | collective-permute-start | bytes 983048 | tf_op jit(solution)/shard_map/ppermute | solution.py:395
  88.3 2.9 %collective-permute-done.10.refs_2_ = bf16[96,1024]{1,0:T(8,128)(2,1)S(1)} collective-permute-done((bf16[96,1024]{1,0:T(8,128)(2,1)S(1)}, bf16[96,1024]{1,0:T(8,128)(2,1)S(1)}, u32[]{:S(2)}, u32[]{:S(2)}) %collective-permute-start.10) | collective-permute-done | bytes 196640 | tf_op jit(solution)/shard_map/ppermute | solution.py:432
  91.3 2.5 %shard_map.85.refs_0_ = f32[256,1024]{1,0:T(8,128)S(1)} custom-call(s32[2,8]{1,0:T(2,128)S(4)} %get-tuple-element.12.facts_ref, bf16[512,256]{1,0:T(8,128)(2,1)S(1)} %get-tuple-element.13.table_ref, bf16[256,1024]{1,0:T(8,128)(2,1)S(1)} %get-tuple-element.14.back_ref, f32[4,512,1024]{2,1,0:T(8,128)S(1)} %get-tuple-element.15.spec_ref, ...), custom_call_target="tpu_custom_call" | custom-call | flops 2147483648 | bytes 1048576 | tf_op jit(solution)/shard_map/pallas_call | solution.py:347
  93.8 2.0 %shard_map.82.refs_3_ = f32[96,1024]{1,0:T(8,128)S(1)} custom-call(s32[2,8]{1,0:T(2,128)S(4)} %get-tuple-element.12.facts_ref, bf16[96,1024]{1,0:T(8,128)(2,1)S(1)} %shard_map.80.refs_0_, bf16[96,1024]{1,0:T(8,128)(2,1)S(1)} %shard_map.81.refs_1_, bf16[96,1024]{1,0:T(8,128)(2,1)S(1)} %collective-permute-done.10.refs_2_, ...), custom_call_target="tpu_custom_call" | custom-call | flops 603979776 | bytes 6881280 | tf_op jit(solution)/shard_map/pallas_call | solution.py:202
  95.8 2.9 %collective-permute-done.11.refs_0_ = bf16[96,1024]{1,0:T(8,128)(2,1)S(1)} collective-permute-done((bf16[96,1024]{1,0:T(8,128)(2,1)S(1)}, bf16[96,1024]{1,0:T(8,128)(2,1)S(1)}, u32[]{:S(2)}, u32[]{:S(2)}) %collective-permute-start.11) | collective-permute-done | bytes 196640 | tf_op jit(solution)/shard_map/ppermute | solution.py:432
  98.7 0.8 shard_map.83.refs_1_
  99.5 1.9 %collective-permute-start.18 = (bf16[96,1024]{1,0:T(8,128)(2,1)S(1)}, bf16[96,1024]{1,0:T(8,128)(2,1)S(1)}, u32[]{:S(2)}, u32[]{:S(2)}) collective-permute-start(bf16[96,1024]{1,0:T(8,128)(2,1)S(1)} %shard_map.83.refs_1_), channel_id=1, source_target_pairs={{4,0},{12,8},{20,16},{28,24},{16,4},{24,12},{5,1},{13,9},{21,17},{... | collective-permute-start | bytes 589832 | tf_op jit(solution)/shard_map/ppermute | solution.py:416
  101.4 1.9 %collective-permute-start.12 = (bf16[96,1024]{1,0:T(8,128)(2,1)S(1)}, bf16[96,1024]{1,0:T(8,128)(2,1)S(1)}, u32[]{:S(2)}, u32[]{:S(2)}) collective-permute-start(bf16[96,1024]{1,0:T(8,128)(2,1)S(1)} %shard_map.83.refs_1_), channel_id=1, source_target_pairs={{8,0},{12,4},{16,8},{20,12},{24,16},{28,20},{9,1},{13,5},{17,9},{2... | collective-permute-start | bytes 589832 | tf_op jit(solution)/shard_map/ppermute | solution.py:395
  103.4 1.9 %collective-permute-start.17 = (bf16[160,1024]{1,0:T(8,128)(2,1)S(1)}, bf16[160,1024]{1,0:T(8,128)(2,1)S(1)}, u32[]{:S(2)}, u32[]{:S(2)}) collective-permute-start(bf16[160,1024]{1,0:T(8,128)(2,1)S(1)} %shard_map.79.refs_0_), channel_id=1, source_target_pairs={{4,0},{12,8},{20,16},{28,24},{16,4},{24,12},{5,1},{13,9},{21,17},{... | collective-permute-start | bytes 983048 | tf_op jit(solution)/shard_map/ppermute | solution.py:416
  105.3 0.6 collective-permute-start.15
  105.9 4.2 %shard_map.86.refs_11_ = f32[1,2,256,1024]{3,2,1,0:T(8,128)} custom-call(s32[2,8]{1,0:T(2,128)S(4)} %get-tuple-element.12.facts_ref, bf16[512,256]{1,0:T(8,128)(2,1)S(1)} %get-tuple-element.13.table_ref, bf16[256,1024]{1,0:T(8,128)(2,1)S(1)} %get-tuple-element.14.back_ref, f32[4,512,1024]{2,1,0:T(8,128)S(1)} %get-tuple-element.15.spec_ref, ...), custom_call_target="tpu_custom_call" | custom-call | flops 2147483648 | bytes 1048576 | tf_op jit(solution)/shard_map/pallas_call | solution.py:347
  110.1 0.5 collective-permute-done.12.refs_2_.refs_6_
  110.6 0.6 collective-permute-start.16
  111.2 7.5 %shard_map.84.refs_0_ = f32[256,1024]{1,0:T(8,128)S(1)} custom-call(s32[2,8]{1,0:T(2,128)S(4)} %get-tuple-element.12.facts_ref, bf16[512,256]{1,0:T(8,128)(2,1)S(1)} %get-tuple-element.13.table_ref, bf16[256,1024]{1,0:T(8,128)(2,1)S(1)} %get-tuple-element.14.back_ref, f32[4,512,1024]{2,1,0:T(8,128)S(1)} %get-tuple-element.15.spec_ref, ...), custom_call_target="tpu_custom_call" | custom-call | flops 2147483648 | bytes 1048576 | tf_op jit(solution)/shard_map/pallas_call | solution.py:347
  118.8 3.3 %shard_map.87 = f32[1,2,256,1024]{3,2,1,0:T(8,128)} custom-call(s32[2,8]{1,0:T(2,128)S(4)} %get-tuple-element.12.facts_ref, bf16[512,256]{1,0:T(8,128)(2,1)S(1)} %get-tuple-element.13.table_ref, bf16[256,1024]{1,0:T(8,128)(2,1)S(1)} %get-tuple-element.14.back_ref, f32[4,512,1024]{2,1,0:T(8,128)S(1)} %get-tuple-element.15.spec_ref, ...), custom_call_target="tpu_custom_call", output_to_operand_aliasing={{}: (15, {})} | custom-call | flops 2147483648 | bytes 1048576 | tf_op jit(solution)/shard_map/pallas_call | solution.py:347
  (28 shorter events, 0.2 us)
Async XLA Ops:
  1.1 15.6 %collective-permute-start = (bf16[256,1024]{1,0:T(8,128)(2,1)S(1)}, bf16[256,1024]{1,0:T(8,128)(2,1)S(1)}, u32[]{:S(2)}, u32[]{:S(2)}) collective-permute-start(bf16[256,1024]{1,0:T(8,128)(2,1)S(1)} %slice_bitcast_fusion.refs_0_), channel_id=1, source_target_pairs={{0,1},{1,2},{2,3},{3,0},{4,5},{5,6},{6,7},{7,4},{8,9},{9,10},{10,1... | collective-permute-start | bytes 1572872 | tf_op jit(solution)/shard_map/ppermute | solution.py:432
  6.0 25.3 %copy-start = (bf16[160,1024]{1,0:T(8,128)(2,1)S(1)}, bf16[160,1024]{1,0:T(8,128)(2,1)}, u32[]{:S(2)}) copy-start(bf16[160,1024]{1,0:T(8,128)(2,1)} %slice_bitcast_fusion.1.refs_8_.refs_0_) | copy-start | bytes 983044
  16.7 14.7 %collective-permute-start.1 = (bf16[256,1024]{1,0:T(8,128)(2,1)S(1)}, bf16[256,1024]{1,0:T(8,128)(2,1)S(1)}, u32[]{:S(2)}, u32[]{:S(2)}) collective-permute-start(bf16[256,1024]{1,0:T(8,128)(2,1)S(1)} %shard_map.74.refs_1_), channel_id=1, source_target_pairs={{0,1},{1,2},{2,3},{3,0},{4,5},{5,6},{6,7},{7,4},{8,9},{9,10},{10,1... | collective-permute-start | bytes 1572872 | tf_op jit(solution)/shard_map/ppermute | solution.py:432
  31.3 20.8 %collective-permute-start.5 = (bf16[256,1024]{1,0:T(8,128)(2,1)S(1)}, bf16[256,1024]{1,0:T(8,128)(2,1)S(1)}, u32[]{:S(2)}, u32[]{:S(2)}) collective-permute-start(bf16[256,1024]{1,0:T(8,128)(2,1)S(1)} %collective-permute-done.1.refs_1_.refs_2_), channel_id=1, source_target_pairs={{0,1},{1,2},{2,3},{3,0},{4,5},{5,6},{6,7},{7,4},{8,9},{9,10},{10,1... | collective-permute-start | bytes 1572872 | tf_op jit(solution)/shard_map/ppermute | solution.py:432
  31.3 20.8 %collective-permute-start.2 = (bf16[160,1024]{1,0:T(8,128)(2,1)S(1)}, bf16[160,1024]{1,0:T(8,128)(2,1)S(1)}, u32[]{:S(2)}, u32[]{:S(2)}) collective-permute-start(bf16[160,1024]{1,0:T(8,128)(2,1)S(1)} %shard_map.75.refs_0_.refs_5_), channel_id=1, source_target_pairs={{0,1},{1,2},{2,3},{3,0},{4,5},{5,6},{6,7},{7,4},{8,9},{9,10},{10,1... | collective-permute-start | bytes 983048 | tf_op jit(solution)/shard_map/ppermute | solution.py:432
  33.2 33.6 %copy-start.1 = (bf16[96,1024]{1,0:T(8,128)(2,1)S(1)}, bf16[96,1024]{1,0:T(8,128)(2,1)}, u32[]{:S(2)}) copy-start(bf16[96,1024]{1,0:T(8,128)(2,1)} %slice_bitcast_fusion.2.refs_9_.refs_0_) | copy-start | bytes 589828
  52.8 13.9 %collective-permute-start.6 = (bf16[256,1024]{1,0:T(8,128)(2,1)S(1)}, bf16[256,1024]{1,0:T(8,128)(2,1)S(1)}, u32[]{:S(2)}, u32[]{:S(2)}) collective-permute-start(bf16[256,1024]{1,0:T(8,128)(2,1)S(1)} %shard_map.78.refs_0_.refs_1_), channel_id=1, source_target_pairs={{0,8},{4,12},{8,16},{12,20},{16,24},{20,28},{1,9},{5,13},{9,17},{1... | collective-permute-start | bytes 1572872 | tf_op jit(solution)/shard_map/ppermute | solution.py:395
  56.2 10.5 %collective-permute-start.3 = (bf16[160,1024]{1,0:T(8,128)(2,1)S(1)}, bf16[160,1024]{1,0:T(8,128)(2,1)S(1)}, u32[]{:S(2)}, u32[]{:S(2)}) collective-permute-start(bf16[160,1024]{1,0:T(8,128)(2,1)S(1)} %collective-permute-done.2.refs_1_.refs_4_), channel_id=1, source_target_pairs={{0,1},{1,2},{2,3},{3,0},{4,5},{5,6},{6,7},{7,4},{8,9},{9,10},{10,1... | collective-permute-start | bytes 983048 | tf_op jit(solution)/shard_map/ppermute | solution.py:432
  56.3 28.8 %collective-permute-start.8 = (bf16[256,1024]{1,0:T(8,128)(2,1)S(1)}, bf16[256,1024]{1,0:T(8,128)(2,1)S(1)}, u32[]{:S(2)}, u32[]{:S(2)}) collective-permute-start(bf16[256,1024]{1,0:T(8,128)(2,1)S(1)} %shard_map.78.refs_0_.refs_1_), channel_id=1, source_target_pairs={{4,16},{12,24},{28,20},{5,17},{13,25},{29,21},{6,18},{14,26},{30,2... | collective-permute-start | bytes 1572872 | tf_op jit(solution)/shard_map/ppermute | solution.py:407
  66.8 18.4 %collective-permute-start.7 = (bf16[256,1024]{1,0:T(8,128)(2,1)S(1)}, bf16[256,1024]{1,0:T(8,128)(2,1)S(1)}, u32[]{:S(2)}, u32[]{:S(2)}) collective-permute-start(bf16[256,1024]{1,0:T(8,128)(2,1)S(1)} %collective-permute-done.6.refs_1_.refs_3_), channel_id=1, source_target_pairs={{0,4},{4,0},{8,12},{12,8},{16,20},{20,16},{24,28},{28,24},{1,5},{5... | collective-permute-start | bytes 1572872 | tf_op jit(solution)/shard_map/ppermute | solution.py:400
  66.8 16.2 %collective-permute-start.4 = (bf16[160,1024]{1,0:T(8,128)(2,1)S(1)}, bf16[160,1024]{1,0:T(8,128)(2,1)S(1)}, u32[]{:S(2)}, u32[]{:S(2)}) collective-permute-start(bf16[160,1024]{1,0:T(8,128)(2,1)S(1)} %collective-permute-done.3.refs_2_), channel_id=1, source_target_pairs={{0,1},{1,2},{2,3},{3,0},{4,5},{5,6},{6,7},{7,4},{8,9},{9,10},{10,1... | collective-permute-start | bytes 983048 | tf_op jit(solution)/shard_map/ppermute | solution.py:432
  66.8 16.1 %collective-permute-start.9 = (bf16[96,1024]{1,0:T(8,128)(2,1)S(1)}, bf16[96,1024]{1,0:T(8,128)(2,1)S(1)}, u32[]{:S(2)}, u32[]{:S(2)}) collective-permute-start(bf16[96,1024]{1,0:T(8,128)(2,1)S(1)} %shard_map.80.refs_0_), channel_id=1, source_target_pairs={{0,1},{1,2},{2,3},{3,0},{4,5},{5,6},{6,7},{7,4},{8,9},{9,10},{10,1... | collective-permute-start | bytes 589832 | tf_op jit(solution)/shard_map/ppermute | solution.py:432
  66.9 39.0 %collective-permute-start.13 = (bf16[256,1024]{1,0:T(8,128)(2,1)S(1)}, bf16[256,1024]{1,0:T(8,128)(2,1)S(1)}, u32[]{:S(2)}, u32[]{:S(2)}) collective-permute-start(bf16[256,1024]{1,0:T(8,128)(2,1)S(1)} %shard_map.78.refs_0_.refs_1_), channel_id=1, source_target_pairs={{0,4},{4,0},{8,12},{12,8},{16,20},{20,16},{24,28},{28,24},{1,5},{5... | collective-permute-start | bytes 1572872 | tf_op jit(solution)/shard_map/ppermute | solution.py:400
  82.9 8.3 %collective-permute-start.10 = (bf16[96,1024]{1,0:T(8,128)(2,1)S(1)}, bf16[96,1024]{1,0:T(8,128)(2,1)S(1)}, u32[]{:S(2)}, u32[]{:S(2)}) collective-permute-start(bf16[96,1024]{1,0:T(8,128)(2,1)S(1)} %shard_map.81.refs_1_), channel_id=1, source_target_pairs={{0,1},{1,2},{2,3},{3,0},{4,5},{5,6},{6,7},{7,4},{8,9},{9,10},{10,1... | collective-permute-start | bytes 589832 | tf_op jit(solution)/shard_map/ppermute | solution.py:432
  86.0 19.3 %collective-permute-start.14 = (bf16[160,1024]{1,0:T(8,128)(2,1)S(1)}, bf16[160,1024]{1,0:T(8,128)(2,1)S(1)}, u32[]{:S(2)}, u32[]{:S(2)}) collective-permute-start(bf16[160,1024]{1,0:T(8,128)(2,1)S(1)} %shard_map.79.refs_0_), channel_id=1, source_target_pairs={{8,0},{12,4},{16,8},{20,12},{24,16},{28,20},{9,1},{13,5},{17,9},{2... | collective-permute-start | bytes 983048 | tf_op jit(solution)/shard_map/ppermute | solution.py:395
  91.3 7.5 %collective-permute-start.11 = (bf16[96,1024]{1,0:T(8,128)(2,1)S(1)}, bf16[96,1024]{1,0:T(8,128)(2,1)S(1)}, u32[]{:S(2)}, u32[]{:S(2)}) collective-permute-start(bf16[96,1024]{1,0:T(8,128)(2,1)S(1)} %collective-permute-done.10.refs_2_), channel_id=1, source_target_pairs={{0,1},{1,2},{2,3},{3,0},{4,5},{5,6},{6,7},{7,4},{8,9},{9,10},{10,1... | collective-permute-start | bytes 589832 | tf_op jit(solution)/shard_map/ppermute | solution.py:432
  99.5 19.2 %collective-permute-start.18 = (bf16[96,1024]{1,0:T(8,128)(2,1)S(1)}, bf16[96,1024]{1,0:T(8,128)(2,1)S(1)}, u32[]{:S(2)}, u32[]{:S(2)}) collective-permute-start(bf16[96,1024]{1,0:T(8,128)(2,1)S(1)} %shard_map.83.refs_1_), channel_id=1, source_target_pairs={{4,0},{12,8},{20,16},{28,24},{16,4},{24,12},{5,1},{13,9},{21,17},{... | collective-permute-start | bytes 589832 | tf_op jit(solution)/shard_map/ppermute | solution.py:416
  101.4 9.2 %collective-permute-start.12 = (bf16[96,1024]{1,0:T(8,128)(2,1)S(1)}, bf16[96,1024]{1,0:T(8,128)(2,1)S(1)}, u32[]{:S(2)}, u32[]{:S(2)}) collective-permute-start(bf16[96,1024]{1,0:T(8,128)(2,1)S(1)} %shard_map.83.refs_1_), channel_id=1, source_target_pairs={{8,0},{12,4},{16,8},{20,12},{24,16},{28,20},{9,1},{13,5},{17,9},{2... | collective-permute-start | bytes 589832 | tf_op jit(solution)/shard_map/ppermute | solution.py:395
  103.4 15.4 %collective-permute-start.17 = (bf16[160,1024]{1,0:T(8,128)(2,1)S(1)}, bf16[160,1024]{1,0:T(8,128)(2,1)S(1)}, u32[]{:S(2)}, u32[]{:S(2)}) collective-permute-start(bf16[160,1024]{1,0:T(8,128)(2,1)S(1)} %shard_map.79.refs_0_), channel_id=1, source_target_pairs={{4,0},{12,8},{20,16},{28,24},{16,4},{24,12},{5,1},{13,9},{21,17},{... | collective-permute-start | bytes 983048 | tf_op jit(solution)/shard_map/ppermute | solution.py:416
  105.3 13.5 %collective-permute-start.15 = (bf16[160,1024]{1,0:T(8,128)(2,1)S(1)}, bf16[160,1024]{1,0:T(8,128)(2,1)S(1)}, u32[]{:S(2)}, u32[]{:S(2)}) collective-permute-start(bf16[160,1024]{1,0:T(8,128)(2,1)S(1)} %collective-permute-done.14.refs_5_), channel_id=1, source_target_pairs={{0,4},{4,0},{8,12},{12,8},{16,20},{20,16},{24,28},{28,24},{1,5},{5... | collective-permute-start | bytes 983048 | tf_op jit(solution)/shard_map/ppermute | solution.py:400
  110.6 8.1 %collective-permute-start.16 = (bf16[96,1024]{1,0:T(8,128)(2,1)S(1)}, bf16[96,1024]{1,0:T(8,128)(2,1)S(1)}, u32[]{:S(2)}, u32[]{:S(2)}) collective-permute-start(bf16[96,1024]{1,0:T(8,128)(2,1)S(1)} %collective-permute-done.12.refs_2_.refs_6_), channel_id=1, source_target_pairs={{0,4},{4,0},{8,12},{12,8},{16,20},{20,16},{24,28},{28,24},{1,5},{5... | collective-permute-start | bytes 589832 | tf_op jit(solution)/shard_map/ppermute | solution.py:400

commit v9 on v8

--- a/solution.py
+++ b/solution.py
@@ -78,13 +78,20 @@
 
 
 def prepare_kernel(pairs, *refs):
-    place_ref, lane_ref, docs_ref, table_ref, back_ref, taps_ref, weight_ref, gate_ref = refs[:8]
-    spec_out, weight_out, gate_out, table_out, back_out, facts_out, token_out, sems = refs[-8:]
+    place_ref, lane_ref, docs_ref, table_ref, back_ref, taps_ref = refs[:6]
+    weight_ref, gate_ref, grad_ref = refs[6:9]
+    spec_out, weight_out, gate_out, lower_out, table_out, back_out = refs[9:15]
+    facts_out, token_out, sems = refs[15:]
     token_out[...] = jnp.zeros_like(token_out)
     copies = [
         pltpu.make_async_copy(source, target, sems.at[at])
         for at, (source, target) in enumerate(
-            [(weight_ref, weight_out), (gate_ref, gate_out), (back_ref, back_out)]
+            [
+                (grad_ref.at[0, 0], lower_out),
+                (weight_ref, weight_out),
+                (gate_ref, gate_out),
+                (back_ref, back_out),
+            ]
         )
     ]
     step = pl.program_id(0)
@@ -134,7 +141,7 @@
             copy.wait()
 
 
-def prepare(pairs, place, lane, docs, table, back, taps, weight, gate, after):
+def prepare(pairs, place, lane, docs, table, back, taps, weight, gate, grad):
     count, width = taps.shape
     length = count // REACH
     return pl.pallas_call(
@@ -144,6 +151,7 @@
             pltpu.VMEM((REACH + 1, 2 * length, width), F32),
             pltpu.VMEM(weight.shape, BF16),
             pltpu.VMEM(gate.shape, BF16),
+            pltpu.VMEM(grad.shape[2:], BF16),
             pltpu.VMEM((2 * length, length), BF16),
             pltpu.VMEM(back.shape, BF16),
             pltpu.SMEM((2, 8), jnp.int32),
@@ -158,17 +166,17 @@
             pl.BlockSpec((count, LANES), lambda c: (0, c)),
             OUTSIDE,
             OUTSIDE,
-        ]
-        + [ANYWHERE] * len(after),
-        out_specs=(WHOLE,) * 5 + (SCALARS, WHOLE),
-        scratch_shapes=[pltpu.SemaphoreType.DMA((3,))],
+            OUTSIDE,
+        ],
+        out_specs=(WHOLE,) * 6 + (SCALARS, WHOLE),
+        scratch_shapes=[pltpu.SemaphoreType.DMA((4,))],
         compiler_params=params(2 * VMEM),
         cost_estimate=pl.CostEstimate(
             flops=2 * 3 * 2 * count * length * width,
             bytes_accessed=4 * (count * width + 8 * length * width),
             transcendentals=0,
         ),
-    )(place, lane, docs, table, back, taps, weight, gate, *after)
+    )(place, lane, docs, table, back, taps, weight, gate, grad)
 
 
 def project_kernel(steps, slot, start, first, last, facts_ref, *refs):
@@ -303,6 +311,9 @@
     else:
         halos = refs[: 4 * pieces]
     out_ref, acc_ref, chosen_ref = refs[-3:]
+    if slot == 1:
+        out_ref, token_ref = refs[-4:-2]
+        token_ref[...] = jnp.zeros_like(token_ref)
     conv = Conv(slot, facts_ref, table_ref, back_ref, spec_ref)
     role = conv.facts[6]
 
@@ -375,6 +386,8 @@
     spec = pl.BlockSpec((1, 1, length, LANES), lambda c: (0, slot, 0, c))
     scratch = [pltpu.VMEM((2 * length, LANES), F32), pltpu.VMEM((length, LANES), BF16)]
     body = functools.partial(far_kernel, slot, count)
+    if slot == 1:
+        shape, spec = (shape, pltpu.VMEM((8, 128), F32)), (spec, WHOLE)
     return conv_call(body, tabs, facts, arrays, shape, spec, scratch, (), result)
 
 
@@ -408,11 +421,11 @@
     return [two, core_swapped(two), mate, far]
 
 
-def lower_halo_of(value):
+def lower_halo_of(value, own):
     count = lax.axis_size("ctx")
     mixed = [(source, source - 1) for source in range(1, count, 2)]
     mixed += [(source, source - 3) for source in range(4, count, 2)]
-    two = shifted(value, -2)
+    two = ordered(shifted(value, -2), own)
     mixed = lax.ppermute(value, "ctx", mixed)
     return [two, core_swapped(two), mixed]
 
@@ -422,7 +435,6 @@
     place = lax.axis_index("ctx")
     length = grad_out.shape[2]
     width = out_weight.shape[0]
-    cut = length * 5 // 8
     count = lax.axis_size("ch")
     lane = lax.axis_index("ch").astype(jnp.int32)[None]
     around = [(source, (source + 1) % count) for source in range(count)]
@@ -431,12 +443,11 @@
     def turned(piece):
         return lax.ppermute(piece, "ch", around)
 
-    slices = [grad_out[0, 0, :cut], grad_out[0, 0, cut:]]
     upper_in = [grad_out[0, 1]]
     upper_in.append(turned(upper_in[0]))
 
     table, back = (jnp.asarray(one) for one in tables(length))
-    spectra, weight, gates, table, back, facts, prepared = prepare(
+    spectra, weight, gates, lower_slice, table, back, facts, prepared = prepare(
         pairs,
         place.astype(jnp.int32)[None],
         lane,
@@ -446,39 +457,41 @@
         filter_taps,
         out_weight,
         gate,
-        slices,
+        grad_out,
     )
     tabs = (table, back, spectra)
 
     upper_in[1] = ordered(upper_in[1], prepared)
     for step in range(2, count):
         upper_in.append(turned(upper_in[-1]))
-    first_in = [ordered(slices[0], upper_in[-2])]
-    for step in range(1, count):
-        first_in.append(turned(first_in[-1]))
-    second_in = [ordered(slices[1], upper_in[-1])]
-    second_in.append(ordered(turned(second_in[0]), first_in[-1]))
+    def partial_of(shards, slot):
+        return project(facts, shards, everything[:-1], weight, gates, slot, 0, last=False)
+
+    def final_of(shard, slot, partial, after=()):
+        last = everything[-1:]
+        return project(facts, [shard], last, weight, gates, slot, 0, partial, after=after)
+
+    partial = partial_of(upper_in[:-1], 1)
+    lower_in = [ordered(lower_slice, upper_in[-1], partial)]
+    upper = final_of(upper_in[-1], 1, partial)
+    upper_halo = upper_halo_of(upper)
+    two, swapped, mate, fold = upper_halo
+    lower_in.append(ordered(turned(lower_in[0]), upper, mate))
+    near = own_terms(1, tabs, facts, [upper])
     for step in range(2, count):
-        second_in.append(turned(second_in[-1]))
-
-    def projected(shards, slot, start, early=(), late=()):
-        args = (weight, gates, slot, start)
-        partial = project(facts, shards[:-1], everything[:-1], *args, last=False, after=early)
-        return project(facts, shards[-1:], everything[-1:], *args, partial, after=late)
-
-    upper = projected(upper_in, 1, 0, early=[first_in[0]], late=[first_in[1]])
-    upper_halo = upper_halo_of(upper)
-    near = own_terms(1, tabs, facts, [upper])
-    result = far_terms(1, 1, tabs, facts, [near, *upper_halo])
-
-    first = projected(first_in, 0, 0, late=[upper_halo[1], upper_halo[3]])
-    first_halo = lower_halo_of(first)
-    second = projected(second_in, 0, cut)
-    second_halo = lower_halo_of(second)
-    near = own_terms(0, tabs, facts, [first, second], after=second_halo[:1])
-    two, _, mate, fold = upper_halo
-    halos = [piece for both in zip(first_halo, second_halo) for piece in both]
-    return far_terms(0, 2, tabs, facts, [near, upper, mate, two, fold, *halos], result)
+        received = turned(lower_in[-1])
+        if step == count - 1:
+            lower_in.append(received)
+        else:
+            lower_in.append(ordered(received, near, two, fold))
+    result, convolved = far_terms(1, 1, tabs, facts, [near, *upper_halo])
+
+    partial = partial_of(lower_in[:-1], 0)
+    lower = final_of(lower_in[-1], 0, partial, [swapped, convolved])
+    near = own_terms(0, tabs, facts, [lower])
+    lower_halo = lower_halo_of(lower, near)
+    arrays = [near, upper, mate, two, fold, *lower_halo]
+    return far_terms(0, 1, tabs, facts, arrays, result)
 
 
 def solution(mesh):

time: 123 us -> 118 us (0.959)
  the two profiles are of different devices: /device:TPU:4 before, /device:TPU:3 now
where the time goes in v9:
time: 118 us
  waiting for transfers between devices  66.6 us (56%)
  Pallas kernels  28.8 us (24%)
  starting transfers between devices  21.3 us (18%)
    ppermute x6, waiting for transfers between devices, turned(): return lax.ppermute(piece, 'ch', around)  60.7 us
    pallas_call x4, Pallas kernels, conv_call(): pl.pallas_call(body, grid=(width // LANES,), out_shape=out_shape, in_spec...  16.3 us
    ppermute x3, starting transfers between devices, core_swapped(): lax.ppermute(value, 'ctx', [(source, source ^ 1) for source in range(coun...  7.93 us
    pallas_call x1, Pallas kernels, prepare(): pl.pallas_call(functools.partial(prepare_kernel, pairs), grid=(width // L...  7.41 us
    ppermute x2, starting transfers between devices, shifted(): lax.ppermute(value, 'ctx', [(source, source + steps) for source in range(...  5.78 us
    pallas_call x4, Pallas kernels, project(): pl.pallas_call(body, out_shape=pltpu.VMEM((rows, width), BF16 if last els...  5.15 us
    ppermute x1, starting transfers between devices, lower_halo_of(): mixed = lax.ppermute(value, 'ctx', mixed)  4.88 us
    ppermute x1, waiting for transfers between devices, lower_halo_of(): mixed = lax.ppermute(value, 'ctx', mixed)  4.82 us
  transfers between devices with their start and end apart: 13, of which 9 were waited for; matrix products, arithmetic and copies ran while one was open for 0% of the time, Pallas kernels for 19%

profile of v9, /device:TPU:3, one launch (start us, length us, event | category | flops | bytes accessed | tf_op | source)
XLA Modules:
  0.0 117.9 jit_solution(15024298188326998431)
XLA Ops:
  0.0 1.1 slice_bitcast_fusion.refs_0_
  1.1 1.3 %collective-permute-start = (bf16[256,1024]{1,0:T(8,128)(2,1)S(1)}, bf16[256,1024]{1,0:T(8,128)(2,1)S(1)}, u32[]{:S(2)}, u32[]{:S(2)}) collective-permute-start(bf16[256,1024]{1,0:T(8,128)(2,1)S(1)} %slice_bitcast_fusion.refs_0_), channel_id=1, source_target_pairs={{0,1},{1,2},{2,3},{3,0},{4,5},{5,6},{6,7},{7,4},{8,9},{9,10},{10,1... | collective-permute-start | bytes 1572872 | tf_op jit(solution)/shard_map/ppermute | solution.py:444
  2.4 7.4 %shard_map.73 = (f32[4,512,1024]{2,1,0:T(8,128)S(1)}, bf16[1024,4096]{1,0:T(8,128)(2,1)S(1)}, bf16[1,2,256,1024]{3,2,1,0:T(8,128)(2,1)S(1)}, bf16[256,1024]{1,0:...) custom-call(s32[1]{0:T(128)} %bitcast.refs_0_, ...), custom_call_target="tpu_custom_call" | custom-call | flops 2415919104 | bytes 11534336 | tf_op jit(solution)/shard_map/pallas_call | solution.py:147
  9.8 6.0 %collective-permute-done.refs_0_ = bf16[256,1024]{1,0:T(8,128)(2,1)S(1)} collective-permute-done((bf16[256,1024]{1,0:T(8,128)(2,1)S(1)}, bf16[256,1024]{1,0:T(8,128)(2,1)S(1)}, u32[]{:S(2)}, u32[]{:S(2)}) %collective-permute-start) | collective-permute-done | bytes 524320 | tf_op jit(solution)/shard_map/ppermute | solution.py:444
  15.9 13.7 %collective-permute-done.1.refs_2_ = bf16[256,1024]{1,0:T(8,128)(2,1)S(1)} collective-permute-done((bf16[256,1024]{1,0:T(8,128)(2,1)S(1)}, bf16[256,1024]{1,0:T(8,128)(2,1)S(1)}, u32[]{:S(2)}, u32[]{:S(2)}) %collective-permute-start.1) | collective-permute-done | bytes 524320 | tf_op jit(solution)/shard_map/ppermute | solution.py:444
  29.6 1.8 %shard_map.75.refs_2_.refs_3_ = f32[256,1024]{1,0:T(8,128)S(1)} custom-call(s32[2,8]{1,0:T(2,128)S(4)} %get-tuple-element.15.facts_ref, bf16[256,1024]{1,0:T(8,128)(2,1)S(1)} %slice_bitcast_fusion.refs_0_, bf16[256,1024]{1,0:T(8,128)(2,1)S(1)} %shard_map.74.refs_1_, bf16[256,1024]{1,0:T(8,128)(2,1)S(1)} %collective-permute-done.1.refs_2_, ...), custom_call_target="tpu_custom_call" | custom-call | flops 1610612736 | bytes 7864320 | tf_op jit(solution)/shard_map/pallas_call | solution.py:210
  31.4 11.0 %collective-permute-done.2.refs_1_.refs_0_ = bf16[256,1024]{1,0:T(8,128)(2,1)S(1)} collective-permute-done((bf16[256,1024]{1,0:T(8,128)(2,1)S(1)}, bf16[256,1024]{1,0:T(8,128)(2,1)S(1)}, u32[]{:S(2)}, u32[]{:S(2)}) %collective-permute-start.2) | collective-permute-done | bytes 524320 | tf_op jit(solution)/shard_map/ppermute | solution.py:444
  42.4 0.7 shard_map.77.refs_1_.refs_0_
  43.2 3.4 %collective-permute-start.4 = (bf16[256,1024]{1,0:T(8,128)(2,1)S(1)}, bf16[256,1024]{1,0:T(8,128)(2,1)S(1)}, u32[]{:S(2)}, u32[]{:S(2)}) collective-permute-start(bf16[256,1024]{1,0:T(8,128)(2,1)S(1)} %shard_map.77.refs_1_.refs_0_), channel_id=1, source_target_pairs={{0,4},{4,0},{8,12},{12,8},{16,20},{20,16},{24,28},{28,24},{1,5},{5... | collective-permute-start | bytes 1572872 | tf_op jit(solution)/shard_map/ppermute | solution.py:413
  46.6 3.1 %collective-permute-start.6 = (bf16[256,1024]{1,0:T(8,128)(2,1)S(1)}, bf16[256,1024]{1,0:T(8,128)(2,1)S(1)}, u32[]{:S(2)}, u32[]{:S(2)}) collective-permute-start(bf16[256,1024]{1,0:T(8,128)(2,1)S(1)} %shard_map.77.refs_1_.refs_0_), channel_id=1, source_target_pairs={{0,8},{4,12},{8,16},{12,20},{16,24},{20,28},{1,9},{5,13},{9,17},{1... | collective-permute-start | bytes 1572872 | tf_op jit(solution)/shard_map/ppermute | solution.py:408
  49.7 1.3 %collective-permute-start.7 = (bf16[256,1024]{1,0:T(8,128)(2,1)S(1)}, bf16[256,1024]{1,0:T(8,128)(2,1)S(1)}, u32[]{:S(2)}, u32[]{:S(2)}) collective-permute-start(bf16[256,1024]{1,0:T(8,128)(2,1)S(1)} %shard_map.77.refs_1_.refs_0_), channel_id=1, source_target_pairs={{4,16},{12,24},{28,20},{5,17},{13,25},{29,21},{6,18},{14,26},{30,2... | collective-permute-start | bytes 1572872 | tf_op jit(solution)/shard_map/ppermute | solution.py:420
  51.0 0.0 collective-permute-done.4.refs_2_.refs_3_
  51.0 10.8 %collective-permute-done.3.refs_0_ = bf16[256,1024]{1,0:T(8,128)(2,1)S(1)} collective-permute-done((bf16[256,1024]{1,0:T(8,128)(2,1)S(1)}, bf16[256,1024]{1,0:T(8,128)(2,1)S(1)}, u32[]{:S(2)}, u32[]{:S(2)}) %collective-permute-start.3) | collective-permute-done | bytes 524320 | tf_op jit(solution)/shard_map/ppermute | solution.py:444
  61.8 0.1 collective-permute-done.6.refs_2_.refs_1_.refs_3_
  61.9 0.9 collective-permute-start.9
  62.8 2.5 %shard_map.79.refs_1_.refs_0_ = f32[256,1024]{1,0:T(8,128)S(1)} custom-call(s32[2,8]{1,0:T(2,128)S(4)} %get-tuple-element.15.facts_ref, bf16[512,256]{1,0:T(8,128)(2,1)S(1)} %get-tuple-element.16.table_ref, bf16[256,1024]{1,0:T(8,128)(2,1)S(1)} %get-tuple-element.17.back_ref, f32[4,512,1024]{2,1,0:T(8,128)S(1)} %get-tuple-element.18.spec_ref, ...), custom_call_target="tpu_custom_call" | custom-call | flops 2147483648 | bytes 1048576 | tf_op jit(solution)/shard_map/pallas_call | solution.py:358
  65.3 0.0 collective-permute-done.7.refs_3_.refs_4_
  65.4 10.8 %collective-permute-done.5.refs_0_ = bf16[256,1024]{1,0:T(8,128)(2,1)S(1)} collective-permute-done((bf16[256,1024]{1,0:T(8,128)(2,1)S(1)}, bf16[256,1024]{1,0:T(8,128)(2,1)S(1)}, u32[]{:S(2)}, u32[]{:S(2)}) %collective-permute-start.5) | collective-permute-done | bytes 524320 | tf_op jit(solution)/shard_map/ppermute | solution.py:444
  76.2 0.0 collective-permute-start.8
  76.2 1.8 %shard_map.81.refs_3_ = f32[256,1024]{1,0:T(8,128)S(1)} custom-call(s32[2,8]{1,0:T(2,128)S(4)} %get-tuple-element.15.facts_ref, bf16[256,1024]{1,0:T(8,128)(2,1)S(1)} %shard_map.76.refs_0_, bf16[256,1024]{1,0:T(8,128)(2,1)S(1)} %shard_map.78.refs_1_, bf16[256,1024]{1,0:T(8,128)(2,1)S(1)} %shard_map.80.refs_2_, ...), custom_call_target="tpu_custom_call" | custom-call | flops 1610612736 | bytes 7864320 | tf_op jit(solution)/shard_map/pallas_call | solution.py:210
  78.0 0.0 collective-permute-done.9.refs_2_.refs_4_
  78.0 3.3 %shard_map.82 = (f32[1,2,256,1024]{3,2,1,0:T(8,128)}, f32[8,128]{1,0:T(8,128)S(1)}) custom-call(s32[2,8]{1,0:T(2,128)S(4)} %get-tuple-element.15.facts_ref, bf16[512,256]{1,0:T(8,128)(2,1)S(1)} %get-tuple-element.16.table_ref, bf16[256,1024]{1,0:T(8,128)(2,1)S(1)} %get-tuple-element.17.back_ref, f32[4,512,1024]{2,1,0:T(8,128)S(1)} %get-tuple-element.18.spec_ref, ...), custom_call_target="tpu_custom_call" | custom-call | flops 2147483648 | bytes 1048576 | tf_op jit(solution)/shard_map/pallas_call | solution.py:358
  81.3 8.3 %collective-permute-done.8.refs_0_ = bf16[256,1024]{1,0:T(8,128)(2,1)S(1)} collective-permute-done((bf16[256,1024]{1,0:T(8,128)(2,1)S(1)}, bf16[256,1024]{1,0:T(8,128)(2,1)S(1)}, u32[]{:S(2)}, u32[]{:S(2)}) %collective-permute-start.8) | collective-permute-done | bytes 524320 | tf_op jit(solution)/shard_map/ppermute | solution.py:444
  89.6 0.8 shard_map.83.refs_0_
  90.4 2.7 %collective-permute-start.10 = (bf16[256,1024]{1,0:T(8,128)(2,1)S(1)}, bf16[256,1024]{1,0:T(8,128)(2,1)S(1)}, u32[]{:S(2)}, u32[]{:S(2)}) collective-permute-start(bf16[256,1024]{1,0:T(8,128)(2,1)S(1)} %shard_map.83.refs_0_), channel_id=1, source_target_pairs={{8,0},{12,4},{16,8},{20,12},{24,16},{28,20},{9,1},{13,5},{17,9},{2... | collective-permute-start | bytes 1572872 | tf_op jit(solution)/shard_map/ppermute | solution.py:408
  93.1 4.9 %collective-permute-start.12 = (bf16[256,1024]{1,0:T(8,128)(2,1)S(1)}, bf16[256,1024]{1,0:T(8,128)(2,1)S(1)}, u32[]{:S(2)}, u32[]{:S(2)}) collective-permute-start(bf16[256,1024]{1,0:T(8,128)(2,1)S(1)} %shard_map.83.refs_0_), channel_id=1, source_target_pairs={{4,0},{12,8},{20,16},{28,24},{16,4},{24,12},{5,1},{13,9},{21,17},{... | collective-permute-start | bytes 1572872 | tf_op jit(solution)/shard_map/ppermute | solution.py:429
  98.0 5.1 %shard_map.84.refs_1_.refs_0_ = f32[256,1024]{1,0:T(8,128)S(1)} custom-call(s32[2,8]{1,0:T(2,128)S(4)} %get-tuple-element.15.facts_ref, bf16[512,256]{1,0:T(8,128)(2,1)S(1)} %get-tuple-element.16.table_ref, bf16[256,1024]{1,0:T(8,128)(2,1)S(1)} %get-tuple-element.17.back_ref, f32[4,512,1024]{2,1,0:T(8,128)S(1)} %get-tuple-element.18.spec_ref, ...), custom_call_target="tpu_custom_call" | custom-call | flops 2147483648 | bytes 1048576 | tf_op jit(solution)/shard_map/pallas_call | solution.py:358
  103.0 0.9 collective-permute-done.10.refs_0_
  104.0 3.7 %collective-permute-start.11 = (bf16[256,1024]{1,0:T(8,128)(2,1)S(1)}, bf16[256,1024]{1,0:T(8,128)(2,1)S(1)}, u32[]{:S(2)}, u32[]{:S(2)}) collective-permute-start(bf16[256,1024]{1,0:T(8,128)(2,1)S(1)} %shard_map.85.refs_5_), channel_id=1, source_target_pairs={{0,4},{4,0},{8,12},{12,8},{16,20},{20,16},{24,28},{28,24},{1,5},{5... | collective-permute-start | bytes 1572872 | tf_op jit(solution)/shard_map/ppermute | solution.py:413
  107.7 4.8 %collective-permute-done.12.refs_7_ = bf16[256,1024]{1,0:T(8,128)(2,1)S(1)} collective-permute-done((bf16[256,1024]{1,0:T(8,128)(2,1)S(1)}, bf16[256,1024]{1,0:T(8,128)(2,1)S(1)}, u32[]{:S(2)}, u32[]{:S(2)}) %collective-permute-start.12) | collective-permute-done | bytes 524320 | tf_op jit(solution)/shard_map/ppermute | solution.py:429
  112.5 0.0 collective-permute-done.11.refs_6_
  112.5 5.4 %shard_map.86 = f32[1,2,256,1024]{3,2,1,0:T(8,128)} custom-call(s32[2,8]{1,0:T(2,128)S(4)} %get-tuple-element.15.facts_ref, bf16[512,256]{1,0:T(8,128)(2,1)S(1)} %get-tuple-element.16.table_ref, bf16[256,1024]{1,0:T(8,128)(2,1)S(1)} %get-tuple-element.17.back_ref, f32[4,512,1024]{2,1,0:T(8,128)S(1)} %get-tuple-element.18.spec_ref, ...), custom_call_target="tpu_custom_call", output_to_operand_aliasing={{}: (12, {})} | custom-call | flops 2147483648 | bytes 1048576 | tf_op jit(solution)/shard_map/pallas_call | solution.py:358
  (9 shorter events, 0.0 us)
Async XLA Ops:
  1.1 14.8 %collective-permute-start = (bf16[256,1024]{1,0:T(8,128)(2,1)S(1)}, bf16[256,1024]{1,0:T(8,128)(2,1)S(1)}, u32[]{:S(2)}, u32[]{:S(2)}) collective-permute-start(bf16[256,1024]{1,0:T(8,128)(2,1)S(1)} %slice_bitcast_fusion.refs_0_), channel_id=1, source_target_pairs={{0,1},{1,2},{2,3},{3,0},{4,5},{5,6},{6,7},{7,4},{8,9},{9,10},{10,1... | collective-permute-start | bytes 1572872 | tf_op jit(solution)/shard_map/ppermute | solution.py:444
  15.9 13.7 %collective-permute-start.1 = (bf16[256,1024]{1,0:T(8,128)(2,1)S(1)}, bf16[256,1024]{1,0:T(8,128)(2,1)S(1)}, u32[]{:S(2)}, u32[]{:S(2)}) collective-permute-start(bf16[256,1024]{1,0:T(8,128)(2,1)S(1)} %shard_map.74.refs_1_), channel_id=1, source_target_pairs={{0,1},{1,2},{2,3},{3,0},{4,5},{5,6},{6,7},{7,4},{8,9},{9,10},{10,1... | collective-permute-start | bytes 1572872 | tf_op jit(solution)/shard_map/ppermute | solution.py:444
  29.6 12.8 %collective-permute-start.2 = (bf16[256,1024]{1,0:T(8,128)(2,1)S(1)}, bf16[256,1024]{1,0:T(8,128)(2,1)S(1)}, u32[]{:S(2)}, u32[]{:S(2)}) collective-permute-start(bf16[256,1024]{1,0:T(8,128)(2,1)S(1)} %collective-permute-done.1.refs_2_), channel_id=1, source_target_pairs={{0,1},{1,2},{2,3},{3,0},{4,5},{5,6},{6,7},{7,4},{8,9},{9,10},{10,1... | collective-permute-start | bytes 1572872 | tf_op jit(solution)/shard_map/ppermute | solution.py:444
  43.2 7.9 %collective-permute-start.4 = (bf16[256,1024]{1,0:T(8,128)(2,1)S(1)}, bf16[256,1024]{1,0:T(8,128)(2,1)S(1)}, u32[]{:S(2)}, u32[]{:S(2)}) collective-permute-start(bf16[256,1024]{1,0:T(8,128)(2,1)S(1)} %shard_map.77.refs_1_.refs_0_), channel_id=1, source_target_pairs={{0,4},{4,0},{8,12},{12,8},{16,20},{20,16},{24,28},{28,24},{1,5},{5... | collective-permute-start | bytes 1572872 | tf_op jit(solution)/shard_map/ppermute | solution.py:413
  46.6 15.3 %collective-permute-start.3 = (bf16[256,1024]{1,0:T(8,128)(2,1)S(1)}, bf16[256,1024]{1,0:T(8,128)(2,1)S(1)}, u32[]{:S(2)}, u32[]{:S(2)}) collective-permute-start(bf16[256,1024]{1,0:T(8,128)(2,1)S(1)} %shard_map.76.refs_0_), channel_id=1, source_target_pairs={{0,1},{1,2},{2,3},{3,0},{4,5},{5,6},{6,7},{7,4},{8,9},{9,10},{10,1... | collective-permute-start | bytes 1572872 | tf_op jit(solution)/shard_map/ppermute | solution.py:444
  46.6 15.4 %collective-permute-start.6 = (bf16[256,1024]{1,0:T(8,128)(2,1)S(1)}, bf16[256,1024]{1,0:T(8,128)(2,1)S(1)}, u32[]{:S(2)}, u32[]{:S(2)}) collective-permute-start(bf16[256,1024]{1,0:T(8,128)(2,1)S(1)} %shard_map.77.refs_1_.refs_0_), channel_id=1, source_target_pairs={{0,8},{4,12},{8,16},{12,20},{16,24},{20,28},{1,9},{5,13},{9,17},{1... | collective-permute-start | bytes 1572872 | tf_op jit(solution)/shard_map/ppermute | solution.py:408
  49.7 15.7 %collective-permute-start.7 = (bf16[256,1024]{1,0:T(8,128)(2,1)S(1)}, bf16[256,1024]{1,0:T(8,128)(2,1)S(1)}, u32[]{:S(2)}, u32[]{:S(2)}) collective-permute-start(bf16[256,1024]{1,0:T(8,128)(2,1)S(1)} %shard_map.77.refs_1_.refs_0_), channel_id=1, source_target_pairs={{4,16},{12,24},{28,20},{5,17},{13,25},{29,21},{6,18},{14,26},{30,2... | collective-permute-start | bytes 1572872 | tf_op jit(solution)/shard_map/ppermute | solution.py:420
  61.8 14.4 %collective-permute-start.5 = (bf16[256,1024]{1,0:T(8,128)(2,1)S(1)}, bf16[256,1024]{1,0:T(8,128)(2,1)S(1)}, u32[]{:S(2)}, u32[]{:S(2)}) collective-permute-start(bf16[256,1024]{1,0:T(8,128)(2,1)S(1)} %shard_map.78.refs_1_), channel_id=1, source_target_pairs={{0,1},{1,2},{2,3},{3,0},{4,5},{5,6},{6,7},{7,4},{8,9},{9,10},{10,1... | collective-permute-start | bytes 1572872 | tf_op jit(solution)/shard_map/ppermute | solution.py:444
  61.9 16.1 %collective-permute-start.9 = (bf16[256,1024]{1,0:T(8,128)(2,1)S(1)}, bf16[256,1024]{1,0:T(8,128)(2,1)S(1)}, u32[]{:S(2)}, u32[]{:S(2)}) collective-permute-start(bf16[256,1024]{1,0:T(8,128)(2,1)S(1)} %collective-permute-done.6.refs_2_.refs_1_.refs_3_), channel_id=1, source_target_pairs={{0,4},{4,0},{8,12},{12,8},{16,20},{20,16},{24,28},{28,24},{1,5},{5... | collective-permute-start | bytes 1572872 | tf_op jit(solution)/shard_map/ppermute | solution.py:413
  76.2 13.4 %collective-permute-start.8 = (bf16[256,1024]{1,0:T(8,128)(2,1)S(1)}, bf16[256,1024]{1,0:T(8,128)(2,1)S(1)}, u32[]{:S(2)}, u32[]{:S(2)}) collective-permute-start(bf16[256,1024]{1,0:T(8,128)(2,1)S(1)} %shard_map.80.refs_2_), channel_id=1, source_target_pairs={{0,1},{1,2},{2,3},{3,0},{4,5},{5,6},{6,7},{7,4},{8,9},{9,10},{10,1... | collective-permute-start | bytes 1572872 | tf_op jit(solution)/shard_map/ppermute | solution.py:444
  90.4 13.6 %collective-permute-start.10 = (bf16[256,1024]{1,0:T(8,128)(2,1)S(1)}, bf16[256,1024]{1,0:T(8,128)(2,1)S(1)}, u32[]{:S(2)}, u32[]{:S(2)}) collective-permute-start(bf16[256,1024]{1,0:T(8,128)(2,1)S(1)} %shard_map.83.refs_0_), channel_id=1, source_target_pairs={{8,0},{12,4},{16,8},{20,12},{24,16},{28,20},{9,1},{13,5},{17,9},{2... | collective-permute-start | bytes 1572872 | tf_op jit(solution)/shard_map/ppermute | solution.py:408
  93.1 19.4 %collective-permute-start.12 = (bf16[256,1024]{1,0:T(8,128)(2,1)S(1)}, bf16[256,1024]{1,0:T(8,128)(2,1)S(1)}, u32[]{:S(2)}, u32[]{:S(2)}) collective-permute-start(bf16[256,1024]{1,0:T(8,128)(2,1)S(1)} %shard_map.83.refs_0_), channel_id=1, source_target_pairs={{4,0},{12,8},{20,16},{28,24},{16,4},{24,12},{5,1},{13,9},{21,17},{... | collective-permute-start | bytes 1572872 | tf_op jit(solution)/shard_map/ppermute | solution.py:429
  104.0 8.5 %collective-permute-start.11 = (bf16[256,1024]{1,0:T(8,128)(2,1)S(1)}, bf16[256,1024]{1,0:T(8,128)(2,1)S(1)}, u32[]{:S(2)}, u32[]{:S(2)}) collective-permute-start(bf16[256,1024]{1,0:T(8,128)(2,1)S(1)} %shard_map.85.refs_5_), channel_id=1, source_target_pairs={{0,4},{4,0},{8,12},{12,8},{16,20},{20,16},{24,28},{28,24},{1,5},{5... | collective-permute-start | bytes 1572872 | tf_op jit(solution)/shard_map/ppermute | solution.py:413

commit v10 on v9

--- a/solution.py
+++ b/solution.py
@@ -179,42 +179,51 @@
     )(place, lane, docs, table, back, taps, weight, gate, grad)
 
 
-def project_kernel(steps, slot, start, first, last, facts_ref, *refs):
-    shards, refs = refs[: len(steps)], refs[len(steps) :]
-    weight_ref, gate_ref, out_ref = refs[0], refs[1], refs[-1]
+def project_kernel(hops, slot, first, last, facts_ref, *refs):
+    shards, refs = refs[: len(hops)], refs[len(hops) :]
+    weight_ref, gate_ref = refs[:2]
     before_ref = None if first else refs[2]
-    rows, depth = shards[0].shape
+    out_ref, acc_ref = refs[-2:] if last else (refs[-1], refs[-1])
+    depth = shards[0].shape[1]
     count = weight_ref.shape[1] // depth
-    for tile in range(weight_ref.shape[0] // LANES):
-        lanes = pl.ds(tile * LANES, LANES)
-        total = None if first else before_ref[:, lanes]
-        for shard, step in zip(shards, steps):
-            at = lax.rem(facts_ref[0, 4 + REACH] + count - step, count)
-            features = pl.ds(pl.multiple_of(at * depth, depth), depth)
-            part = nt(shard[...], weight_ref[lanes, features])
-            total = part if total is None else total + part
-        if last:
-            gate = gate_ref[0, slot, start : start + rows, lanes].astype(F32)
-            out_ref[:, lanes] = (total * gate).astype(BF16)
+    tiles = [pl.ds(tile * LANES, LANES) for tile in range(weight_ref.shape[0] // LANES)]
+    if not first:
+        acc_ref[...] = before_ref[...]
+    for shard, hop in zip(shards, hops):
+        at = facts_ref[0, 4 + REACH] + hop
+        features = pl.ds(pl.multiple_of(jnp.clip(at, 0, count - 1) * depth, depth), depth)
+
+        def add(shard=shard, hop=hop, features=features):
+            for lanes in tiles:
+                part = nt(shard[...], weight_ref[lanes, features])
+                if hop == 0:
+                    acc_ref[:, lanes] = part
+                else:
+                    acc_ref[:, lanes] += part
+
+        if hop == 0:
+            add()
         else:
-            out_ref[:, lanes] = total
-
-
-def project(facts, shards, steps, weight, gate, slot, start, before=None, last=True, after=()):
+            pl.when((at >= 0) & (at < count))(add)
+    if last:
+        out_ref[...] = (acc_ref[...] * gate_ref[0, slot].astype(F32)).astype(BF16)
+
+
+def project(facts, shards, hops, weight, gate, slot, before=None, last=True, after=()):
     rows, depth = shards[0].shape
     width = weight.shape[0]
     operands = [facts, *shards, weight, gate]
     if before is not None:
         operands.append(before)
-    body = functools.partial(project_kernel, steps, slot, start, before is None, last)
     return pl.pallas_call(
-        body,
+        functools.partial(project_kernel, hops, slot, before is None, last),
         out_shape=pltpu.VMEM((rows, width), BF16 if last else F32),
         in_specs=[SCALARS] + [WHOLE] * (len(operands) - 1) + [ANYWHERE] * len(after),
         out_specs=WHOLE,
+        scratch_shapes=[pltpu.VMEM((rows, width), F32)] if last else [],
         compiler_params=params(),
         cost_estimate=pl.CostEstimate(
-            flops=2 * rows * depth * len(shards) * width,
+            flops=2 * rows * depth * (len(shards) + 1) // 2 * width,
             bytes_accessed=2 * (rows + width) * depth * len(shards),
             transcendentals=0,
         ),
@@ -437,14 +446,14 @@
     width = out_weight.shape[0]
     count = lax.axis_size("ch")
     lane = lax.axis_index("ch").astype(jnp.int32)[None]
-    around = [(source, (source + 1) % count) for source in range(count)]
-    everything = tuple(range(count))
-
-    def turned(piece):
-        return lax.ppermute(piece, "ch", around)
-
-    upper_in = [grad_out[0, 1]]
-    upper_in.append(turned(upper_in[0]))
+
+    def sent(step, up, down):
+        upward = [(source, source + 1) for source in range(step - 1, count - 1)]
+        downward = [(source, source - 1) for source in range(1, count - step + 1)]
+        return lax.ppermute(up, "ch", upward), lax.ppermute(down, "ch", downward)
+
+    start = grad_out[0, 1]
+    upper_in = [sent(1, start, start)]
 
     table, back = (jnp.asarray(one) for one in tables(length))
     spectra, weight, gates, lower_slice, table, back, facts, prepared = prepare(
@@ -461,33 +470,37 @@
     )
     tabs = (table, back, spectra)
 
-    upper_in[1] = ordered(upper_in[1], prepared)
-    for step in range(2, count):
-        upper_in.append(turned(upper_in[-1]))
-    def partial_of(shards, slot):
-        return project(facts, shards, everything[:-1], weight, gates, slot, 0, last=False)
-
-    def final_of(shard, slot, partial, after=()):
-        last = everything[-1:]
-        return project(facts, [shard], last, weight, gates, slot, 0, partial, after=after)
-
-    partial = partial_of(upper_in[:-1], 1)
-    lower_in = [ordered(lower_slice, upper_in[-1], partial)]
-    upper = final_of(upper_in[-1], 1, partial)
+    def pass_on(chain, *earlier):
+        if earlier:
+            chain[-1] = [ordered(one, *earlier) for one in chain[-1]]
+        chain.append(sent(len(chain) + 1, *chain[-1]))
+
+    hops = [0] + [way * step for step in range(1, count) for way in (-1, 1)]
+
+    def partial_of(own, arrived, slot):
+        shards = [own] + [one for pair in arrived[: count - 2] for one in pair]
+        return project(facts, shards, hops[:-2], weight, gates, slot, last=False)
+
+    def final_of(arrived, slot, partial, after=()):
+        return project(facts, arrived[-1], hops[-2:], weight, gates, slot, partial, after=after)
+
+    pass_on(upper_in, prepared)
+    for _ in range(3, count):
+        pass_on(upper_in)
+    partial = partial_of(start, upper_in, 1)
+    own = ordered(lower_slice, *upper_in[-1], partial)
+    lower_in = [sent(1, own, own)]
+    upper = final_of(upper_in, 1, partial)
     upper_halo = upper_halo_of(upper)
     two, swapped, mate, fold = upper_halo
-    lower_in.append(ordered(turned(lower_in[0]), upper, mate))
+    pass_on(lower_in, upper)
     near = own_terms(1, tabs, facts, [upper])
-    for step in range(2, count):
-        received = turned(lower_in[-1])
-        if step == count - 1:
-            lower_in.append(received)
-        else:
-            lower_in.append(ordered(received, near, two, fold))
+    for _ in range(3, count):
+        pass_on(lower_in, near, two, mate, fold)
     result, convolved = far_terms(1, 1, tabs, facts, [near, *upper_halo])
 
-    partial = partial_of(lower_in[:-1], 0)
-    lower = final_of(lower_in[-1], 0, partial, [swapped, convolved])
+    partial = partial_of(own, lower_in, 0)
+    lower = final_of(lower_in, 0, partial, [swapped, convolved])
     near = own_terms(0, tabs, facts, [lower])
     lower_halo = lower_halo_of(lower, near)
     arrays = [near, upper, mate, two, fold, *lower_halo]

time: 118 us -> 115 us (0.975)
  the two profiles are of different devices: /device:TPU:3 before, /device:TPU:1 now
where the time goes in v10:
time: 115 us; the launch traced here: 112 us
  waiting for transfers between devices  44.7 us (39%)
  starting transfers between devices  38.2 us (33%)
  Pallas kernels  28.1 us (24%)
    ppermute x12, waiting for transfers between devices, sent(): return (lax.ppermute(up, 'ch', upward), lax.ppermute(down, 'ch', downward))  37.7 us
    ppermute x12, starting transfers between devices, sent(): return (lax.ppermute(up, 'ch', upward), lax.ppermute(down, 'ch', downward))  15.8 us
    pallas_call x4, Pallas kernels, conv_call(): pl.pallas_call(body, grid=(width // LANES,), out_shape=out_shape, in_spec...  14.2 us
    pallas_call x1, Pallas kernels, prepare(): pl.pallas_call(functools.partial(prepare_kernel, pairs), grid=(width // L...  7.44 us
    ppermute x1, starting transfers between devices, upper_halo_of(): mate, far = (core_swapped(value), lax.ppermute(value, 'ctx', far))  7 us
    ppermute x3, starting transfers between devices, core_swapped(): lax.ppermute(value, 'ctx', [(source, source ^ 1) for source in range(coun...  6.56 us
    pallas_call x4, Pallas kernels, project(): pl.pallas_call(functools.partial(project_kernel, hops, slot, before is No...  6.54 us
    ppermute x2, waiting for transfers between devices, shifted(): lax.ppermute(value, 'ctx', [(source, source + steps) for source in range(...  4.58 us
  transfers between devices with their start and end apart: 19, of which 9 were waited for; matrix products, arithmetic and copies ran while one was open for 0% of the time, Pallas kernels for 21%

profile of v10, /device:TPU:1, one launch (start us, length us, event | category | flops | bytes accessed | tf_op | source)
XLA Modules:
  0.0 112.4 jit_solution(11621977261753134657)
XLA Ops:
  0.0 1.1 slice_bitcast_fusion.refs_0_
  1.1 4.1 %collective-permute-start = (bf16[256,1024]{1,0:T(8,128)(2,1)S(1)}, bf16[256,1024]{1,0:T(8,128)(2,1)S(1)}, u32[]{:S(2)}, u32[]{:S(2)}) collective-permute-start(bf16[256,1024]{1,0:T(8,128)(2,1)S(1)} %slice_bitcast_fusion.refs_0_), channel_id=1, source_target_pairs={{0,1},{1,2},{2,3},{4,5},{5,6},{6,7},{8,9},{9,10},{10,11},{12,13},{... | collective-permute-start | bytes 1572872 | tf_op jit(solution)/shard_map/ppermute | solution.py:453
  5.1 1.3 %collective-permute-start.3 = (bf16[256,1024]{1,0:T(8,128)(2,1)S(1)}, bf16[256,1024]{1,0:T(8,128)(2,1)S(1)}, u32[]{:S(2)}, u32[]{:S(2)}) collective-permute-start(bf16[256,1024]{1,0:T(8,128)(2,1)S(1)} %slice_bitcast_fusion.refs_0_), channel_id=1, source_target_pairs={{1,0},{2,1},{3,2},{5,4},{6,5},{7,6},{9,8},{10,9},{11,10},{13,12},{... | collective-permute-start | bytes 1572872 | tf_op jit(solution)/shard_map/ppermute | solution.py:453
  6.5 7.4 %shard_map.73 = (f32[4,512,1024]{2,1,0:T(8,128)S(1)}, bf16[1024,4096]{1,0:T(8,128)(2,1)S(1)}, bf16[1,2,256,1024]{3,2,1,0:T(8,128)(2,1)S(1)}, bf16[256,1024]{1,0:...) custom-call(s32[1]{0:T(128)} %bitcast.refs_0_, ...), custom_call_target="tpu_custom_call" | custom-call | flops 2415919104 | bytes 11534336 | tf_op jit(solution)/shard_map/pallas_call | solution.py:147
  13.9 1.8 %collective-permute-done.refs_0_ = bf16[256,1024]{1,0:T(8,128)(2,1)S(1)} collective-permute-done((bf16[256,1024]{1,0:T(8,128)(2,1)S(1)}, bf16[256,1024]{1,0:T(8,128)(2,1)S(1)}, u32[]{:S(2)}, u32[]{:S(2)}) %collective-permute-start) | collective-permute-done | bytes 524320 | tf_op jit(solution)/shard_map/ppermute | solution.py:453
  16.4 3.1 %collective-permute-done.3.refs_0_ = bf16[256,1024]{1,0:T(8,128)(2,1)S(1)} collective-permute-done((bf16[256,1024]{1,0:T(8,128)(2,1)S(1)}, bf16[256,1024]{1,0:T(8,128)(2,1)S(1)}, u32[]{:S(2)}, u32[]{:S(2)}) %collective-permute-start.3) | collective-permute-done | bytes 524320 | tf_op jit(solution)/shard_map/ppermute | solution.py:453
  19.5 1.3 %collective-permute-start.4 = (bf16[256,1024]{1,0:T(8,128)(2,1)S(1)}, bf16[256,1024]{1,0:T(8,128)(2,1)S(1)}, u32[]{:S(2)}, u32[]{:S(2)}) collective-permute-start(bf16[256,1024]{1,0:T(8,128)(2,1)S(1)} %shard_map.75.refs_2_), channel_id=1, source_target_pairs={{1,0},{2,1},{5,4},{6,5},{9,8},{10,9},{13,12},{14,13},{17,16},{18,1... | collective-permute-start | bytes 1572872 | tf_op jit(solution)/shard_map/ppermute | solution.py:453
  21.5 11.8 %collective-permute-done.4.refs_4_ = bf16[256,1024]{1,0:T(8,128)(2,1)S(1)} collective-permute-done((bf16[256,1024]{1,0:T(8,128)(2,1)S(1)}, bf16[256,1024]{1,0:T(8,128)(2,1)S(1)}, u32[]{:S(2)}, u32[]{:S(2)}) %collective-permute-start.4) | collective-permute-done | bytes 524320 | tf_op jit(solution)/shard_map/ppermute | solution.py:453
  33.3 1.3 %collective-permute-start.5 = (bf16[256,1024]{1,0:T(8,128)(2,1)S(1)}, bf16[256,1024]{1,0:T(8,128)(2,1)S(1)}, u32[]{:S(2)}, u32[]{:S(2)}) collective-permute-start(bf16[256,1024]{1,0:T(8,128)(2,1)S(1)} %collective-permute-done.4.refs_4_), channel_id=1, source_target_pairs={{1,0},{5,4},{9,8},{13,12},{17,16},{21,20},{25,24},{29,28}} | collective-permute-start | bytes 1572872 | tf_op jit(solution)/shard_map/ppermute | solution.py:453
  34.6 2.3 %shard_map.76.refs_3_.refs_4_ = f32[256,1024]{1,0:T(8,128)S(1)} custom-call(s32[2,8]{1,0:T(2,128)S(4)} %get-tuple-element.15.facts_ref, bf16[256,1024]{1,0:T(8,128)(2,1)S(1)} %slice_bitcast_fusion.refs_0_, bf16[256,1024]{1,0:T(8,128)(2,1)S(1)} %shard_map.74.refs_1_, bf16[256,1024]{1,0:T(8,128)(2,1)S(1)} %shard_map.75.refs_2_, ...), custom_call_target="tpu_custom_call" | custom-call | flops 1610612736 | bytes 13107200 | tf_op jit(solution)/shard_map/pallas_call | solution.py:218
  36.9 9.1 %collective-permute-done.5.refs_2_.refs_1_ = bf16[256,1024]{1,0:T(8,128)(2,1)S(1)} collective-permute-done((bf16[256,1024]{1,0:T(8,128)(2,1)S(1)}, bf16[256,1024]{1,0:T(8,128)(2,1)S(1)}, u32[]{:S(2)}, u32[]{:S(2)}) %collective-permute-start.5) | collective-permute-done | bytes 524320 | tf_op jit(solution)/shard_map/ppermute | solution.py:453
  46.0 1.3 %collective-permute-start.6 = (bf16[256,1024]{1,0:T(8,128)(2,1)S(1)}, bf16[256,1024]{1,0:T(8,128)(2,1)S(1)}, u32[]{:S(2)}, u32[]{:S(2)}) collective-permute-start(bf16[256,1024]{1,0:T(8,128)(2,1)S(1)} %shard_map.77.refs_0_), channel_id=1, source_target_pairs={{0,1},{1,2},{2,3},{4,5},{5,6},{6,7},{8,9},{9,10},{10,11},{12,13},{... | collective-permute-start | bytes 1572872 | tf_op jit(solution)/shard_map/ppermute | solution.py:453
  47.3 1.3 %collective-permute-start.12 = (bf16[256,1024]{1,0:T(8,128)(2,1)S(1)}, bf16[256,1024]{1,0:T(8,128)(2,1)S(1)}, u32[]{:S(2)}, u32[]{:S(2)}) collective-permute-start(bf16[256,1024]{1,0:T(8,128)(2,1)S(1)} %shard_map.77.refs_0_), channel_id=1, source_target_pairs={{1,0},{2,1},{3,2},{5,4},{6,5},{7,6},{9,8},{10,9},{11,10},{13,12},{... | collective-permute-start | bytes 1572872 | tf_op jit(solution)/shard_map/ppermute | solution.py:453
  49.5 3.1 %collective-permute-start.8 = (bf16[256,1024]{1,0:T(8,128)(2,1)S(1)}, bf16[256,1024]{1,0:T(8,128)(2,1)S(1)}, u32[]{:S(2)}, u32[]{:S(2)}) collective-permute-start(bf16[256,1024]{1,0:T(8,128)(2,1)S(1)} %shard_map.78.refs_1_.refs_0_), channel_id=1, source_target_pairs={{0,8},{4,12},{8,16},{12,20},{16,24},{20,28},{1,9},{5,13},{9,17},{1... | collective-permute-start | bytes 1572872 | tf_op jit(solution)/shard_map/ppermute | solution.py:417
  52.7 7.0 %collective-permute-start.10 = (bf16[256,1024]{1,0:T(8,128)(2,1)S(1)}, bf16[256,1024]{1,0:T(8,128)(2,1)S(1)}, u32[]{:S(2)}, u32[]{:S(2)}) collective-permute-start(bf16[256,1024]{1,0:T(8,128)(2,1)S(1)} %shard_map.78.refs_1_.refs_0_), channel_id=1, source_target_pairs={{4,16},{12,24},{28,20},{5,17},{13,25},{29,21},{6,18},{14,26},{30,2... | collective-permute-start | bytes 1572872 | tf_op jit(solution)/shard_map/ppermute | solution.py:429
  60.5 1.3 %collective-permute-start.13 = (bf16[256,1024]{1,0:T(8,128)(2,1)S(1)}, bf16[256,1024]{1,0:T(8,128)(2,1)S(1)}, u32[]{:S(2)}, u32[]{:S(2)}) collective-permute-start(bf16[256,1024]{1,0:T(8,128)(2,1)S(1)} %shard_map.82.refs_2_), channel_id=1, source_target_pairs={{1,0},{2,1},{5,4},{6,5},{9,8},{10,9},{13,12},{14,13},{17,16},{18,1... | collective-permute-start | bytes 1572872 | tf_op jit(solution)/shard_map/ppermute | solution.py:453
  61.8 3.1 %collective-permute-start.15 = (bf16[256,1024]{1,0:T(8,128)(2,1)S(1)}, bf16[256,1024]{1,0:T(8,128)(2,1)S(1)}, u32[]{:S(2)}, u32[]{:S(2)}) collective-permute-start(bf16[256,1024]{1,0:T(8,128)(2,1)S(1)} %collective-permute-done.8.refs_2_.refs_1_.refs_3_), channel_id=1, source_target_pairs={{0,4},{4,0},{8,12},{12,8},{16,20},{20,16},{24,28},{28,24},{1,5},{5... | collective-permute-start | bytes 1572872 | tf_op jit(solution)/shard_map/ppermute | solution.py:422
  64.9 5.0 %shard_map.80.refs_1_.refs_0_ = f32[256,1024]{1,0:T(8,128)S(1)} custom-call(s32[2,8]{1,0:T(2,128)S(4)} %get-tuple-element.15.facts_ref, bf16[512,256]{1,0:T(8,128)(2,1)S(1)} %get-tuple-element.16.table_ref, bf16[256,1024]{1,0:T(8,128)(2,1)S(1)} %get-tuple-element.17.back_ref, f32[4,512,1024]{2,1,0:T(8,128)S(1)} %get-tuple-element.18.spec_ref, ...), custom_call_target="tpu_custom_call" | custom-call | flops 2147483648 | bytes 1048576 | tf_op jit(solution)/shard_map/pallas_call | solution.py:367
  70.0 1.0 collective-permute-done.10.refs_4_
  71.6 3.8 %collective-permute-done.13.refs_0_ = bf16[256,1024]{1,0:T(8,128)(2,1)S(1)} collective-permute-done((bf16[256,1024]{1,0:T(8,128)(2,1)S(1)}, bf16[256,1024]{1,0:T(8,128)(2,1)S(1)}, u32[]{:S(2)}, u32[]{:S(2)}) %collective-permute-start.13) | collective-permute-done | bytes 524320 | tf_op jit(solution)/shard_map/ppermute | solution.py:453
  75.4 1.3 %collective-permute-start.14 = (bf16[256,1024]{1,0:T(8,128)(2,1)S(1)}, bf16[256,1024]{1,0:T(8,128)(2,1)S(1)}, u32[]{:S(2)}, u32[]{:S(2)}) collective-permute-start(bf16[256,1024]{1,0:T(8,128)(2,1)S(1)} %shard_map.83.refs_4_), channel_id=1, source_target_pairs={{1,0},{5,4},{9,8},{13,12},{17,16},{21,20},{25,24},{29,28}} | collective-permute-start | bytes 1572872 | tf_op jit(solution)/shard_map/ppermute | solution.py:453
  76.7 2.3 %shard_map.84.refs_4_ = f32[256,1024]{1,0:T(8,128)S(1)} custom-call(s32[2,8]{1,0:T(2,128)S(4)} %get-tuple-element.15.facts_ref, bf16[256,1024]{1,0:T(8,128)(2,1)S(1)} %shard_map.77.refs_0_, bf16[256,1024]{1,0:T(8,128)(2,1)S(1)} %shard_map.79.refs_1_, bf16[256,1024]{1,0:T(8,128)(2,1)S(1)} %shard_map.82.refs_2_, bf16[256,1024]{1,0:T(8,128)(2,1)S(1)} %shard_map.81.refs_3_, ...), custom_call_target="tpu_custom_call" | custom-call | flops 1610612736 | bytes 13107200 | tf_op jit(solution)/shard_map/pallas_call | solution.py:218
  79.0 3.3 %shard_map.85 = (f32[1,2,256,1024]{3,2,1,0:T(8,128)}, f32[8,128]{1,0:T(8,128)S(1)}) custom-call(s32[2,8]{1,0:T(2,128)S(4)} %get-tuple-element.15.facts_ref, bf16[512,256]{1,0:T(8,128)(2,1)S(1)} %get-tuple-element.16.table_ref, bf16[256,1024]{1,0:T(8,128)(2,1)S(1)} %get-tuple-element.17.back_ref, f32[4,512,1024]{2,1,0:T(8,128)S(1)} %get-tuple-element.18.spec_ref, ...), custom_call_target="tpu_custom_call" | custom-call | flops 2147483648 | bytes 1048576 | tf_op jit(solution)/shard_map/pallas_call | solution.py:367
  82.3 8.0 %collective-permute-done.14.refs_1_ = bf16[256,1024]{1,0:T(8,128)(2,1)S(1)} collective-permute-done((bf16[256,1024]{1,0:T(8,128)(2,1)S(1)}, bf16[256,1024]{1,0:T(8,128)(2,1)S(1)}, u32[]{:S(2)}, u32[]{:S(2)}) %collective-permute-start.14) | collective-permute-done | bytes 524320 | tf_op jit(solution)/shard_map/ppermute | solution.py:453
  90.3 1.1 shard_map.86.refs_0_
  91.4 1.3 %collective-permute-start.16 = (bf16[256,1024]{1,0:T(8,128)(2,1)S(1)}, bf16[256,1024]{1,0:T(8,128)(2,1)S(1)}, u32[]{:S(2)}, u32[]{:S(2)}) collective-permute-start(bf16[256,1024]{1,0:T(8,128)(2,1)S(1)} %shard_map.86.refs_0_), channel_id=1, source_target_pairs={{8,0},{12,4},{16,8},{20,12},{24,16},{28,20},{9,1},{13,5},{17,9},{2... | collective-permute-start | bytes 1572872 | tf_op jit(solution)/shard_map/ppermute | solution.py:417
  92.7 4.4 %collective-permute-start.18 = (bf16[256,1024]{1,0:T(8,128)(2,1)S(1)}, bf16[256,1024]{1,0:T(8,128)(2,1)S(1)}, u32[]{:S(2)}, u32[]{:S(2)}) collective-permute-start(bf16[256,1024]{1,0:T(8,128)(2,1)S(1)} %shard_map.86.refs_0_), channel_id=1, source_target_pairs={{4,0},{12,8},{20,16},{28,24},{16,4},{24,12},{5,1},{13,9},{21,17},{... | collective-permute-start | bytes 1572872 | tf_op jit(solution)/shard_map/ppermute | solution.py:438
  97.1 2.6 %shard_map.87.refs_1_.refs_0_ = f32[256,1024]{1,0:T(8,128)S(1)} custom-call(s32[2,8]{1,0:T(2,128)S(4)} %get-tuple-element.15.facts_ref, bf16[512,256]{1,0:T(8,128)(2,1)S(1)} %get-tuple-element.16.table_ref, bf16[256,1024]{1,0:T(8,128)(2,1)S(1)} %get-tuple-element.17.back_ref, f32[4,512,1024]{2,1,0:T(8,128)S(1)} %get-tuple-element.18.spec_ref, ...), custom_call_target="tpu_custom_call" | custom-call | flops 2147483648 | bytes 1048576 | tf_op jit(solution)/shard_map/pallas_call | solution.py:367
  99.6 4.6 %collective-permute-done.16.refs_0_ = bf16[256,1024]{1,0:T(8,128)(2,1)S(1)} collective-permute-done((bf16[256,1024]{1,0:T(8,128)(2,1)S(1)}, bf16[256,1024]{1,0:T(8,128)(2,1)S(1)}, u32[]{:S(2)}, u32[]{:S(2)}) %collective-permute-start.16) | collective-permute-done | bytes 524320 | tf_op jit(solution)/shard_map/ppermute | solution.py:417
  104.2 3.4 %collective-permute-start.17 = (bf16[256,1024]{1,0:T(8,128)(2,1)S(1)}, bf16[256,1024]{1,0:T(8,128)(2,1)S(1)}, u32[]{:S(2)}, u32[]{:S(2)}) collective-permute-start(bf16[256,1024]{1,0:T(8,128)(2,1)S(1)} %shard_map.88.refs_5_), channel_id=1, source_target_pairs={{0,4},{4,0},{8,12},{12,8},{16,20},{20,16},{24,28},{28,24},{1,5},{5... | collective-permute-start | bytes 1572872 | tf_op jit(solution)/shard_map/ppermute | solution.py:422
  107.6 1.5 %collective-permute-done.17.refs_6_ = bf16[256,1024]{1,0:T(8,128)(2,1)S(1)} collective-permute-done((bf16[256,1024]{1,0:T(8,128)(2,1)S(1)}, bf16[256,1024]{1,0:T(8,128)(2,1)S(1)}, u32[]{:S(2)}, u32[]{:S(2)}) %collective-permute-start.17) | collective-permute-done | bytes 524320 | tf_op jit(solution)/shard_map/ppermute | solution.py:422
  109.2 3.3 %shard_map.89 = f32[1,2,256,1024]{3,2,1,0:T(8,128)} custom-call(s32[2,8]{1,0:T(2,128)S(4)} %get-tuple-element.15.facts_ref, bf16[512,256]{1,0:T(8,128)(2,1)S(1)} %get-tuple-element.16.table_ref, bf16[256,1024]{1,0:T(8,128)(2,1)S(1)} %get-tuple-element.17.back_ref, f32[4,512,1024]{2,1,0:T(8,128)S(1)} %get-tuple-element.18.spec_ref, ...), custom_call_target="tpu_custom_call", output_to_operand_aliasing={{}: (12, {})} | custom-call | flops 2147483648 | bytes 1048576 | tf_op jit(solution)/shard_map/pallas_call | solution.py:367
  (24 shorter events, 3.8 us)
Async XLA Ops:
  1.1 14.6 %collective-permute-start = (bf16[256,1024]{1,0:T(8,128)(2,1)S(1)}, bf16[256,1024]{1,0:T(8,128)(2,1)S(1)}, u32[]{:S(2)}, u32[]{:S(2)}) collective-permute-start(bf16[256,1024]{1,0:T(8,128)(2,1)S(1)} %slice_bitcast_fusion.refs_0_), channel_id=1, source_target_pairs={{0,1},{1,2},{2,3},{4,5},{5,6},{6,7},{8,9},{9,10},{10,11},{12,13},{... | collective-permute-start | bytes 1572872 | tf_op jit(solution)/shard_map/ppermute | solution.py:453
  5.1 14.4 %collective-permute-start.3 = (bf16[256,1024]{1,0:T(8,128)(2,1)S(1)}, bf16[256,1024]{1,0:T(8,128)(2,1)S(1)}, u32[]{:S(2)}, u32[]{:S(2)}) collective-permute-start(bf16[256,1024]{1,0:T(8,128)(2,1)S(1)} %slice_bitcast_fusion.refs_0_), channel_id=1, source_target_pairs={{1,0},{2,1},{3,2},{5,4},{6,5},{7,6},{9,8},{10,9},{11,10},{13,12},{... | collective-permute-start | bytes 1572872 | tf_op jit(solution)/shard_map/ppermute | solution.py:453
  15.7 5.1 %collective-permute-start.1 = (bf16[256,1024]{1,0:T(8,128)(2,1)S(1)}, bf16[256,1024]{1,0:T(8,128)(2,1)S(1)}, u32[]{:S(2)}, u32[]{:S(2)}) collective-permute-start(bf16[256,1024]{1,0:T(8,128)(2,1)S(1)} %shard_map.74.refs_1_), channel_id=1, source_target_pairs={{1,2},{2,3},{5,6},{6,7},{9,10},{10,11},{13,14},{14,15},{17,18},{18... | collective-permute-start | bytes 1572872 | tf_op jit(solution)/shard_map/ppermute | solution.py:453
  19.5 13.8 %collective-permute-start.4 = (bf16[256,1024]{1,0:T(8,128)(2,1)S(1)}, bf16[256,1024]{1,0:T(8,128)(2,1)S(1)}, u32[]{:S(2)}, u32[]{:S(2)}) collective-permute-start(bf16[256,1024]{1,0:T(8,128)(2,1)S(1)} %shard_map.75.refs_2_), channel_id=1, source_target_pairs={{1,0},{2,1},{5,4},{6,5},{9,8},{10,9},{13,12},{14,13},{17,16},{18,1... | collective-permute-start | bytes 1572872 | tf_op jit(solution)/shard_map/ppermute | solution.py:453
  20.8 16.1 %collective-permute-start.2 = (bf16[256,1024]{1,0:T(8,128)(2,1)S(1)}, bf16[256,1024]{1,0:T(8,128)(2,1)S(1)}, u32[]{:S(2)}, u32[]{:S(2)}) collective-permute-start(bf16[256,1024]{1,0:T(8,128)(2,1)S(1)} %collective-permute-done.1.refs_3_), channel_id=1, source_target_pairs={{2,3},{6,7},{10,11},{14,15},{18,19},{22,23},{26,27},{30,31}} | collective-permute-start | bytes 1572872 | tf_op jit(solution)/shard_map/ppermute | solution.py:453
  33.3 12.7 %collective-permute-start.5 = (bf16[256,1024]{1,0:T(8,128)(2,1)S(1)}, bf16[256,1024]{1,0:T(8,128)(2,1)S(1)}, u32[]{:S(2)}, u32[]{:S(2)}) collective-permute-start(bf16[256,1024]{1,0:T(8,128)(2,1)S(1)} %collective-permute-done.4.refs_4_), channel_id=1, source_target_pairs={{1,0},{5,4},{9,8},{13,12},{17,16},{21,20},{25,24},{29,28}} | collective-permute-start | bytes 1572872 | tf_op jit(solution)/shard_map/ppermute | solution.py:453
  46.0 13.8 %collective-permute-start.6 = (bf16[256,1024]{1,0:T(8,128)(2,1)S(1)}, bf16[256,1024]{1,0:T(8,128)(2,1)S(1)}, u32[]{:S(2)}, u32[]{:S(2)}) collective-permute-start(bf16[256,1024]{1,0:T(8,128)(2,1)S(1)} %shard_map.77.refs_0_), channel_id=1, source_target_pairs={{0,1},{1,2},{2,3},{4,5},{5,6},{6,7},{8,9},{9,10},{10,11},{12,13},{... | collective-permute-start | bytes 1572872 | tf_op jit(solution)/shard_map/ppermute | solution.py:453
  47.3 13.2 %collective-permute-start.12 = (bf16[256,1024]{1,0:T(8,128)(2,1)S(1)}, bf16[256,1024]{1,0:T(8,128)(2,1)S(1)}, u32[]{:S(2)}, u32[]{:S(2)}) collective-permute-start(bf16[256,1024]{1,0:T(8,128)(2,1)S(1)} %shard_map.77.refs_0_), channel_id=1, source_target_pairs={{1,0},{2,1},{3,2},{5,4},{6,5},{7,6},{9,8},{10,9},{11,10},{13,12},{... | collective-permute-start | bytes 1572872 | tf_op jit(solution)/shard_map/ppermute | solution.py:453
  49.5 12.3 %collective-permute-start.8 = (bf16[256,1024]{1,0:T(8,128)(2,1)S(1)}, bf16[256,1024]{1,0:T(8,128)(2,1)S(1)}, u32[]{:S(2)}, u32[]{:S(2)}) collective-permute-start(bf16[256,1024]{1,0:T(8,128)(2,1)S(1)} %shard_map.78.refs_1_.refs_0_), channel_id=1, source_target_pairs={{0,8},{4,12},{8,16},{12,20},{16,24},{20,28},{1,9},{5,13},{9,17},{1... | collective-permute-start | bytes 1572872 | tf_op jit(solution)/shard_map/ppermute | solution.py:417
  52.7 18.2 %collective-permute-start.10 = (bf16[256,1024]{1,0:T(8,128)(2,1)S(1)}, bf16[256,1024]{1,0:T(8,128)(2,1)S(1)}, u32[]{:S(2)}, u32[]{:S(2)}) collective-permute-start(bf16[256,1024]{1,0:T(8,128)(2,1)S(1)} %shard_map.78.refs_1_.refs_0_), channel_id=1, source_target_pairs={{4,16},{12,24},{28,20},{5,17},{13,25},{29,21},{6,18},{14,26},{30,2... | collective-permute-start | bytes 1572872 | tf_op jit(solution)/shard_map/ppermute | solution.py:429
  59.7 11.2 %collective-permute-start.9 = (bf16[256,1024]{1,0:T(8,128)(2,1)S(1)}, bf16[256,1024]{1,0:T(8,128)(2,1)S(1)}, u32[]{:S(2)}, u32[]{:S(2)}) collective-permute-start(bf16[256,1024]{1,0:T(8,128)(2,1)S(1)} %shard_map.78.refs_1_.refs_0_), channel_id=1, source_target_pairs={{0,4},{4,0},{8,12},{12,8},{16,20},{20,16},{24,28},{28,24},{1,5},{5... | collective-permute-start | bytes 1572872 | tf_op jit(solution)/shard_map/ppermute | solution.py:422
  59.8 11.1 %collective-permute-start.7 = (bf16[256,1024]{1,0:T(8,128)(2,1)S(1)}, bf16[256,1024]{1,0:T(8,128)(2,1)S(1)}, u32[]{:S(2)}, u32[]{:S(2)}) collective-permute-start(bf16[256,1024]{1,0:T(8,128)(2,1)S(1)} %shard_map.79.refs_1_), channel_id=1, source_target_pairs={{1,2},{2,3},{5,6},{6,7},{9,10},{10,11},{13,14},{14,15},{17,18},{18... | collective-permute-start | bytes 1572872 | tf_op jit(solution)/shard_map/ppermute | solution.py:453
  60.5 14.9 %collective-permute-start.13 = (bf16[256,1024]{1,0:T(8,128)(2,1)S(1)}, bf16[256,1024]{1,0:T(8,128)(2,1)S(1)}, u32[]{:S(2)}, u32[]{:S(2)}) collective-permute-start(bf16[256,1024]{1,0:T(8,128)(2,1)S(1)} %shard_map.82.refs_2_), channel_id=1, source_target_pairs={{1,0},{2,1},{5,4},{6,5},{9,8},{10,9},{13,12},{14,13},{17,16},{18,1... | collective-permute-start | bytes 1572872 | tf_op jit(solution)/shard_map/ppermute | solution.py:453
  61.8 17.2 %collective-permute-start.15 = (bf16[256,1024]{1,0:T(8,128)(2,1)S(1)}, bf16[256,1024]{1,0:T(8,128)(2,1)S(1)}, u32[]{:S(2)}, u32[]{:S(2)}) collective-permute-start(bf16[256,1024]{1,0:T(8,128)(2,1)S(1)} %collective-permute-done.8.refs_2_.refs_1_.refs_3_), channel_id=1, source_target_pairs={{0,4},{4,0},{8,12},{12,8},{16,20},{20,16},{24,28},{28,24},{1,5},{5... | collective-permute-start | bytes 1572872 | tf_op jit(solution)/shard_map/ppermute | solution.py:422
  70.9 11.3 %collective-permute-start.11 = (bf16[256,1024]{1,0:T(8,128)(2,1)S(1)}, bf16[256,1024]{1,0:T(8,128)(2,1)S(1)}, u32[]{:S(2)}, u32[]{:S(2)}) collective-permute-start(bf16[256,1024]{1,0:T(8,128)(2,1)S(1)} %shard_map.81.refs_3_), channel_id=1, source_target_pairs={{2,3},{6,7},{10,11},{14,15},{18,19},{22,23},{26,27},{30,31}} | collective-permute-start | bytes 1572872 | tf_op jit(solution)/shard_map/ppermute | solution.py:453
  75.4 14.8 %collective-permute-start.14 = (bf16[256,1024]{1,0:T(8,128)(2,1)S(1)}, bf16[256,1024]{1,0:T(8,128)(2,1)S(1)}, u32[]{:S(2)}, u32[]{:S(2)}) collective-permute-start(bf16[256,1024]{1,0:T(8,128)(2,1)S(1)} %shard_map.83.refs_4_), channel_id=1, source_target_pairs={{1,0},{5,4},{9,8},{13,12},{17,16},{21,20},{25,24},{29,28}} | collective-permute-start | bytes 1572872 | tf_op jit(solution)/shard_map/ppermute | solution.py:453
  91.4 12.8 %collective-permute-start.16 = (bf16[256,1024]{1,0:T(8,128)(2,1)S(1)}, bf16[256,1024]{1,0:T(8,128)(2,1)S(1)}, u32[]{:S(2)}, u32[]{:S(2)}) collective-permute-start(bf16[256,1024]{1,0:T(8,128)(2,1)S(1)} %shard_map.86.refs_0_), channel_id=1, source_target_pairs={{8,0},{12,4},{16,8},{20,12},{24,16},{28,20},{9,1},{13,5},{17,9},{2... | collective-permute-start | bytes 1572872 | tf_op jit(solution)/shard_map/ppermute | solution.py:417
  92.7 14.9 %collective-permute-start.18 = (bf16[256,1024]{1,0:T(8,128)(2,1)S(1)}, bf16[256,1024]{1,0:T(8,128)(2,1)S(1)}, u32[]{:S(2)}, u32[]{:S(2)}) collective-permute-start(bf16[256,1024]{1,0:T(8,128)(2,1)S(1)} %shard_map.86.refs_0_), channel_id=1, source_target_pairs={{4,0},{12,8},{20,16},{28,24},{16,4},{24,12},{5,1},{13,9},{21,17},{... | collective-permute-start | bytes 1572872 | tf_op jit(solution)/shard_map/ppermute | solution.py:438
  104.2 4.9 %collective-permute-start.17 = (bf16[256,1024]{1,0:T(8,128)(2,1)S(1)}, bf16[256,1024]{1,0:T(8,128)(2,1)S(1)}, u32[]{:S(2)}, u32[]{:S(2)}) collective-permute-start(bf16[256,1024]{1,0:T(8,128)(2,1)S(1)} %shard_map.88.refs_5_), channel_id=1, source_target_pairs={{0,4},{4,0},{8,12},{12,8},{16,20},{20,16},{24,28},{28,24},{1,5},{5... | collective-permute-start | bytes 1572872 | tf_op jit(solution)/shard_map/ppermute | solution.py:422

commit v11 on v10

--- a/solution.py
+++ b/solution.py
@@ -34,7 +34,7 @@
     forward = np.concatenate([np.cos(angle), -np.sin(angle)], axis=0)
     high, low = parts_of(forward)
     back_high, back_low = parts_of(forward.T / length)
-    return np.concatenate([high, low], axis=1), np.concatenate([back_high, back_low], axis=1)
+    return np.concatenate([high, low], axis=1), np.concatenate([back_high, back_low], axis=0)
 
 
 def nn(a, b):
@@ -255,8 +255,9 @@
         return k_real * real - k_imag * imag, k_real * imag + k_imag * real
 
     def signal(self, real, imag):
-        real, imag = real.astype(BF16), imag.astype(BF16)
-        return nn(self.back[...], jnp.concatenate([real, imag, real, imag], axis=0))
+        total = jnp.concatenate([real.astype(BF16), imag.astype(BF16)], axis=0)
+        both = nn(self.back[...], total)
+        return both[: self.length] + both[self.length :]
 
     def far_terms(self, acc, chosen, choices):
         for distance in range(1, REACH + 1):
@@ -383,14 +384,14 @@
 
 def own_terms(slot, tabs, facts, pieces, after=()):
     _, back, spectra = tabs
-    shape = pltpu.VMEM((back.shape[0], spectra.shape[2]), F32)
+    shape = pltpu.VMEM((back.shape[0] // 2, spectra.shape[2]), F32)
     body = functools.partial(own_kernel, slot, len(pieces))
     return conv_call(body, tabs, facts, pieces, shape, WHOLE, [], after)
 
 
 def far_terms(slot, count, tabs, facts, arrays, result=None):
     _, back, spectra = tabs
-    length, width = back.shape[0], spectra.shape[2]
+    length, width = back.shape[0] // 2, spectra.shape[2]
     shape = jax.ShapeDtypeStruct((1, 2, length, width), F32)
     spec = pl.BlockSpec((1, 1, length, LANES), lambda c: (0, slot, 0, c))
     scratch = [pltpu.VMEM((2 * length, LANES), F32), pltpu.VMEM((length, LANES), BF16)]

time: 115 us -> 114 us (level)
  the two profiles are of different devices: /device:TPU:1 before, /device:TPU:0 now
where the time goes in v11:
time: 114 us
  waiting for transfers between devices  60.9 us (53%)
  starting transfers between devices  26.6 us (23%)
  Pallas kernels  24.9 us (22%)
    ppermute x12, waiting for transfers between devices, sent(): return (lax.ppermute(up, 'ch', upward), lax.ppermute(down, 'ch', downward))  50.4 us
    ppermute x12, starting transfers between devices, sent(): return (lax.ppermute(up, 'ch', upward), lax.ppermute(down, 'ch', downward))  16.9 us
    pallas_call x4, Pallas kernels, conv_call(): pl.pallas_call(body, grid=(width // LANES,), out_shape=out_shape, in_spec...  10.9 us
    ppermute x2, waiting for transfers between devices, shifted(): lax.ppermute(value, 'ctx', [(source, source + steps) for source in range(...  8.63 us
    pallas_call x1, Pallas kernels, prepare(): pl.pallas_call(functools.partial(prepare_kernel, pairs), grid=(width // L...  7.43 us
    pallas_call x4, Pallas kernels, project(): pl.pallas_call(functools.partial(project_kernel, hops, slot, before is No...  6.54 us
    ppermute x2, starting transfers between devices, shifted(): lax.ppermute(value, 'ctx', [(source, source + steps) for source in range(...  4.72 us
    ppermute x3, starting transfers between devices, core_swapped(): lax.ppermute(value, 'ctx', [(source, source ^ 1) for source in range(coun...  2.99 us
  transfers between devices with their start and end apart: 19, of which 9 were waited for; matrix products, arithmetic and copies ran while one was open for 0% of the time, Pallas kernels for 17%

profile of v11, /device:TPU:0, one launch (start us, length us, event | category | flops | bytes accessed | tf_op | source)
XLA Modules:
  0.0 113.7 jit_solution(7396513825701843520)
XLA Ops:
  0.0 1.1 slice_bitcast_fusion.refs_0_
  1.1 5.0 %collective-permute-start = (bf16[256,1024]{1,0:T(8,128)(2,1)S(1)}, bf16[256,1024]{1,0:T(8,128)(2,1)S(1)}, u32[]{:S(2)}, u32[]{:S(2)}) collective-permute-start(bf16[256,1024]{1,0:T(8,128)(2,1)S(1)} %slice_bitcast_fusion.refs_0_), channel_id=1, source_target_pairs={{0,1},{1,2},{2,3},{4,5},{5,6},{6,7},{8,9},{9,10},{10,11},{12,13},{... | collective-permute-start | bytes 1572872 | tf_op jit(solution)/shard_map/ppermute | solution.py:454
  6.0 1.3 %collective-permute-start.3 = (bf16[256,1024]{1,0:T(8,128)(2,1)S(1)}, bf16[256,1024]{1,0:T(8,128)(2,1)S(1)}, u32[]{:S(2)}, u32[]{:S(2)}) collective-permute-start(bf16[256,1024]{1,0:T(8,128)(2,1)S(1)} %slice_bitcast_fusion.refs_0_), channel_id=1, source_target_pairs={{1,0},{2,1},{3,2},{5,4},{6,5},{7,6},{9,8},{10,9},{11,10},{13,12},{... | collective-permute-start | bytes 1572872 | tf_op jit(solution)/shard_map/ppermute | solution.py:454
  7.4 7.4 %shard_map.73 = (f32[4,512,1024]{2,1,0:T(8,128)S(1)}, bf16[1024,4096]{1,0:T(8,128)(2,1)S(1)}, bf16[1,2,256,1024]{3,2,1,0:T(8,128)(2,1)S(1)}, bf16[256,1024]{1,0:...) custom-call(s32[1]{0:T(128)} %bitcast.refs_0_, ...), custom_call_target="tpu_custom_call" | custom-call | flops 2415919104 | bytes 11534336 | tf_op jit(solution)/shard_map/pallas_call | solution.py:147
  14.8 2.4 %collective-permute-done.refs_0_ = bf16[256,1024]{1,0:T(8,128)(2,1)S(1)} collective-permute-done((bf16[256,1024]{1,0:T(8,128)(2,1)S(1)}, bf16[256,1024]{1,0:T(8,128)(2,1)S(1)}, u32[]{:S(2)}, u32[]{:S(2)}) %collective-permute-start) | collective-permute-done | bytes 524320 | tf_op jit(solution)/shard_map/ppermute | solution.py:454
  17.9 3.5 %collective-permute-done.3.refs_0_ = bf16[256,1024]{1,0:T(8,128)(2,1)S(1)} collective-permute-done((bf16[256,1024]{1,0:T(8,128)(2,1)S(1)}, bf16[256,1024]{1,0:T(8,128)(2,1)S(1)}, u32[]{:S(2)}, u32[]{:S(2)}) %collective-permute-start.3) | collective-permute-done | bytes 524320 | tf_op jit(solution)/shard_map/ppermute | solution.py:454
  21.3 1.3 %collective-permute-start.4 = (bf16[256,1024]{1,0:T(8,128)(2,1)S(1)}, bf16[256,1024]{1,0:T(8,128)(2,1)S(1)}, u32[]{:S(2)}, u32[]{:S(2)}) collective-permute-start(bf16[256,1024]{1,0:T(8,128)(2,1)S(1)} %shard_map.75.refs_2_), channel_id=1, source_target_pairs={{1,0},{2,1},{5,4},{6,5},{9,8},{10,9},{13,12},{14,13},{17,16},{18,1... | collective-permute-start | bytes 1572872 | tf_op jit(solution)/shard_map/ppermute | solution.py:454
  22.6 0.7 collective-permute-start.2
  23.3 12.5 %collective-permute-done.4.refs_4_ = bf16[256,1024]{1,0:T(8,128)(2,1)S(1)} collective-permute-done((bf16[256,1024]{1,0:T(8,128)(2,1)S(1)}, bf16[256,1024]{1,0:T(8,128)(2,1)S(1)}, u32[]{:S(2)}, u32[]{:S(2)}) %collective-permute-start.4) | collective-permute-done | bytes 524320 | tf_op jit(solution)/shard_map/ppermute | solution.py:454
  35.9 1.3 %collective-permute-start.5 = (bf16[256,1024]{1,0:T(8,128)(2,1)S(1)}, bf16[256,1024]{1,0:T(8,128)(2,1)S(1)}, u32[]{:S(2)}, u32[]{:S(2)}) collective-permute-start(bf16[256,1024]{1,0:T(8,128)(2,1)S(1)} %collective-permute-done.4.refs_4_), channel_id=1, source_target_pairs={{1,0},{5,4},{9,8},{13,12},{17,16},{21,20},{25,24},{29,28}} | collective-permute-start | bytes 1572872 | tf_op jit(solution)/shard_map/ppermute | solution.py:454
  37.2 2.3 %shard_map.76.refs_3_.refs_4_ = f32[256,1024]{1,0:T(8,128)S(1)} custom-call(s32[2,8]{1,0:T(2,128)S(4)} %get-tuple-element.15.facts_ref, bf16[256,1024]{1,0:T(8,128)(2,1)S(1)} %slice_bitcast_fusion.refs_0_, bf16[256,1024]{1,0:T(8,128)(2,1)S(1)} %shard_map.74.refs_1_, bf16[256,1024]{1,0:T(8,128)(2,1)S(1)} %shard_map.75.refs_2_, ...), custom_call_target="tpu_custom_call" | custom-call | flops 1610612736 | bytes 13107200 | tf_op jit(solution)/shard_map/pallas_call | solution.py:218
  39.4 10.0 %collective-permute-done.5.refs_2_.refs_1_ = bf16[256,1024]{1,0:T(8,128)(2,1)S(1)} collective-permute-done((bf16[256,1024]{1,0:T(8,128)(2,1)S(1)}, bf16[256,1024]{1,0:T(8,128)(2,1)S(1)}, u32[]{:S(2)}, u32[]{:S(2)}) %collective-permute-start.5) | collective-permute-done | bytes 524320 | tf_op jit(solution)/shard_map/ppermute | solution.py:454
  49.5 1.5 %collective-permute-start.6 = (bf16[256,1024]{1,0:T(8,128)(2,1)S(1)}, bf16[256,1024]{1,0:T(8,128)(2,1)S(1)}, u32[]{:S(2)}, u32[]{:S(2)}) collective-permute-start(bf16[256,1024]{1,0:T(8,128)(2,1)S(1)} %shard_map.77.refs_0_), channel_id=1, source_target_pairs={{0,1},{1,2},{2,3},{4,5},{5,6},{6,7},{8,9},{9,10},{10,11},{12,13},{... | collective-permute-start | bytes 1572872 | tf_op jit(solution)/shard_map/ppermute | solution.py:454
  51.0 1.3 %collective-permute-start.12 = (bf16[256,1024]{1,0:T(8,128)(2,1)S(1)}, bf16[256,1024]{1,0:T(8,128)(2,1)S(1)}, u32[]{:S(2)}, u32[]{:S(2)}) collective-permute-start(bf16[256,1024]{1,0:T(8,128)(2,1)S(1)} %shard_map.77.refs_0_), channel_id=1, source_target_pairs={{1,0},{2,1},{3,2},{5,4},{6,5},{7,6},{9,8},{10,9},{11,10},{13,12},{... | collective-permute-start | bytes 1572872 | tf_op jit(solution)/shard_map/ppermute | solution.py:454
  52.3 0.9 shard_map.78.refs_1_.refs_0_
  53.2 3.4 %collective-permute-start.8 = (bf16[256,1024]{1,0:T(8,128)(2,1)S(1)}, bf16[256,1024]{1,0:T(8,128)(2,1)S(1)}, u32[]{:S(2)}, u32[]{:S(2)}) collective-permute-start(bf16[256,1024]{1,0:T(8,128)(2,1)S(1)} %shard_map.78.refs_1_.refs_0_), channel_id=1, source_target_pairs={{0,8},{4,12},{8,16},{12,20},{16,24},{20,28},{1,9},{5,13},{9,17},{1... | collective-permute-start | bytes 1572872 | tf_op jit(solution)/shard_map/ppermute | solution.py:418
  57.3 2.9 %collective-permute-start.9 = (bf16[256,1024]{1,0:T(8,128)(2,1)S(1)}, bf16[256,1024]{1,0:T(8,128)(2,1)S(1)}, u32[]{:S(2)}, u32[]{:S(2)}) collective-permute-start(bf16[256,1024]{1,0:T(8,128)(2,1)S(1)} %shard_map.78.refs_1_.refs_0_), channel_id=1, source_target_pairs={{0,4},{4,0},{8,12},{12,8},{16,20},{20,16},{24,28},{28,24},{1,5},{5... | collective-permute-start | bytes 1572872 | tf_op jit(solution)/shard_map/ppermute | solution.py:423
  60.9 2.6 %collective-permute-done.12.refs_0_ = bf16[256,1024]{1,0:T(8,128)(2,1)S(1)} collective-permute-done((bf16[256,1024]{1,0:T(8,128)(2,1)S(1)}, bf16[256,1024]{1,0:T(8,128)(2,1)S(1)}, u32[]{:S(2)}, u32[]{:S(2)}) %collective-permute-start.12) | collective-permute-done | bytes 524320 | tf_op jit(solution)/shard_map/ppermute | solution.py:454
  63.5 1.3 %collective-permute-start.13 = (bf16[256,1024]{1,0:T(8,128)(2,1)S(1)}, bf16[256,1024]{1,0:T(8,128)(2,1)S(1)}, u32[]{:S(2)}, u32[]{:S(2)}) collective-permute-start(bf16[256,1024]{1,0:T(8,128)(2,1)S(1)} %shard_map.82.refs_2_), channel_id=1, source_target_pairs={{1,0},{2,1},{5,4},{6,5},{9,8},{10,9},{13,12},{14,13},{17,16},{18,1... | collective-permute-start | bytes 1572872 | tf_op jit(solution)/shard_map/ppermute | solution.py:454
  64.9 2.5 %shard_map.80.refs_1_.refs_0_ = f32[256,1024]{1,0:T(8,128)S(1)} custom-call(s32[2,8]{1,0:T(2,128)S(4)} %get-tuple-element.15.facts_ref, bf16[512,256]{1,0:T(8,128)(2,1)S(1)} %get-tuple-element.16.table_ref, bf16[512,512]{1,0:T(8,128)(2,1)S(1)} %get-tuple-element.17.back_ref, f32[4,512,1024]{2,1,0:T(8,128)S(1)} %get-tuple-element.18.spec_ref, ...), custom_call_target="tpu_custom_call" | custom-call | flops 2147483648 | bytes 1048576 | tf_op jit(solution)/shard_map/pallas_call | solution.py:368
  68.2 9.8 %collective-permute-done.13.refs_0_ = bf16[256,1024]{1,0:T(8,128)(2,1)S(1)} collective-permute-done((bf16[256,1024]{1,0:T(8,128)(2,1)S(1)}, bf16[256,1024]{1,0:T(8,128)(2,1)S(1)}, u32[]{:S(2)}, u32[]{:S(2)}) %collective-permute-start.13) | collective-permute-done | bytes 524320 | tf_op jit(solution)/shard_map/ppermute | solution.py:454
  78.0 1.3 %collective-permute-start.14 = (bf16[256,1024]{1,0:T(8,128)(2,1)S(1)}, bf16[256,1024]{1,0:T(8,128)(2,1)S(1)}, u32[]{:S(2)}, u32[]{:S(2)}) collective-permute-start(bf16[256,1024]{1,0:T(8,128)(2,1)S(1)} %shard_map.83.refs_4_), channel_id=1, source_target_pairs={{1,0},{5,4},{9,8},{13,12},{17,16},{21,20},{25,24},{29,28}} | collective-permute-start | bytes 1572872 | tf_op jit(solution)/shard_map/ppermute | solution.py:454
  79.3 2.3 %shard_map.84.refs_4_ = f32[256,1024]{1,0:T(8,128)S(1)} custom-call(s32[2,8]{1,0:T(2,128)S(4)} %get-tuple-element.15.facts_ref, bf16[256,1024]{1,0:T(8,128)(2,1)S(1)} %shard_map.77.refs_0_, bf16[256,1024]{1,0:T(8,128)(2,1)S(1)} %shard_map.79.refs_1_, bf16[256,1024]{1,0:T(8,128)(2,1)S(1)} %shard_map.82.refs_2_, bf16[256,1024]{1,0:T(8,128)(2,1)S(1)} %shard_map.81.refs_3_, ...), custom_call_target="tpu_custom_call" | custom-call | flops 1610612736 | bytes 13107200 | tf_op jit(solution)/shard_map/pallas_call | solution.py:218
  81.6 1.6 %shard_map.85 = (f32[1,2,256,1024]{3,2,1,0:T(8,128)}, f32[8,128]{1,0:T(8,128)S(1)}) custom-call(s32[2,8]{1,0:T(2,128)S(4)} %get-tuple-element.15.facts_ref, bf16[512,256]{1,0:T(8,128)(2,1)S(1)} %get-tuple-element.16.table_ref, bf16[512,512]{1,0:T(8,128)(2,1)S(1)} %get-tuple-element.17.back_ref, f32[4,512,1024]{2,1,0:T(8,128)S(1)} %get-tuple-element.18.spec_ref, ...), custom_call_target="tpu_custom_call" | custom-call | flops 2147483648 | bytes 1048576 | tf_op jit(solution)/shard_map/pallas_call | solution.py:368
  83.2 9.5 %collective-permute-done.14.refs_1_ = bf16[256,1024]{1,0:T(8,128)(2,1)S(1)} collective-permute-done((bf16[256,1024]{1,0:T(8,128)(2,1)S(1)}, bf16[256,1024]{1,0:T(8,128)(2,1)S(1)}, u32[]{:S(2)}, u32[]{:S(2)}) %collective-permute-start.14) | collective-permute-done | bytes 524320 | tf_op jit(solution)/shard_map/ppermute | solution.py:454
  92.7 1.1 shard_map.86.refs_0_
  93.8 1.3 %collective-permute-start.16 = (bf16[256,1024]{1,0:T(8,128)(2,1)S(1)}, bf16[256,1024]{1,0:T(8,128)(2,1)S(1)}, u32[]{:S(2)}, u32[]{:S(2)}) collective-permute-start(bf16[256,1024]{1,0:T(8,128)(2,1)S(1)} %shard_map.86.refs_0_), channel_id=1, source_target_pairs={{8,0},{12,4},{16,8},{20,12},{24,16},{28,20},{9,1},{13,5},{17,9},{2... | collective-permute-start | bytes 1572872 | tf_op jit(solution)/shard_map/ppermute | solution.py:418
  95.1 1.3 %collective-permute-start.18 = (bf16[256,1024]{1,0:T(8,128)(2,1)S(1)}, bf16[256,1024]{1,0:T(8,128)(2,1)S(1)}, u32[]{:S(2)}, u32[]{:S(2)}) collective-permute-start(bf16[256,1024]{1,0:T(8,128)(2,1)S(1)} %shard_map.86.refs_0_), channel_id=1, source_target_pairs={{4,0},{12,8},{20,16},{28,24},{16,4},{24,12},{5,1},{13,9},{21,17},{... | collective-permute-start | bytes 1572872 | tf_op jit(solution)/shard_map/ppermute | solution.py:439
  96.4 2.5 %shard_map.87.refs_1_.refs_0_ = f32[256,1024]{1,0:T(8,128)S(1)} custom-call(s32[2,8]{1,0:T(2,128)S(4)} %get-tuple-element.15.facts_ref, bf16[512,256]{1,0:T(8,128)(2,1)S(1)} %get-tuple-element.16.table_ref, bf16[512,512]{1,0:T(8,128)(2,1)S(1)} %get-tuple-element.17.back_ref, f32[4,512,1024]{2,1,0:T(8,128)S(1)} %get-tuple-element.18.spec_ref, ...), custom_call_target="tpu_custom_call" | custom-call | flops 2147483648 | bytes 1048576 | tf_op jit(solution)/shard_map/pallas_call | solution.py:368
  98.9 8.6 %collective-permute-done.16.refs_0_ = bf16[256,1024]{1,0:T(8,128)(2,1)S(1)} collective-permute-done((bf16[256,1024]{1,0:T(8,128)(2,1)S(1)}, bf16[256,1024]{1,0:T(8,128)(2,1)S(1)}, u32[]{:S(2)}, u32[]{:S(2)}) %collective-permute-start.16) | collective-permute-done | bytes 524320 | tf_op jit(solution)/shard_map/ppermute | solution.py:418
  107.6 1.9 %collective-permute-done.17.refs_6_ = bf16[256,1024]{1,0:T(8,128)(2,1)S(1)} collective-permute-done((bf16[256,1024]{1,0:T(8,128)(2,1)S(1)}, bf16[256,1024]{1,0:T(8,128)(2,1)S(1)}, u32[]{:S(2)}, u32[]{:S(2)}) %collective-permute-start.17) | collective-permute-done | bytes 524320 | tf_op jit(solution)/shard_map/ppermute | solution.py:423
  109.5 4.2 %shard_map.89 = f32[1,2,256,1024]{3,2,1,0:T(8,128)} custom-call(s32[2,8]{1,0:T(2,128)S(4)} %get-tuple-element.15.facts_ref, bf16[512,256]{1,0:T(8,128)(2,1)S(1)} %get-tuple-element.16.table_ref, bf16[512,512]{1,0:T(8,128)(2,1)S(1)} %get-tuple-element.17.back_ref, f32[4,512,1024]{2,1,0:T(8,128)S(1)} %get-tuple-element.18.spec_ref, ...), custom_call_target="tpu_custom_call", output_to_operand_aliasing={{}: (12, {})} | custom-call | flops 2147483648 | bytes 1048576 | tf_op jit(solution)/shard_map/pallas_call | solution.py:368
  (24 shorter events, 2.9 us)
Async XLA Ops:
  1.1 16.1 %collective-permute-start = (bf16[256,1024]{1,0:T(8,128)(2,1)S(1)}, bf16[256,1024]{1,0:T(8,128)(2,1)S(1)}, u32[]{:S(2)}, u32[]{:S(2)}) collective-permute-start(bf16[256,1024]{1,0:T(8,128)(2,1)S(1)} %slice_bitcast_fusion.refs_0_), channel_id=1, source_target_pairs={{0,1},{1,2},{2,3},{4,5},{5,6},{6,7},{8,9},{9,10},{10,11},{12,13},{... | collective-permute-start | bytes 1572872 | tf_op jit(solution)/shard_map/ppermute | solution.py:454
  6.0 15.3 %collective-permute-start.3 = (bf16[256,1024]{1,0:T(8,128)(2,1)S(1)}, bf16[256,1024]{1,0:T(8,128)(2,1)S(1)}, u32[]{:S(2)}, u32[]{:S(2)}) collective-permute-start(bf16[256,1024]{1,0:T(8,128)(2,1)S(1)} %slice_bitcast_fusion.refs_0_), channel_id=1, source_target_pairs={{1,0},{2,1},{3,2},{5,4},{6,5},{7,6},{9,8},{10,9},{11,10},{13,12},{... | collective-permute-start | bytes 1572872 | tf_op jit(solution)/shard_map/ppermute | solution.py:454
  17.2 5.4 %collective-permute-start.1 = (bf16[256,1024]{1,0:T(8,128)(2,1)S(1)}, bf16[256,1024]{1,0:T(8,128)(2,1)S(1)}, u32[]{:S(2)}, u32[]{:S(2)}) collective-permute-start(bf16[256,1024]{1,0:T(8,128)(2,1)S(1)} %shard_map.74.refs_1_), channel_id=1, source_target_pairs={{1,2},{2,3},{5,6},{6,7},{9,10},{10,11},{13,14},{14,15},{17,18},{18... | collective-permute-start | bytes 1572872 | tf_op jit(solution)/shard_map/ppermute | solution.py:454
  21.3 14.5 %collective-permute-start.4 = (bf16[256,1024]{1,0:T(8,128)(2,1)S(1)}, bf16[256,1024]{1,0:T(8,128)(2,1)S(1)}, u32[]{:S(2)}, u32[]{:S(2)}) collective-permute-start(bf16[256,1024]{1,0:T(8,128)(2,1)S(1)} %shard_map.75.refs_2_), channel_id=1, source_target_pairs={{1,0},{2,1},{5,4},{6,5},{9,8},{10,9},{13,12},{14,13},{17,16},{18,1... | collective-permute-start | bytes 1572872 | tf_op jit(solution)/shard_map/ppermute | solution.py:454
  22.6 16.8 %collective-permute-start.2 = (bf16[256,1024]{1,0:T(8,128)(2,1)S(1)}, bf16[256,1024]{1,0:T(8,128)(2,1)S(1)}, u32[]{:S(2)}, u32[]{:S(2)}) collective-permute-start(bf16[256,1024]{1,0:T(8,128)(2,1)S(1)} %collective-permute-done.1.refs_3_), channel_id=1, source_target_pairs={{2,3},{6,7},{10,11},{14,15},{18,19},{22,23},{26,27},{30,31}} | collective-permute-start | bytes 1572872 | tf_op jit(solution)/shard_map/ppermute | solution.py:454
  35.9 13.6 %collective-permute-start.5 = (bf16[256,1024]{1,0:T(8,128)(2,1)S(1)}, bf16[256,1024]{1,0:T(8,128)(2,1)S(1)}, u32[]{:S(2)}, u32[]{:S(2)}) collective-permute-start(bf16[256,1024]{1,0:T(8,128)(2,1)S(1)} %collective-permute-done.4.refs_4_), channel_id=1, source_target_pairs={{1,0},{5,4},{9,8},{13,12},{17,16},{21,20},{25,24},{29,28}} | collective-permute-start | bytes 1572872 | tf_op jit(solution)/shard_map/ppermute | solution.py:454
  49.5 10.7 %collective-permute-start.6 = (bf16[256,1024]{1,0:T(8,128)(2,1)S(1)}, bf16[256,1024]{1,0:T(8,128)(2,1)S(1)}, u32[]{:S(2)}, u32[]{:S(2)}) collective-permute-start(bf16[256,1024]{1,0:T(8,128)(2,1)S(1)} %shard_map.77.refs_0_), channel_id=1, source_target_pairs={{0,1},{1,2},{2,3},{4,5},{5,6},{6,7},{8,9},{9,10},{10,11},{12,13},{... | collective-permute-start | bytes 1572872 | tf_op jit(solution)/shard_map/ppermute | solution.py:454
  51.0 12.5 %collective-permute-start.12 = (bf16[256,1024]{1,0:T(8,128)(2,1)S(1)}, bf16[256,1024]{1,0:T(8,128)(2,1)S(1)}, u32[]{:S(2)}, u32[]{:S(2)}) collective-permute-start(bf16[256,1024]{1,0:T(8,128)(2,1)S(1)} %shard_map.77.refs_0_), channel_id=1, source_target_pairs={{1,0},{2,1},{3,2},{5,4},{6,5},{7,6},{9,8},{10,9},{11,10},{13,12},{... | collective-permute-start | bytes 1572872 | tf_op jit(solution)/shard_map/ppermute | solution.py:454
  53.2 11.6 %collective-permute-start.8 = (bf16[256,1024]{1,0:T(8,128)(2,1)S(1)}, bf16[256,1024]{1,0:T(8,128)(2,1)S(1)}, u32[]{:S(2)}, u32[]{:S(2)}) collective-permute-start(bf16[256,1024]{1,0:T(8,128)(2,1)S(1)} %shard_map.78.refs_1_.refs_0_), channel_id=1, source_target_pairs={{0,8},{4,12},{8,16},{12,20},{16,24},{20,28},{1,9},{5,13},{9,17},{1... | collective-permute-start | bytes 1572872 | tf_op jit(solution)/shard_map/ppermute | solution.py:418
  56.6 10.8 %collective-permute-start.10 = (bf16[256,1024]{1,0:T(8,128)(2,1)S(1)}, bf16[256,1024]{1,0:T(8,128)(2,1)S(1)}, u32[]{:S(2)}, u32[]{:S(2)}) collective-permute-start(bf16[256,1024]{1,0:T(8,128)(2,1)S(1)} %shard_map.78.refs_1_.refs_0_), channel_id=1, source_target_pairs={{4,16},{12,24},{28,20},{5,17},{13,25},{29,21},{6,18},{14,26},{30,2... | collective-permute-start | bytes 1572872 | tf_op jit(solution)/shard_map/ppermute | solution.py:430
  57.3 10.1 %collective-permute-start.9 = (bf16[256,1024]{1,0:T(8,128)(2,1)S(1)}, bf16[256,1024]{1,0:T(8,128)(2,1)S(1)}, u32[]{:S(2)}, u32[]{:S(2)}) collective-permute-start(bf16[256,1024]{1,0:T(8,128)(2,1)S(1)} %shard_map.78.refs_1_.refs_0_), channel_id=1, source_target_pairs={{0,4},{4,0},{8,12},{12,8},{16,20},{20,16},{24,28},{28,24},{1,5},{5... | collective-permute-start | bytes 1572872 | tf_op jit(solution)/shard_map/ppermute | solution.py:423
  60.2 7.2 %collective-permute-start.7 = (bf16[256,1024]{1,0:T(8,128)(2,1)S(1)}, bf16[256,1024]{1,0:T(8,128)(2,1)S(1)}, u32[]{:S(2)}, u32[]{:S(2)}) collective-permute-start(bf16[256,1024]{1,0:T(8,128)(2,1)S(1)} %shard_map.79.refs_1_), channel_id=1, source_target_pairs={{1,2},{2,3},{5,6},{6,7},{9,10},{10,11},{13,14},{14,15},{17,18},{18... | collective-permute-start | bytes 1572872 | tf_op jit(solution)/shard_map/ppermute | solution.py:454
  63.5 14.5 %collective-permute-start.13 = (bf16[256,1024]{1,0:T(8,128)(2,1)S(1)}, bf16[256,1024]{1,0:T(8,128)(2,1)S(1)}, u32[]{:S(2)}, u32[]{:S(2)}) collective-permute-start(bf16[256,1024]{1,0:T(8,128)(2,1)S(1)} %shard_map.82.refs_2_), channel_id=1, source_target_pairs={{1,0},{2,1},{5,4},{6,5},{9,8},{10,9},{13,12},{14,13},{17,16},{18,1... | collective-permute-start | bytes 1572872 | tf_op jit(solution)/shard_map/ppermute | solution.py:454
  64.8 16.8 %collective-permute-start.15 = (bf16[256,1024]{1,0:T(8,128)(2,1)S(1)}, bf16[256,1024]{1,0:T(8,128)(2,1)S(1)}, u32[]{:S(2)}, u32[]{:S(2)}) collective-permute-start(bf16[256,1024]{1,0:T(8,128)(2,1)S(1)} %collective-permute-done.8.refs_2_.refs_1_.refs_3_), channel_id=1, source_target_pairs={{0,4},{4,0},{8,12},{12,8},{16,20},{20,16},{24,28},{28,24},{1,5},{5... | collective-permute-start | bytes 1572872 | tf_op jit(solution)/shard_map/ppermute | solution.py:423
  67.5 15.7 %collective-permute-start.11 = (bf16[256,1024]{1,0:T(8,128)(2,1)S(1)}, bf16[256,1024]{1,0:T(8,128)(2,1)S(1)}, u32[]{:S(2)}, u32[]{:S(2)}) collective-permute-start(bf16[256,1024]{1,0:T(8,128)(2,1)S(1)} %shard_map.81.refs_3_), channel_id=1, source_target_pairs={{2,3},{6,7},{10,11},{14,15},{18,19},{22,23},{26,27},{30,31}} | collective-permute-start | bytes 1572872 | tf_op jit(solution)/shard_map/ppermute | solution.py:454
  78.0 14.7 %collective-permute-start.14 = (bf16[256,1024]{1,0:T(8,128)(2,1)S(1)}, bf16[256,1024]{1,0:T(8,128)(2,1)S(1)}, u32[]{:S(2)}, u32[]{:S(2)}) collective-permute-start(bf16[256,1024]{1,0:T(8,128)(2,1)S(1)} %shard_map.83.refs_4_), channel_id=1, source_target_pairs={{1,0},{5,4},{9,8},{13,12},{17,16},{21,20},{25,24},{29,28}} | collective-permute-start | bytes 1572872 | tf_op jit(solution)/shard_map/ppermute | solution.py:454
  93.8 13.8 %collective-permute-start.16 = (bf16[256,1024]{1,0:T(8,128)(2,1)S(1)}, bf16[256,1024]{1,0:T(8,128)(2,1)S(1)}, u32[]{:S(2)}, u32[]{:S(2)}) collective-permute-start(bf16[256,1024]{1,0:T(8,128)(2,1)S(1)} %shard_map.86.refs_0_), channel_id=1, source_target_pairs={{8,0},{12,4},{16,8},{20,12},{24,16},{28,20},{9,1},{13,5},{17,9},{2... | collective-permute-start | bytes 1572872 | tf_op jit(solution)/shard_map/ppermute | solution.py:418
  95.1 12.5 %collective-permute-start.18 = (bf16[256,1024]{1,0:T(8,128)(2,1)S(1)}, bf16[256,1024]{1,0:T(8,128)(2,1)S(1)}, u32[]{:S(2)}, u32[]{:S(2)}) collective-permute-start(bf16[256,1024]{1,0:T(8,128)(2,1)S(1)} %shard_map.86.refs_0_), channel_id=1, source_target_pairs={{4,0},{12,8},{20,16},{28,24},{16,4},{24,12},{5,1},{13,9},{21,17},{... | collective-permute-start | bytes 1572872 | tf_op jit(solution)/shard_map/ppermute | solution.py:439
  107.6 1.9 %collective-permute-start.17 = (bf16[256,1024]{1,0:T(8,128)(2,1)S(1)}, bf16[256,1024]{1,0:T(8,128)(2,1)S(1)}, u32[]{:S(2)}, u32[]{:S(2)}) collective-permute-start(bf16[256,1024]{1,0:T(8,128)(2,1)S(1)} %shard_map.88.refs_5_), channel_id=1, source_target_pairs={{0,4},{4,0},{8,12},{12,8},{16,20},{20,16},{24,28},{28,24},{1,5},{5... | collective-permute-start | bytes 1572872 | tf_op jit(solution)/shard_map/ppermute | solution.py:423

commit v12 on v11

--- a/solution.py
+++ b/solution.py
@@ -11,7 +11,7 @@
 from jax.sharding import PartitionSpec as P
 
 REACH = 3
-LANES = 256
+LANES = 512
 VMEM = 20 * 1024 * 1024
 F32 = jnp.float32
 BF16 = jnp.bfloat16

time: 114 us -> 113 us (level)
  Pallas kernels: 24.9 us -> 21.5 us
  waiting for transfers between devices: 60.9 us -> 63.5 us
    pallas_call x1, Pallas kernels: 7.43 us -> 5.59 us  [prepare(): pl.pallas_call(functools.partial(prepare_kernel, pairs), grid=(width // L...]
    ppermute x12, waiting for transfers between devices: 50.4 us -> 52 us  [sent(): return (lax.ppermute(up, 'ch', upward), lax.ppermute(down, 'ch', downward))]
    pallas_call x4, Pallas kernels: 10.9 us -> 9.32 us  [conv_call(): pl.pallas_call(body, grid=(width // LANES,), out_shape=out_shape, in_spec...]
  transfers between devices with their start and end apart: 19 -> 19, of which waited for: 9 -> 9; matrix products, arithmetic and copies ran while one was open for 0% -> 0% of each run, Pallas kernels for 17% -> 15%
where the time goes in v12:
time: 113 us
  waiting for transfers between devices  63.5 us (56%)
  starting transfers between devices  26.6 us (24%)
  Pallas kernels  21.5 us (19%)
    ppermute x12, waiting for transfers between devices, sent(): return (lax.ppermute(up, 'ch', upward), lax.ppermute(down, 'ch', downward))  52 us
    ppermute x12, starting transfers between devices, sent(): return (lax.ppermute(up, 'ch', upward), lax.ppermute(down, 'ch', downward))  16.9 us
    ppermute x2, waiting for transfers between devices, shifted(): lax.ppermute(value, 'ctx', [(source, source + steps) for source in range(...  9.58 us
    pallas_call x4, Pallas kernels, conv_call(): pl.pallas_call(body, grid=(width // LANES,), out_shape=out_shape, in_spec...  9.32 us
    pallas_call x4, Pallas kernels, project(): pl.pallas_call(functools.partial(project_kernel, hops, slot, before is No...  6.53 us
    pallas_call x1, Pallas kernels, prepare(): pl.pallas_call(functools.partial(prepare_kernel, pairs), grid=(width // L...  5.59 us
    ppermute x2, starting transfers between devices, shifted(): lax.ppermute(value, 'ctx', [(source, source + steps) for source in range(...  4.72 us
    ppermute x3, starting transfers between devices, core_swapped(): lax.ppermute(value, 'ctx', [(source, source ^ 1) for source in range(coun...  2.99 us
  transfers between devices with their start and end apart: 19, of which 9 were waited for; matrix products, arithmetic and copies ran while one was open for 0% of the time, Pallas kernels for 15%

profile of v12, /device:TPU:0, one launch (start us, length us, event | category | flops | bytes accessed | tf_op | source)
XLA Modules:
  0.0 112.9 jit_solution(8353203943919532833)
XLA Ops:
  0.0 1.1 slice_bitcast_fusion.refs_0_
  1.1 5.0 %collective-permute-start = (bf16[256,1024]{1,0:T(8,128)(2,1)S(1)}, bf16[256,1024]{1,0:T(8,128)(2,1)S(1)}, u32[]{:S(2)}, u32[]{:S(2)}) collective-permute-start(bf16[256,1024]{1,0:T(8,128)(2,1)S(1)} %slice_bitcast_fusion.refs_0_), channel_id=1, source_target_pairs={{0,1},{1,2},{2,3},{4,5},{5,6},{6,7},{8,9},{9,10},{10,11},{12,13},{... | collective-permute-start | bytes 1572872 | tf_op jit(solution)/shard_map/ppermute | solution.py:454
  6.0 1.3 %collective-permute-start.3 = (bf16[256,1024]{1,0:T(8,128)(2,1)S(1)}, bf16[256,1024]{1,0:T(8,128)(2,1)S(1)}, u32[]{:S(2)}, u32[]{:S(2)}) collective-permute-start(bf16[256,1024]{1,0:T(8,128)(2,1)S(1)} %slice_bitcast_fusion.refs_0_), channel_id=1, source_target_pairs={{1,0},{2,1},{3,2},{5,4},{6,5},{7,6},{9,8},{10,9},{11,10},{13,12},{... | collective-permute-start | bytes 1572872 | tf_op jit(solution)/shard_map/ppermute | solution.py:454
  7.4 5.6 %shard_map.73 = (f32[4,512,1024]{2,1,0:T(8,128)S(1)}, bf16[1024,4096]{1,0:T(8,128)(2,1)S(1)}, bf16[1,2,256,1024]{3,2,1,0:T(8,128)(2,1)S(1)}, bf16[256,1024]{1,0:...) custom-call(s32[1]{0:T(128)} %bitcast.refs_0_, ...), custom_call_target="tpu_custom_call" | custom-call | flops 2415919104 | bytes 11534336 | tf_op jit(solution)/shard_map/pallas_call | solution.py:147
  13.0 4.2 %collective-permute-done.refs_0_ = bf16[256,1024]{1,0:T(8,128)(2,1)S(1)} collective-permute-done((bf16[256,1024]{1,0:T(8,128)(2,1)S(1)}, bf16[256,1024]{1,0:T(8,128)(2,1)S(1)}, u32[]{:S(2)}, u32[]{:S(2)}) %collective-permute-start) | collective-permute-done | bytes 524320 | tf_op jit(solution)/shard_map/ppermute | solution.py:454
  17.9 3.5 %collective-permute-done.3.refs_0_ = bf16[256,1024]{1,0:T(8,128)(2,1)S(1)} collective-permute-done((bf16[256,1024]{1,0:T(8,128)(2,1)S(1)}, bf16[256,1024]{1,0:T(8,128)(2,1)S(1)}, u32[]{:S(2)}, u32[]{:S(2)}) %collective-permute-start.3) | collective-permute-done | bytes 524320 | tf_op jit(solution)/shard_map/ppermute | solution.py:454
  21.3 1.3 %collective-permute-start.4 = (bf16[256,1024]{1,0:T(8,128)(2,1)S(1)}, bf16[256,1024]{1,0:T(8,128)(2,1)S(1)}, u32[]{:S(2)}, u32[]{:S(2)}) collective-permute-start(bf16[256,1024]{1,0:T(8,128)(2,1)S(1)} %shard_map.75.refs_2_), channel_id=1, source_target_pairs={{1,0},{2,1},{5,4},{6,5},{9,8},{10,9},{13,12},{14,13},{17,16},{18,1... | collective-permute-start | bytes 1572872 | tf_op jit(solution)/shard_map/ppermute | solution.py:454
  23.3 12.5 %collective-permute-done.4.refs_4_ = bf16[256,1024]{1,0:T(8,128)(2,1)S(1)} collective-permute-done((bf16[256,1024]{1,0:T(8,128)(2,1)S(1)}, bf16[256,1024]{1,0:T(8,128)(2,1)S(1)}, u32[]{:S(2)}, u32[]{:S(2)}) %collective-permute-start.4) | collective-permute-done | bytes 524320 | tf_op jit(solution)/shard_map/ppermute | solution.py:454
  35.9 1.3 %collective-permute-start.5 = (bf16[256,1024]{1,0:T(8,128)(2,1)S(1)}, bf16[256,1024]{1,0:T(8,128)(2,1)S(1)}, u32[]{:S(2)}, u32[]{:S(2)}) collective-permute-start(bf16[256,1024]{1,0:T(8,128)(2,1)S(1)} %collective-permute-done.4.refs_4_), channel_id=1, source_target_pairs={{1,0},{5,4},{9,8},{13,12},{17,16},{21,20},{25,24},{29,28}} | collective-permute-start | bytes 1572872 | tf_op jit(solution)/shard_map/ppermute | solution.py:454
  37.2 2.3 %shard_map.76.refs_3_.refs_4_ = f32[256,1024]{1,0:T(8,128)S(1)} custom-call(s32[2,8]{1,0:T(2,128)S(4)} %get-tuple-element.15.facts_ref, bf16[256,1024]{1,0:T(8,128)(2,1)S(1)} %slice_bitcast_fusion.refs_0_, bf16[256,1024]{1,0:T(8,128)(2,1)S(1)} %shard_map.74.refs_1_, bf16[256,1024]{1,0:T(8,128)(2,1)S(1)} %shard_map.75.refs_2_, ...), custom_call_target="tpu_custom_call" | custom-call | flops 1610612736 | bytes 13107200 | tf_op jit(solution)/shard_map/pallas_call | solution.py:218
  39.4 10.0 %collective-permute-done.5.refs_2_.refs_1_ = bf16[256,1024]{1,0:T(8,128)(2,1)S(1)} collective-permute-done((bf16[256,1024]{1,0:T(8,128)(2,1)S(1)}, bf16[256,1024]{1,0:T(8,128)(2,1)S(1)}, u32[]{:S(2)}, u32[]{:S(2)}) %collective-permute-start.5) | collective-permute-done | bytes 524320 | tf_op jit(solution)/shard_map/ppermute | solution.py:454
  49.5 1.5 %collective-permute-start.6 = (bf16[256,1024]{1,0:T(8,128)(2,1)S(1)}, bf16[256,1024]{1,0:T(8,128)(2,1)S(1)}, u32[]{:S(2)}, u32[]{:S(2)}) collective-permute-start(bf16[256,1024]{1,0:T(8,128)(2,1)S(1)} %shard_map.77.refs_0_), channel_id=1, source_target_pairs={{0,1},{1,2},{2,3},{4,5},{5,6},{6,7},{8,9},{9,10},{10,11},{12,13},{... | collective-permute-start | bytes 1572872 | tf_op jit(solution)/shard_map/ppermute | solution.py:454
  51.0 1.3 %collective-permute-start.12 = (bf16[256,1024]{1,0:T(8,128)(2,1)S(1)}, bf16[256,1024]{1,0:T(8,128)(2,1)S(1)}, u32[]{:S(2)}, u32[]{:S(2)}) collective-permute-start(bf16[256,1024]{1,0:T(8,128)(2,1)S(1)} %shard_map.77.refs_0_), channel_id=1, source_target_pairs={{1,0},{2,1},{3,2},{5,4},{6,5},{7,6},{9,8},{10,9},{11,10},{13,12},{... | collective-permute-start | bytes 1572872 | tf_op jit(solution)/shard_map/ppermute | solution.py:454
  52.3 0.9 shard_map.78.refs_1_.refs_0_
  53.2 3.4 %collective-permute-start.8 = (bf16[256,1024]{1,0:T(8,128)(2,1)S(1)}, bf16[256,1024]{1,0:T(8,128)(2,1)S(1)}, u32[]{:S(2)}, u32[]{:S(2)}) collective-permute-start(bf16[256,1024]{1,0:T(8,128)(2,1)S(1)} %shard_map.78.refs_1_.refs_0_), channel_id=1, source_target_pairs={{0,8},{4,12},{8,16},{12,20},{16,24},{20,28},{1,9},{5,13},{9,17},{1... | collective-permute-start | bytes 1572872 | tf_op jit(solution)/shard_map/ppermute | solution.py:418
  56.6 0.7 collective-permute-start.10
  57.3 2.9 %collective-permute-start.9 = (bf16[256,1024]{1,0:T(8,128)(2,1)S(1)}, bf16[256,1024]{1,0:T(8,128)(2,1)S(1)}, u32[]{:S(2)}, u32[]{:S(2)}) collective-permute-start(bf16[256,1024]{1,0:T(8,128)(2,1)S(1)} %shard_map.78.refs_1_.refs_0_), channel_id=1, source_target_pairs={{0,4},{4,0},{8,12},{12,8},{16,20},{20,16},{24,28},{28,24},{1,5},{5... | collective-permute-start | bytes 1572872 | tf_op jit(solution)/shard_map/ppermute | solution.py:423
  60.9 2.6 %collective-permute-done.12.refs_0_ = bf16[256,1024]{1,0:T(8,128)(2,1)S(1)} collective-permute-done((bf16[256,1024]{1,0:T(8,128)(2,1)S(1)}, bf16[256,1024]{1,0:T(8,128)(2,1)S(1)}, u32[]{:S(2)}, u32[]{:S(2)}) %collective-permute-start.12) | collective-permute-done | bytes 524320 | tf_op jit(solution)/shard_map/ppermute | solution.py:454
  63.5 1.3 %collective-permute-start.13 = (bf16[256,1024]{1,0:T(8,128)(2,1)S(1)}, bf16[256,1024]{1,0:T(8,128)(2,1)S(1)}, u32[]{:S(2)}, u32[]{:S(2)}) collective-permute-start(bf16[256,1024]{1,0:T(8,128)(2,1)S(1)} %shard_map.82.refs_2_), channel_id=1, source_target_pairs={{1,0},{2,1},{5,4},{6,5},{9,8},{10,9},{13,12},{14,13},{17,16},{18,1... | collective-permute-start | bytes 1572872 | tf_op jit(solution)/shard_map/ppermute | solution.py:454
  64.9 3.1 %shard_map.80.refs_1_.refs_0_ = f32[256,1024]{1,0:T(8,128)S(1)} custom-call(s32[2,8]{1,0:T(2,128)S(4)} %get-tuple-element.15.facts_ref, bf16[512,256]{1,0:T(8,128)(2,1)S(1)} %get-tuple-element.16.table_ref, bf16[512,512]{1,0:T(8,128)(2,1)S(1)} %get-tuple-element.17.back_ref, f32[4,512,1024]{2,1,0:T(8,128)S(1)} %get-tuple-element.18.spec_ref, ...), custom_call_target="tpu_custom_call" | custom-call | flops 2147483648 | bytes 1048576 | tf_op jit(solution)/shard_map/pallas_call | solution.py:368
  68.7 9.3 %collective-permute-done.13.refs_0_ = bf16[256,1024]{1,0:T(8,128)(2,1)S(1)} collective-permute-done((bf16[256,1024]{1,0:T(8,128)(2,1)S(1)}, bf16[256,1024]{1,0:T(8,128)(2,1)S(1)}, u32[]{:S(2)}, u32[]{:S(2)}) %collective-permute-start.13) | collective-permute-done | bytes 524320 | tf_op jit(solution)/shard_map/ppermute | solution.py:454
  78.0 1.3 %collective-permute-start.14 = (bf16[256,1024]{1,0:T(8,128)(2,1)S(1)}, bf16[256,1024]{1,0:T(8,128)(2,1)S(1)}, u32[]{:S(2)}, u32[]{:S(2)}) collective-permute-start(bf16[256,1024]{1,0:T(8,128)(2,1)S(1)} %shard_map.83.refs_4_), channel_id=1, source_target_pairs={{1,0},{5,4},{9,8},{13,12},{17,16},{21,20},{25,24},{29,28}} | collective-permute-start | bytes 1572872 | tf_op jit(solution)/shard_map/ppermute | solution.py:454
  79.3 2.4 %shard_map.84.refs_4_ = f32[256,1024]{1,0:T(8,128)S(1)} custom-call(s32[2,8]{1,0:T(2,128)S(4)} %get-tuple-element.15.facts_ref, bf16[256,1024]{1,0:T(8,128)(2,1)S(1)} %shard_map.77.refs_0_, bf16[256,1024]{1,0:T(8,128)(2,1)S(1)} %shard_map.79.refs_1_, bf16[256,1024]{1,0:T(8,128)(2,1)S(1)} %shard_map.82.refs_2_, bf16[256,1024]{1,0:T(8,128)(2,1)S(1)} %shard_map.81.refs_3_, ...), custom_call_target="tpu_custom_call" | custom-call | flops 1610612736 | bytes 13107200 | tf_op jit(solution)/shard_map/pallas_call | solution.py:218
  81.8 1.0 shard_map.85
  82.8 9.9 %collective-permute-done.14.refs_1_ = bf16[256,1024]{1,0:T(8,128)(2,1)S(1)} collective-permute-done((bf16[256,1024]{1,0:T(8,128)(2,1)S(1)}, bf16[256,1024]{1,0:T(8,128)(2,1)S(1)}, u32[]{:S(2)}, u32[]{:S(2)}) %collective-permute-start.14) | collective-permute-done | bytes 524320 | tf_op jit(solution)/shard_map/ppermute | solution.py:454
  92.7 0.9 shard_map.86.refs_0_
  93.6 1.3 %collective-permute-start.16 = (bf16[256,1024]{1,0:T(8,128)(2,1)S(1)}, bf16[256,1024]{1,0:T(8,128)(2,1)S(1)}, u32[]{:S(2)}, u32[]{:S(2)}) collective-permute-start(bf16[256,1024]{1,0:T(8,128)(2,1)S(1)} %shard_map.86.refs_0_), channel_id=1, source_target_pairs={{8,0},{12,4},{16,8},{20,12},{24,16},{28,20},{9,1},{13,5},{17,9},{2... | collective-permute-start | bytes 1572872 | tf_op jit(solution)/shard_map/ppermute | solution.py:418
  94.9 1.3 %collective-permute-start.18 = (bf16[256,1024]{1,0:T(8,128)(2,1)S(1)}, bf16[256,1024]{1,0:T(8,128)(2,1)S(1)}, u32[]{:S(2)}, u32[]{:S(2)}) collective-permute-start(bf16[256,1024]{1,0:T(8,128)(2,1)S(1)} %shard_map.86.refs_0_), channel_id=1, source_target_pairs={{4,0},{12,8},{20,16},{28,24},{16,4},{24,12},{5,1},{13,9},{21,17},{... | collective-permute-start | bytes 1572872 | tf_op jit(solution)/shard_map/ppermute | solution.py:439
  96.2 1.6 %shard_map.87.refs_1_.refs_0_ = f32[256,1024]{1,0:T(8,128)S(1)} custom-call(s32[2,8]{1,0:T(2,128)S(4)} %get-tuple-element.15.facts_ref, bf16[512,256]{1,0:T(8,128)(2,1)S(1)} %get-tuple-element.16.table_ref, bf16[512,512]{1,0:T(8,128)(2,1)S(1)} %get-tuple-element.17.back_ref, f32[4,512,1024]{2,1,0:T(8,128)S(1)} %get-tuple-element.18.spec_ref, ...), custom_call_target="tpu_custom_call" | custom-call | flops 2147483648 | bytes 1048576 | tf_op jit(solution)/shard_map/pallas_call | solution.py:368
  97.8 9.6 %collective-permute-done.16.refs_0_ = bf16[256,1024]{1,0:T(8,128)(2,1)S(1)} collective-permute-done((bf16[256,1024]{1,0:T(8,128)(2,1)S(1)}, bf16[256,1024]{1,0:T(8,128)(2,1)S(1)}, u32[]{:S(2)}, u32[]{:S(2)}) %collective-permute-start.16) | collective-permute-done | bytes 524320 | tf_op jit(solution)/shard_map/ppermute | solution.py:418
  107.4 1.9 %collective-permute-done.17.refs_6_ = bf16[256,1024]{1,0:T(8,128)(2,1)S(1)} collective-permute-done((bf16[256,1024]{1,0:T(8,128)(2,1)S(1)}, bf16[256,1024]{1,0:T(8,128)(2,1)S(1)}, u32[]{:S(2)}, u32[]{:S(2)}) %collective-permute-start.17) | collective-permute-done | bytes 524320 | tf_op jit(solution)/shard_map/ppermute | solution.py:423
  109.3 3.6 %shard_map.89 = f32[1,2,256,1024]{3,2,1,0:T(8,128)} custom-call(s32[2,8]{1,0:T(2,128)S(4)} %get-tuple-element.15.facts_ref, bf16[512,256]{1,0:T(8,128)(2,1)S(1)} %get-tuple-element.16.table_ref, bf16[512,512]{1,0:T(8,128)(2,1)S(1)} %get-tuple-element.17.back_ref, f32[4,512,1024]{2,1,0:T(8,128)S(1)} %get-tuple-element.18.spec_ref, ...), custom_call_target="tpu_custom_call", output_to_operand_aliasing={{}: (12, {})} | custom-call | flops 2147483648 | bytes 1048576 | tf_op jit(solution)/shard_map/pallas_call | solution.py:368
  (24 shorter events, 2.9 us)
Async XLA Ops:
  1.1 16.1 %collective-permute-start = (bf16[256,1024]{1,0:T(8,128)(2,1)S(1)}, bf16[256,1024]{1,0:T(8,128)(2,1)S(1)}, u32[]{:S(2)}, u32[]{:S(2)}) collective-permute-start(bf16[256,1024]{1,0:T(8,128)(2,1)S(1)} %slice_bitcast_fusion.refs_0_), channel_id=1, source_target_pairs={{0,1},{1,2},{2,3},{4,5},{5,6},{6,7},{8,9},{9,10},{10,11},{12,13},{... | collective-permute-start | bytes 1572872 | tf_op jit(solution)/shard_map/ppermute | solution.py:454
  6.0 15.3 %collective-permute-start.3 = (bf16[256,1024]{1,0:T(8,128)(2,1)S(1)}, bf16[256,1024]{1,0:T(8,128)(2,1)S(1)}, u32[]{:S(2)}, u32[]{:S(2)}) collective-permute-start(bf16[256,1024]{1,0:T(8,128)(2,1)S(1)} %slice_bitcast_fusion.refs_0_), channel_id=1, source_target_pairs={{1,0},{2,1},{3,2},{5,4},{6,5},{7,6},{9,8},{10,9},{11,10},{13,12},{... | collective-permute-start | bytes 1572872 | tf_op jit(solution)/shard_map/ppermute | solution.py:454
  17.2 5.4 %collective-permute-start.1 = (bf16[256,1024]{1,0:T(8,128)(2,1)S(1)}, bf16[256,1024]{1,0:T(8,128)(2,1)S(1)}, u32[]{:S(2)}, u32[]{:S(2)}) collective-permute-start(bf16[256,1024]{1,0:T(8,128)(2,1)S(1)} %shard_map.74.refs_1_), channel_id=1, source_target_pairs={{1,2},{2,3},{5,6},{6,7},{9,10},{10,11},{13,14},{14,15},{17,18},{18... | collective-permute-start | bytes 1572872 | tf_op jit(solution)/shard_map/ppermute | solution.py:454
  21.3 14.5 %collective-permute-start.4 = (bf16[256,1024]{1,0:T(8,128)(2,1)S(1)}, bf16[256,1024]{1,0:T(8,128)(2,1)S(1)}, u32[]{:S(2)}, u32[]{:S(2)}) collective-permute-start(bf16[256,1024]{1,0:T(8,128)(2,1)S(1)} %shard_map.75.refs_2_), channel_id=1, source_target_pairs={{1,0},{2,1},{5,4},{6,5},{9,8},{10,9},{13,12},{14,13},{17,16},{18,1... | collective-permute-start | bytes 1572872 | tf_op jit(solution)/shard_map/ppermute | solution.py:454
  22.6 16.8 %collective-permute-start.2 = (bf16[256,1024]{1,0:T(8,128)(2,1)S(1)}, bf16[256,1024]{1,0:T(8,128)(2,1)S(1)}, u32[]{:S(2)}, u32[]{:S(2)}) collective-permute-start(bf16[256,1024]{1,0:T(8,128)(2,1)S(1)} %collective-permute-done.1.refs_3_), channel_id=1, source_target_pairs={{2,3},{6,7},{10,11},{14,15},{18,19},{22,23},{26,27},{30,31}} | collective-permute-start | bytes 1572872 | tf_op jit(solution)/shard_map/ppermute | solution.py:454
  35.9 13.6 %collective-permute-start.5 = (bf16[256,1024]{1,0:T(8,128)(2,1)S(1)}, bf16[256,1024]{1,0:T(8,128)(2,1)S(1)}, u32[]{:S(2)}, u32[]{:S(2)}) collective-permute-start(bf16[256,1024]{1,0:T(8,128)(2,1)S(1)} %collective-permute-done.4.refs_4_), channel_id=1, source_target_pairs={{1,0},{5,4},{9,8},{13,12},{17,16},{21,20},{25,24},{29,28}} | collective-permute-start | bytes 1572872 | tf_op jit(solution)/shard_map/ppermute | solution.py:454
  49.5 10.7 %collective-permute-start.6 = (bf16[256,1024]{1,0:T(8,128)(2,1)S(1)}, bf16[256,1024]{1,0:T(8,128)(2,1)S(1)}, u32[]{:S(2)}, u32[]{:S(2)}) collective-permute-start(bf16[256,1024]{1,0:T(8,128)(2,1)S(1)} %shard_map.77.refs_0_), channel_id=1, source_target_pairs={{0,1},{1,2},{2,3},{4,5},{5,6},{6,7},{8,9},{9,10},{10,11},{12,13},{... | collective-permute-start | bytes 1572872 | tf_op jit(solution)/shard_map/ppermute | solution.py:454
  51.0 12.5 %collective-permute-start.12 = (bf16[256,1024]{1,0:T(8,128)(2,1)S(1)}, bf16[256,1024]{1,0:T(8,128)(2,1)S(1)}, u32[]{:S(2)}, u32[]{:S(2)}) collective-permute-start(bf16[256,1024]{1,0:T(8,128)(2,1)S(1)} %shard_map.77.refs_0_), channel_id=1, source_target_pairs={{1,0},{2,1},{3,2},{5,4},{6,5},{7,6},{9,8},{10,9},{11,10},{13,12},{... | collective-permute-start | bytes 1572872 | tf_op jit(solution)/shard_map/ppermute | solution.py:454
  53.2 11.6 %collective-permute-start.8 = (bf16[256,1024]{1,0:T(8,128)(2,1)S(1)}, bf16[256,1024]{1,0:T(8,128)(2,1)S(1)}, u32[]{:S(2)}, u32[]{:S(2)}) collective-permute-start(bf16[256,1024]{1,0:T(8,128)(2,1)S(1)} %shard_map.78.refs_1_.refs_0_), channel_id=1, source_target_pairs={{0,8},{4,12},{8,16},{12,20},{16,24},{20,28},{1,9},{5,13},{9,17},{1... | collective-permute-start | bytes 1572872 | tf_op jit(solution)/shard_map/ppermute | solution.py:418
  56.6 11.4 %collective-permute-start.10 = (bf16[256,1024]{1,0:T(8,128)(2,1)S(1)}, bf16[256,1024]{1,0:T(8,128)(2,1)S(1)}, u32[]{:S(2)}, u32[]{:S(2)}) collective-permute-start(bf16[256,1024]{1,0:T(8,128)(2,1)S(1)} %shard_map.78.refs_1_.refs_0_), channel_id=1, source_target_pairs={{4,16},{12,24},{28,20},{5,17},{13,25},{29,21},{6,18},{14,26},{30,2... | collective-permute-start | bytes 1572872 | tf_op jit(solution)/shard_map/ppermute | solution.py:430
  57.3 10.7 %collective-permute-start.9 = (bf16[256,1024]{1,0:T(8,128)(2,1)S(1)}, bf16[256,1024]{1,0:T(8,128)(2,1)S(1)}, u32[]{:S(2)}, u32[]{:S(2)}) collective-permute-start(bf16[256,1024]{1,0:T(8,128)(2,1)S(1)} %shard_map.78.refs_1_.refs_0_), channel_id=1, source_target_pairs={{0,4},{4,0},{8,12},{12,8},{16,20},{20,16},{24,28},{28,24},{1,5},{5... | collective-permute-start | bytes 1572872 | tf_op jit(solution)/shard_map/ppermute | solution.py:423
  60.2 7.8 %collective-permute-start.7 = (bf16[256,1024]{1,0:T(8,128)(2,1)S(1)}, bf16[256,1024]{1,0:T(8,128)(2,1)S(1)}, u32[]{:S(2)}, u32[]{:S(2)}) collective-permute-start(bf16[256,1024]{1,0:T(8,128)(2,1)S(1)} %shard_map.79.refs_1_), channel_id=1, source_target_pairs={{1,2},{2,3},{5,6},{6,7},{9,10},{10,11},{13,14},{14,15},{17,18},{18... | collective-permute-start | bytes 1572872 | tf_op jit(solution)/shard_map/ppermute | solution.py:454
  63.5 14.5 %collective-permute-start.13 = (bf16[256,1024]{1,0:T(8,128)(2,1)S(1)}, bf16[256,1024]{1,0:T(8,128)(2,1)S(1)}, u32[]{:S(2)}, u32[]{:S(2)}) collective-permute-start(bf16[256,1024]{1,0:T(8,128)(2,1)S(1)} %shard_map.82.refs_2_), channel_id=1, source_target_pairs={{1,0},{2,1},{5,4},{6,5},{9,8},{10,9},{13,12},{14,13},{17,16},{18,1... | collective-permute-start | bytes 1572872 | tf_op jit(solution)/shard_map/ppermute | solution.py:454
  64.8 17.0 %collective-permute-start.15 = (bf16[256,1024]{1,0:T(8,128)(2,1)S(1)}, bf16[256,1024]{1,0:T(8,128)(2,1)S(1)}, u32[]{:S(2)}, u32[]{:S(2)}) collective-permute-start(bf16[256,1024]{1,0:T(8,128)(2,1)S(1)} %collective-permute-done.8.refs_2_.refs_1_.refs_3_), channel_id=1, source_target_pairs={{0,4},{4,0},{8,12},{12,8},{16,20},{20,16},{24,28},{28,24},{1,5},{5... | collective-permute-start | bytes 1572872 | tf_op jit(solution)/shard_map/ppermute | solution.py:423
  68.0 14.8 %collective-permute-start.11 = (bf16[256,1024]{1,0:T(8,128)(2,1)S(1)}, bf16[256,1024]{1,0:T(8,128)(2,1)S(1)}, u32[]{:S(2)}, u32[]{:S(2)}) collective-permute-start(bf16[256,1024]{1,0:T(8,128)(2,1)S(1)} %shard_map.81.refs_3_), channel_id=1, source_target_pairs={{2,3},{6,7},{10,11},{14,15},{18,19},{22,23},{26,27},{30,31}} | collective-permute-start | bytes 1572872 | tf_op jit(solution)/shard_map/ppermute | solution.py:454
  78.0 14.7 %collective-permute-start.14 = (bf16[256,1024]{1,0:T(8,128)(2,1)S(1)}, bf16[256,1024]{1,0:T(8,128)(2,1)S(1)}, u32[]{:S(2)}, u32[]{:S(2)}) collective-permute-start(bf16[256,1024]{1,0:T(8,128)(2,1)S(1)} %shard_map.83.refs_4_), channel_id=1, source_target_pairs={{1,0},{5,4},{9,8},{13,12},{17,16},{21,20},{25,24},{29,28}} | collective-permute-start | bytes 1572872 | tf_op jit(solution)/shard_map/ppermute | solution.py:454
  93.6 13.8 %collective-permute-start.16 = (bf16[256,1024]{1,0:T(8,128)(2,1)S(1)}, bf16[256,1024]{1,0:T(8,128)(2,1)S(1)}, u32[]{:S(2)}, u32[]{:S(2)}) collective-permute-start(bf16[256,1024]{1,0:T(8,128)(2,1)S(1)} %shard_map.86.refs_0_), channel_id=1, source_target_pairs={{8,0},{12,4},{16,8},{20,12},{24,16},{28,20},{9,1},{13,5},{17,9},{2... | collective-permute-start | bytes 1572872 | tf_op jit(solution)/shard_map/ppermute | solution.py:418
  94.9 12.5 %collective-permute-start.18 = (bf16[256,1024]{1,0:T(8,128)(2,1)S(1)}, bf16[256,1024]{1,0:T(8,128)(2,1)S(1)}, u32[]{:S(2)}, u32[]{:S(2)}) collective-permute-start(bf16[256,1024]{1,0:T(8,128)(2,1)S(1)} %shard_map.86.refs_0_), channel_id=1, source_target_pairs={{4,0},{12,8},{20,16},{28,24},{16,4},{24,12},{5,1},{13,9},{21,17},{... | collective-permute-start | bytes 1572872 | tf_op jit(solution)/shard_map/ppermute | solution.py:439
  107.4 1.9 %collective-permute-start.17 = (bf16[256,1024]{1,0:T(8,128)(2,1)S(1)}, bf16[256,1024]{1,0:T(8,128)(2,1)S(1)}, u32[]{:S(2)}, u32[]{:S(2)}) collective-permute-start(bf16[256,1024]{1,0:T(8,128)(2,1)S(1)} %shard_map.88.refs_5_), channel_id=1, source_target_pairs={{0,4},{4,0},{8,12},{12,8},{16,20},{20,16},{24,28},{28,24},{1,5},{5... | collective-permute-start | bytes 1572872 | tf_op jit(solution)/shard_map/ppermute | solution.py:423

commit v13 on v12

--- a/solution.py
+++ b/solution.py
@@ -478,30 +478,32 @@
 
     hops = [0] + [way * step for step in range(1, count) for way in (-1, 1)]
 
-    def partial_of(own, arrived, slot):
+    def partial_of(own, arrived, slot, after=()):
         shards = [own] + [one for pair in arrived[: count - 2] for one in pair]
-        return project(facts, shards, hops[:-2], weight, gates, slot, last=False)
+        return project(
+            facts, shards, hops[:-2], weight, gates, slot, last=False, after=after
+        )
 
     def final_of(arrived, slot, partial, after=()):
         return project(facts, arrived[-1], hops[-2:], weight, gates, slot, partial, after=after)
 
     pass_on(upper_in, prepared)
+    own = ordered(lower_slice, *upper_in[0])
+    lower_in = [sent(1, own, own)]
     for _ in range(3, count):
         pass_on(upper_in)
+        pass_on(lower_in, *upper_in[-2])
     partial = partial_of(start, upper_in, 1)
-    own = ordered(lower_slice, *upper_in[-1], partial)
-    lower_in = [sent(1, own, own)]
+    pass_on(lower_in, partial)
+
     upper = final_of(upper_in, 1, partial)
     upper_halo = upper_halo_of(upper)
     two, swapped, mate, fold = upper_halo
-    pass_on(lower_in, upper)
     near = own_terms(1, tabs, facts, [upper])
-    for _ in range(3, count):
-        pass_on(lower_in, near, two, mate, fold)
-    result, convolved = far_terms(1, 1, tabs, facts, [near, *upper_halo])
-
-    partial = partial_of(own, lower_in, 0)
-    lower = final_of(lower_in, 0, partial, [swapped, convolved])
+    result, _ = far_terms(1, 1, tabs, facts, [near, *upper_halo])
+
+    partial = partial_of(own, lower_in, 0, [near, mate])
+    lower = final_of(lower_in, 0, partial, [two, fold])
     near = own_terms(0, tabs, facts, [lower])
     lower_halo = lower_halo_of(lower, near)
     arrays = [near, upper, mate, two, fold, *lower_halo]

time: 113 us -> 111 us (0.982)
  the two profiles are of different devices: /device:TPU:0 before, /device:TPU:3 now
where the time goes in v13:
time: 111 us; the launch traced here: 110 us
  starting transfers between devices  45.6 us (41%)
  waiting for transfers between devices  39.6 us (36%)
  Pallas kernels  23.1 us (21%)
    ppermute x12, waiting for transfers between devices, sent(): return (lax.ppermute(up, 'ch', upward), lax.ppermute(down, 'ch', downward))  34.7 us
    ppermute x12, starting transfers between devices, sent(): return (lax.ppermute(up, 'ch', upward), lax.ppermute(down, 'ch', downward))  17.9 us
    ppermute x2, starting transfers between devices, shifted(): lax.ppermute(value, 'ctx', [(source, source + steps) for source in range(...  13.6 us
    pallas_call x4, Pallas kernels, conv_call(): pl.pallas_call(body, grid=(width // LANES,), out_shape=out_shape, in_spec...  11 us
    ppermute x3, starting transfers between devices, core_swapped(): lax.ppermute(value, 'ctx', [(source, source ^ 1) for source in range(coun...  8.28 us
    pallas_call x4, Pallas kernels, project(): pl.pallas_call(functools.partial(project_kernel, hops, slot, before is No...  6.47 us
    pallas_call x1, Pallas kernels, prepare(): pl.pallas_call(functools.partial(prepare_kernel, pairs), grid=(width // L...  5.59 us
    ppermute x1, starting transfers between devices, upper_halo_of(): mate, far = (core_swapped(value), lax.ppermute(value, 'ctx', far))  3.84 us
  transfers between devices with their start and end apart: 19, of which 10 were waited for; matrix products, arithmetic and copies ran while one was open for 0% of the time, Pallas kernels for 18%

profile of v13, /device:TPU:3, one launch (start us, length us, event | category | flops | bytes accessed | tf_op | source)
XLA Modules:
  0.0 109.5 jit_solution(5723844078866893193)
XLA Ops:
  0.0 1.1 slice_bitcast_fusion.refs_0_
  1.1 3.2 %collective-permute-start = (bf16[256,1024]{1,0:T(8,128)(2,1)S(1)}, bf16[256,1024]{1,0:T(8,128)(2,1)S(1)}, u32[]{:S(2)}, u32[]{:S(2)}) collective-permute-start(bf16[256,1024]{1,0:T(8,128)(2,1)S(1)} %slice_bitcast_fusion.refs_0_), channel_id=1, source_target_pairs={{0,1},{1,2},{2,3},{4,5},{5,6},{6,7},{8,9},{9,10},{10,11},{12,13},{... | collective-permute-start | bytes 1572872 | tf_op jit(solution)/shard_map/ppermute | solution.py:454
  4.3 1.3 %collective-permute-start.1 = (bf16[256,1024]{1,0:T(8,128)(2,1)S(1)}, bf16[256,1024]{1,0:T(8,128)(2,1)S(1)}, u32[]{:S(2)}, u32[]{:S(2)}) collective-permute-start(bf16[256,1024]{1,0:T(8,128)(2,1)S(1)} %slice_bitcast_fusion.refs_0_), channel_id=1, source_target_pairs={{1,0},{2,1},{3,2},{5,4},{6,5},{7,6},{9,8},{10,9},{11,10},{13,12},{... | collective-permute-start | bytes 1572872 | tf_op jit(solution)/shard_map/ppermute | solution.py:454
  5.6 5.6 %shard_map.73 = (f32[4,512,1024]{2,1,0:T(8,128)S(1)}, bf16[1024,4096]{1,0:T(8,128)(2,1)S(1)}, bf16[1,2,256,1024]{3,2,1,0:T(8,128)(2,1)S(1)}, bf16[256,1024]{1,0:...) custom-call(s32[1]{0:T(128)} %bitcast.refs_0_, ...), custom_call_target="tpu_custom_call" | custom-call | flops 2415919104 | bytes 11534336 | tf_op jit(solution)/shard_map/pallas_call | solution.py:147
  11.2 3.6 %collective-permute-done.refs_0_ = bf16[256,1024]{1,0:T(8,128)(2,1)S(1)} collective-permute-done((bf16[256,1024]{1,0:T(8,128)(2,1)S(1)}, bf16[256,1024]{1,0:T(8,128)(2,1)S(1)}, u32[]{:S(2)}, u32[]{:S(2)}) %collective-permute-start) | collective-permute-done | bytes 524320 | tf_op jit(solution)/shard_map/ppermute | solution.py:454
  15.6 3.1 %collective-permute-done.1.refs_0_ = bf16[256,1024]{1,0:T(8,128)(2,1)S(1)} collective-permute-done((bf16[256,1024]{1,0:T(8,128)(2,1)S(1)}, bf16[256,1024]{1,0:T(8,128)(2,1)S(1)}, u32[]{:S(2)}, u32[]{:S(2)}) %collective-permute-start.1) | collective-permute-done | bytes 524320 | tf_op jit(solution)/shard_map/ppermute | solution.py:454
  18.7 1.3 %collective-permute-start.4 = (bf16[256,1024]{1,0:T(8,128)(2,1)S(1)}, bf16[256,1024]{1,0:T(8,128)(2,1)S(1)}, u32[]{:S(2)}, u32[]{:S(2)}) collective-permute-start(bf16[256,1024]{1,0:T(8,128)(2,1)S(1)} %shard_map.75.refs_2_), channel_id=1, source_target_pairs={{1,0},{2,1},{5,4},{6,5},{9,8},{10,9},{13,12},{14,13},{17,16},{18,1... | collective-permute-start | bytes 1572872 | tf_op jit(solution)/shard_map/ppermute | solution.py:454
  20.0 4.2 %collective-permute-start.2 = (bf16[256,1024]{1,0:T(8,128)(2,1)S(1)}, bf16[256,1024]{1,0:T(8,128)(2,1)S(1)}, u32[]{:S(2)}, u32[]{:S(2)}) collective-permute-start(bf16[256,1024]{1,0:T(8,128)(2,1)S(1)} %shard_map.76.refs_0_), channel_id=1, source_target_pairs={{0,1},{1,2},{2,3},{4,5},{5,6},{6,7},{8,9},{9,10},{10,11},{12,13},{... | collective-permute-start | bytes 1572872 | tf_op jit(solution)/shard_map/ppermute | solution.py:454
  24.2 1.3 %collective-permute-start.7 = (bf16[256,1024]{1,0:T(8,128)(2,1)S(1)}, bf16[256,1024]{1,0:T(8,128)(2,1)S(1)}, u32[]{:S(2)}, u32[]{:S(2)}) collective-permute-start(bf16[256,1024]{1,0:T(8,128)(2,1)S(1)} %shard_map.76.refs_0_), channel_id=1, source_target_pairs={{1,0},{2,1},{3,2},{5,4},{6,5},{7,6},{9,8},{10,9},{11,10},{13,12},{... | collective-permute-start | bytes 1572872 | tf_op jit(solution)/shard_map/ppermute | solution.py:454
  26.2 6.3 %collective-permute-done.4.refs_2_.refs_4_ = bf16[256,1024]{1,0:T(8,128)(2,1)S(1)} collective-permute-done((bf16[256,1024]{1,0:T(8,128)(2,1)S(1)}, bf16[256,1024]{1,0:T(8,128)(2,1)S(1)}, u32[]{:S(2)}, u32[]{:S(2)}) %collective-permute-start.4) | collective-permute-done | bytes 524320 | tf_op jit(solution)/shard_map/ppermute | solution.py:454
  32.5 1.3 %collective-permute-start.11 = (bf16[256,1024]{1,0:T(8,128)(2,1)S(1)}, bf16[256,1024]{1,0:T(8,128)(2,1)S(1)}, u32[]{:S(2)}, u32[]{:S(2)}) collective-permute-start(bf16[256,1024]{1,0:T(8,128)(2,1)S(1)} %collective-permute-done.4.refs_2_.refs_4_), channel_id=1, source_target_pairs={{1,0},{5,4},{9,8},{13,12},{17,16},{21,20},{25,24},{29,28}} | collective-permute-start | bytes 1572872 | tf_op jit(solution)/shard_map/ppermute | solution.py:454
  34.5 9.2 %collective-permute-done.7.refs_0_ = bf16[256,1024]{1,0:T(8,128)(2,1)S(1)} collective-permute-done((bf16[256,1024]{1,0:T(8,128)(2,1)S(1)}, bf16[256,1024]{1,0:T(8,128)(2,1)S(1)}, u32[]{:S(2)}, u32[]{:S(2)}) %collective-permute-start.7) | collective-permute-done | bytes 524320 | tf_op jit(solution)/shard_map/ppermute | solution.py:454
  43.7 1.3 %collective-permute-start.8 = (bf16[256,1024]{1,0:T(8,128)(2,1)S(1)}, bf16[256,1024]{1,0:T(8,128)(2,1)S(1)}, u32[]{:S(2)}, u32[]{:S(2)}) collective-permute-start(bf16[256,1024]{1,0:T(8,128)(2,1)S(1)} %shard_map.80.refs_2_), channel_id=1, source_target_pairs={{1,0},{2,1},{5,4},{6,5},{9,8},{10,9},{13,12},{14,13},{17,16},{18,1... | collective-permute-start | bytes 1572872 | tf_op jit(solution)/shard_map/ppermute | solution.py:454
  45.0 2.3 %shard_map.78.refs_1_.refs_4_ = f32[256,1024]{1,0:T(8,128)S(1)} custom-call(s32[2,8]{1,0:T(2,128)S(4)} %get-tuple-element.14.facts_ref, bf16[256,1024]{1,0:T(8,128)(2,1)S(1)} %slice_bitcast_fusion.refs_0_, bf16[256,1024]{1,0:T(8,128)(2,1)S(1)} %shard_map.74.refs_1_, bf16[256,1024]{1,0:T(8,128)(2,1)S(1)} %shard_map.75.refs_2_, ...), custom_call_target="tpu_custom_call" | custom-call | flops 1610612736 | bytes 13107200 | tf_op jit(solution)/shard_map/pallas_call | solution.py:218
  47.3 7.7 %collective-permute-done.11.refs_1_ = bf16[256,1024]{1,0:T(8,128)(2,1)S(1)} collective-permute-done((bf16[256,1024]{1,0:T(8,128)(2,1)S(1)}, bf16[256,1024]{1,0:T(8,128)(2,1)S(1)}, u32[]{:S(2)}, u32[]{:S(2)}) %collective-permute-start.11) | collective-permute-done | bytes 524320 | tf_op jit(solution)/shard_map/ppermute | solution.py:454
  55.0 0.9 shard_map.82.refs_0_.refs_1_
  55.9 4.9 %collective-permute-start.12 = (bf16[256,1024]{1,0:T(8,128)(2,1)S(1)}, bf16[256,1024]{1,0:T(8,128)(2,1)S(1)}, u32[]{:S(2)}, u32[]{:S(2)}) collective-permute-start(bf16[256,1024]{1,0:T(8,128)(2,1)S(1)} %shard_map.82.refs_0_.refs_1_), channel_id=1, source_target_pairs={{0,4},{4,0},{8,12},{12,8},{16,20},{20,16},{24,28},{28,24},{1,5},{5... | collective-permute-start | bytes 1572872 | tf_op jit(solution)/shard_map/ppermute | solution.py:423
  61.4 4.8 %collective-permute-done.8.refs_0_ = bf16[256,1024]{1,0:T(8,128)(2,1)S(1)} collective-permute-done((bf16[256,1024]{1,0:T(8,128)(2,1)S(1)}, bf16[256,1024]{1,0:T(8,128)(2,1)S(1)}, u32[]{:S(2)}, u32[]{:S(2)}) %collective-permute-start.8) | collective-permute-done | bytes 524320 | tf_op jit(solution)/shard_map/ppermute | solution.py:454
  66.2 1.3 %collective-permute-start.9 = (bf16[256,1024]{1,0:T(8,128)(2,1)S(1)}, bf16[256,1024]{1,0:T(8,128)(2,1)S(1)}, u32[]{:S(2)}, u32[]{:S(2)}) collective-permute-start(bf16[256,1024]{1,0:T(8,128)(2,1)S(1)} %shard_map.81.refs_4_), channel_id=1, source_target_pairs={{1,0},{5,4},{9,8},{13,12},{17,16},{21,20},{25,24},{29,28}} | collective-permute-start | bytes 1572872 | tf_op jit(solution)/shard_map/ppermute | solution.py:454
  67.5 3.1 %collective-permute-start.13 = (bf16[256,1024]{1,0:T(8,128)(2,1)S(1)}, bf16[256,1024]{1,0:T(8,128)(2,1)S(1)}, u32[]{:S(2)}, u32[]{:S(2)}) collective-permute-start(bf16[256,1024]{1,0:T(8,128)(2,1)S(1)} %shard_map.82.refs_0_.refs_1_), channel_id=1, source_target_pairs={{0,8},{4,12},{8,16},{12,20},{16,24},{20,28},{1,9},{5,13},{9,17},{1... | collective-permute-start | bytes 1572872 | tf_op jit(solution)/shard_map/ppermute | solution.py:418
  70.6 3.8 %collective-permute-start.14 = (bf16[256,1024]{1,0:T(8,128)(2,1)S(1)}, bf16[256,1024]{1,0:T(8,128)(2,1)S(1)}, u32[]{:S(2)}, u32[]{:S(2)}) collective-permute-start(bf16[256,1024]{1,0:T(8,128)(2,1)S(1)} %shard_map.82.refs_0_.refs_1_), channel_id=1, source_target_pairs={{4,16},{12,24},{28,20},{5,17},{13,25},{29,21},{6,18},{14,26},{30,2... | collective-permute-start | bytes 1572872 | tf_op jit(solution)/shard_map/ppermute | solution.py:430
  74.5 3.1 %shard_map.83.refs_7_.refs_0_ = f32[256,1024]{1,0:T(8,128)S(1)} custom-call(s32[2,8]{1,0:T(2,128)S(4)} %get-tuple-element.14.facts_ref, bf16[512,256]{1,0:T(8,128)(2,1)S(1)} %get-tuple-element.15.table_ref, bf16[512,512]{1,0:T(8,128)(2,1)S(1)} %get-tuple-element.16.back_ref, f32[4,512,1024]{2,1,0:T(8,128)S(1)} %get-tuple-element.17.spec_ref, ...), custom_call_target="tpu_custom_call" | custom-call | flops 2147483648 | bytes 1048576 | tf_op jit(solution)/shard_map/pallas_call | solution.py:368
  77.6 2.2 %shard_map.84.refs_4_ = f32[256,1024]{1,0:T(8,128)S(1)} custom-call(s32[2,8]{1,0:T(2,128)S(4)} %get-tuple-element.14.facts_ref, bf16[256,1024]{1,0:T(8,128)(2,1)S(1)} %shard_map.76.refs_0_, bf16[256,1024]{1,0:T(8,128)(2,1)S(1)} %shard_map.77.refs_1_, bf16[256,1024]{1,0:T(8,128)(2,1)S(1)} %shard_map.80.refs_2_, bf16[256,1024]{1,0:T(8,128)(2,1)S(1)} %shard_map.79.refs_3_, ...), custom_call_target="tpu_custom_call" | custom-call | flops 1610612736 | bytes 13107200 | tf_op jit(solution)/shard_map/pallas_call | solution.py:218
  80.5 1.1 shard_map.85.refs_0_
  81.6 10.5 %collective-permute-start.15 = (bf16[256,1024]{1,0:T(8,128)(2,1)S(1)}, bf16[256,1024]{1,0:T(8,128)(2,1)S(1)}, u32[]{:S(2)}, u32[]{:S(2)}) collective-permute-start(bf16[256,1024]{1,0:T(8,128)(2,1)S(1)} %shard_map.85.refs_0_), channel_id=1, source_target_pairs={{8,0},{12,4},{16,8},{20,12},{24,16},{28,20},{9,1},{13,5},{17,9},{2... | collective-permute-start | bytes 1572872 | tf_op jit(solution)/shard_map/ppermute | solution.py:418
  92.1 1.9 %collective-permute-start.17 = (bf16[256,1024]{1,0:T(8,128)(2,1)S(1)}, bf16[256,1024]{1,0:T(8,128)(2,1)S(1)}, u32[]{:S(2)}, u32[]{:S(2)}) collective-permute-start(bf16[256,1024]{1,0:T(8,128)(2,1)S(1)} %shard_map.85.refs_0_), channel_id=1, source_target_pairs={{4,0},{12,8},{20,16},{28,24},{16,4},{24,12},{5,1},{13,9},{21,17},{... | collective-permute-start | bytes 1572872 | tf_op jit(solution)/shard_map/ppermute | solution.py:439
  94.1 1.6 %shard_map.86.refs_1_.refs_0_ = f32[256,1024]{1,0:T(8,128)S(1)} custom-call(s32[2,8]{1,0:T(2,128)S(4)} %get-tuple-element.14.facts_ref, bf16[512,256]{1,0:T(8,128)(2,1)S(1)} %get-tuple-element.15.table_ref, bf16[512,512]{1,0:T(8,128)(2,1)S(1)} %get-tuple-element.16.back_ref, f32[4,512,1024]{2,1,0:T(8,128)S(1)} %get-tuple-element.17.spec_ref, ...), custom_call_target="tpu_custom_call" | custom-call | flops 2147483648 | bytes 1048576 | tf_op jit(solution)/shard_map/pallas_call | solution.py:368
  95.7 2.9 %collective-permute-done.15.refs_0_ = bf16[256,1024]{1,0:T(8,128)(2,1)S(1)} collective-permute-done((bf16[256,1024]{1,0:T(8,128)(2,1)S(1)}, bf16[256,1024]{1,0:T(8,128)(2,1)S(1)}, u32[]{:S(2)}, u32[]{:S(2)}) %collective-permute-start.15) | collective-permute-done | bytes 524320 | tf_op jit(solution)/shard_map/ppermute | solution.py:418
  98.6 3.3 %collective-permute-start.16 = (bf16[256,1024]{1,0:T(8,128)(2,1)S(1)}, bf16[256,1024]{1,0:T(8,128)(2,1)S(1)}, u32[]{:S(2)}, u32[]{:S(2)}) collective-permute-start(bf16[256,1024]{1,0:T(8,128)(2,1)S(1)} %shard_map.87.refs_5_), channel_id=1, source_target_pairs={{0,4},{4,0},{8,12},{12,8},{16,20},{20,16},{24,28},{28,24},{1,5},{5... | collective-permute-start | bytes 1572872 | tf_op jit(solution)/shard_map/ppermute | solution.py:423
  102.0 3.6 %shard_map.88 = (f32[1,2,256,1024]{3,2,1,0:T(8,128)}, f32[8,128]{1,0:T(8,128)}) custom-call(s32[2,8]{1,0:T(2,128)S(4)} %get-tuple-element.14.facts_ref, bf16[512,256]{1,0:T(8,128)(2,1)S(1)} %get-tuple-element.15.table_ref, bf16[512,512]{1,0:T(8,128)(2,1)S(1)} %get-tuple-element.16.back_ref, f32[4,512,1024]{2,1,0:T(8,128)S(1)} %get-tuple-element.17.spec_ref, ...), custom_call_target="tpu_custom_call" | custom-call | flops 2147483648 | bytes 1048576 | tf_op jit(solution)/shard_map/pallas_call | solution.py:368
  105.6 1.2 %collective-permute-done.17.refs_7_ = bf16[256,1024]{1,0:T(8,128)(2,1)S(1)} collective-permute-done((bf16[256,1024]{1,0:T(8,128)(2,1)S(1)}, bf16[256,1024]{1,0:T(8,128)(2,1)S(1)}, u32[]{:S(2)}, u32[]{:S(2)}) %collective-permute-start.17) | collective-permute-done | bytes 524320 | tf_op jit(solution)/shard_map/ppermute | solution.py:439
  106.8 2.7 %shard_map.89 = f32[1,2,256,1024]{3,2,1,0:T(8,128)} custom-call(s32[2,8]{1,0:T(2,128)S(4)} %get-tuple-element.14.facts_ref, bf16[512,256]{1,0:T(8,128)(2,1)S(1)} %get-tuple-element.15.table_ref, bf16[512,512]{1,0:T(8,128)(2,1)S(1)} %get-tuple-element.16.back_ref, f32[4,512,1024]{2,1,0:T(8,128)S(1)} %get-tuple-element.17.spec_ref, ...), custom_call_target="tpu_custom_call", output_to_operand_aliasing={{}: (12, {})} | custom-call | flops 2147483648 | bytes 1048576 | tf_op jit(solution)/shard_map/pallas_call | solution.py:368
  (24 shorter events, 3.6 us)
Async XLA Ops:
  1.1 13.8 %collective-permute-start = (bf16[256,1024]{1,0:T(8,128)(2,1)S(1)}, bf16[256,1024]{1,0:T(8,128)(2,1)S(1)}, u32[]{:S(2)}, u32[]{:S(2)}) collective-permute-start(bf16[256,1024]{1,0:T(8,128)(2,1)S(1)} %slice_bitcast_fusion.refs_0_), channel_id=1, source_target_pairs={{0,1},{1,2},{2,3},{4,5},{5,6},{6,7},{8,9},{9,10},{10,11},{12,13},{... | collective-permute-start | bytes 1572872 | tf_op jit(solution)/shard_map/ppermute | solution.py:454
  4.3 14.4 %collective-permute-start.1 = (bf16[256,1024]{1,0:T(8,128)(2,1)S(1)}, bf16[256,1024]{1,0:T(8,128)(2,1)S(1)}, u32[]{:S(2)}, u32[]{:S(2)}) collective-permute-start(bf16[256,1024]{1,0:T(8,128)(2,1)S(1)} %slice_bitcast_fusion.refs_0_), channel_id=1, source_target_pairs={{1,0},{2,1},{3,2},{5,4},{6,5},{7,6},{9,8},{10,9},{11,10},{13,12},{... | collective-permute-start | bytes 1572872 | tf_op jit(solution)/shard_map/ppermute | solution.py:454
  14.9 10.6 %collective-permute-start.3 = (bf16[256,1024]{1,0:T(8,128)(2,1)S(1)}, bf16[256,1024]{1,0:T(8,128)(2,1)S(1)}, u32[]{:S(2)}, u32[]{:S(2)}) collective-permute-start(bf16[256,1024]{1,0:T(8,128)(2,1)S(1)} %shard_map.74.refs_1_), channel_id=1, source_target_pairs={{1,2},{2,3},{5,6},{6,7},{9,10},{10,11},{13,14},{14,15},{17,18},{18... | collective-permute-start | bytes 1572872 | tf_op jit(solution)/shard_map/ppermute | solution.py:454
  18.7 13.8 %collective-permute-start.4 = (bf16[256,1024]{1,0:T(8,128)(2,1)S(1)}, bf16[256,1024]{1,0:T(8,128)(2,1)S(1)}, u32[]{:S(2)}, u32[]{:S(2)}) collective-permute-start(bf16[256,1024]{1,0:T(8,128)(2,1)S(1)} %shard_map.75.refs_2_), channel_id=1, source_target_pairs={{1,0},{2,1},{5,4},{6,5},{9,8},{10,9},{13,12},{14,13},{17,16},{18,1... | collective-permute-start | bytes 1572872 | tf_op jit(solution)/shard_map/ppermute | solution.py:454
  20.0 13.8 %collective-permute-start.2 = (bf16[256,1024]{1,0:T(8,128)(2,1)S(1)}, bf16[256,1024]{1,0:T(8,128)(2,1)S(1)}, u32[]{:S(2)}, u32[]{:S(2)}) collective-permute-start(bf16[256,1024]{1,0:T(8,128)(2,1)S(1)} %shard_map.76.refs_0_), channel_id=1, source_target_pairs={{0,1},{1,2},{2,3},{4,5},{5,6},{6,7},{8,9},{9,10},{10,11},{12,13},{... | collective-permute-start | bytes 1572872 | tf_op jit(solution)/shard_map/ppermute | solution.py:454
  24.2 19.5 %collective-permute-start.7 = (bf16[256,1024]{1,0:T(8,128)(2,1)S(1)}, bf16[256,1024]{1,0:T(8,128)(2,1)S(1)}, u32[]{:S(2)}, u32[]{:S(2)}) collective-permute-start(bf16[256,1024]{1,0:T(8,128)(2,1)S(1)} %shard_map.76.refs_0_), channel_id=1, source_target_pairs={{1,0},{2,1},{3,2},{5,4},{6,5},{7,6},{9,8},{10,9},{11,10},{13,12},{... | collective-permute-start | bytes 1572872 | tf_op jit(solution)/shard_map/ppermute | solution.py:454
  25.5 21.8 %collective-permute-start.10 = (bf16[256,1024]{1,0:T(8,128)(2,1)S(1)}, bf16[256,1024]{1,0:T(8,128)(2,1)S(1)}, u32[]{:S(2)}, u32[]{:S(2)}) collective-permute-start(bf16[256,1024]{1,0:T(8,128)(2,1)S(1)} %collective-permute-done.3.refs_1_.refs_3_), channel_id=1, source_target_pairs={{2,3},{6,7},{10,11},{14,15},{18,19},{22,23},{26,27},{30,31}} | collective-permute-start | bytes 1572872 | tf_op jit(solution)/shard_map/ppermute | solution.py:454
  32.5 22.5 %collective-permute-start.11 = (bf16[256,1024]{1,0:T(8,128)(2,1)S(1)}, bf16[256,1024]{1,0:T(8,128)(2,1)S(1)}, u32[]{:S(2)}, u32[]{:S(2)}) collective-permute-start(bf16[256,1024]{1,0:T(8,128)(2,1)S(1)} %collective-permute-done.4.refs_2_.refs_4_), channel_id=1, source_target_pairs={{1,0},{5,4},{9,8},{13,12},{17,16},{21,20},{25,24},{29,28}} | collective-permute-start | bytes 1572872 | tf_op jit(solution)/shard_map/ppermute | solution.py:454
  33.8 26.9 %collective-permute-start.5 = (bf16[256,1024]{1,0:T(8,128)(2,1)S(1)}, bf16[256,1024]{1,0:T(8,128)(2,1)S(1)}, u32[]{:S(2)}, u32[]{:S(2)}) collective-permute-start(bf16[256,1024]{1,0:T(8,128)(2,1)S(1)} %shard_map.77.refs_1_), channel_id=1, source_target_pairs={{1,2},{2,3},{5,6},{6,7},{9,10},{10,11},{13,14},{14,15},{17,18},{18... | collective-permute-start | bytes 1572872 | tf_op jit(solution)/shard_map/ppermute | solution.py:454
  43.7 22.5 %collective-permute-start.8 = (bf16[256,1024]{1,0:T(8,128)(2,1)S(1)}, bf16[256,1024]{1,0:T(8,128)(2,1)S(1)}, u32[]{:S(2)}, u32[]{:S(2)}) collective-permute-start(bf16[256,1024]{1,0:T(8,128)(2,1)S(1)} %shard_map.80.refs_2_), channel_id=1, source_target_pairs={{1,0},{2,1},{5,4},{6,5},{9,8},{10,9},{13,12},{14,13},{17,16},{18,1... | collective-permute-start | bytes 1572872 | tf_op jit(solution)/shard_map/ppermute | solution.py:454
  55.9 21.7 %collective-permute-start.12 = (bf16[256,1024]{1,0:T(8,128)(2,1)S(1)}, bf16[256,1024]{1,0:T(8,128)(2,1)S(1)}, u32[]{:S(2)}, u32[]{:S(2)}) collective-permute-start(bf16[256,1024]{1,0:T(8,128)(2,1)S(1)} %shard_map.82.refs_0_.refs_1_), channel_id=1, source_target_pairs={{0,4},{4,0},{8,12},{12,8},{16,20},{20,16},{24,28},{28,24},{1,5},{5... | collective-permute-start | bytes 1572872 | tf_op jit(solution)/shard_map/ppermute | solution.py:423
  60.7 19.1 %collective-permute-start.6 = (bf16[256,1024]{1,0:T(8,128)(2,1)S(1)}, bf16[256,1024]{1,0:T(8,128)(2,1)S(1)}, u32[]{:S(2)}, u32[]{:S(2)}) collective-permute-start(bf16[256,1024]{1,0:T(8,128)(2,1)S(1)} %shard_map.79.refs_3_), channel_id=1, source_target_pairs={{2,3},{6,7},{10,11},{14,15},{18,19},{22,23},{26,27},{30,31}} | collective-permute-start | bytes 1572872 | tf_op jit(solution)/shard_map/ppermute | solution.py:454
  66.2 13.6 %collective-permute-start.9 = (bf16[256,1024]{1,0:T(8,128)(2,1)S(1)}, bf16[256,1024]{1,0:T(8,128)(2,1)S(1)}, u32[]{:S(2)}, u32[]{:S(2)}) collective-permute-start(bf16[256,1024]{1,0:T(8,128)(2,1)S(1)} %shard_map.81.refs_4_), channel_id=1, source_target_pairs={{1,0},{5,4},{9,8},{13,12},{17,16},{21,20},{25,24},{29,28}} | collective-permute-start | bytes 1572872 | tf_op jit(solution)/shard_map/ppermute | solution.py:454
  67.5 12.7 %collective-permute-start.13 = (bf16[256,1024]{1,0:T(8,128)(2,1)S(1)}, bf16[256,1024]{1,0:T(8,128)(2,1)S(1)}, u32[]{:S(2)}, u32[]{:S(2)}) collective-permute-start(bf16[256,1024]{1,0:T(8,128)(2,1)S(1)} %shard_map.82.refs_0_.refs_1_), channel_id=1, source_target_pairs={{0,8},{4,12},{8,16},{12,20},{16,24},{20,28},{1,9},{5,13},{9,17},{1... | collective-permute-start | bytes 1572872 | tf_op jit(solution)/shard_map/ppermute | solution.py:418
  70.6 9.9 %collective-permute-start.14 = (bf16[256,1024]{1,0:T(8,128)(2,1)S(1)}, bf16[256,1024]{1,0:T(8,128)(2,1)S(1)}, u32[]{:S(2)}, u32[]{:S(2)}) collective-permute-start(bf16[256,1024]{1,0:T(8,128)(2,1)S(1)} %shard_map.82.refs_0_.refs_1_), channel_id=1, source_target_pairs={{4,16},{12,24},{28,20},{5,17},{13,25},{29,21},{6,18},{14,26},{30,2... | collective-permute-start | bytes 1572872 | tf_op jit(solution)/shard_map/ppermute | solution.py:430
  81.6 17.0 %collective-permute-start.15 = (bf16[256,1024]{1,0:T(8,128)(2,1)S(1)}, bf16[256,1024]{1,0:T(8,128)(2,1)S(1)}, u32[]{:S(2)}, u32[]{:S(2)}) collective-permute-start(bf16[256,1024]{1,0:T(8,128)(2,1)S(1)} %shard_map.85.refs_0_), channel_id=1, source_target_pairs={{8,0},{12,4},{16,8},{20,12},{24,16},{28,20},{9,1},{13,5},{17,9},{2... | collective-permute-start | bytes 1572872 | tf_op jit(solution)/shard_map/ppermute | solution.py:418
  92.1 14.7 %collective-permute-start.17 = (bf16[256,1024]{1,0:T(8,128)(2,1)S(1)}, bf16[256,1024]{1,0:T(8,128)(2,1)S(1)}, u32[]{:S(2)}, u32[]{:S(2)}) collective-permute-start(bf16[256,1024]{1,0:T(8,128)(2,1)S(1)} %shard_map.85.refs_0_), channel_id=1, source_target_pairs={{4,0},{12,8},{20,16},{28,24},{16,4},{24,12},{5,1},{13,9},{21,17},{... | collective-permute-start | bytes 1572872 | tf_op jit(solution)/shard_map/ppermute | solution.py:439
  94.1 7.9 %collective-permute-start.18 = (bf16[256,1024]{1,0:T(8,128)(2,1)S(1)}, bf16[256,1024]{1,0:T(8,128)(2,1)S(1)}, u32[]{:S(2)}, u32[]{:S(2)}) collective-permute-start(bf16[256,1024]{1,0:T(8,128)(2,1)S(1)} %collective-permute-done.13.refs_5_.refs_1_.refs_3_), channel_id=1, source_target_pairs={{0,4},{4,0},{8,12},{12,8},{16,20},{20,16},{24,28},{28,24},{1,5},{5... | collective-permute-start | bytes 1572872 | tf_op jit(solution)/shard_map/ppermute | solution.py:423
  98.6 8.2 %collective-permute-start.16 = (bf16[256,1024]{1,0:T(8,128)(2,1)S(1)}, bf16[256,1024]{1,0:T(8,128)(2,1)S(1)}, u32[]{:S(2)}, u32[]{:S(2)}) collective-permute-start(bf16[256,1024]{1,0:T(8,128)(2,1)S(1)} %shard_map.87.refs_5_), channel_id=1, source_target_pairs={{0,4},{4,0},{8,12},{12,8},{16,20},{20,16},{24,28},{28,24},{1,5},{5... | collective-permute-start | bytes 1572872 | tf_op jit(solution)/shard_map/ppermute | solution.py:423

commit v14 on v13

--- a/solution.py
+++ b/solution.py
@@ -494,17 +494,17 @@
         pass_on(upper_in)
         pass_on(lower_in, *upper_in[-2])
     partial = partial_of(start, upper_in, 1)
-    pass_on(lower_in, partial)
-
     upper = final_of(upper_in, 1, partial)
+    pass_on(lower_in, upper)
+
     upper_halo = upper_halo_of(upper)
     two, swapped, mate, fold = upper_halo
     near = own_terms(1, tabs, facts, [upper])
     result, _ = far_terms(1, 1, tabs, facts, [near, *upper_halo])
 
-    partial = partial_of(own, lower_in, 0, [near, mate])
-    lower = final_of(lower_in, 0, partial, [two, fold])
-    near = own_terms(0, tabs, facts, [lower])
+    partial = partial_of(own, lower_in, 0, [near])
+    lower = final_of(lower_in, 0, partial, [two, mate])
+    near = own_terms(0, tabs, facts, [lower], after=[fold])
     lower_halo = lower_halo_of(lower, near)
     arrays = [near, upper, mate, two, fold, *lower_halo]
     return far_terms(0, 1, tabs, facts, arrays, result)

time: 111 us -> 108 us (0.973)
  starting transfers between devices: 45.6 us -> 35.9 us
  waiting for transfers between devices: 39.6 us -> 45.8 us
    ppermute x2, starting transfers between devices: 13.6 us -> 7.05 us  [shifted(): lax.ppermute(value, 'ctx', [(source, source + steps) for source in range(...]
    ppermute x12, waiting for transfers between devices: 34.7 us -> 39.6 us  [sent(): return (lax.ppermute(up, 'ch', upward), lax.ppermute(down, 'ch', downward))]
    ppermute x1, starting transfers between devices: 3.84 us -> 1.31 us  [upper_halo_of(): mate, far = (core_swapped(value), lax.ppermute(value, 'ctx', far))]
    ppermute x3, starting transfers between devices: 8.28 us -> 6.28 us  [core_swapped(): lax.ppermute(value, 'ctx', [(source, source ^ 1) for source in range(coun...]
    ppermute x2, waiting for transfers between devices: 3.27 us -> 5.03 us  [shifted(): lax.ppermute(value, 'ctx', [(source, source + steps) for source in range(...]
    ppermute x1, starting transfers between devices: 1.92 us -> 3.34 us  [lower_halo_of(): mixed = lax.ppermute(value, 'ctx', mixed)]
  transfers between devices with their start and end apart: 19 -> 19, of which waited for: 10 -> 8; matrix products, arithmetic and copies ran while one was open for 0% -> 0% of each run, Pallas kernels for 18% -> 19%
where the time goes in v14:
time: 108 us; the launch traced here: 106 us
  waiting for transfers between devices  45.8 us (42%)
  starting transfers between devices  35.9 us (33%)
  Pallas kernels  23.1 us (21%)
  local copies, waits for them, and re-layouts  1.08 us (1%)
    ppermute x12, waiting for transfers between devices, sent(): return (lax.ppermute(up, 'ch', upward), lax.ppermute(down, 'ch', downward))  39.6 us
    ppermute x12, starting transfers between devices, sent(): return (lax.ppermute(up, 'ch', upward), lax.ppermute(down, 'ch', downward))  17.9 us
    pallas_call x4, Pallas kernels, conv_call(): pl.pallas_call(body, grid=(width // LANES,), out_shape=out_shape, in_spec...  11 us
    ppermute x2, starting transfers between devices, shifted(): lax.ppermute(value, 'ctx', [(source, source + steps) for source in range(...  7.05 us
    pallas_call x4, Pallas kernels, project(): pl.pallas_call(functools.partial(project_kernel, hops, slot, before is No...  6.49 us
    ppermute x3, starting transfers between devices, core_swapped(): lax.ppermute(value, 'ctx', [(source, source ^ 1) for source in range(coun...  6.28 us
    pallas_call x1, Pallas kernels, prepare(): pl.pallas_call(functools.partial(prepare_kernel, pairs), grid=(width // L...  5.59 us
    ppermute x2, waiting for transfers between devices, shifted(): lax.ppermute(value, 'ctx', [(source, source + steps) for source in range(...  5.03 us
  transfers between devices with their start and end apart: 19, of which 8 were waited for; matrix products, arithmetic and copies ran while one was open for 0% of the time, Pallas kernels for 19%

profile of v14, /device:TPU:3, one launch (start us, length us, event | category | flops | bytes accessed | tf_op | source)
XLA Modules:
  0.0 106.2 jit_solution(5304309109981658304)
XLA Ops:
  0.0 1.1 %slice_bitcast_fusion.refs_0_ = bf16[256,1024]{1,0:T(8,128)(2,1)S(1)} fusion(bf16[1,2,256,1024]{3,2,1,0:T(8,128)(2,1)} %refs_8_.1), kind=kLoop, calls=%fused_computation | loop fusion | bytes 1048576 | tf_op jit(solution)/shard_map/squeeze | solution.py:456
  1.1 3.2 %collective-permute-start = (bf16[256,1024]{1,0:T(8,128)(2,1)S(1)}, bf16[256,1024]{1,0:T(8,128)(2,1)S(1)}, u32[]{:S(2)}, u32[]{:S(2)}) collective-permute-start(bf16[256,1024]{1,0:T(8,128)(2,1)S(1)} %slice_bitcast_fusion.refs_0_), channel_id=1, source_target_pairs={{0,1},{1,2},{2,3},{4,5},{5,6},{6,7},{8,9},{9,10},{10,11},{12,13},{... | collective-permute-start | bytes 1572872 | tf_op jit(solution)/shard_map/ppermute | solution.py:454
  4.3 1.3 %collective-permute-start.1 = (bf16[256,1024]{1,0:T(8,128)(2,1)S(1)}, bf16[256,1024]{1,0:T(8,128)(2,1)S(1)}, u32[]{:S(2)}, u32[]{:S(2)}) collective-permute-start(bf16[256,1024]{1,0:T(8,128)(2,1)S(1)} %slice_bitcast_fusion.refs_0_), channel_id=1, source_target_pairs={{1,0},{2,1},{3,2},{5,4},{6,5},{7,6},{9,8},{10,9},{11,10},{13,12},{... | collective-permute-start | bytes 1572872 | tf_op jit(solution)/shard_map/ppermute | solution.py:454
  5.6 5.6 %shard_map.73 = (f32[4,512,1024]{2,1,0:T(8,128)S(1)}, bf16[1024,4096]{1,0:T(8,128)(2,1)S(1)}, bf16[1,2,256,1024]{3,2,1,0:T(8,128)(2,1)S(1)}, bf16[256,1024]{1,0:...) custom-call(s32[1]{0:T(128)} %bitcast.refs_0_, ...), custom_call_target="tpu_custom_call" | custom-call | flops 2415919104 | bytes 11534336 | tf_op jit(solution)/shard_map/pallas_call | solution.py:147
  11.2 3.6 %collective-permute-done.refs_0_ = bf16[256,1024]{1,0:T(8,128)(2,1)S(1)} collective-permute-done((bf16[256,1024]{1,0:T(8,128)(2,1)S(1)}, bf16[256,1024]{1,0:T(8,128)(2,1)S(1)}, u32[]{:S(2)}, u32[]{:S(2)}) %collective-permute-start) | collective-permute-done | bytes 524320 | tf_op jit(solution)/shard_map/ppermute | solution.py:454
  15.6 3.1 %collective-permute-done.1.refs_0_ = bf16[256,1024]{1,0:T(8,128)(2,1)S(1)} collective-permute-done((bf16[256,1024]{1,0:T(8,128)(2,1)S(1)}, bf16[256,1024]{1,0:T(8,128)(2,1)S(1)}, u32[]{:S(2)}, u32[]{:S(2)}) %collective-permute-start.1) | collective-permute-done | bytes 524320 | tf_op jit(solution)/shard_map/ppermute | solution.py:454
  18.7 1.3 %collective-permute-start.4 = (bf16[256,1024]{1,0:T(8,128)(2,1)S(1)}, bf16[256,1024]{1,0:T(8,128)(2,1)S(1)}, u32[]{:S(2)}, u32[]{:S(2)}) collective-permute-start(bf16[256,1024]{1,0:T(8,128)(2,1)S(1)} %shard_map.75.refs_2_), channel_id=1, source_target_pairs={{1,0},{2,1},{5,4},{6,5},{9,8},{10,9},{13,12},{14,13},{17,16},{18,1... | collective-permute-start | bytes 1572872 | tf_op jit(solution)/shard_map/ppermute | solution.py:454
  20.0 4.2 %collective-permute-start.2 = (bf16[256,1024]{1,0:T(8,128)(2,1)S(1)}, bf16[256,1024]{1,0:T(8,128)(2,1)S(1)}, u32[]{:S(2)}, u32[]{:S(2)}) collective-permute-start(bf16[256,1024]{1,0:T(8,128)(2,1)S(1)} %shard_map.76.refs_0_), channel_id=1, source_target_pairs={{0,1},{1,2},{2,3},{4,5},{5,6},{6,7},{8,9},{9,10},{10,11},{12,13},{... | collective-permute-start | bytes 1572872 | tf_op jit(solution)/shard_map/ppermute | solution.py:454
  24.2 1.3 %collective-permute-start.9 = (bf16[256,1024]{1,0:T(8,128)(2,1)S(1)}, bf16[256,1024]{1,0:T(8,128)(2,1)S(1)}, u32[]{:S(2)}, u32[]{:S(2)}) collective-permute-start(bf16[256,1024]{1,0:T(8,128)(2,1)S(1)} %shard_map.76.refs_0_), channel_id=1, source_target_pairs={{1,0},{2,1},{3,2},{5,4},{6,5},{7,6},{9,8},{10,9},{11,10},{13,12},{... | collective-permute-start | bytes 1572872 | tf_op jit(solution)/shard_map/ppermute | solution.py:454
  26.2 6.3 %collective-permute-done.4.refs_2_.refs_4_ = bf16[256,1024]{1,0:T(8,128)(2,1)S(1)} collective-permute-done((bf16[256,1024]{1,0:T(8,128)(2,1)S(1)}, bf16[256,1024]{1,0:T(8,128)(2,1)S(1)}, u32[]{:S(2)}, u32[]{:S(2)}) %collective-permute-start.4) | collective-permute-done | bytes 524320 | tf_op jit(solution)/shard_map/ppermute | solution.py:454
  32.5 1.3 %collective-permute-start.7 = (bf16[256,1024]{1,0:T(8,128)(2,1)S(1)}, bf16[256,1024]{1,0:T(8,128)(2,1)S(1)}, u32[]{:S(2)}, u32[]{:S(2)}) collective-permute-start(bf16[256,1024]{1,0:T(8,128)(2,1)S(1)} %collective-permute-done.4.refs_2_.refs_4_), channel_id=1, source_target_pairs={{1,0},{5,4},{9,8},{13,12},{17,16},{21,20},{25,24},{29,28}} | collective-permute-start | bytes 1572872 | tf_op jit(solution)/shard_map/ppermute | solution.py:454
  34.5 9.2 %collective-permute-done.9.refs_0_ = bf16[256,1024]{1,0:T(8,128)(2,1)S(1)} collective-permute-done((bf16[256,1024]{1,0:T(8,128)(2,1)S(1)}, bf16[256,1024]{1,0:T(8,128)(2,1)S(1)}, u32[]{:S(2)}, u32[]{:S(2)}) %collective-permute-start.9) | collective-permute-done | bytes 524320 | tf_op jit(solution)/shard_map/ppermute | solution.py:454
  43.7 1.3 %collective-permute-start.10 = (bf16[256,1024]{1,0:T(8,128)(2,1)S(1)}, bf16[256,1024]{1,0:T(8,128)(2,1)S(1)}, u32[]{:S(2)}, u32[]{:S(2)}) collective-permute-start(bf16[256,1024]{1,0:T(8,128)(2,1)S(1)} %shard_map.81.refs_2_), channel_id=1, source_target_pairs={{1,0},{2,1},{5,4},{6,5},{9,8},{10,9},{13,12},{14,13},{17,16},{18,1... | collective-permute-start | bytes 1572872 | tf_op jit(solution)/shard_map/ppermute | solution.py:454
  45.0 2.3 %shard_map.78.refs_4_ = f32[256,1024]{1,0:T(8,128)S(1)} custom-call(s32[2,8]{1,0:T(2,128)S(4)} %get-tuple-element.14.facts_ref, bf16[256,1024]{1,0:T(8,128)(2,1)S(1)} %slice_bitcast_fusion.refs_0_, bf16[256,1024]{1,0:T(8,128)(2,1)S(1)} %shard_map.74.refs_1_, bf16[256,1024]{1,0:T(8,128)(2,1)S(1)} %shard_map.75.refs_2_, ...), custom_call_target="tpu_custom_call" | custom-call | flops 1610612736 | bytes 13107200 | tf_op jit(solution)/shard_map/pallas_call | solution.py:218
  47.3 7.7 %collective-permute-done.7.refs_1_ = bf16[256,1024]{1,0:T(8,128)(2,1)S(1)} collective-permute-done((bf16[256,1024]{1,0:T(8,128)(2,1)S(1)}, bf16[256,1024]{1,0:T(8,128)(2,1)S(1)}, u32[]{:S(2)}, u32[]{:S(2)}) %collective-permute-start.7) | collective-permute-done | bytes 524320 | tf_op jit(solution)/shard_map/ppermute | solution.py:454
  55.0 0.9 shard_map.79.refs_1_.refs_0_
  56.6 9.6 %collective-permute-done.10.refs_0_ = bf16[256,1024]{1,0:T(8,128)(2,1)S(1)} collective-permute-done((bf16[256,1024]{1,0:T(8,128)(2,1)S(1)}, bf16[256,1024]{1,0:T(8,128)(2,1)S(1)}, u32[]{:S(2)}, u32[]{:S(2)}) %collective-permute-start.10) | collective-permute-done | bytes 524320 | tf_op jit(solution)/shard_map/ppermute | solution.py:454
  66.2 1.3 %collective-permute-start.11 = (bf16[256,1024]{1,0:T(8,128)(2,1)S(1)}, bf16[256,1024]{1,0:T(8,128)(2,1)S(1)}, u32[]{:S(2)}, u32[]{:S(2)}) collective-permute-start(bf16[256,1024]{1,0:T(8,128)(2,1)S(1)} %shard_map.82.refs_4_), channel_id=1, source_target_pairs={{1,0},{5,4},{9,8},{13,12},{17,16},{21,20},{25,24},{29,28}} | collective-permute-start | bytes 1572872 | tf_op jit(solution)/shard_map/ppermute | solution.py:454
  67.5 3.1 %collective-permute-start.12 = (bf16[256,1024]{1,0:T(8,128)(2,1)S(1)}, bf16[256,1024]{1,0:T(8,128)(2,1)S(1)}, u32[]{:S(2)}, u32[]{:S(2)}) collective-permute-start(bf16[256,1024]{1,0:T(8,128)(2,1)S(1)} %shard_map.79.refs_1_.refs_0_), channel_id=1, source_target_pairs={{0,8},{4,12},{8,16},{12,20},{16,24},{20,28},{1,9},{5,13},{9,17},{1... | collective-permute-start | bytes 1572872 | tf_op jit(solution)/shard_map/ppermute | solution.py:418
  70.6 3.0 %collective-permute-start.13 = (bf16[256,1024]{1,0:T(8,128)(2,1)S(1)}, bf16[256,1024]{1,0:T(8,128)(2,1)S(1)}, u32[]{:S(2)}, u32[]{:S(2)}) collective-permute-start(bf16[256,1024]{1,0:T(8,128)(2,1)S(1)} %shard_map.79.refs_1_.refs_0_), channel_id=1, source_target_pairs={{0,4},{4,0},{8,12},{12,8},{16,20},{20,16},{24,28},{28,24},{1,5},{5... | collective-permute-start | bytes 1572872 | tf_op jit(solution)/shard_map/ppermute | solution.py:423
  73.6 1.3 %collective-permute-start.14 = (bf16[256,1024]{1,0:T(8,128)(2,1)S(1)}, bf16[256,1024]{1,0:T(8,128)(2,1)S(1)}, u32[]{:S(2)}, u32[]{:S(2)}) collective-permute-start(bf16[256,1024]{1,0:T(8,128)(2,1)S(1)} %shard_map.79.refs_1_.refs_0_), channel_id=1, source_target_pairs={{4,16},{12,24},{28,20},{5,17},{13,25},{29,21},{6,18},{14,26},{30,2... | collective-permute-start | bytes 1572872 | tf_op jit(solution)/shard_map/ppermute | solution.py:430
  74.9 3.1 %shard_map.83.refs_7_.refs_0_ = f32[256,1024]{1,0:T(8,128)S(1)} custom-call(s32[2,8]{1,0:T(2,128)S(4)} %get-tuple-element.14.facts_ref, bf16[512,256]{1,0:T(8,128)(2,1)S(1)} %get-tuple-element.15.table_ref, bf16[512,512]{1,0:T(8,128)(2,1)S(1)} %get-tuple-element.16.back_ref, f32[4,512,1024]{2,1,0:T(8,128)S(1)} %get-tuple-element.17.spec_ref, ...), custom_call_target="tpu_custom_call" | custom-call | flops 2147483648 | bytes 1048576 | tf_op jit(solution)/shard_map/pallas_call | solution.py:368
  78.0 2.3 %shard_map.84.refs_4_ = f32[256,1024]{1,0:T(8,128)S(1)} custom-call(s32[2,8]{1,0:T(2,128)S(4)} %get-tuple-element.14.facts_ref, bf16[256,1024]{1,0:T(8,128)(2,1)S(1)} %shard_map.76.refs_0_, bf16[256,1024]{1,0:T(8,128)(2,1)S(1)} %shard_map.77.refs_1_, bf16[256,1024]{1,0:T(8,128)(2,1)S(1)} %shard_map.81.refs_2_, bf16[256,1024]{1,0:T(8,128)(2,1)S(1)} %shard_map.80.refs_3_, ...), custom_call_target="tpu_custom_call" | custom-call | flops 1610612736 | bytes 13107200 | tf_op jit(solution)/shard_map/pallas_call | solution.py:218
  80.3 1.1 %shard_map.85.refs_0_ = bf16[256,1024]{1,0:T(8,128)(2,1)S(1)} custom-call(s32[2,8]{1,0:T(2,128)S(4)} %get-tuple-element.14.facts_ref, bf16[256,1024]{1,0:T(8,128)(2,1)S(1)} %collective-permute-done.8.refs_0_, bf16[256,1024]{1,0:T(8,128)(2,1)S(1)} %collective-permute-done.11.refs_1_, bf16[1024,4096]{1,0:T(8,128)(2,1)S(1)} %get-tuple-element.20.refs_5_.refs_2_, ...), custom_call_target="tpu_custom_call" | custom-call | flops 805306368 | bytes 5242880 | tf_op jit(solution)/shard_map/pallas_call | solution.py:218
  81.4 3.9 %collective-permute-start.15 = (bf16[256,1024]{1,0:T(8,128)(2,1)S(1)}, bf16[256,1024]{1,0:T(8,128)(2,1)S(1)}, u32[]{:S(2)}, u32[]{:S(2)}) collective-permute-start(bf16[256,1024]{1,0:T(8,128)(2,1)S(1)} %shard_map.85.refs_0_), channel_id=1, source_target_pairs={{8,0},{12,4},{16,8},{20,12},{24,16},{28,20},{9,1},{13,5},{17,9},{2... | collective-permute-start | bytes 1572872 | tf_op jit(solution)/shard_map/ppermute | solution.py:418
  85.3 3.3 %collective-permute-start.17 = (bf16[256,1024]{1,0:T(8,128)(2,1)S(1)}, bf16[256,1024]{1,0:T(8,128)(2,1)S(1)}, u32[]{:S(2)}, u32[]{:S(2)}) collective-permute-start(bf16[256,1024]{1,0:T(8,128)(2,1)S(1)} %shard_map.85.refs_0_), channel_id=1, source_target_pairs={{4,0},{12,8},{20,16},{28,24},{16,4},{24,12},{5,1},{13,9},{21,17},{... | collective-permute-start | bytes 1572872 | tf_op jit(solution)/shard_map/ppermute | solution.py:439
  88.7 1.6 %shard_map.86.refs_1_.refs_0_ = f32[256,1024]{1,0:T(8,128)S(1)} custom-call(s32[2,8]{1,0:T(2,128)S(4)} %get-tuple-element.14.facts_ref, bf16[512,256]{1,0:T(8,128)(2,1)S(1)} %get-tuple-element.15.table_ref, bf16[512,512]{1,0:T(8,128)(2,1)S(1)} %get-tuple-element.16.back_ref, f32[4,512,1024]{2,1,0:T(8,128)S(1)} %get-tuple-element.17.spec_ref, ...), custom_call_target="tpu_custom_call" | custom-call | flops 2147483648 | bytes 1048576 | tf_op jit(solution)/shard_map/pallas_call | solution.py:368
  90.3 5.0 %collective-permute-done.15.refs_0_ = bf16[256,1024]{1,0:T(8,128)(2,1)S(1)} collective-permute-done((bf16[256,1024]{1,0:T(8,128)(2,1)S(1)}, bf16[256,1024]{1,0:T(8,128)(2,1)S(1)}, u32[]{:S(2)}, u32[]{:S(2)}) %collective-permute-start.15) | collective-permute-done | bytes 524320 | tf_op jit(solution)/shard_map/ppermute | solution.py:418
  95.3 3.3 %collective-permute-start.16 = (bf16[256,1024]{1,0:T(8,128)(2,1)S(1)}, bf16[256,1024]{1,0:T(8,128)(2,1)S(1)}, u32[]{:S(2)}, u32[]{:S(2)}) collective-permute-start(bf16[256,1024]{1,0:T(8,128)(2,1)S(1)} %shard_map.87.refs_5_), channel_id=1, source_target_pairs={{0,4},{4,0},{8,12},{12,8},{16,20},{20,16},{24,28},{28,24},{1,5},{5... | collective-permute-start | bytes 1572872 | tf_op jit(solution)/shard_map/ppermute | solution.py:423
  98.6 3.6 %shard_map.88 = (f32[1,2,256,1024]{3,2,1,0:T(8,128)}, f32[8,128]{1,0:T(8,128)}) custom-call(s32[2,8]{1,0:T(2,128)S(4)} %get-tuple-element.14.facts_ref, bf16[512,256]{1,0:T(8,128)(2,1)S(1)} %get-tuple-element.15.table_ref, bf16[512,512]{1,0:T(8,128)(2,1)S(1)} %get-tuple-element.16.back_ref, f32[4,512,1024]{2,1,0:T(8,128)S(1)} %get-tuple-element.17.spec_ref, ...), custom_call_target="tpu_custom_call" | custom-call | flops 2147483648 | bytes 1048576 | tf_op jit(solution)/shard_map/pallas_call | solution.py:368
  102.2 1.2 %collective-permute-done.17.refs_7_ = bf16[256,1024]{1,0:T(8,128)(2,1)S(1)} collective-permute-done((bf16[256,1024]{1,0:T(8,128)(2,1)S(1)}, bf16[256,1024]{1,0:T(8,128)(2,1)S(1)}, u32[]{:S(2)}, u32[]{:S(2)}) %collective-permute-start.17) | collective-permute-done | bytes 524320 | tf_op jit(solution)/shard_map/ppermute | solution.py:439
  103.4 2.7 %shard_map.89 = f32[1,2,256,1024]{3,2,1,0:T(8,128)} custom-call(s32[2,8]{1,0:T(2,128)S(4)} %get-tuple-element.14.facts_ref, bf16[512,256]{1,0:T(8,128)(2,1)S(1)} %get-tuple-element.15.table_ref, bf16[512,512]{1,0:T(8,128)(2,1)S(1)} %get-tuple-element.16.back_ref, f32[4,512,1024]{2,1,0:T(8,128)S(1)} %get-tuple-element.17.spec_ref, ...), custom_call_target="tpu_custom_call", output_to_operand_aliasing={{}: (12, {})} | custom-call | flops 2147483648 | bytes 1048576 | tf_op jit(solution)/shard_map/pallas_call | solution.py:368
  (24 shorter events, 2.9 us)
Async XLA Ops:
  1.1 13.8 %collective-permute-start = (bf16[256,1024]{1,0:T(8,128)(2,1)S(1)}, bf16[256,1024]{1,0:T(8,128)(2,1)S(1)}, u32[]{:S(2)}, u32[]{:S(2)}) collective-permute-start(bf16[256,1024]{1,0:T(8,128)(2,1)S(1)} %slice_bitcast_fusion.refs_0_), channel_id=1, source_target_pairs={{0,1},{1,2},{2,3},{4,5},{5,6},{6,7},{8,9},{9,10},{10,11},{12,13},{... | collective-permute-start | bytes 1572872 | tf_op jit(solution)/shard_map/ppermute | solution.py:454
  4.3 14.4 %collective-permute-start.1 = (bf16[256,1024]{1,0:T(8,128)(2,1)S(1)}, bf16[256,1024]{1,0:T(8,128)(2,1)S(1)}, u32[]{:S(2)}, u32[]{:S(2)}) collective-permute-start(bf16[256,1024]{1,0:T(8,128)(2,1)S(1)} %slice_bitcast_fusion.refs_0_), channel_id=1, source_target_pairs={{1,0},{2,1},{3,2},{5,4},{6,5},{7,6},{9,8},{10,9},{11,10},{13,12},{... | collective-permute-start | bytes 1572872 | tf_op jit(solution)/shard_map/ppermute | solution.py:454
  14.9 10.6 %collective-permute-start.3 = (bf16[256,1024]{1,0:T(8,128)(2,1)S(1)}, bf16[256,1024]{1,0:T(8,128)(2,1)S(1)}, u32[]{:S(2)}, u32[]{:S(2)}) collective-permute-start(bf16[256,1024]{1,0:T(8,128)(2,1)S(1)} %shard_map.74.refs_1_), channel_id=1, source_target_pairs={{1,2},{2,3},{5,6},{6,7},{9,10},{10,11},{13,14},{14,15},{17,18},{18... | collective-permute-start | bytes 1572872 | tf_op jit(solution)/shard_map/ppermute | solution.py:454
  18.7 13.8 %collective-permute-start.4 = (bf16[256,1024]{1,0:T(8,128)(2,1)S(1)}, bf16[256,1024]{1,0:T(8,128)(2,1)S(1)}, u32[]{:S(2)}, u32[]{:S(2)}) collective-permute-start(bf16[256,1024]{1,0:T(8,128)(2,1)S(1)} %shard_map.75.refs_2_), channel_id=1, source_target_pairs={{1,0},{2,1},{5,4},{6,5},{9,8},{10,9},{13,12},{14,13},{17,16},{18,1... | collective-permute-start | bytes 1572872 | tf_op jit(solution)/shard_map/ppermute | solution.py:454
  20.0 13.8 %collective-permute-start.2 = (bf16[256,1024]{1,0:T(8,128)(2,1)S(1)}, bf16[256,1024]{1,0:T(8,128)(2,1)S(1)}, u32[]{:S(2)}, u32[]{:S(2)}) collective-permute-start(bf16[256,1024]{1,0:T(8,128)(2,1)S(1)} %shard_map.76.refs_0_), channel_id=1, source_target_pairs={{0,1},{1,2},{2,3},{4,5},{5,6},{6,7},{8,9},{9,10},{10,11},{12,13},{... | collective-permute-start | bytes 1572872 | tf_op jit(solution)/shard_map/ppermute | solution.py:454
  24.2 19.5 %collective-permute-start.9 = (bf16[256,1024]{1,0:T(8,128)(2,1)S(1)}, bf16[256,1024]{1,0:T(8,128)(2,1)S(1)}, u32[]{:S(2)}, u32[]{:S(2)}) collective-permute-start(bf16[256,1024]{1,0:T(8,128)(2,1)S(1)} %shard_map.76.refs_0_), channel_id=1, source_target_pairs={{1,0},{2,1},{3,2},{5,4},{6,5},{7,6},{9,8},{10,9},{11,10},{13,12},{... | collective-permute-start | bytes 1572872 | tf_op jit(solution)/shard_map/ppermute | solution.py:454
  25.5 21.8 %collective-permute-start.6 = (bf16[256,1024]{1,0:T(8,128)(2,1)S(1)}, bf16[256,1024]{1,0:T(8,128)(2,1)S(1)}, u32[]{:S(2)}, u32[]{:S(2)}) collective-permute-start(bf16[256,1024]{1,0:T(8,128)(2,1)S(1)} %collective-permute-done.3.refs_1_.refs_3_), channel_id=1, source_target_pairs={{2,3},{6,7},{10,11},{14,15},{18,19},{22,23},{26,27},{30,31}} | collective-permute-start | bytes 1572872 | tf_op jit(solution)/shard_map/ppermute | solution.py:454
  32.5 22.5 %collective-permute-start.7 = (bf16[256,1024]{1,0:T(8,128)(2,1)S(1)}, bf16[256,1024]{1,0:T(8,128)(2,1)S(1)}, u32[]{:S(2)}, u32[]{:S(2)}) collective-permute-start(bf16[256,1024]{1,0:T(8,128)(2,1)S(1)} %collective-permute-done.4.refs_2_.refs_4_), channel_id=1, source_target_pairs={{1,0},{5,4},{9,8},{13,12},{17,16},{21,20},{25,24},{29,28}} | collective-permute-start | bytes 1572872 | tf_op jit(solution)/shard_map/ppermute | solution.py:454
  33.8 22.1 %collective-permute-start.5 = (bf16[256,1024]{1,0:T(8,128)(2,1)S(1)}, bf16[256,1024]{1,0:T(8,128)(2,1)S(1)}, u32[]{:S(2)}, u32[]{:S(2)}) collective-permute-start(bf16[256,1024]{1,0:T(8,128)(2,1)S(1)} %shard_map.77.refs_1_), channel_id=1, source_target_pairs={{1,2},{2,3},{5,6},{6,7},{9,10},{10,11},{13,14},{14,15},{17,18},{18... | collective-permute-start | bytes 1572872 | tf_op jit(solution)/shard_map/ppermute | solution.py:454
  43.7 22.5 %collective-permute-start.10 = (bf16[256,1024]{1,0:T(8,128)(2,1)S(1)}, bf16[256,1024]{1,0:T(8,128)(2,1)S(1)}, u32[]{:S(2)}, u32[]{:S(2)}) collective-permute-start(bf16[256,1024]{1,0:T(8,128)(2,1)S(1)} %shard_map.81.refs_2_), channel_id=1, source_target_pairs={{1,0},{2,1},{5,4},{6,5},{9,8},{10,9},{13,12},{14,13},{17,16},{18,1... | collective-permute-start | bytes 1572872 | tf_op jit(solution)/shard_map/ppermute | solution.py:454
  55.9 24.3 %collective-permute-start.8 = (bf16[256,1024]{1,0:T(8,128)(2,1)S(1)}, bf16[256,1024]{1,0:T(8,128)(2,1)S(1)}, u32[]{:S(2)}, u32[]{:S(2)}) collective-permute-start(bf16[256,1024]{1,0:T(8,128)(2,1)S(1)} %shard_map.80.refs_3_), channel_id=1, source_target_pairs={{2,3},{6,7},{10,11},{14,15},{18,19},{22,23},{26,27},{30,31}} | collective-permute-start | bytes 1572872 | tf_op jit(solution)/shard_map/ppermute | solution.py:454
  66.2 14.1 %collective-permute-start.11 = (bf16[256,1024]{1,0:T(8,128)(2,1)S(1)}, bf16[256,1024]{1,0:T(8,128)(2,1)S(1)}, u32[]{:S(2)}, u32[]{:S(2)}) collective-permute-start(bf16[256,1024]{1,0:T(8,128)(2,1)S(1)} %shard_map.82.refs_4_), channel_id=1, source_target_pairs={{1,0},{5,4},{9,8},{13,12},{17,16},{21,20},{25,24},{29,28}} | collective-permute-start | bytes 1572872 | tf_op jit(solution)/shard_map/ppermute | solution.py:454
  67.5 12.8 %collective-permute-start.12 = (bf16[256,1024]{1,0:T(8,128)(2,1)S(1)}, bf16[256,1024]{1,0:T(8,128)(2,1)S(1)}, u32[]{:S(2)}, u32[]{:S(2)}) collective-permute-start(bf16[256,1024]{1,0:T(8,128)(2,1)S(1)} %shard_map.79.refs_1_.refs_0_), channel_id=1, source_target_pairs={{0,8},{4,12},{8,16},{12,20},{16,24},{20,28},{1,9},{5,13},{9,17},{1... | collective-permute-start | bytes 1572872 | tf_op jit(solution)/shard_map/ppermute | solution.py:418
  70.6 9.7 %collective-permute-start.13 = (bf16[256,1024]{1,0:T(8,128)(2,1)S(1)}, bf16[256,1024]{1,0:T(8,128)(2,1)S(1)}, u32[]{:S(2)}, u32[]{:S(2)}) collective-permute-start(bf16[256,1024]{1,0:T(8,128)(2,1)S(1)} %shard_map.79.refs_1_.refs_0_), channel_id=1, source_target_pairs={{0,4},{4,0},{8,12},{12,8},{16,20},{20,16},{24,28},{28,24},{1,5},{5... | collective-permute-start | bytes 1572872 | tf_op jit(solution)/shard_map/ppermute | solution.py:423
  73.6 15.2 %collective-permute-start.14 = (bf16[256,1024]{1,0:T(8,128)(2,1)S(1)}, bf16[256,1024]{1,0:T(8,128)(2,1)S(1)}, u32[]{:S(2)}, u32[]{:S(2)}) collective-permute-start(bf16[256,1024]{1,0:T(8,128)(2,1)S(1)} %shard_map.79.refs_1_.refs_0_), channel_id=1, source_target_pairs={{4,16},{12,24},{28,20},{5,17},{13,25},{29,21},{6,18},{14,26},{30,2... | collective-permute-start | bytes 1572872 | tf_op jit(solution)/shard_map/ppermute | solution.py:430
  81.4 14.0 %collective-permute-start.15 = (bf16[256,1024]{1,0:T(8,128)(2,1)S(1)}, bf16[256,1024]{1,0:T(8,128)(2,1)S(1)}, u32[]{:S(2)}, u32[]{:S(2)}) collective-permute-start(bf16[256,1024]{1,0:T(8,128)(2,1)S(1)} %shard_map.85.refs_0_), channel_id=1, source_target_pairs={{8,0},{12,4},{16,8},{20,12},{24,16},{28,20},{9,1},{13,5},{17,9},{2... | collective-permute-start | bytes 1572872 | tf_op jit(solution)/shard_map/ppermute | solution.py:418
  85.3 18.1 %collective-permute-start.17 = (bf16[256,1024]{1,0:T(8,128)(2,1)S(1)}, bf16[256,1024]{1,0:T(8,128)(2,1)S(1)}, u32[]{:S(2)}, u32[]{:S(2)}) collective-permute-start(bf16[256,1024]{1,0:T(8,128)(2,1)S(1)} %shard_map.85.refs_0_), channel_id=1, source_target_pairs={{4,0},{12,8},{20,16},{28,24},{16,4},{24,12},{5,1},{13,9},{21,17},{... | collective-permute-start | bytes 1572872 | tf_op jit(solution)/shard_map/ppermute | solution.py:439
  88.7 10.0 %collective-permute-start.18 = (bf16[256,1024]{1,0:T(8,128)(2,1)S(1)}, bf16[256,1024]{1,0:T(8,128)(2,1)S(1)}, u32[]{:S(2)}, u32[]{:S(2)}) collective-permute-start(bf16[256,1024]{1,0:T(8,128)(2,1)S(1)} %collective-permute-done.12.refs_5_.refs_1_.refs_3_), channel_id=1, source_target_pairs={{0,4},{4,0},{8,12},{12,8},{16,20},{20,16},{24,28},{28,24},{1,5},{5... | collective-permute-start | bytes 1572872 | tf_op jit(solution)/shard_map/ppermute | solution.py:423
  95.3 8.1 %collective-permute-start.16 = (bf16[256,1024]{1,0:T(8,128)(2,1)S(1)}, bf16[256,1024]{1,0:T(8,128)(2,1)S(1)}, u32[]{:S(2)}, u32[]{:S(2)}) collective-permute-start(bf16[256,1024]{1,0:T(8,128)(2,1)S(1)} %shard_map.87.refs_5_), channel_id=1, source_target_pairs={{0,4},{4,0},{8,12},{12,8},{16,20},{20,16},{24,28},{28,24},{1,5},{5... | collective-permute-start | bytes 1572872 | tf_op jit(solution)/shard_map/ppermute | solution.py:423

commit v15 on v14

--- a/solution.py
+++ b/solution.py
@@ -401,15 +401,19 @@
     return conv_call(body, tabs, facts, arrays, shape, spec, scratch, (), result)
 
 
-def ordered(value, *earlier):
+def together(values, *earlier):
     return pl.pallas_call(
         lambda *refs: None,
-        out_shape=jax.ShapeDtypeStruct(value.shape, value.dtype),
-        in_specs=[ANYWHERE] * (1 + len(earlier)),
-        out_specs=ANYWHERE,
-        input_output_aliases={0: 0},
+        out_shape=[jax.ShapeDtypeStruct(one.shape, one.dtype) for one in values],
+        in_specs=[ANYWHERE] * (len(values) + len(earlier)),
+        out_specs=[ANYWHERE] * len(values),
+        input_output_aliases={at: at for at in range(len(values))},
         compiler_params=params(VMEM // 20),
-    )(value, *earlier)
+    )(*values, *earlier)
+
+
+def ordered(value, *earlier):
+    return together([value], *earlier)[0]
 
 
 def shifted(value, steps):
@@ -436,7 +440,7 @@
     mixed = [(source, source - 1) for source in range(1, count, 2)]
     mixed += [(source, source - 3) for source in range(4, count, 2)]
     two = ordered(shifted(value, -2), own)
-    mixed = lax.ppermute(value, "ctx", mixed)
+    mixed = lax.ppermute(ordered(value, two), "ctx", mixed)
     return [two, core_swapped(two), mixed]
 
 
@@ -473,7 +477,7 @@
 
     def pass_on(chain, *earlier):
         if earlier:
-            chain[-1] = [ordered(one, *earlier) for one in chain[-1]]
+            chain[-1] = together(chain[-1], *earlier)
         chain.append(sent(len(chain) + 1, *chain[-1]))
 
     hops = [0] + [way * step for step in range(1, count) for way in (-1, 1)]
@@ -495,15 +499,14 @@
         pass_on(lower_in, *upper_in[-2])
     partial = partial_of(start, upper_in, 1)
     upper = final_of(upper_in, 1, partial)
-    pass_on(lower_in, upper)
-
     upper_halo = upper_halo_of(upper)
     two, swapped, mate, fold = upper_halo
     near = own_terms(1, tabs, facts, [upper])
+    pass_on(lower_in, upper, mate, near)
     result, _ = far_terms(1, 1, tabs, facts, [near, *upper_halo])
 
-    partial = partial_of(own, lower_in, 0, [near])
-    lower = final_of(lower_in, 0, partial, [two, mate])
+    partial = partial_of(own, lower_in, 0)
+    lower = final_of(lower_in, 0, partial, [two])
     near = own_terms(0, tabs, facts, [lower], after=[fold])
     lower_halo = lower_halo_of(lower, near)
     arrays = [near, upper, mate, two, fold, *lower_halo]

time: 108 us -> 117 us (1.083); the launches traced: 106 us -> 117 us
  starting transfers between devices: 35.9 us -> 43 us
  waiting for transfers between devices: 45.8 us -> 49.3 us
    ppermute x3, starting transfers between devices: 6.28 us -> 11.3 us  [core_swapped(): lax.ppermute(value, 'ctx', [(source, source ^ 1) for source in range(coun...]
    ppermute x1, waiting for transfers between devices: 1.22 us -> 5.79 us  [lower_halo_of(): mixed = lax.ppermute(ordered(value, two), 'ctx', mixed)]
    ppermute x12, waiting for transfers between devices: 39.6 us -> 35.7 us  [sent(): return (lax.ppermute(up, 'ch', upward), lax.ppermute(down, 'ch', downward))]
    ppermute x1, starting transfers between devices: 1.31 us -> 4.68 us  [upper_halo_of(): mate, far = (core_swapped(value), lax.ppermute(value, 'ctx', far))]
    ppermute x2, waiting for transfers between devices: 5.03 us -> 7.74 us  [shifted(): lax.ppermute(value, 'ctx', [(source, source + steps) for source in range(...]
    ppermute x12, starting transfers between devices: 17.9 us -> 20.1 us  [sent(): return (lax.ppermute(up, 'ch', upward), lax.ppermute(down, 'ch', downward))]
    ppermute x2, starting transfers between devices: 7.05 us -> 5.03 us  [shifted(): lax.ppermute(value, 'ctx', [(source, source + steps) for source in range(...]
    ppermute x1, starting transfers between devices: 3.34 us -> 1.91 us  [lower_halo_of(): mixed = lax.ppermute(ordered(value, two), 'ctx', mixed)]
  transfers between devices with their start and end apart: 19 -> 19, of which waited for: 8 -> 9; matrix products, arithmetic and copies ran while one was open for 0% -> 0% of each run, Pallas kernels for 19% -> 17%
where the time goes in v15:
time: 117 us
  waiting for transfers between devices  49.3 us (42%)
  starting transfers between devices  43 us (37%)
  Pallas kernels  23.2 us (20%)
    ppermute x12, waiting for transfers between devices, sent(): return (lax.ppermute(up, 'ch', upward), lax.ppermute(down, 'ch', downward))  35.7 us
    ppermute x12, starting transfers between devices, sent(): return (lax.ppermute(up, 'ch', upward), lax.ppermute(down, 'ch', downward))  20.1 us
    ppermute x3, starting transfers between devices, core_swapped(): lax.ppermute(value, 'ctx', [(source, source ^ 1) for source in range(coun...  11.3 us
    pallas_call x4, Pallas kernels, conv_call(): pl.pallas_call(body, grid=(width // LANES,), out_shape=out_shape, in_spec...  11 us
    ppermute x2, waiting for transfers between devices, shifted(): lax.ppermute(value, 'ctx', [(source, source + steps) for source in range(...  7.74 us
    pallas_call x4, Pallas kernels, project(): pl.pallas_call(functools.partial(project_kernel, hops, slot, before is No...  6.52 us
    ppermute x1, waiting for transfers between devices, lower_halo_of(): mixed = lax.ppermute(ordered(value, two), 'ctx', mixed)  5.79 us
    pallas_call x1, Pallas kernels, prepare(): pl.pallas_call(functools.partial(prepare_kernel, pairs), grid=(width // L...  5.59 us
  transfers between devices with their start and end apart: 19, of which 9 were waited for; matrix products, arithmetic and copies ran while one was open for 0% of the time, Pallas kernels for 17%

profile of v15, /device:TPU:3, one launch (start us, length us, event | category | flops | bytes accessed | tf_op | source)
XLA Modules:
  0.0 116.8 jit_solution(11782765179361369325)
XLA Ops:
  0.0 1.1 slice_bitcast_fusion.refs_0_
  1.1 3.2 %collective-permute-start = (bf16[256,1024]{1,0:T(8,128)(2,1)S(1)}, bf16[256,1024]{1,0:T(8,128)(2,1)S(1)}, u32[]{:S(2)}, u32[]{:S(2)}) collective-permute-start(bf16[256,1024]{1,0:T(8,128)(2,1)S(1)} %slice_bitcast_fusion.refs_0_), channel_id=1, source_target_pairs={{0,1},{1,2},{2,3},{4,5},{5,6},{6,7},{8,9},{9,10},{10,11},{12,13},{... | collective-permute-start | bytes 1572872 | tf_op jit(solution)/shard_map/ppermute | solution.py:458
  4.3 1.3 %collective-permute-start.1 = (bf16[256,1024]{1,0:T(8,128)(2,1)S(1)}, bf16[256,1024]{1,0:T(8,128)(2,1)S(1)}, u32[]{:S(2)}, u32[]{:S(2)}) collective-permute-start(bf16[256,1024]{1,0:T(8,128)(2,1)S(1)} %slice_bitcast_fusion.refs_0_), channel_id=1, source_target_pairs={{1,0},{2,1},{3,2},{5,4},{6,5},{7,6},{9,8},{10,9},{11,10},{13,12},{... | collective-permute-start | bytes 1572872 | tf_op jit(solution)/shard_map/ppermute | solution.py:458
  5.6 5.6 %shard_map.73 = (f32[4,512,1024]{2,1,0:T(8,128)S(1)}, bf16[1024,4096]{1,0:T(8,128)(2,1)S(1)}, bf16[1,2,256,1024]{3,2,1,0:T(8,128)(2,1)S(1)}, bf16[256,1024]{1,0:...) custom-call(s32[1]{0:T(128)} %bitcast.refs_0_, ...), custom_call_target="tpu_custom_call" | custom-call | flops 2415919104 | bytes 11534336 | tf_op jit(solution)/shard_map/pallas_call | solution.py:147
  11.2 3.6 %collective-permute-done.refs_0_ = bf16[256,1024]{1,0:T(8,128)(2,1)S(1)} collective-permute-done((bf16[256,1024]{1,0:T(8,128)(2,1)S(1)}, bf16[256,1024]{1,0:T(8,128)(2,1)S(1)}, u32[]{:S(2)}, u32[]{:S(2)}) %collective-permute-start) | collective-permute-done | bytes 524320 | tf_op jit(solution)/shard_map/ppermute | solution.py:458
  14.9 3.8 %collective-permute-done.1.refs_1_ = bf16[256,1024]{1,0:T(8,128)(2,1)S(1)} collective-permute-done((bf16[256,1024]{1,0:T(8,128)(2,1)S(1)}, bf16[256,1024]{1,0:T(8,128)(2,1)S(1)}, u32[]{:S(2)}, u32[]{:S(2)}) %collective-permute-start.1) | collective-permute-done | bytes 524320 | tf_op jit(solution)/shard_map/ppermute | solution.py:458
  19.4 1.3 %collective-permute-start.5 = (bf16[256,1024]{1,0:T(8,128)(2,1)S(1)}, bf16[256,1024]{1,0:T(8,128)(2,1)S(1)}, u32[]{:S(2)}, u32[]{:S(2)}) collective-permute-start(bf16[256,1024]{1,0:T(8,128)(2,1)S(1)} %get-tuple-element.27.refs_2_), channel_id=1, source_target_pairs={{1,0},{2,1},{5,4},{6,5},{9,8},{10,9},{13,12},{14,13},{17,16},{18,1... | collective-permute-start | bytes 1572872 | tf_op jit(solution)/shard_map/ppermute | solution.py:458
  20.7 6.4 %collective-permute-start.2 = (bf16[256,1024]{1,0:T(8,128)(2,1)S(1)}, bf16[256,1024]{1,0:T(8,128)(2,1)S(1)}, u32[]{:S(2)}, u32[]{:S(2)}) collective-permute-start(bf16[256,1024]{1,0:T(8,128)(2,1)S(1)} %shard_map.75.refs_0_), channel_id=1, source_target_pairs={{0,1},{1,2},{2,3},{4,5},{5,6},{6,7},{8,9},{9,10},{10,11},{12,13},{... | collective-permute-start | bytes 1572872 | tf_op jit(solution)/shard_map/ppermute | solution.py:458
  27.1 1.3 %collective-permute-start.3 = (bf16[256,1024]{1,0:T(8,128)(2,1)S(1)}, bf16[256,1024]{1,0:T(8,128)(2,1)S(1)}, u32[]{:S(2)}, u32[]{:S(2)}) collective-permute-start(bf16[256,1024]{1,0:T(8,128)(2,1)S(1)} %shard_map.75.refs_0_), channel_id=1, source_target_pairs={{1,0},{2,1},{3,2},{5,4},{6,5},{7,6},{9,8},{10,9},{11,10},{13,12},{... | collective-permute-start | bytes 1572872 | tf_op jit(solution)/shard_map/ppermute | solution.py:458
  29.1 6.1 %collective-permute-done.5.refs_3_.refs_4_ = bf16[256,1024]{1,0:T(8,128)(2,1)S(1)} collective-permute-done((bf16[256,1024]{1,0:T(8,128)(2,1)S(1)}, bf16[256,1024]{1,0:T(8,128)(2,1)S(1)}, u32[]{:S(2)}, u32[]{:S(2)}) %collective-permute-start.5) | collective-permute-done | bytes 524320 | tf_op jit(solution)/shard_map/ppermute | solution.py:458
  35.2 1.3 %collective-permute-start.9 = (bf16[256,1024]{1,0:T(8,128)(2,1)S(1)}, bf16[256,1024]{1,0:T(8,128)(2,1)S(1)}, u32[]{:S(2)}, u32[]{:S(2)}) collective-permute-start(bf16[256,1024]{1,0:T(8,128)(2,1)S(1)} %collective-permute-done.5.refs_3_.refs_4_), channel_id=1, source_target_pairs={{1,0},{5,4},{9,8},{13,12},{17,16},{21,20},{25,24},{29,28}} | collective-permute-start | bytes 1572872 | tf_op jit(solution)/shard_map/ppermute | solution.py:458
  36.5 9.9 %collective-permute-done.3.refs_1_ = bf16[256,1024]{1,0:T(8,128)(2,1)S(1)} collective-permute-done((bf16[256,1024]{1,0:T(8,128)(2,1)S(1)}, bf16[256,1024]{1,0:T(8,128)(2,1)S(1)}, u32[]{:S(2)}, u32[]{:S(2)}) %collective-permute-start.3) | collective-permute-done | bytes 524320 | tf_op jit(solution)/shard_map/ppermute | solution.py:458
  47.1 1.3 %collective-permute-start.7 = (bf16[256,1024]{1,0:T(8,128)(2,1)S(1)}, bf16[256,1024]{1,0:T(8,128)(2,1)S(1)}, u32[]{:S(2)}, u32[]{:S(2)}) collective-permute-start(bf16[256,1024]{1,0:T(8,128)(2,1)S(1)} %get-tuple-element.29.refs_2_), channel_id=1, source_target_pairs={{1,0},{2,1},{5,4},{6,5},{9,8},{10,9},{13,12},{14,13},{17,16},{18,1... | collective-permute-start | bytes 1572872 | tf_op jit(solution)/shard_map/ppermute | solution.py:458
  48.4 2.3 %shard_map.77.refs_4_ = f32[256,1024]{1,0:T(8,128)S(1)} custom-call(s32[2,8]{1,0:T(2,128)S(4)} %get-tuple-element.20.facts_ref, bf16[256,1024]{1,0:T(8,128)(2,1)S(1)} %slice_bitcast_fusion.refs_0_, bf16[256,1024]{1,0:T(8,128)(2,1)S(1)} %get-tuple-element.26.refs_1_, bf16[256,1024]{1,0:T(8,128)(2,1)S(1)} %get-tuple-element.27.refs_2_, ...), custom_call_target="tpu_custom_call" | custom-call | flops 1610612736 | bytes 13107200 | tf_op jit(solution)/shard_map/pallas_call | solution.py:218
  50.7 7.0 %collective-permute-done.9.refs_1_ = bf16[256,1024]{1,0:T(8,128)(2,1)S(1)} collective-permute-done((bf16[256,1024]{1,0:T(8,128)(2,1)S(1)}, bf16[256,1024]{1,0:T(8,128)(2,1)S(1)}, u32[]{:S(2)}, u32[]{:S(2)}) %collective-permute-start.9) | collective-permute-done | bytes 524320 | tf_op jit(solution)/shard_map/ppermute | solution.py:458
  58.6 5.2 %collective-permute-start.10 = (bf16[256,1024]{1,0:T(8,128)(2,1)S(1)}, bf16[256,1024]{1,0:T(8,128)(2,1)S(1)}, u32[]{:S(2)}, u32[]{:S(2)}) collective-permute-start(bf16[256,1024]{1,0:T(8,128)(2,1)S(1)} %shard_map.78.refs_0_.refs_2_.refs_1_), channel_id=1, source_target_pairs={{0,4},{4,0},{8,12},{12,8},{16,20},{20,16},{24,28},{28,24},{1,5},{5... | collective-permute-start | bytes 1572872 | tf_op jit(solution)/shard_map/ppermute | solution.py:427
  63.8 3.1 %collective-permute-start.13 = (bf16[256,1024]{1,0:T(8,128)(2,1)S(1)}, bf16[256,1024]{1,0:T(8,128)(2,1)S(1)}, u32[]{:S(2)}, u32[]{:S(2)}) collective-permute-start(bf16[256,1024]{1,0:T(8,128)(2,1)S(1)} %shard_map.78.refs_0_.refs_2_.refs_1_), channel_id=1, source_target_pairs={{0,8},{4,12},{8,16},{12,20},{16,24},{20,28},{1,9},{5,13},{9,17},{1... | collective-permute-start | bytes 1572872 | tf_op jit(solution)/shard_map/ppermute | solution.py:422
  66.9 3.1 %shard_map.79.refs_4_.refs_0_ = f32[256,1024]{1,0:T(8,128)S(1)} custom-call(s32[2,8]{1,0:T(2,128)S(4)} %get-tuple-element.20.facts_ref, bf16[512,256]{1,0:T(8,128)(2,1)S(1)} %get-tuple-element.21.table_ref, bf16[512,512]{1,0:T(8,128)(2,1)S(1)} %get-tuple-element.22.back_ref, f32[4,512,1024]{2,1,0:T(8,128)S(1)} %get-tuple-element.23.spec_ref, ...), custom_call_target="tpu_custom_call" | custom-call | flops 2147483648 | bytes 1048576 | tf_op jit(solution)/shard_map/pallas_call | solution.py:368
  70.8 1.3 %collective-permute-start.12 = (bf16[256,1024]{1,0:T(8,128)(2,1)S(1)}, bf16[256,1024]{1,0:T(8,128)(2,1)S(1)}, u32[]{:S(2)}, u32[]{:S(2)}) collective-permute-start(bf16[256,1024]{1,0:T(8,128)(2,1)S(1)} %get-tuple-element.33.refs_4_), channel_id=1, source_target_pairs={{1,0},{5,4},{9,8},{13,12},{17,16},{21,20},{25,24},{29,28}} | collective-permute-start | bytes 1572872 | tf_op jit(solution)/shard_map/ppermute | solution.py:458
  72.1 4.7 %collective-permute-start.14 = (bf16[256,1024]{1,0:T(8,128)(2,1)S(1)}, bf16[256,1024]{1,0:T(8,128)(2,1)S(1)}, u32[]{:S(2)}, u32[]{:S(2)}) collective-permute-start(bf16[256,1024]{1,0:T(8,128)(2,1)S(1)} %shard_map.78.refs_0_.refs_2_.refs_1_), channel_id=1, source_target_pairs={{4,16},{12,24},{28,20},{5,17},{13,25},{29,21},{6,18},{14,26},{30,2... | collective-permute-start | bytes 1572872 | tf_op jit(solution)/shard_map/ppermute | solution.py:434
  76.7 2.3 %shard_map.81.refs_4_ = f32[256,1024]{1,0:T(8,128)S(1)} custom-call(s32[2,8]{1,0:T(2,128)S(4)} %get-tuple-element.20.facts_ref, bf16[256,1024]{1,0:T(8,128)(2,1)S(1)} %shard_map.75.refs_0_, bf16[256,1024]{1,0:T(8,128)(2,1)S(1)} %get-tuple-element.28.refs_1_, bf16[256,1024]{1,0:T(8,128)(2,1)S(1)} %get-tuple-element.29.refs_2_, ...), custom_call_target="tpu_custom_call" | custom-call | flops 1610612736 | bytes 13107200 | tf_op jit(solution)/shard_map/pallas_call | solution.py:218
  79.2 5.2 %collective-permute-done.12.refs_1_ = bf16[256,1024]{1,0:T(8,128)(2,1)S(1)} collective-permute-done((bf16[256,1024]{1,0:T(8,128)(2,1)S(1)}, bf16[256,1024]{1,0:T(8,128)(2,1)S(1)}, u32[]{:S(2)}, u32[]{:S(2)}) %collective-permute-start.12) | collective-permute-done | bytes 524320 | tf_op jit(solution)/shard_map/ppermute | solution.py:458
  84.4 1.1 shard_map.82.refs_0_
  85.5 1.9 %collective-permute-start.15 = (bf16[256,1024]{1,0:T(8,128)(2,1)S(1)}, bf16[256,1024]{1,0:T(8,128)(2,1)S(1)}, u32[]{:S(2)}, u32[]{:S(2)}) collective-permute-start(bf16[256,1024]{1,0:T(8,128)(2,1)S(1)} %shard_map.82.refs_0_), channel_id=1, source_target_pairs={{8,0},{12,4},{16,8},{20,12},{24,16},{28,20},{9,1},{13,5},{17,9},{2... | collective-permute-start | bytes 1572872 | tf_op jit(solution)/shard_map/ppermute | solution.py:422
  87.5 2.6 %collective-permute-start.18 = (bf16[256,1024]{1,0:T(8,128)(2,1)S(1)}, bf16[256,1024]{1,0:T(8,128)(2,1)S(1)}, u32[]{:S(2)}, u32[]{:S(2)}) collective-permute-start(bf16[256,1024]{1,0:T(8,128)(2,1)S(1)} %collective-permute-done.13.refs_5_.refs_1_.refs_3_), channel_id=1, source_target_pairs={{0,4},{4,0},{8,12},{12,8},{16,20},{20,16},{24,28},{28,24},{1,5},{5... | collective-permute-start | bytes 1572872 | tf_op jit(solution)/shard_map/ppermute | solution.py:427
  90.1 1.6 %shard_map.83.refs_1_.refs_0_ = f32[256,1024]{1,0:T(8,128)S(1)} custom-call(s32[2,8]{1,0:T(2,128)S(4)} %get-tuple-element.20.facts_ref, bf16[512,256]{1,0:T(8,128)(2,1)S(1)} %get-tuple-element.21.table_ref, bf16[512,512]{1,0:T(8,128)(2,1)S(1)} %get-tuple-element.22.back_ref, f32[4,512,1024]{2,1,0:T(8,128)S(1)} %get-tuple-element.23.spec_ref, ...), custom_call_target="tpu_custom_call" | custom-call | flops 2147483648 | bytes 1048576 | tf_op jit(solution)/shard_map/pallas_call | solution.py:368
  91.6 7.6 %collective-permute-done.15.refs_0_ = bf16[256,1024]{1,0:T(8,128)(2,1)S(1)} collective-permute-done((bf16[256,1024]{1,0:T(8,128)(2,1)S(1)}, bf16[256,1024]{1,0:T(8,128)(2,1)S(1)}, u32[]{:S(2)}, u32[]{:S(2)}) %collective-permute-start.15) | collective-permute-done | bytes 524320 | tf_op jit(solution)/shard_map/ppermute | solution.py:422
  99.2 3.5 %collective-permute-start.16 = (bf16[256,1024]{1,0:T(8,128)(2,1)S(1)}, bf16[256,1024]{1,0:T(8,128)(2,1)S(1)}, u32[]{:S(2)}, u32[]{:S(2)}) collective-permute-start(bf16[256,1024]{1,0:T(8,128)(2,1)S(1)} %shard_map.84.refs_1_.refs_5_), channel_id=1, source_target_pairs={{0,4},{4,0},{8,12},{12,8},{16,20},{20,16},{24,28},{28,24},{1,5},{5... | collective-permute-start | bytes 1572872 | tf_op jit(solution)/shard_map/ppermute | solution.py:427
  102.7 1.9 %collective-permute-start.17 = (bf16[256,1024]{1,0:T(8,128)(2,1)S(1)}, bf16[256,1024]{1,0:T(8,128)(2,1)S(1)}, u32[]{:S(2)}, u32[]{:S(2)}) collective-permute-start(bf16[256,1024]{1,0:T(8,128)(2,1)S(1)} %shard_map.85), channel_id=1, source_target_pairs={{4,0},{12,8},{20,16},{28,24},{16,4},{24,12},{5,1},{13,9},{21,17},{... | collective-permute-start | bytes 1572872 | tf_op jit(solution)/shard_map/ppermute | solution.py:443
  104.6 2.8 %shard_map.86 = (f32[1,2,256,1024]{3,2,1,0:T(8,128)}, f32[8,128]{1,0:T(8,128)}) custom-call(s32[2,8]{1,0:T(2,128)S(4)} %get-tuple-element.20.facts_ref, bf16[512,256]{1,0:T(8,128)(2,1)S(1)} %get-tuple-element.21.table_ref, bf16[512,512]{1,0:T(8,128)(2,1)S(1)} %get-tuple-element.22.back_ref, f32[4,512,1024]{2,1,0:T(8,128)S(1)} %get-tuple-element.23.spec_ref, ...), custom_call_target="tpu_custom_call" | custom-call | flops 2147483648 | bytes 1048576 | tf_op jit(solution)/shard_map/pallas_call | solution.py:368
  107.4 5.8 %collective-permute-done.17.refs_7_ = bf16[256,1024]{1,0:T(8,128)(2,1)S(1)} collective-permute-done((bf16[256,1024]{1,0:T(8,128)(2,1)S(1)}, bf16[256,1024]{1,0:T(8,128)(2,1)S(1)}, u32[]{:S(2)}, u32[]{:S(2)}) %collective-permute-start.17) | collective-permute-done | bytes 524320 | tf_op jit(solution)/shard_map/ppermute | solution.py:443
  113.2 3.6 %shard_map.87 = f32[1,2,256,1024]{3,2,1,0:T(8,128)} custom-call(s32[2,8]{1,0:T(2,128)S(4)} %get-tuple-element.20.facts_ref, bf16[512,256]{1,0:T(8,128)(2,1)S(1)} %get-tuple-element.21.table_ref, bf16[512,512]{1,0:T(8,128)(2,1)S(1)} %get-tuple-element.22.back_ref, f32[4,512,1024]{2,1,0:T(8,128)S(1)} %get-tuple-element.23.spec_ref, ...), custom_call_target="tpu_custom_call", output_to_operand_aliasing={{}: (12, {})} | custom-call | flops 2147483648 | bytes 1048576 | tf_op jit(solution)/shard_map/pallas_call | solution.py:368
  (22 shorter events, 3.9 us)
Async XLA Ops:
  1.1 13.8 %collective-permute-start = (bf16[256,1024]{1,0:T(8,128)(2,1)S(1)}, bf16[256,1024]{1,0:T(8,128)(2,1)S(1)}, u32[]{:S(2)}, u32[]{:S(2)}) collective-permute-start(bf16[256,1024]{1,0:T(8,128)(2,1)S(1)} %slice_bitcast_fusion.refs_0_), channel_id=1, source_target_pairs={{0,1},{1,2},{2,3},{4,5},{5,6},{6,7},{8,9},{9,10},{10,11},{12,13},{... | collective-permute-start | bytes 1572872 | tf_op jit(solution)/shard_map/ppermute | solution.py:458
  4.3 14.4 %collective-permute-start.1 = (bf16[256,1024]{1,0:T(8,128)(2,1)S(1)}, bf16[256,1024]{1,0:T(8,128)(2,1)S(1)}, u32[]{:S(2)}, u32[]{:S(2)}) collective-permute-start(bf16[256,1024]{1,0:T(8,128)(2,1)S(1)} %slice_bitcast_fusion.refs_0_), channel_id=1, source_target_pairs={{1,0},{2,1},{3,2},{5,4},{6,5},{7,6},{9,8},{10,9},{11,10},{13,12},{... | collective-permute-start | bytes 1572872 | tf_op jit(solution)/shard_map/ppermute | solution.py:458
  18.7 9.7 %collective-permute-start.4 = (bf16[256,1024]{1,0:T(8,128)(2,1)S(1)}, bf16[256,1024]{1,0:T(8,128)(2,1)S(1)}, u32[]{:S(2)}, u32[]{:S(2)}) collective-permute-start(bf16[256,1024]{1,0:T(8,128)(2,1)S(1)} %get-tuple-element.26.refs_1_), channel_id=1, source_target_pairs={{1,2},{2,3},{5,6},{6,7},{9,10},{10,11},{13,14},{14,15},{17,18},{18... | collective-permute-start | bytes 1572872 | tf_op jit(solution)/shard_map/ppermute | solution.py:458
  19.4 15.8 %collective-permute-start.5 = (bf16[256,1024]{1,0:T(8,128)(2,1)S(1)}, bf16[256,1024]{1,0:T(8,128)(2,1)S(1)}, u32[]{:S(2)}, u32[]{:S(2)}) collective-permute-start(bf16[256,1024]{1,0:T(8,128)(2,1)S(1)} %get-tuple-element.27.refs_2_), channel_id=1, source_target_pairs={{1,0},{2,1},{5,4},{6,5},{9,8},{10,9},{13,12},{14,13},{17,16},{18,1... | collective-permute-start | bytes 1572872 | tf_op jit(solution)/shard_map/ppermute | solution.py:458
  20.7 15.8 %collective-permute-start.2 = (bf16[256,1024]{1,0:T(8,128)(2,1)S(1)}, bf16[256,1024]{1,0:T(8,128)(2,1)S(1)}, u32[]{:S(2)}, u32[]{:S(2)}) collective-permute-start(bf16[256,1024]{1,0:T(8,128)(2,1)S(1)} %shard_map.75.refs_0_), channel_id=1, source_target_pairs={{0,1},{1,2},{2,3},{4,5},{5,6},{6,7},{8,9},{9,10},{10,11},{12,13},{... | collective-permute-start | bytes 1572872 | tf_op jit(solution)/shard_map/ppermute | solution.py:458
  27.1 19.3 %collective-permute-start.3 = (bf16[256,1024]{1,0:T(8,128)(2,1)S(1)}, bf16[256,1024]{1,0:T(8,128)(2,1)S(1)}, u32[]{:S(2)}, u32[]{:S(2)}) collective-permute-start(bf16[256,1024]{1,0:T(8,128)(2,1)S(1)} %shard_map.75.refs_0_), channel_id=1, source_target_pairs={{1,0},{2,1},{3,2},{5,4},{6,5},{7,6},{9,8},{10,9},{11,10},{13,12},{... | collective-permute-start | bytes 1572872 | tf_op jit(solution)/shard_map/ppermute | solution.py:458
  28.4 22.3 %collective-permute-start.8 = (bf16[256,1024]{1,0:T(8,128)(2,1)S(1)}, bf16[256,1024]{1,0:T(8,128)(2,1)S(1)}, u32[]{:S(2)}, u32[]{:S(2)}) collective-permute-start(bf16[256,1024]{1,0:T(8,128)(2,1)S(1)} %collective-permute-done.4.refs_2_.refs_3_), channel_id=1, source_target_pairs={{2,3},{6,7},{10,11},{14,15},{18,19},{22,23},{26,27},{30,31}} | collective-permute-start | bytes 1572872 | tf_op jit(solution)/shard_map/ppermute | solution.py:458
  35.2 22.5 %collective-permute-start.9 = (bf16[256,1024]{1,0:T(8,128)(2,1)S(1)}, bf16[256,1024]{1,0:T(8,128)(2,1)S(1)}, u32[]{:S(2)}, u32[]{:S(2)}) collective-permute-start(bf16[256,1024]{1,0:T(8,128)(2,1)S(1)} %collective-permute-done.5.refs_3_.refs_4_), channel_id=1, source_target_pairs={{1,0},{5,4},{9,8},{13,12},{17,16},{21,20},{25,24},{29,28}} | collective-permute-start | bytes 1572872 | tf_op jit(solution)/shard_map/ppermute | solution.py:458
  46.4 23.6 %collective-permute-start.6 = (bf16[256,1024]{1,0:T(8,128)(2,1)S(1)}, bf16[256,1024]{1,0:T(8,128)(2,1)S(1)}, u32[]{:S(2)}, u32[]{:S(2)}) collective-permute-start(bf16[256,1024]{1,0:T(8,128)(2,1)S(1)} %get-tuple-element.28.refs_1_), channel_id=1, source_target_pairs={{1,2},{2,3},{5,6},{6,7},{9,10},{10,11},{13,14},{14,15},{17,18},{18... | collective-permute-start | bytes 1572872 | tf_op jit(solution)/shard_map/ppermute | solution.py:458
  47.1 22.9 %collective-permute-start.7 = (bf16[256,1024]{1,0:T(8,128)(2,1)S(1)}, bf16[256,1024]{1,0:T(8,128)(2,1)S(1)}, u32[]{:S(2)}, u32[]{:S(2)}) collective-permute-start(bf16[256,1024]{1,0:T(8,128)(2,1)S(1)} %get-tuple-element.29.refs_2_), channel_id=1, source_target_pairs={{1,0},{2,1},{5,4},{6,5},{9,8},{10,9},{13,12},{14,13},{17,16},{18,1... | collective-permute-start | bytes 1572872 | tf_op jit(solution)/shard_map/ppermute | solution.py:458
  58.6 11.5 %collective-permute-start.10 = (bf16[256,1024]{1,0:T(8,128)(2,1)S(1)}, bf16[256,1024]{1,0:T(8,128)(2,1)S(1)}, u32[]{:S(2)}, u32[]{:S(2)}) collective-permute-start(bf16[256,1024]{1,0:T(8,128)(2,1)S(1)} %shard_map.78.refs_0_.refs_2_.refs_1_), channel_id=1, source_target_pairs={{0,4},{4,0},{8,12},{12,8},{16,20},{20,16},{24,28},{28,24},{1,5},{5... | collective-permute-start | bytes 1572872 | tf_op jit(solution)/shard_map/ppermute | solution.py:427
  63.8 15.4 %collective-permute-start.13 = (bf16[256,1024]{1,0:T(8,128)(2,1)S(1)}, bf16[256,1024]{1,0:T(8,128)(2,1)S(1)}, u32[]{:S(2)}, u32[]{:S(2)}) collective-permute-start(bf16[256,1024]{1,0:T(8,128)(2,1)S(1)} %shard_map.78.refs_0_.refs_2_.refs_1_), channel_id=1, source_target_pairs={{0,8},{4,12},{8,16},{12,20},{16,24},{20,28},{1,9},{5,13},{9,17},{1... | collective-permute-start | bytes 1572872 | tf_op jit(solution)/shard_map/ppermute | solution.py:422
  70.0 9.2 %collective-permute-start.11 = (bf16[256,1024]{1,0:T(8,128)(2,1)S(1)}, bf16[256,1024]{1,0:T(8,128)(2,1)S(1)}, u32[]{:S(2)}, u32[]{:S(2)}) collective-permute-start(bf16[256,1024]{1,0:T(8,128)(2,1)S(1)} %get-tuple-element.32.refs_3_), channel_id=1, source_target_pairs={{2,3},{6,7},{10,11},{14,15},{18,19},{22,23},{26,27},{30,31}} | collective-permute-start | bytes 1572872 | tf_op jit(solution)/shard_map/ppermute | solution.py:458
  70.8 13.7 %collective-permute-start.12 = (bf16[256,1024]{1,0:T(8,128)(2,1)S(1)}, bf16[256,1024]{1,0:T(8,128)(2,1)S(1)}, u32[]{:S(2)}, u32[]{:S(2)}) collective-permute-start(bf16[256,1024]{1,0:T(8,128)(2,1)S(1)} %get-tuple-element.33.refs_4_), channel_id=1, source_target_pairs={{1,0},{5,4},{9,8},{13,12},{17,16},{21,20},{25,24},{29,28}} | collective-permute-start | bytes 1572872 | tf_op jit(solution)/shard_map/ppermute | solution.py:458
  72.1 18.0 %collective-permute-start.14 = (bf16[256,1024]{1,0:T(8,128)(2,1)S(1)}, bf16[256,1024]{1,0:T(8,128)(2,1)S(1)}, u32[]{:S(2)}, u32[]{:S(2)}) collective-permute-start(bf16[256,1024]{1,0:T(8,128)(2,1)S(1)} %shard_map.78.refs_0_.refs_2_.refs_1_), channel_id=1, source_target_pairs={{4,16},{12,24},{28,20},{5,17},{13,25},{29,21},{6,18},{14,26},{30,2... | collective-permute-start | bytes 1572872 | tf_op jit(solution)/shard_map/ppermute | solution.py:434
  85.5 13.7 %collective-permute-start.15 = (bf16[256,1024]{1,0:T(8,128)(2,1)S(1)}, bf16[256,1024]{1,0:T(8,128)(2,1)S(1)}, u32[]{:S(2)}, u32[]{:S(2)}) collective-permute-start(bf16[256,1024]{1,0:T(8,128)(2,1)S(1)} %shard_map.82.refs_0_), channel_id=1, source_target_pairs={{8,0},{12,4},{16,8},{20,12},{24,16},{28,20},{9,1},{13,5},{17,9},{2... | collective-permute-start | bytes 1572872 | tf_op jit(solution)/shard_map/ppermute | solution.py:422
  87.5 17.1 %collective-permute-start.18 = (bf16[256,1024]{1,0:T(8,128)(2,1)S(1)}, bf16[256,1024]{1,0:T(8,128)(2,1)S(1)}, u32[]{:S(2)}, u32[]{:S(2)}) collective-permute-start(bf16[256,1024]{1,0:T(8,128)(2,1)S(1)} %collective-permute-done.13.refs_5_.refs_1_.refs_3_), channel_id=1, source_target_pairs={{0,4},{4,0},{8,12},{12,8},{16,20},{20,16},{24,28},{28,24},{1,5},{5... | collective-permute-start | bytes 1572872 | tf_op jit(solution)/shard_map/ppermute | solution.py:427
  99.2 8.2 %collective-permute-start.16 = (bf16[256,1024]{1,0:T(8,128)(2,1)S(1)}, bf16[256,1024]{1,0:T(8,128)(2,1)S(1)}, u32[]{:S(2)}, u32[]{:S(2)}) collective-permute-start(bf16[256,1024]{1,0:T(8,128)(2,1)S(1)} %shard_map.84.refs_1_.refs_5_), channel_id=1, source_target_pairs={{0,4},{4,0},{8,12},{12,8},{16,20},{20,16},{24,28},{28,24},{1,5},{5... | collective-permute-start | bytes 1572872 | tf_op jit(solution)/shard_map/ppermute | solution.py:427
  102.7 10.5 %collective-permute-start.17 = (bf16[256,1024]{1,0:T(8,128)(2,1)S(1)}, bf16[256,1024]{1,0:T(8,128)(2,1)S(1)}, u32[]{:S(2)}, u32[]{:S(2)}) collective-permute-start(bf16[256,1024]{1,0:T(8,128)(2,1)S(1)} %shard_map.85), channel_id=1, source_target_pairs={{4,0},{12,8},{20,16},{28,24},{16,4},{24,12},{5,1},{13,9},{21,17},{... | collective-permute-start | bytes 1572872 | tf_op jit(solution)/shard_map/ppermute | solution.py:443

commit v16 on v15

--- a/solution.py
+++ b/solution.py
@@ -80,14 +80,14 @@
 def prepare_kernel(pairs, *refs):
     place_ref, lane_ref, docs_ref, table_ref, back_ref, taps_ref = refs[:6]
     weight_ref, gate_ref, grad_ref = refs[6:9]
-    spec_out, weight_out, gate_out, lower_out, table_out, back_out = refs[9:15]
+    spec_out, weight_out, gate_out, grad_out, table_out, back_out = refs[9:15]
     facts_out, token_out, sems = refs[15:]
     token_out[...] = jnp.zeros_like(token_out)
     copies = [
         pltpu.make_async_copy(source, target, sems.at[at])
         for at, (source, target) in enumerate(
             [
-                (grad_ref.at[0, 0], lower_out),
+                (grad_ref, grad_out),
                 (weight_ref, weight_out),
                 (gate_ref, gate_out),
                 (back_ref, back_out),
@@ -151,7 +151,7 @@
             pltpu.VMEM((REACH + 1, 2 * length, width), F32),
             pltpu.VMEM(weight.shape, BF16),
             pltpu.VMEM(gate.shape, BF16),
-            pltpu.VMEM(grad.shape[2:], BF16),
+            pltpu.VMEM(grad.shape, BF16),
             pltpu.VMEM((2 * length, length), BF16),
             pltpu.VMEM(back.shape, BF16),
             pltpu.SMEM((2, 8), jnp.int32),
@@ -184,7 +184,7 @@
     weight_ref, gate_ref = refs[:2]
     before_ref = None if first else refs[2]
     out_ref, acc_ref = refs[-2:] if last else (refs[-1], refs[-1])
-    depth = shards[0].shape[1]
+    depth = shards[0].shape[-1]
     count = weight_ref.shape[1] // depth
     tiles = [pl.ds(tile * LANES, LANES) for tile in range(weight_ref.shape[0] // LANES)]
     if not first:
@@ -195,7 +195,8 @@
 
         def add(shard=shard, hop=hop, features=features):
             for lanes in tiles:
-                part = nt(shard[...], weight_ref[lanes, features])
+                values = shard[...] if len(shard.shape) == 2 else shard[0, slot]
+                part = nt(values, weight_ref[lanes, features])
                 if hop == 0:
                     acc_ref[:, lanes] = part
                 else:
@@ -210,7 +211,7 @@
 
 
 def project(facts, shards, hops, weight, gate, slot, before=None, last=True, after=()):
-    rows, depth = shards[0].shape
+    rows, depth = shards[0].shape[-2:]
     width = weight.shape[0]
     operands = [facts, *shards, weight, gate]
     if before is not None:
@@ -416,6 +417,23 @@
     return together([value], *earlier)[0]
 
 
+def block_kernel(slot, *refs):
+    count = len(refs) // 2
+    for source, target in zip(refs[:count], refs[count:]):
+        target[...] = source[0, slot]
+
+
+def block_of(values, slot):
+    shape = values[0].shape[2:]
+    return pl.pallas_call(
+        functools.partial(block_kernel, slot),
+        out_shape=[pltpu.VMEM(shape, BF16)] * len(values),
+        in_specs=[WHOLE] * len(values),
+        out_specs=[WHOLE] * len(values),
+        compiler_params=params(),
+    )(*values)
+
+
 def shifted(value, steps):
     count = lax.axis_size("ctx")
     initial, last = (max(0, -steps), min(count, count - steps))
@@ -440,7 +458,7 @@
     mixed = [(source, source - 1) for source in range(1, count, 2)]
     mixed += [(source, source - 3) for source in range(4, count, 2)]
     two = ordered(shifted(value, -2), own)
-    mixed = lax.ppermute(ordered(value, two), "ctx", mixed)
+    mixed = lax.ppermute(value, "ctx", mixed)
     return [two, core_swapped(two), mixed]
 
 
@@ -457,11 +475,10 @@
         downward = [(source, source - 1) for source in range(1, count - step + 1)]
         return lax.ppermute(up, "ch", upward), lax.ppermute(down, "ch", downward)
 
-    start = grad_out[0, 1]
-    upper_in = [sent(1, start, start)]
+    chain = [sent(1, grad_out, grad_out)]
 
     table, back = (jnp.asarray(one) for one in tables(length))
-    spectra, weight, gates, lower_slice, table, back, facts, prepared = prepare(
+    spectra, weight, gates, own, table, back, facts, prepared = prepare(
         pairs,
         place.astype(jnp.int32)[None],
         lane,
@@ -475,38 +492,31 @@
     )
     tabs = (table, back, spectra)
 
-    def pass_on(chain, *earlier):
-        if earlier:
-            chain[-1] = together(chain[-1], *earlier)
-        chain.append(sent(len(chain) + 1, *chain[-1]))
-
     hops = [0] + [way * step for step in range(1, count) for way in (-1, 1)]
 
-    def partial_of(own, arrived, slot, after=()):
-        shards = [own] + [one for pair in arrived[: count - 2] for one in pair]
-        return project(
-            facts, shards, hops[:-2], weight, gates, slot, last=False, after=after
-        )
+    def partial_of(slot, after=()):
+        shards = [own] + [one for pair in chain for one in pair]
+        args = (weight, gates, slot)
+        return project(facts, shards, hops[:-2], *args, last=False, after=after)
 
     def final_of(arrived, slot, partial, after=()):
-        return project(facts, arrived[-1], hops[-2:], weight, gates, slot, partial, after=after)
-
-    pass_on(upper_in, prepared)
-    own = ordered(lower_slice, *upper_in[0])
-    lower_in = [sent(1, own, own)]
-    for _ in range(3, count):
-        pass_on(upper_in)
-        pass_on(lower_in, *upper_in[-2])
-    partial = partial_of(start, upper_in, 1)
-    upper = final_of(upper_in, 1, partial)
+        return project(facts, arrived, hops[-2:], weight, gates, slot, partial, after=after)
+
+    chain[0] = together(chain[0], prepared)
+    for step in range(2, count - 1):
+        chain.append(sent(step, *chain[-1]))
+    arrived = sent(count - 1, *block_of(chain[-1], 1))
+    partial, lower_partial = partial_of(1), partial_of(0)
+    lower_part = together(block_of(chain[-1], 0), *arrived, partial)
+    lower_arrived = sent(count - 1, *lower_part)
+
+    upper = final_of(arrived, 1, partial, [lower_partial])
     upper_halo = upper_halo_of(upper)
     two, swapped, mate, fold = upper_halo
     near = own_terms(1, tabs, facts, [upper])
-    pass_on(lower_in, upper, mate, near)
     result, _ = far_terms(1, 1, tabs, facts, [near, *upper_halo])
 
-    partial = partial_of(own, lower_in, 0)
-    lower = final_of(lower_in, 0, partial, [two])
+    lower = final_of(lower_arrived, 0, lower_partial, [mate, near])
     near = own_terms(0, tabs, facts, [lower], after=[fold])
     lower_halo = lower_halo_of(lower, near)
     arrays = [near, upper, mate, two, fold, *lower_halo]

time: 117 us -> 113 us (0.966)
  starting transfers between devices: 43 us -> 28.1 us
  waiting for transfers between devices: 49.3 us -> 59.4 us
    ppermute x12 -> x8, waiting for transfers between devices: 35.7 us -> 49.2 us  [sent(): return (lax.ppermute(up, 'ch', upward), lax.ppermute(down, 'ch', downward))]
    ppermute x12 -> x8, starting transfers between devices: 20.1 us -> 11.3 us  [sent(): return (lax.ppermute(up, 'ch', upward), lax.ppermute(down, 'ch', downward))]
    ppermute x3, starting transfers between devices: 11.3 us -> 5.32 us  [core_swapped(): lax.ppermute(value, 'ctx', [(source, source ^ 1) for source in range(coun...]
    ppermute x1, waiting for transfers between devices: 5.79 us -> 2.08 us  [lower_halo_of(): mixed = lax.ppermute(value, 'ctx', mixed)]
    ppermute x1, starting transfers between devices: 4.68 us -> 1.32 us  [upper_halo_of(): mate, far = (core_swapped(value), lax.ppermute(value, 'ctx', far))]
    ppermute x1, starting transfers between devices: 1.91 us -> 4.33 us  [lower_halo_of(): mixed = lax.ppermute(value, 'ctx', mixed)]
  transfers between devices with their start and end apart: 19 -> 15, of which waited for: 9 -> 6; matrix products, arithmetic and copies ran while one was open for 0% -> 0% of each run, Pallas kernels for 17% -> 19%
where the time goes in v16:
time: 113 us; the launch traced here: 112 us
  waiting for transfers between devices  59.4 us (53%)
  starting transfers between devices  28.1 us (25%)
  Pallas kernels  24 us (21%)
    ppermute x8, waiting for transfers between devices, sent(): return (lax.ppermute(up, 'ch', upward), lax.ppermute(down, 'ch', downward))  49.2 us
    pallas_call x4, Pallas kernels, conv_call(): pl.pallas_call(body, grid=(width // LANES,), out_shape=out_shape, in_spec...  11.6 us
    ppermute x8, starting transfers between devices, sent(): return (lax.ppermute(up, 'ch', upward), lax.ppermute(down, 'ch', downward))  11.3 us
    ppermute x2, waiting for transfers between devices, shifted(): lax.ppermute(value, 'ctx', [(source, source + steps) for source in range(...  8.18 us
    pallas_call x4, Pallas kernels, project(): pl.pallas_call(functools.partial(project_kernel, hops, slot, before is No...  6.49 us
    ppermute x2, starting transfers between devices, shifted(): lax.ppermute(value, 'ctx', [(source, source + steps) for source in range(...  5.8 us
    pallas_call x1, Pallas kernels, prepare(): pl.pallas_call(functools.partial(prepare_kernel, pairs), grid=(width // L...  5.75 us
    ppermute x3, starting transfers between devices, core_swapped(): lax.ppermute(value, 'ctx', [(source, source ^ 1) for source in range(coun...  5.32 us
  transfers between devices with their start and end apart: 15, of which 6 were waited for; matrix products, arithmetic and copies ran while one was open for 0% of the time, Pallas kernels for 19%

profile of v16, /device:TPU:3, one launch (start us, length us, event | category | flops | bytes accessed | tf_op | source)
XLA Modules:
  0.0 111.7 jit_solution(4186550360456133382)
XLA Ops:
  0.0 1.3 %collective-permute-start.1 = (bf16[1,2,256,1024]{3,2,1,0:T(8,128)(2,1)}, bf16[1,2,256,1024]{3,2,1,0:T(8,128)(2,1)S(1)}, u32[]{:S(2)}, u32[]{:S(2)}) collective-permute-start(bf16[1,2,256,1024]{3,2,1,0:T(8,128)(2,1)} %refs_8_.1), channel_id=1, source_target_pairs={{1,0},{2,1},{3,2},{5,4},{6,5},{7,6},{9,8},{10,9},{11,10},{13,12},{... | collective-permute-start | bytes 3145736 | tf_op jit(solution)/shard_map/ppermute | solution.py:476
  1.3 4.1 %collective-permute-start = (bf16[1,2,256,1024]{3,2,1,0:T(8,128)(2,1)}, bf16[1,2,256,1024]{3,2,1,0:T(8,128)(2,1)S(1)}, u32[]{:S(2)}, u32[]{:S(2)}) collective-permute-start(bf16[1,2,256,1024]{3,2,1,0:T(8,128)(2,1)} %refs_8_.1), channel_id=1, source_target_pairs={{0,1},{1,2},{2,3},{4,5},{5,6},{6,7},{8,9},{9,10},{10,11},{12,13},{... | collective-permute-start | bytes 3145736 | tf_op jit(solution)/shard_map/ppermute | solution.py:476
  5.4 5.7 %shard_map.73 = (f32[4,512,1024]{2,1,0:T(8,128)S(1)}, bf16[1024,4096]{1,0:T(8,128)(2,1)S(1)}, bf16[1,2,256,1024]{3,2,1,0:T(8,128)(2,1)S(1)}, bf16[1,2,256,1024]{...) custom-call(s32[1]{0:T(128)} %bitcast.refs_0_, ...), custom_call_target="tpu_custom_call" | custom-call | flops 2415919104 | bytes 11534336 | tf_op jit(solution)/shard_map/pallas_call | solution.py:147
  11.1 15.0 %collective-permute-done.1.refs_1_ = bf16[1,2,256,1024]{3,2,1,0:T(8,128)(2,1)S(1)} collective-permute-done((bf16[1,2,256,1024]{3,2,1,0:T(8,128)(2,1)}, bf16[1,2,256,1024]{3,2,1,0:T(8,128)(2,1)S(1)}, u32[]{:S(2)}, u32[]{:S(2)}) %collective-permute-start.1) | collective-permute-done | bytes 1048608 | tf_op jit(solution)/shard_map/ppermute | solution.py:476
  26.1 1.0 collective-permute-done.refs_0_
  27.1 0.7 collective-permute-start.2
  27.8 1.3 %collective-permute-start.3 = (bf16[1,2,256,1024]{3,2,1,0:T(8,128)(2,1)S(1)}, bf16[1,2,256,1024]{3,2,1,0:T(8,128)(2,1)S(1)}, u32[]{:S(2)}, u32[]{:S(2)}) collective-permute-start(bf16[1,2,256,1024]{3,2,1,0:T(8,128)(2,1)S(1)} %get-tuple-element.28.refs_2_), channel_id=1, source_target_pairs={{1,0},{2,1},{5,4},{6,5},{9,8},{10,9},{13,12},{14,13},{17,16},{18,1... | collective-permute-start | bytes 3145736 | tf_op jit(solution)/shard_map/ppermute | solution.py:476
  29.1 26.6 %collective-permute-done.3.refs_1_.refs_4_ = bf16[1,2,256,1024]{3,2,1,0:T(8,128)(2,1)S(1)} collective-permute-done((bf16[1,2,256,1024]{3,2,1,0:T(8,128)(2,1)S(1)}, bf16[1,2,256,1024]{3,2,1,0:T(8,128)(2,1)S(1)}, u32[]{:S(2)}, u32[]{:S(2)}) %collective-permute-start.3) | collective-permute-done | bytes 1048608 | tf_op jit(solution)/shard_map/ppermute | solution.py:476
  55.7 0.1 shard_map.76
  55.7 0.7 collective-permute-start.4
  56.4 1.3 %collective-permute-start.5 = (bf16[256,1024]{1,0:T(8,128)(2,1)S(1)}, bf16[256,1024]{1,0:T(8,128)(2,1)S(1)}, u32[]{:S(2)}, u32[]{:S(2)}) collective-permute-start(bf16[256,1024]{1,0:T(8,128)(2,1)S(1)} %get-tuple-element.32), channel_id=1, source_target_pairs={{1,0},{5,4},{9,8},{13,12},{17,16},{21,20},{25,24},{29,28}} | collective-permute-start | bytes 1572872 | tf_op jit(solution)/shard_map/ppermute | solution.py:476
  57.7 0.1 shard_map.75
  57.8 2.3 %shard_map.79.refs_5_.refs_4_ = f32[256,1024]{1,0:T(8,128)S(1)} custom-call(s32[2,8]{1,0:T(2,128)S(4)} %get-tuple-element.22.facts_ref, bf16[1,2,256,1024]{3,2,1,0:T(8,128)(2,1)S(1)} %get-tuple-element.33.refs_0_, bf16[1,2,256,1024]{3,2,1,0:T(8,128)(2,1)S(1)} %get-tuple-element.27.refs_1_, bf16[1,2,256,1024]{3,2,1,0:T(8,128)(2,1)S(1)} %get-tuple-element.28.refs_2_, ...), custom_call_target="tpu_custom_call" | custom-call | flops 1610612736 | bytes 13107200 | tf_op jit(solution)/shard_map/pallas_call | solution.py:219
  60.1 2.3 %shard_map.77.refs_4_ = f32[256,1024]{1,0:T(8,128)S(1)} custom-call(s32[2,8]{1,0:T(2,128)S(4)} %get-tuple-element.22.facts_ref, bf16[1,2,256,1024]{3,2,1,0:T(8,128)(2,1)S(1)} %get-tuple-element.33.refs_0_, bf16[1,2,256,1024]{3,2,1,0:T(8,128)(2,1)S(1)} %get-tuple-element.27.refs_1_, bf16[1,2,256,1024]{3,2,1,0:T(8,128)(2,1)S(1)} %get-tuple-element.28.refs_2_, ...), custom_call_target="tpu_custom_call" | custom-call | flops 1610612736 | bytes 13107200 | tf_op jit(solution)/shard_map/pallas_call | solution.py:219
  62.4 6.6 %collective-permute-done.5.refs_3_.refs_1_ = bf16[256,1024]{1,0:T(8,128)(2,1)S(1)} collective-permute-done((bf16[256,1024]{1,0:T(8,128)(2,1)S(1)}, bf16[256,1024]{1,0:T(8,128)(2,1)S(1)}, u32[]{:S(2)}, u32[]{:S(2)}) %collective-permute-start.5) | collective-permute-done | bytes 524320 | tf_op jit(solution)/shard_map/ppermute | solution.py:476
  69.0 0.7 collective-permute-start.6
  69.7 1.3 %collective-permute-start.7 = (bf16[256,1024]{1,0:T(8,128)(2,1)S(1)}, bf16[256,1024]{1,0:T(8,128)(2,1)S(1)}, u32[]{:S(2)}, u32[]{:S(2)}) collective-permute-start(bf16[256,1024]{1,0:T(8,128)(2,1)S(1)} %get-tuple-element.37), channel_id=1, source_target_pairs={{1,0},{5,4},{9,8},{13,12},{17,16},{21,20},{25,24},{29,28}} | collective-permute-start | bytes 1572872 | tf_op jit(solution)/shard_map/ppermute | solution.py:476
  71.0 0.9 shard_map.80.refs_0_.refs_1_
  71.9 3.8 %collective-permute-start.8 = (bf16[256,1024]{1,0:T(8,128)(2,1)S(1)}, bf16[256,1024]{1,0:T(8,128)(2,1)S(1)}, u32[]{:S(2)}, u32[]{:S(2)}) collective-permute-start(bf16[256,1024]{1,0:T(8,128)(2,1)S(1)} %shard_map.80.refs_0_.refs_1_), channel_id=1, source_target_pairs={{0,4},{4,0},{8,12},{12,8},{16,20},{20,16},{24,28},{28,24},{1,5},{5... | collective-permute-start | bytes 1572872 | tf_op jit(solution)/shard_map/ppermute | solution.py:445
  75.7 3.1 %collective-permute-start.10 = (bf16[256,1024]{1,0:T(8,128)(2,1)S(1)}, bf16[256,1024]{1,0:T(8,128)(2,1)S(1)}, u32[]{:S(2)}, u32[]{:S(2)}) collective-permute-start(bf16[256,1024]{1,0:T(8,128)(2,1)S(1)} %shard_map.80.refs_0_.refs_1_), channel_id=1, source_target_pairs={{0,8},{4,12},{8,16},{12,20},{16,24},{20,28},{1,9},{5,13},{9,17},{1... | collective-permute-start | bytes 1572872 | tf_op jit(solution)/shard_map/ppermute | solution.py:440
  78.8 1.3 %collective-permute-start.9 = (bf16[256,1024]{1,0:T(8,128)(2,1)S(1)}, bf16[256,1024]{1,0:T(8,128)(2,1)S(1)}, u32[]{:S(2)}, u32[]{:S(2)}) collective-permute-start(bf16[256,1024]{1,0:T(8,128)(2,1)S(1)} %shard_map.80.refs_0_.refs_1_), channel_id=1, source_target_pairs={{4,16},{12,24},{28,20},{5,17},{13,25},{29,21},{6,18},{14,26},{30,2... | collective-permute-start | bytes 1572872 | tf_op jit(solution)/shard_map/ppermute | solution.py:452
  80.1 3.1 %shard_map.81.refs_6_.refs_0_ = f32[256,1024]{1,0:T(8,128)S(1)} custom-call(s32[2,8]{1,0:T(2,128)S(4)} %get-tuple-element.22.facts_ref, bf16[512,256]{1,0:T(8,128)(2,1)S(1)} %get-tuple-element.23.table_ref, bf16[512,512]{1,0:T(8,128)(2,1)S(1)} %get-tuple-element.24.back_ref, f32[4,512,1024]{2,1,0:T(8,128)S(1)} %get-tuple-element.25.spec_ref, ...), custom_call_target="tpu_custom_call" | custom-call | flops 2147483648 | bytes 1048576 | tf_op jit(solution)/shard_map/pallas_call | solution.py:369
  83.2 1.1 shard_map.82.refs_0_
  84.3 2.7 %collective-permute-start.11 = (bf16[256,1024]{1,0:T(8,128)(2,1)S(1)}, bf16[256,1024]{1,0:T(8,128)(2,1)S(1)}, u32[]{:S(2)}, u32[]{:S(2)}) collective-permute-start(bf16[256,1024]{1,0:T(8,128)(2,1)S(1)} %shard_map.82.refs_0_), channel_id=1, source_target_pairs={{8,0},{12,4},{16,8},{20,12},{24,16},{28,20},{9,1},{13,5},{17,9},{2... | collective-permute-start | bytes 1572872 | tf_op jit(solution)/shard_map/ppermute | solution.py:440
  87.0 4.3 %collective-permute-start.13 = (bf16[256,1024]{1,0:T(8,128)(2,1)S(1)}, bf16[256,1024]{1,0:T(8,128)(2,1)S(1)}, u32[]{:S(2)}, u32[]{:S(2)}) collective-permute-start(bf16[256,1024]{1,0:T(8,128)(2,1)S(1)} %shard_map.82.refs_0_), channel_id=1, source_target_pairs={{4,0},{12,8},{20,16},{28,24},{16,4},{24,12},{5,1},{13,9},{21,17},{... | collective-permute-start | bytes 1572872 | tf_op jit(solution)/shard_map/ppermute | solution.py:461
  91.4 0.5 collective-permute-start.14
  91.9 3.1 %shard_map.83.refs_1_.refs_0_ = f32[256,1024]{1,0:T(8,128)S(1)} custom-call(s32[2,8]{1,0:T(2,128)S(4)} %get-tuple-element.22.facts_ref, bf16[512,256]{1,0:T(8,128)(2,1)S(1)} %get-tuple-element.23.table_ref, bf16[512,512]{1,0:T(8,128)(2,1)S(1)} %get-tuple-element.24.back_ref, f32[4,512,1024]{2,1,0:T(8,128)S(1)} %get-tuple-element.25.spec_ref, ...), custom_call_target="tpu_custom_call" | custom-call | flops 2147483648 | bytes 1048576 | tf_op jit(solution)/shard_map/pallas_call | solution.py:369
  95.0 8.2 %collective-permute-done.11.refs_0_ = bf16[256,1024]{1,0:T(8,128)(2,1)S(1)} collective-permute-done((bf16[256,1024]{1,0:T(8,128)(2,1)S(1)}, bf16[256,1024]{1,0:T(8,128)(2,1)S(1)}, u32[]{:S(2)}, u32[]{:S(2)}) %collective-permute-start.11) | collective-permute-done | bytes 524320 | tf_op jit(solution)/shard_map/ppermute | solution.py:440
  103.1 1.0 collective-permute-start.12
  104.2 2.7 %shard_map.85 = (f32[1,2,256,1024]{3,2,1,0:T(8,128)}, f32[8,128]{1,0:T(8,128)}) custom-call(s32[2,8]{1,0:T(2,128)S(4)} %get-tuple-element.22.facts_ref, bf16[512,256]{1,0:T(8,128)(2,1)S(1)} %get-tuple-element.23.table_ref, bf16[512,512]{1,0:T(8,128)(2,1)S(1)} %get-tuple-element.24.back_ref, f32[4,512,1024]{2,1,0:T(8,128)S(1)} %get-tuple-element.25.spec_ref, ...), custom_call_target="tpu_custom_call" | custom-call | flops 2147483648 | bytes 1048576 | tf_op jit(solution)/shard_map/pallas_call | solution.py:369
  106.9 2.1 %collective-permute-done.13.refs_7_ = bf16[256,1024]{1,0:T(8,128)(2,1)S(1)} collective-permute-done((bf16[256,1024]{1,0:T(8,128)(2,1)S(1)}, bf16[256,1024]{1,0:T(8,128)(2,1)S(1)}, u32[]{:S(2)}, u32[]{:S(2)}) %collective-permute-start.13) | collective-permute-done | bytes 524320 | tf_op jit(solution)/shard_map/ppermute | solution.py:461
  109.0 2.7 %shard_map.86 = f32[1,2,256,1024]{3,2,1,0:T(8,128)} custom-call(s32[2,8]{1,0:T(2,128)S(4)} %get-tuple-element.22.facts_ref, bf16[512,256]{1,0:T(8,128)(2,1)S(1)} %get-tuple-element.23.table_ref, bf16[512,512]{1,0:T(8,128)(2,1)S(1)} %get-tuple-element.24.back_ref, f32[4,512,1024]{2,1,0:T(8,128)S(1)} %get-tuple-element.25.spec_ref, ...), custom_call_target="tpu_custom_call", output_to_operand_aliasing={{}: (12, {})} | custom-call | flops 2147483648 | bytes 1048576 | tf_op jit(solution)/shard_map/pallas_call | solution.py:369
  (12 shorter events, 0.0 us)
Async XLA Ops:
  0.0 26.1 %collective-permute-start.1 = (bf16[1,2,256,1024]{3,2,1,0:T(8,128)(2,1)}, bf16[1,2,256,1024]{3,2,1,0:T(8,128)(2,1)S(1)}, u32[]{:S(2)}, u32[]{:S(2)}) collective-permute-start(bf16[1,2,256,1024]{3,2,1,0:T(8,128)(2,1)} %refs_8_.1), channel_id=1, source_target_pairs={{1,0},{2,1},{3,2},{5,4},{6,5},{7,6},{9,8},{10,9},{11,10},{13,12},{... | collective-permute-start | bytes 3145736 | tf_op jit(solution)/shard_map/ppermute | solution.py:476
  1.3 25.8 %collective-permute-start = (bf16[1,2,256,1024]{3,2,1,0:T(8,128)(2,1)}, bf16[1,2,256,1024]{3,2,1,0:T(8,128)(2,1)S(1)}, u32[]{:S(2)}, u32[]{:S(2)}) collective-permute-start(bf16[1,2,256,1024]{3,2,1,0:T(8,128)(2,1)} %refs_8_.1), channel_id=1, source_target_pairs={{0,1},{1,2},{2,3},{4,5},{5,6},{6,7},{8,9},{9,10},{10,11},{12,13},{... | collective-permute-start | bytes 3145736 | tf_op jit(solution)/shard_map/ppermute | solution.py:476
  27.1 2.0 %collective-permute-start.2 = (bf16[1,2,256,1024]{3,2,1,0:T(8,128)(2,1)S(1)}, bf16[1,2,256,1024]{3,2,1,0:T(8,128)(2,1)S(1)}, u32[]{:S(2)}, u32[]{:S(2)}) collective-permute-start(bf16[1,2,256,1024]{3,2,1,0:T(8,128)(2,1)S(1)} %get-tuple-element.27.refs_1_), channel_id=1, source_target_pairs={{1,2},{2,3},{5,6},{6,7},{9,10},{10,11},{13,14},{14,15},{17,18},{18... | collective-permute-start | bytes 3145736 | tf_op jit(solution)/shard_map/ppermute | solution.py:476
  27.8 27.9 %collective-permute-start.3 = (bf16[1,2,256,1024]{3,2,1,0:T(8,128)(2,1)S(1)}, bf16[1,2,256,1024]{3,2,1,0:T(8,128)(2,1)S(1)}, u32[]{:S(2)}, u32[]{:S(2)}) collective-permute-start(bf16[1,2,256,1024]{3,2,1,0:T(8,128)(2,1)S(1)} %get-tuple-element.28.refs_2_), channel_id=1, source_target_pairs={{1,0},{2,1},{5,4},{6,5},{9,8},{10,9},{13,12},{14,13},{17,16},{18,1... | collective-permute-start | bytes 3145736 | tf_op jit(solution)/shard_map/ppermute | solution.py:476
  55.7 6.6 %collective-permute-start.4 = (bf16[256,1024]{1,0:T(8,128)(2,1)S(1)}, bf16[256,1024]{1,0:T(8,128)(2,1)S(1)}, u32[]{:S(2)}, u32[]{:S(2)}) collective-permute-start(bf16[256,1024]{1,0:T(8,128)(2,1)S(1)} %get-tuple-element.31), channel_id=1, source_target_pairs={{2,3},{6,7},{10,11},{14,15},{18,19},{22,23},{26,27},{30,31}} | collective-permute-start | bytes 1572872 | tf_op jit(solution)/shard_map/ppermute | solution.py:476
  56.4 12.5 %collective-permute-start.5 = (bf16[256,1024]{1,0:T(8,128)(2,1)S(1)}, bf16[256,1024]{1,0:T(8,128)(2,1)S(1)}, u32[]{:S(2)}, u32[]{:S(2)}) collective-permute-start(bf16[256,1024]{1,0:T(8,128)(2,1)S(1)} %get-tuple-element.32), channel_id=1, source_target_pairs={{1,0},{5,4},{9,8},{13,12},{17,16},{21,20},{25,24},{29,28}} | collective-permute-start | bytes 1572872 | tf_op jit(solution)/shard_map/ppermute | solution.py:476
  69.0 14.2 %collective-permute-start.6 = (bf16[256,1024]{1,0:T(8,128)(2,1)S(1)}, bf16[256,1024]{1,0:T(8,128)(2,1)S(1)}, u32[]{:S(2)}, u32[]{:S(2)}) collective-permute-start(bf16[256,1024]{1,0:T(8,128)(2,1)S(1)} %get-tuple-element.36), channel_id=1, source_target_pairs={{2,3},{6,7},{10,11},{14,15},{18,19},{22,23},{26,27},{30,31}} | collective-permute-start | bytes 1572872 | tf_op jit(solution)/shard_map/ppermute | solution.py:476
  69.7 13.5 %collective-permute-start.7 = (bf16[256,1024]{1,0:T(8,128)(2,1)S(1)}, bf16[256,1024]{1,0:T(8,128)(2,1)S(1)}, u32[]{:S(2)}, u32[]{:S(2)}) collective-permute-start(bf16[256,1024]{1,0:T(8,128)(2,1)S(1)} %get-tuple-element.37), channel_id=1, source_target_pairs={{1,0},{5,4},{9,8},{13,12},{17,16},{21,20},{25,24},{29,28}} | collective-permute-start | bytes 1572872 | tf_op jit(solution)/shard_map/ppermute | solution.py:476
  71.9 11.3 %collective-permute-start.8 = (bf16[256,1024]{1,0:T(8,128)(2,1)S(1)}, bf16[256,1024]{1,0:T(8,128)(2,1)S(1)}, u32[]{:S(2)}, u32[]{:S(2)}) collective-permute-start(bf16[256,1024]{1,0:T(8,128)(2,1)S(1)} %shard_map.80.refs_0_.refs_1_), channel_id=1, source_target_pairs={{0,4},{4,0},{8,12},{12,8},{16,20},{20,16},{24,28},{28,24},{1,5},{5... | collective-permute-start | bytes 1572872 | tf_op jit(solution)/shard_map/ppermute | solution.py:445
  75.7 15.7 %collective-permute-start.10 = (bf16[256,1024]{1,0:T(8,128)(2,1)S(1)}, bf16[256,1024]{1,0:T(8,128)(2,1)S(1)}, u32[]{:S(2)}, u32[]{:S(2)}) collective-permute-start(bf16[256,1024]{1,0:T(8,128)(2,1)S(1)} %shard_map.80.refs_0_.refs_1_), channel_id=1, source_target_pairs={{0,8},{4,12},{8,16},{12,20},{16,24},{20,28},{1,9},{5,13},{9,17},{1... | collective-permute-start | bytes 1572872 | tf_op jit(solution)/shard_map/ppermute | solution.py:440
  78.8 13.1 %collective-permute-start.9 = (bf16[256,1024]{1,0:T(8,128)(2,1)S(1)}, bf16[256,1024]{1,0:T(8,128)(2,1)S(1)}, u32[]{:S(2)}, u32[]{:S(2)}) collective-permute-start(bf16[256,1024]{1,0:T(8,128)(2,1)S(1)} %shard_map.80.refs_0_.refs_1_), channel_id=1, source_target_pairs={{4,16},{12,24},{28,20},{5,17},{13,25},{29,21},{6,18},{14,26},{30,2... | collective-permute-start | bytes 1572872 | tf_op jit(solution)/shard_map/ppermute | solution.py:452
  84.3 18.8 %collective-permute-start.11 = (bf16[256,1024]{1,0:T(8,128)(2,1)S(1)}, bf16[256,1024]{1,0:T(8,128)(2,1)S(1)}, u32[]{:S(2)}, u32[]{:S(2)}) collective-permute-start(bf16[256,1024]{1,0:T(8,128)(2,1)S(1)} %shard_map.82.refs_0_), channel_id=1, source_target_pairs={{8,0},{12,4},{16,8},{20,12},{24,16},{28,20},{9,1},{13,5},{17,9},{2... | collective-permute-start | bytes 1572872 | tf_op jit(solution)/shard_map/ppermute | solution.py:440
  87.0 22.0 %collective-permute-start.13 = (bf16[256,1024]{1,0:T(8,128)(2,1)S(1)}, bf16[256,1024]{1,0:T(8,128)(2,1)S(1)}, u32[]{:S(2)}, u32[]{:S(2)}) collective-permute-start(bf16[256,1024]{1,0:T(8,128)(2,1)S(1)} %shard_map.82.refs_0_), channel_id=1, source_target_pairs={{4,0},{12,8},{20,16},{28,24},{16,4},{24,12},{5,1},{13,9},{21,17},{... | collective-permute-start | bytes 1572872 | tf_op jit(solution)/shard_map/ppermute | solution.py:461
  91.4 12.8 %collective-permute-start.14 = (bf16[256,1024]{1,0:T(8,128)(2,1)S(1)}, bf16[256,1024]{1,0:T(8,128)(2,1)S(1)}, u32[]{:S(2)}, u32[]{:S(2)}) collective-permute-start(bf16[256,1024]{1,0:T(8,128)(2,1)S(1)} %collective-permute-done.10.refs_1_.refs_3_), channel_id=1, source_target_pairs={{0,4},{4,0},{8,12},{12,8},{16,20},{20,16},{24,28},{28,24},{1,5},{5... | collective-permute-start | bytes 1572872 | tf_op jit(solution)/shard_map/ppermute | solution.py:445
  103.1 5.9 %collective-permute-start.12 = (bf16[256,1024]{1,0:T(8,128)(2,1)S(1)}, bf16[256,1024]{1,0:T(8,128)(2,1)S(1)}, u32[]{:S(2)}, u32[]{:S(2)}) collective-permute-start(bf16[256,1024]{1,0:T(8,128)(2,1)S(1)} %shard_map.84.refs_5_), channel_id=1, source_target_pairs={{0,4},{4,0},{8,12},{12,8},{16,20},{20,16},{24,28},{28,24},{1,5},{5... | collective-permute-start | bytes 1572872 | tf_op jit(solution)/shard_map/ppermute | solution.py:445

commit v17 on v15

--- a/solution.py
+++ b/solution.py
@@ -440,7 +440,7 @@
     mixed = [(source, source - 1) for source in range(1, count, 2)]
     mixed += [(source, source - 3) for source in range(4, count, 2)]
     two = ordered(shifted(value, -2), own)
-    mixed = lax.ppermute(ordered(value, two), "ctx", mixed)
+    mixed = lax.ppermute(value, "ctx", mixed)
     return [two, core_swapped(two), mixed]
 
 
@@ -502,10 +502,10 @@
     upper_halo = upper_halo_of(upper)
     two, swapped, mate, fold = upper_halo
     near = own_terms(1, tabs, facts, [upper])
-    pass_on(lower_in, upper, mate, near)
+    pass_on(lower_in, upper, mate)
     result, _ = far_terms(1, 1, tabs, facts, [near, *upper_halo])
 
-    partial = partial_of(own, lower_in, 0)
+    partial = partial_of(own, lower_in, 0, [near])
     lower = final_of(lower_in, 0, partial, [two])
     near = own_terms(0, tabs, facts, [lower], after=[fold])
     lower_halo = lower_halo_of(lower, near)

time: 117 us -> 108 us (0.923)
  waiting for transfers between devices: 49.3 us -> 38.8 us
  starting transfers between devices: 43 us -> 47.2 us
  Pallas kernels: 23.2 us -> 20.7 us
    ppermute x2, waiting for transfers between devices: 7.74 us -> 2.75 us  [shifted(): lax.ppermute(value, 'ctx', [(source, source + steps) for source in range(...]
    ppermute x1, waiting for transfers between devices: 5.79 us -> 2.09 us  [lower_halo_of(): mixed = lax.ppermute(value, 'ctx', mixed)]
    ppermute x3, starting transfers between devices: 11.3 us -> 14 us  [core_swapped(): lax.ppermute(value, 'ctx', [(source, source ^ 1) for source in range(coun...]
    pallas_call x4, Pallas kernels: 11 us -> 8.62 us  [conv_call(): pl.pallas_call(body, grid=(width // LANES,), out_shape=out_shape, in_spec...]
    ppermute x12, waiting for transfers between devices: 35.7 us -> 33.9 us  [sent(): return (lax.ppermute(up, 'ch', upward), lax.ppermute(down, 'ch', downward))]
where the time goes in v17:
time: 108 us
  starting transfers between devices  47.2 us (44%)
  waiting for transfers between devices  38.8 us (36%)
  Pallas kernels  20.7 us (19%)
  local copies, waits for them, and re-layouts  1.08 us (1%)
    ppermute x12, waiting for transfers between devices, sent(): return (lax.ppermute(up, 'ch', upward), lax.ppermute(down, 'ch', downward))  33.9 us
    ppermute x12, starting transfers between devices, sent(): return (lax.ppermute(up, 'ch', upward), lax.ppermute(down, 'ch', downward))  20.1 us
    ppermute x3, starting transfers between devices, core_swapped(): lax.ppermute(value, 'ctx', [(source, source ^ 1) for source in range(coun...  14 us
    pallas_call x4, Pallas kernels, conv_call(): pl.pallas_call(body, grid=(width // LANES,), out_shape=out_shape, in_spec...  8.62 us
    pallas_call x4, Pallas kernels, project(): pl.pallas_call(functools.partial(project_kernel, hops, slot, before is No...  6.49 us
    ppermute x1, starting transfers between devices, upper_halo_of(): mate, far = (core_swapped(value), lax.ppermute(value, 'ctx', far))  5.85 us
    pallas_call x1, Pallas kernels, prepare(): pl.pallas_call(functools.partial(prepare_kernel, pairs), grid=(width // L...  5.59 us
    ppermute x2, starting transfers between devices, shifted(): lax.ppermute(value, 'ctx', [(source, source + steps) for source in range(...  5.27 us
  transfers between devices with their start and end apart: 19, of which 9 were waited for; matrix products, arithmetic and copies ran while one was open for 0% of the time, Pallas kernels for 17%

profile of v17, /device:TPU:3, one launch (start us, length us, event | category | flops | bytes accessed | tf_op | source)
XLA Modules:
  0.0 108.0 jit_solution(14476466697187577912)
XLA Ops:
  1.1 3.2 %collective-permute-start = (bf16[256,1024]{1,0:T(8,128)(2,1)S(1)}, bf16[256,1024]{1,0:T(8,128)(2,1)S(1)}, u32[]{:S(2)}, u32[]{:S(2)}) collective-permute-start(bf16[256,1024]{1,0:T(8,128)(2,1)S(1)} %slice_bitcast_fusion.refs_0_), channel_id=1, source_target_pairs={{0,1},{1,2},{2,3},{4,5},{5,6},{6,7},{8,9},{9,10},{10,11},{12,13},{... | collective-permute-start | bytes 1572872 | tf_op jit(solution)/shard_map/ppermute | solution.py:458
  4.3 1.3 %collective-permute-start.1 = (bf16[256,1024]{1,0:T(8,128)(2,1)S(1)}, bf16[256,1024]{1,0:T(8,128)(2,1)S(1)}, u32[]{:S(2)}, u32[]{:S(2)}) collective-permute-start(bf16[256,1024]{1,0:T(8,128)(2,1)S(1)} %slice_bitcast_fusion.refs_0_), channel_id=1, source_target_pairs={{1,0},{2,1},{3,2},{5,4},{6,5},{7,6},{9,8},{10,9},{11,10},{13,12},{... | collective-permute-start | bytes 1572872 | tf_op jit(solution)/shard_map/ppermute | solution.py:458
  5.6 5.6 %shard_map.73 = (f32[4,512,1024]{2,1,0:T(8,128)S(1)}, bf16[1024,4096]{1,0:T(8,128)(2,1)S(1)}, bf16[1,2,256,1024]{3,2,1,0:T(8,128)(2,1)S(1)}, bf16[256,1024]{1,0:...) custom-call(s32[1]{0:T(128)} %bitcast.refs_0_, ...), custom_call_target="tpu_custom_call" | custom-call | flops 2415919104 | bytes 11534336 | tf_op jit(solution)/shard_map/pallas_call | solution.py:147
  11.2 3.6 %collective-permute-done.refs_0_ = bf16[256,1024]{1,0:T(8,128)(2,1)S(1)} collective-permute-done((bf16[256,1024]{1,0:T(8,128)(2,1)S(1)}, bf16[256,1024]{1,0:T(8,128)(2,1)S(1)}, u32[]{:S(2)}, u32[]{:S(2)}) %collective-permute-start) | collective-permute-done | bytes 524320 | tf_op jit(solution)/shard_map/ppermute | solution.py:458
  14.9 3.8 %collective-permute-done.1.refs_1_ = bf16[256,1024]{1,0:T(8,128)(2,1)S(1)} collective-permute-done((bf16[256,1024]{1,0:T(8,128)(2,1)S(1)}, bf16[256,1024]{1,0:T(8,128)(2,1)S(1)}, u32[]{:S(2)}, u32[]{:S(2)}) %collective-permute-start.1) | collective-permute-done | bytes 524320 | tf_op jit(solution)/shard_map/ppermute | solution.py:458
  19.4 1.3 %collective-permute-start.5 = (bf16[256,1024]{1,0:T(8,128)(2,1)S(1)}, bf16[256,1024]{1,0:T(8,128)(2,1)S(1)}, u32[]{:S(2)}, u32[]{:S(2)}) collective-permute-start(bf16[256,1024]{1,0:T(8,128)(2,1)S(1)} %get-tuple-element.27.refs_2_), channel_id=1, source_target_pairs={{1,0},{2,1},{5,4},{6,5},{9,8},{10,9},{13,12},{14,13},{17,16},{18,1... | collective-permute-start | bytes 1572872 | tf_op jit(solution)/shard_map/ppermute | solution.py:458
  20.7 6.4 %collective-permute-start.2 = (bf16[256,1024]{1,0:T(8,128)(2,1)S(1)}, bf16[256,1024]{1,0:T(8,128)(2,1)S(1)}, u32[]{:S(2)}, u32[]{:S(2)}) collective-permute-start(bf16[256,1024]{1,0:T(8,128)(2,1)S(1)} %shard_map.75.refs_0_), channel_id=1, source_target_pairs={{0,1},{1,2},{2,3},{4,5},{5,6},{6,7},{8,9},{9,10},{10,11},{12,13},{... | collective-permute-start | bytes 1572872 | tf_op jit(solution)/shard_map/ppermute | solution.py:458
  27.1 1.3 %collective-permute-start.3 = (bf16[256,1024]{1,0:T(8,128)(2,1)S(1)}, bf16[256,1024]{1,0:T(8,128)(2,1)S(1)}, u32[]{:S(2)}, u32[]{:S(2)}) collective-permute-start(bf16[256,1024]{1,0:T(8,128)(2,1)S(1)} %shard_map.75.refs_0_), channel_id=1, source_target_pairs={{1,0},{2,1},{3,2},{5,4},{6,5},{7,6},{9,8},{10,9},{11,10},{13,12},{... | collective-permute-start | bytes 1572872 | tf_op jit(solution)/shard_map/ppermute | solution.py:458
  29.1 6.1 %collective-permute-done.5.refs_3_.refs_4_ = bf16[256,1024]{1,0:T(8,128)(2,1)S(1)} collective-permute-done((bf16[256,1024]{1,0:T(8,128)(2,1)S(1)}, bf16[256,1024]{1,0:T(8,128)(2,1)S(1)}, u32[]{:S(2)}, u32[]{:S(2)}) %collective-permute-start.5) | collective-permute-done | bytes 524320 | tf_op jit(solution)/shard_map/ppermute | solution.py:458
  35.2 1.3 %collective-permute-start.9 = (bf16[256,1024]{1,0:T(8,128)(2,1)S(1)}, bf16[256,1024]{1,0:T(8,128)(2,1)S(1)}, u32[]{:S(2)}, u32[]{:S(2)}) collective-permute-start(bf16[256,1024]{1,0:T(8,128)(2,1)S(1)} %collective-permute-done.5.refs_3_.refs_4_), channel_id=1, source_target_pairs={{1,0},{5,4},{9,8},{13,12},{17,16},{21,20},{25,24},{29,28}} | collective-permute-start | bytes 1572872 | tf_op jit(solution)/shard_map/ppermute | solution.py:458
  36.5 9.9 %collective-permute-done.3.refs_1_ = bf16[256,1024]{1,0:T(8,128)(2,1)S(1)} collective-permute-done((bf16[256,1024]{1,0:T(8,128)(2,1)S(1)}, bf16[256,1024]{1,0:T(8,128)(2,1)S(1)}, u32[]{:S(2)}, u32[]{:S(2)}) %collective-permute-start.3) | collective-permute-done | bytes 524320 | tf_op jit(solution)/shard_map/ppermute | solution.py:458
  47.1 1.3 %collective-permute-start.7 = (bf16[256,1024]{1,0:T(8,128)(2,1)S(1)}, bf16[256,1024]{1,0:T(8,128)(2,1)S(1)}, u32[]{:S(2)}, u32[]{:S(2)}) collective-permute-start(bf16[256,1024]{1,0:T(8,128)(2,1)S(1)} %get-tuple-element.29.refs_2_), channel_id=1, source_target_pairs={{1,0},{2,1},{5,4},{6,5},{9,8},{10,9},{13,12},{14,13},{17,16},{18,1... | collective-permute-start | bytes 1572872 | tf_op jit(solution)/shard_map/ppermute | solution.py:458
  48.4 2.3 %shard_map.77.refs_4_ = f32[256,1024]{1,0:T(8,128)S(1)} custom-call(s32[2,8]{1,0:T(2,128)S(4)} %get-tuple-element.20.facts_ref, bf16[256,1024]{1,0:T(8,128)(2,1)S(1)} %slice_bitcast_fusion.refs_0_, bf16[256,1024]{1,0:T(8,128)(2,1)S(1)} %get-tuple-element.26.refs_1_, bf16[256,1024]{1,0:T(8,128)(2,1)S(1)} %get-tuple-element.27.refs_2_, ...), custom_call_target="tpu_custom_call" | custom-call | flops 1610612736 | bytes 13107200 | tf_op jit(solution)/shard_map/pallas_call | solution.py:218
  50.7 7.0 %collective-permute-done.9.refs_1_ = bf16[256,1024]{1,0:T(8,128)(2,1)S(1)} collective-permute-done((bf16[256,1024]{1,0:T(8,128)(2,1)S(1)}, bf16[256,1024]{1,0:T(8,128)(2,1)S(1)}, u32[]{:S(2)}, u32[]{:S(2)}) %collective-permute-start.9) | collective-permute-done | bytes 524320 | tf_op jit(solution)/shard_map/ppermute | solution.py:458
  58.6 5.2 %collective-permute-start.10 = (bf16[256,1024]{1,0:T(8,128)(2,1)S(1)}, bf16[256,1024]{1,0:T(8,128)(2,1)S(1)}, u32[]{:S(2)}, u32[]{:S(2)}) collective-permute-start(bf16[256,1024]{1,0:T(8,128)(2,1)S(1)} %shard_map.78.refs_2_.refs_0_.refs_1_), channel_id=1, source_target_pairs={{0,4},{4,0},{8,12},{12,8},{16,20},{20,16},{24,28},{28,24},{1,5},{5... | collective-permute-start | bytes 1572872 | tf_op jit(solution)/shard_map/ppermute | solution.py:427
  63.8 3.1 %collective-permute-start.13 = (bf16[256,1024]{1,0:T(8,128)(2,1)S(1)}, bf16[256,1024]{1,0:T(8,128)(2,1)S(1)}, u32[]{:S(2)}, u32[]{:S(2)}) collective-permute-start(bf16[256,1024]{1,0:T(8,128)(2,1)S(1)} %shard_map.78.refs_2_.refs_0_.refs_1_), channel_id=1, source_target_pairs={{0,8},{4,12},{8,16},{12,20},{16,24},{20,28},{1,9},{5,13},{9,17},{1... | collective-permute-start | bytes 1572872 | tf_op jit(solution)/shard_map/ppermute | solution.py:422
  66.9 2.0 %collective-permute-done.7.refs_1_ = bf16[256,1024]{1,0:T(8,128)(2,1)S(1)} collective-permute-done((bf16[256,1024]{1,0:T(8,128)(2,1)S(1)}, bf16[256,1024]{1,0:T(8,128)(2,1)S(1)}, u32[]{:S(2)}, u32[]{:S(2)}) %collective-permute-start.7) | collective-permute-done | bytes 524320 | tf_op jit(solution)/shard_map/ppermute | solution.py:458
  69.6 1.3 %collective-permute-start.12 = (bf16[256,1024]{1,0:T(8,128)(2,1)S(1)}, bf16[256,1024]{1,0:T(8,128)(2,1)S(1)}, u32[]{:S(2)}, u32[]{:S(2)}) collective-permute-start(bf16[256,1024]{1,0:T(8,128)(2,1)S(1)} %get-tuple-element.33.refs_4_), channel_id=1, source_target_pairs={{1,0},{5,4},{9,8},{13,12},{17,16},{21,20},{25,24},{29,28}} | collective-permute-start | bytes 1572872 | tf_op jit(solution)/shard_map/ppermute | solution.py:458
  70.9 5.8 %collective-permute-start.14 = (bf16[256,1024]{1,0:T(8,128)(2,1)S(1)}, bf16[256,1024]{1,0:T(8,128)(2,1)S(1)}, u32[]{:S(2)}, u32[]{:S(2)}) collective-permute-start(bf16[256,1024]{1,0:T(8,128)(2,1)S(1)} %shard_map.78.refs_2_.refs_0_.refs_1_), channel_id=1, source_target_pairs={{4,16},{12,24},{28,20},{5,17},{13,25},{29,21},{6,18},{14,26},{30,2... | collective-permute-start | bytes 1572872 | tf_op jit(solution)/shard_map/ppermute | solution.py:434
  76.7 1.6 %shard_map.80.refs_7_.refs_0_ = f32[256,1024]{1,0:T(8,128)S(1)} custom-call(s32[2,8]{1,0:T(2,128)S(4)} %get-tuple-element.20.facts_ref, bf16[512,256]{1,0:T(8,128)(2,1)S(1)} %get-tuple-element.21.table_ref, bf16[512,512]{1,0:T(8,128)(2,1)S(1)} %get-tuple-element.22.back_ref, f32[4,512,1024]{2,1,0:T(8,128)S(1)} %get-tuple-element.23.spec_ref, ...), custom_call_target="tpu_custom_call" | custom-call | flops 2147483648 | bytes 1048576 | tf_op jit(solution)/shard_map/pallas_call | solution.py:368
  78.3 2.3 %shard_map.81.refs_4_ = f32[256,1024]{1,0:T(8,128)S(1)} custom-call(s32[2,8]{1,0:T(2,128)S(4)} %get-tuple-element.20.facts_ref, bf16[256,1024]{1,0:T(8,128)(2,1)S(1)} %shard_map.75.refs_0_, bf16[256,1024]{1,0:T(8,128)(2,1)S(1)} %get-tuple-element.28.refs_1_, bf16[256,1024]{1,0:T(8,128)(2,1)S(1)} %get-tuple-element.29.refs_2_, ...), custom_call_target="tpu_custom_call" | custom-call | flops 1610612736 | bytes 13107200 | tf_op jit(solution)/shard_map/pallas_call | solution.py:218
  80.6 1.5 %collective-permute-done.12.refs_1_ = bf16[256,1024]{1,0:T(8,128)(2,1)S(1)} collective-permute-done((bf16[256,1024]{1,0:T(8,128)(2,1)S(1)}, bf16[256,1024]{1,0:T(8,128)(2,1)S(1)}, u32[]{:S(2)}, u32[]{:S(2)}) %collective-permute-start.12) | collective-permute-done | bytes 524320 | tf_op jit(solution)/shard_map/ppermute | solution.py:458
  82.1 1.1 shard_map.82.refs_0_
  83.2 2.2 %collective-permute-start.15 = (bf16[256,1024]{1,0:T(8,128)(2,1)S(1)}, bf16[256,1024]{1,0:T(8,128)(2,1)S(1)}, u32[]{:S(2)}, u32[]{:S(2)}) collective-permute-start(bf16[256,1024]{1,0:T(8,128)(2,1)S(1)} %shard_map.82.refs_0_), channel_id=1, source_target_pairs={{8,0},{12,4},{16,8},{20,12},{24,16},{28,20},{9,1},{13,5},{17,9},{2... | collective-permute-start | bytes 1572872 | tf_op jit(solution)/shard_map/ppermute | solution.py:422
  85.4 4.1 %collective-permute-start.18 = (bf16[256,1024]{1,0:T(8,128)(2,1)S(1)}, bf16[256,1024]{1,0:T(8,128)(2,1)S(1)}, u32[]{:S(2)}, u32[]{:S(2)}) collective-permute-start(bf16[256,1024]{1,0:T(8,128)(2,1)S(1)} %collective-permute-done.13.refs_5_.refs_1_.refs_3_), channel_id=1, source_target_pairs={{0,4},{4,0},{8,12},{12,8},{16,20},{20,16},{24,28},{28,24},{1,5},{5... | collective-permute-start | bytes 1572872 | tf_op jit(solution)/shard_map/ppermute | solution.py:427
  89.4 1.9 %collective-permute-start.17 = (bf16[256,1024]{1,0:T(8,128)(2,1)S(1)}, bf16[256,1024]{1,0:T(8,128)(2,1)S(1)}, u32[]{:S(2)}, u32[]{:S(2)}) collective-permute-start(bf16[256,1024]{1,0:T(8,128)(2,1)S(1)} %shard_map.82.refs_0_), channel_id=1, source_target_pairs={{4,0},{12,8},{20,16},{28,24},{16,4},{24,12},{5,1},{13,9},{21,17},{... | collective-permute-start | bytes 1572872 | tf_op jit(solution)/shard_map/ppermute | solution.py:443
  91.4 1.6 %shard_map.83.refs_1_.refs_0_ = f32[256,1024]{1,0:T(8,128)S(1)} custom-call(s32[2,8]{1,0:T(2,128)S(4)} %get-tuple-element.20.facts_ref, bf16[512,256]{1,0:T(8,128)(2,1)S(1)} %get-tuple-element.21.table_ref, bf16[512,512]{1,0:T(8,128)(2,1)S(1)} %get-tuple-element.22.back_ref, f32[4,512,1024]{2,1,0:T(8,128)S(1)} %get-tuple-element.23.spec_ref, ...), custom_call_target="tpu_custom_call" | custom-call | flops 2147483648 | bytes 1048576 | tf_op jit(solution)/shard_map/pallas_call | solution.py:368
  92.9 2.8 %collective-permute-done.15.refs_0_ = bf16[256,1024]{1,0:T(8,128)(2,1)S(1)} collective-permute-done((bf16[256,1024]{1,0:T(8,128)(2,1)S(1)}, bf16[256,1024]{1,0:T(8,128)(2,1)S(1)}, u32[]{:S(2)}, u32[]{:S(2)}) %collective-permute-start.15) | collective-permute-done | bytes 524320 | tf_op jit(solution)/shard_map/ppermute | solution.py:422
  95.7 4.7 %collective-permute-start.16 = (bf16[256,1024]{1,0:T(8,128)(2,1)S(1)}, bf16[256,1024]{1,0:T(8,128)(2,1)S(1)}, u32[]{:S(2)}, u32[]{:S(2)}) collective-permute-start(bf16[256,1024]{1,0:T(8,128)(2,1)S(1)} %shard_map.84.refs_5_), channel_id=1, source_target_pairs={{0,4},{4,0},{8,12},{12,8},{16,20},{20,16},{24,28},{28,24},{1,5},{5... | collective-permute-start | bytes 1572872 | tf_op jit(solution)/shard_map/ppermute | solution.py:427
  100.4 2.7 %shard_map.85 = (f32[1,2,256,1024]{3,2,1,0:T(8,128)}, f32[8,128]{1,0:T(8,128)}) custom-call(s32[2,8]{1,0:T(2,128)S(4)} %get-tuple-element.20.facts_ref, bf16[512,256]{1,0:T(8,128)(2,1)S(1)} %get-tuple-element.21.table_ref, bf16[512,512]{1,0:T(8,128)(2,1)S(1)} %get-tuple-element.22.back_ref, f32[4,512,1024]{2,1,0:T(8,128)S(1)} %get-tuple-element.23.spec_ref, ...), custom_call_target="tpu_custom_call" | custom-call | flops 2147483648 | bytes 1048576 | tf_op jit(solution)/shard_map/pallas_call | solution.py:368
  103.2 2.1 %collective-permute-done.17.refs_7_ = bf16[256,1024]{1,0:T(8,128)(2,1)S(1)} collective-permute-done((bf16[256,1024]{1,0:T(8,128)(2,1)S(1)}, bf16[256,1024]{1,0:T(8,128)(2,1)S(1)}, u32[]{:S(2)}, u32[]{:S(2)}) %collective-permute-start.17) | collective-permute-done | bytes 524320 | tf_op jit(solution)/shard_map/ppermute | solution.py:443
  105.3 2.7 %shard_map.86 = f32[1,2,256,1024]{3,2,1,0:T(8,128)} custom-call(s32[2,8]{1,0:T(2,128)S(4)} %get-tuple-element.20.facts_ref, bf16[512,256]{1,0:T(8,128)(2,1)S(1)} %get-tuple-element.21.table_ref, bf16[512,512]{1,0:T(8,128)(2,1)S(1)} %get-tuple-element.22.back_ref, f32[4,512,1024]{2,1,0:T(8,128)S(1)} %get-tuple-element.23.spec_ref, ...), custom_call_target="tpu_custom_call", output_to_operand_aliasing={{}: (12, {})} | custom-call | flops 2147483648 | bytes 1048576 | tf_op jit(solution)/shard_map/pallas_call | solution.py:368
  (21 shorter events, 4.7 us)
Async XLA Ops:
  1.1 13.8 %collective-permute-start = (bf16[256,1024]{1,0:T(8,128)(2,1)S(1)}, bf16[256,1024]{1,0:T(8,128)(2,1)S(1)}, u32[]{:S(2)}, u32[]{:S(2)}) collective-permute-start(bf16[256,1024]{1,0:T(8,128)(2,1)S(1)} %slice_bitcast_fusion.refs_0_), channel_id=1, source_target_pairs={{0,1},{1,2},{2,3},{4,5},{5,6},{6,7},{8,9},{9,10},{10,11},{12,13},{... | collective-permute-start | bytes 1572872 | tf_op jit(solution)/shard_map/ppermute | solution.py:458
  4.3 14.4 %collective-permute-start.1 = (bf16[256,1024]{1,0:T(8,128)(2,1)S(1)}, bf16[256,1024]{1,0:T(8,128)(2,1)S(1)}, u32[]{:S(2)}, u32[]{:S(2)}) collective-permute-start(bf16[256,1024]{1,0:T(8,128)(2,1)S(1)} %slice_bitcast_fusion.refs_0_), channel_id=1, source_target_pairs={{1,0},{2,1},{3,2},{5,4},{6,5},{7,6},{9,8},{10,9},{11,10},{13,12},{... | collective-permute-start | bytes 1572872 | tf_op jit(solution)/shard_map/ppermute | solution.py:458
  18.7 9.7 %collective-permute-start.4 = (bf16[256,1024]{1,0:T(8,128)(2,1)S(1)}, bf16[256,1024]{1,0:T(8,128)(2,1)S(1)}, u32[]{:S(2)}, u32[]{:S(2)}) collective-permute-start(bf16[256,1024]{1,0:T(8,128)(2,1)S(1)} %get-tuple-element.26.refs_1_), channel_id=1, source_target_pairs={{1,2},{2,3},{5,6},{6,7},{9,10},{10,11},{13,14},{14,15},{17,18},{18... | collective-permute-start | bytes 1572872 | tf_op jit(solution)/shard_map/ppermute | solution.py:458
  19.4 15.8 %collective-permute-start.5 = (bf16[256,1024]{1,0:T(8,128)(2,1)S(1)}, bf16[256,1024]{1,0:T(8,128)(2,1)S(1)}, u32[]{:S(2)}, u32[]{:S(2)}) collective-permute-start(bf16[256,1024]{1,0:T(8,128)(2,1)S(1)} %get-tuple-element.27.refs_2_), channel_id=1, source_target_pairs={{1,0},{2,1},{5,4},{6,5},{9,8},{10,9},{13,12},{14,13},{17,16},{18,1... | collective-permute-start | bytes 1572872 | tf_op jit(solution)/shard_map/ppermute | solution.py:458
  20.7 15.8 %collective-permute-start.2 = (bf16[256,1024]{1,0:T(8,128)(2,1)S(1)}, bf16[256,1024]{1,0:T(8,128)(2,1)S(1)}, u32[]{:S(2)}, u32[]{:S(2)}) collective-permute-start(bf16[256,1024]{1,0:T(8,128)(2,1)S(1)} %shard_map.75.refs_0_), channel_id=1, source_target_pairs={{0,1},{1,2},{2,3},{4,5},{5,6},{6,7},{8,9},{9,10},{10,11},{12,13},{... | collective-permute-start | bytes 1572872 | tf_op jit(solution)/shard_map/ppermute | solution.py:458
  27.1 19.3 %collective-permute-start.3 = (bf16[256,1024]{1,0:T(8,128)(2,1)S(1)}, bf16[256,1024]{1,0:T(8,128)(2,1)S(1)}, u32[]{:S(2)}, u32[]{:S(2)}) collective-permute-start(bf16[256,1024]{1,0:T(8,128)(2,1)S(1)} %shard_map.75.refs_0_), channel_id=1, source_target_pairs={{1,0},{2,1},{3,2},{5,4},{6,5},{7,6},{9,8},{10,9},{11,10},{13,12},{... | collective-permute-start | bytes 1572872 | tf_op jit(solution)/shard_map/ppermute | solution.py:458
  28.4 22.3 %collective-permute-start.8 = (bf16[256,1024]{1,0:T(8,128)(2,1)S(1)}, bf16[256,1024]{1,0:T(8,128)(2,1)S(1)}, u32[]{:S(2)}, u32[]{:S(2)}) collective-permute-start(bf16[256,1024]{1,0:T(8,128)(2,1)S(1)} %collective-permute-done.4.refs_2_.refs_3_), channel_id=1, source_target_pairs={{2,3},{6,7},{10,11},{14,15},{18,19},{22,23},{26,27},{30,31}} | collective-permute-start | bytes 1572872 | tf_op jit(solution)/shard_map/ppermute | solution.py:458
  35.2 22.5 %collective-permute-start.9 = (bf16[256,1024]{1,0:T(8,128)(2,1)S(1)}, bf16[256,1024]{1,0:T(8,128)(2,1)S(1)}, u32[]{:S(2)}, u32[]{:S(2)}) collective-permute-start(bf16[256,1024]{1,0:T(8,128)(2,1)S(1)} %collective-permute-done.5.refs_3_.refs_4_), channel_id=1, source_target_pairs={{1,0},{5,4},{9,8},{13,12},{17,16},{21,20},{25,24},{29,28}} | collective-permute-start | bytes 1572872 | tf_op jit(solution)/shard_map/ppermute | solution.py:458
  46.4 20.5 %collective-permute-start.6 = (bf16[256,1024]{1,0:T(8,128)(2,1)S(1)}, bf16[256,1024]{1,0:T(8,128)(2,1)S(1)}, u32[]{:S(2)}, u32[]{:S(2)}) collective-permute-start(bf16[256,1024]{1,0:T(8,128)(2,1)S(1)} %get-tuple-element.28.refs_1_), channel_id=1, source_target_pairs={{1,2},{2,3},{5,6},{6,7},{9,10},{10,11},{13,14},{14,15},{17,18},{18... | collective-permute-start | bytes 1572872 | tf_op jit(solution)/shard_map/ppermute | solution.py:458
  47.1 21.8 %collective-permute-start.7 = (bf16[256,1024]{1,0:T(8,128)(2,1)S(1)}, bf16[256,1024]{1,0:T(8,128)(2,1)S(1)}, u32[]{:S(2)}, u32[]{:S(2)}) collective-permute-start(bf16[256,1024]{1,0:T(8,128)(2,1)S(1)} %get-tuple-element.29.refs_2_), channel_id=1, source_target_pairs={{1,0},{2,1},{5,4},{6,5},{9,8},{10,9},{13,12},{14,13},{17,16},{18,1... | collective-permute-start | bytes 1572872 | tf_op jit(solution)/shard_map/ppermute | solution.py:458
  58.6 10.3 %collective-permute-start.10 = (bf16[256,1024]{1,0:T(8,128)(2,1)S(1)}, bf16[256,1024]{1,0:T(8,128)(2,1)S(1)}, u32[]{:S(2)}, u32[]{:S(2)}) collective-permute-start(bf16[256,1024]{1,0:T(8,128)(2,1)S(1)} %shard_map.78.refs_2_.refs_0_.refs_1_), channel_id=1, source_target_pairs={{0,4},{4,0},{8,12},{12,8},{16,20},{20,16},{24,28},{28,24},{1,5},{5... | collective-permute-start | bytes 1572872 | tf_op jit(solution)/shard_map/ppermute | solution.py:427
  63.8 16.8 %collective-permute-start.13 = (bf16[256,1024]{1,0:T(8,128)(2,1)S(1)}, bf16[256,1024]{1,0:T(8,128)(2,1)S(1)}, u32[]{:S(2)}, u32[]{:S(2)}) collective-permute-start(bf16[256,1024]{1,0:T(8,128)(2,1)S(1)} %shard_map.78.refs_2_.refs_0_.refs_1_), channel_id=1, source_target_pairs={{0,8},{4,12},{8,16},{12,20},{16,24},{20,28},{1,9},{5,13},{9,17},{1... | collective-permute-start | bytes 1572872 | tf_op jit(solution)/shard_map/ppermute | solution.py:422
  68.9 11.7 %collective-permute-start.11 = (bf16[256,1024]{1,0:T(8,128)(2,1)S(1)}, bf16[256,1024]{1,0:T(8,128)(2,1)S(1)}, u32[]{:S(2)}, u32[]{:S(2)}) collective-permute-start(bf16[256,1024]{1,0:T(8,128)(2,1)S(1)} %get-tuple-element.32.refs_3_), channel_id=1, source_target_pairs={{2,3},{6,7},{10,11},{14,15},{18,19},{22,23},{26,27},{30,31}} | collective-permute-start | bytes 1572872 | tf_op jit(solution)/shard_map/ppermute | solution.py:458
  69.6 12.5 %collective-permute-start.12 = (bf16[256,1024]{1,0:T(8,128)(2,1)S(1)}, bf16[256,1024]{1,0:T(8,128)(2,1)S(1)}, u32[]{:S(2)}, u32[]{:S(2)}) collective-permute-start(bf16[256,1024]{1,0:T(8,128)(2,1)S(1)} %get-tuple-element.33.refs_4_), channel_id=1, source_target_pairs={{1,0},{5,4},{9,8},{13,12},{17,16},{21,20},{25,24},{29,28}} | collective-permute-start | bytes 1572872 | tf_op jit(solution)/shard_map/ppermute | solution.py:458
  70.9 20.5 %collective-permute-start.14 = (bf16[256,1024]{1,0:T(8,128)(2,1)S(1)}, bf16[256,1024]{1,0:T(8,128)(2,1)S(1)}, u32[]{:S(2)}, u32[]{:S(2)}) collective-permute-start(bf16[256,1024]{1,0:T(8,128)(2,1)S(1)} %shard_map.78.refs_2_.refs_0_.refs_1_), channel_id=1, source_target_pairs={{4,16},{12,24},{28,20},{5,17},{13,25},{29,21},{6,18},{14,26},{30,2... | collective-permute-start | bytes 1572872 | tf_op jit(solution)/shard_map/ppermute | solution.py:434
  83.2 12.5 %collective-permute-start.15 = (bf16[256,1024]{1,0:T(8,128)(2,1)S(1)}, bf16[256,1024]{1,0:T(8,128)(2,1)S(1)}, u32[]{:S(2)}, u32[]{:S(2)}) collective-permute-start(bf16[256,1024]{1,0:T(8,128)(2,1)S(1)} %shard_map.82.refs_0_), channel_id=1, source_target_pairs={{8,0},{12,4},{16,8},{20,12},{24,16},{28,20},{9,1},{13,5},{17,9},{2... | collective-permute-start | bytes 1572872 | tf_op jit(solution)/shard_map/ppermute | solution.py:422
  85.4 15.1 %collective-permute-start.18 = (bf16[256,1024]{1,0:T(8,128)(2,1)S(1)}, bf16[256,1024]{1,0:T(8,128)(2,1)S(1)}, u32[]{:S(2)}, u32[]{:S(2)}) collective-permute-start(bf16[256,1024]{1,0:T(8,128)(2,1)S(1)} %collective-permute-done.13.refs_5_.refs_1_.refs_3_), channel_id=1, source_target_pairs={{0,4},{4,0},{8,12},{12,8},{16,20},{20,16},{24,28},{28,24},{1,5},{5... | collective-permute-start | bytes 1572872 | tf_op jit(solution)/shard_map/ppermute | solution.py:427
  89.4 15.8 %collective-permute-start.17 = (bf16[256,1024]{1,0:T(8,128)(2,1)S(1)}, bf16[256,1024]{1,0:T(8,128)(2,1)S(1)}, u32[]{:S(2)}, u32[]{:S(2)}) collective-permute-start(bf16[256,1024]{1,0:T(8,128)(2,1)S(1)} %shard_map.82.refs_0_), channel_id=1, source_target_pairs={{4,0},{12,8},{20,16},{28,24},{16,4},{24,12},{5,1},{13,9},{21,17},{... | collective-permute-start | bytes 1572872 | tf_op jit(solution)/shard_map/ppermute | solution.py:443
  95.7 9.6 %collective-permute-start.16 = (bf16[256,1024]{1,0:T(8,128)(2,1)S(1)}, bf16[256,1024]{1,0:T(8,128)(2,1)S(1)}, u32[]{:S(2)}, u32[]{:S(2)}) collective-permute-start(bf16[256,1024]{1,0:T(8,128)(2,1)S(1)} %shard_map.84.refs_5_), channel_id=1, source_target_pairs={{0,4},{4,0},{8,12},{12,8},{16,20},{20,16},{24,28},{28,24},{1,5},{5... | collective-permute-start | bytes 1572872 | tf_op jit(solution)/shard_map/ppermute | solution.py:427

commit v18 on v17

--- a/solution.py
+++ b/solution.py
@@ -435,11 +435,11 @@
     return [two, core_swapped(two), mate, far]
 
 
-def lower_halo_of(value, own):
+def lower_halo_of(value, *own):
     count = lax.axis_size("ctx")
     mixed = [(source, source - 1) for source in range(1, count, 2)]
     mixed += [(source, source - 3) for source in range(4, count, 2)]
-    two = ordered(shifted(value, -2), own)
+    two = ordered(shifted(value, -2), *own)
     mixed = lax.ppermute(value, "ctx", mixed)
     return [two, core_swapped(two), mixed]
 
@@ -501,14 +501,14 @@
     upper = final_of(upper_in, 1, partial)
     upper_halo = upper_halo_of(upper)
     two, swapped, mate, fold = upper_halo
-    near = own_terms(1, tabs, facts, [upper])
     pass_on(lower_in, upper, mate)
-    result, _ = far_terms(1, 1, tabs, facts, [near, *upper_halo])
-
-    partial = partial_of(own, lower_in, 0, [near])
+
+    partial = partial_of(own, lower_in, 0)
     lower = final_of(lower_in, 0, partial, [two])
+    upper_near = own_terms(1, tabs, facts, [upper], after=[lower])
+    result, _ = far_terms(1, 1, tabs, facts, [upper_near, *upper_halo])
     near = own_terms(0, tabs, facts, [lower], after=[fold])
-    lower_halo = lower_halo_of(lower, near)
+    lower_halo = lower_halo_of(lower, near, upper_near)
     arrays = [near, upper, mate, two, fold, *lower_halo]
     return far_terms(0, 1, tabs, facts, arrays, result)
 

time: 108 us -> 110 us (1.019)
  Pallas kernels: 20.7 us -> 24.7 us
  waiting for transfers between devices: 38.8 us -> 36.8 us
    pallas_call x4, Pallas kernels: 8.62 us -> 12.8 us  [conv_call(): pl.pallas_call(body, grid=(width // LANES,), out_shape=out_shape, in_spec...]
    ppermute x2, waiting for transfers between devices: 2.75 us -> 0.21 us  [shifted(): lax.ppermute(value, 'ctx', [(source, source + steps) for source in range(...]
    ppermute x12, waiting for transfers between devices: 33.9 us -> 35.3 us  [sent(): return (lax.ppermute(up, 'ch', upward), lax.ppermute(down, 'ch', downward))]
  transfers between devices with their start and end apart: 19 -> 19, of which waited for: 9 -> 9; matrix products, arithmetic and copies ran while one was open for 0% -> 0% of each run, Pallas kernels for 17% -> 18%
where the time goes in v18:
time: 110 us
  starting transfers between devices  46.8 us (43%)
  waiting for transfers between devices  36.8 us (33%)
  Pallas kernels  24.7 us (22%)
    ppermute x12, waiting for transfers between devices, sent(): return (lax.ppermute(up, 'ch', upward), lax.ppermute(down, 'ch', downward))  35.3 us
    ppermute x12, starting transfers between devices, sent(): return (lax.ppermute(up, 'ch', upward), lax.ppermute(down, 'ch', downward))  20.1 us
    ppermute x3, starting transfers between devices, core_swapped(): lax.ppermute(value, 'ctx', [(source, source ^ 1) for source in range(coun...  13.5 us
    pallas_call x4, Pallas kernels, conv_call(): pl.pallas_call(body, grid=(width // LANES,), out_shape=out_shape, in_spec...  12.8 us
    pallas_call x4, Pallas kernels, project(): pl.pallas_call(functools.partial(project_kernel, hops, slot, before is No...  6.3 us
    ppermute x1, starting transfers between devices, upper_halo_of(): mate, far = (core_swapped(value), lax.ppermute(value, 'ctx', far))  5.85 us
    pallas_call x1, Pallas kernels, prepare(): pl.pallas_call(functools.partial(prepare_kernel, pairs), grid=(width // L...  5.59 us
    ppermute x2, starting transfers between devices, shifted(): lax.ppermute(value, 'ctx', [(source, source + steps) for source in range(...  5.27 us
  transfers between devices with their start and end apart: 19, of which 9 were waited for; matrix products, arithmetic and copies ran while one was open for 0% of the time, Pallas kernels for 18%

profile of v18, /device:TPU:3, one launch (start us, length us, event | category | flops | bytes accessed | tf_op | source)
XLA Modules:
  0.0 109.6 jit_solution(8720304664010848861)
XLA Ops:
  0.0 1.1 slice_bitcast_fusion.refs_0_
  1.1 3.2 %collective-permute-start = (bf16[256,1024]{1,0:T(8,128)(2,1)S(1)}, bf16[256,1024]{1,0:T(8,128)(2,1)S(1)}, u32[]{:S(2)}, u32[]{:S(2)}) collective-permute-start(bf16[256,1024]{1,0:T(8,128)(2,1)S(1)} %slice_bitcast_fusion.refs_0_), channel_id=1, source_target_pairs={{0,1},{1,2},{2,3},{4,5},{5,6},{6,7},{8,9},{9,10},{10,11},{12,13},{... | collective-permute-start | bytes 1572872 | tf_op jit(solution)/shard_map/ppermute | solution.py:458
  4.3 1.3 %collective-permute-start.1 = (bf16[256,1024]{1,0:T(8,128)(2,1)S(1)}, bf16[256,1024]{1,0:T(8,128)(2,1)S(1)}, u32[]{:S(2)}, u32[]{:S(2)}) collective-permute-start(bf16[256,1024]{1,0:T(8,128)(2,1)S(1)} %slice_bitcast_fusion.refs_0_), channel_id=1, source_target_pairs={{1,0},{2,1},{3,2},{5,4},{6,5},{7,6},{9,8},{10,9},{11,10},{13,12},{... | collective-permute-start | bytes 1572872 | tf_op jit(solution)/shard_map/ppermute | solution.py:458
  5.6 5.6 %shard_map.73 = (f32[4,512,1024]{2,1,0:T(8,128)S(1)}, bf16[1024,4096]{1,0:T(8,128)(2,1)S(1)}, bf16[1,2,256,1024]{3,2,1,0:T(8,128)(2,1)S(1)}, bf16[256,1024]{1,0:...) custom-call(s32[1]{0:T(128)} %bitcast.refs_0_, ...), custom_call_target="tpu_custom_call" | custom-call | flops 2415919104 | bytes 11534336 | tf_op jit(solution)/shard_map/pallas_call | solution.py:147
  11.2 3.6 %collective-permute-done.refs_0_ = bf16[256,1024]{1,0:T(8,128)(2,1)S(1)} collective-permute-done((bf16[256,1024]{1,0:T(8,128)(2,1)S(1)}, bf16[256,1024]{1,0:T(8,128)(2,1)S(1)}, u32[]{:S(2)}, u32[]{:S(2)}) %collective-permute-start) | collective-permute-done | bytes 524320 | tf_op jit(solution)/shard_map/ppermute | solution.py:458
  14.9 3.8 %collective-permute-done.1.refs_1_ = bf16[256,1024]{1,0:T(8,128)(2,1)S(1)} collective-permute-done((bf16[256,1024]{1,0:T(8,128)(2,1)S(1)}, bf16[256,1024]{1,0:T(8,128)(2,1)S(1)}, u32[]{:S(2)}, u32[]{:S(2)}) %collective-permute-start.1) | collective-permute-done | bytes 524320 | tf_op jit(solution)/shard_map/ppermute | solution.py:458
  19.4 1.3 %collective-permute-start.5 = (bf16[256,1024]{1,0:T(8,128)(2,1)S(1)}, bf16[256,1024]{1,0:T(8,128)(2,1)S(1)}, u32[]{:S(2)}, u32[]{:S(2)}) collective-permute-start(bf16[256,1024]{1,0:T(8,128)(2,1)S(1)} %get-tuple-element.27.refs_2_), channel_id=1, source_target_pairs={{1,0},{2,1},{5,4},{6,5},{9,8},{10,9},{13,12},{14,13},{17,16},{18,1... | collective-permute-start | bytes 1572872 | tf_op jit(solution)/shard_map/ppermute | solution.py:458
  20.7 6.4 %collective-permute-start.2 = (bf16[256,1024]{1,0:T(8,128)(2,1)S(1)}, bf16[256,1024]{1,0:T(8,128)(2,1)S(1)}, u32[]{:S(2)}, u32[]{:S(2)}) collective-permute-start(bf16[256,1024]{1,0:T(8,128)(2,1)S(1)} %shard_map.75.refs_0_), channel_id=1, source_target_pairs={{0,1},{1,2},{2,3},{4,5},{5,6},{6,7},{8,9},{9,10},{10,11},{12,13},{... | collective-permute-start | bytes 1572872 | tf_op jit(solution)/shard_map/ppermute | solution.py:458
  27.1 1.3 %collective-permute-start.3 = (bf16[256,1024]{1,0:T(8,128)(2,1)S(1)}, bf16[256,1024]{1,0:T(8,128)(2,1)S(1)}, u32[]{:S(2)}, u32[]{:S(2)}) collective-permute-start(bf16[256,1024]{1,0:T(8,128)(2,1)S(1)} %shard_map.75.refs_0_), channel_id=1, source_target_pairs={{1,0},{2,1},{3,2},{5,4},{6,5},{7,6},{9,8},{10,9},{11,10},{13,12},{... | collective-permute-start | bytes 1572872 | tf_op jit(solution)/shard_map/ppermute | solution.py:458
  29.1 6.1 %collective-permute-done.5.refs_3_.refs_4_ = bf16[256,1024]{1,0:T(8,128)(2,1)S(1)} collective-permute-done((bf16[256,1024]{1,0:T(8,128)(2,1)S(1)}, bf16[256,1024]{1,0:T(8,128)(2,1)S(1)}, u32[]{:S(2)}, u32[]{:S(2)}) %collective-permute-start.5) | collective-permute-done | bytes 524320 | tf_op jit(solution)/shard_map/ppermute | solution.py:458
  35.2 1.3 %collective-permute-start.9 = (bf16[256,1024]{1,0:T(8,128)(2,1)S(1)}, bf16[256,1024]{1,0:T(8,128)(2,1)S(1)}, u32[]{:S(2)}, u32[]{:S(2)}) collective-permute-start(bf16[256,1024]{1,0:T(8,128)(2,1)S(1)} %collective-permute-done.5.refs_3_.refs_4_), channel_id=1, source_target_pairs={{1,0},{5,4},{9,8},{13,12},{17,16},{21,20},{25,24},{29,28}} | collective-permute-start | bytes 1572872 | tf_op jit(solution)/shard_map/ppermute | solution.py:458
  36.5 9.9 %collective-permute-done.3.refs_1_ = bf16[256,1024]{1,0:T(8,128)(2,1)S(1)} collective-permute-done((bf16[256,1024]{1,0:T(8,128)(2,1)S(1)}, bf16[256,1024]{1,0:T(8,128)(2,1)S(1)}, u32[]{:S(2)}, u32[]{:S(2)}) %collective-permute-start.3) | collective-permute-done | bytes 524320 | tf_op jit(solution)/shard_map/ppermute | solution.py:458
  47.1 1.3 %collective-permute-start.7 = (bf16[256,1024]{1,0:T(8,128)(2,1)S(1)}, bf16[256,1024]{1,0:T(8,128)(2,1)S(1)}, u32[]{:S(2)}, u32[]{:S(2)}) collective-permute-start(bf16[256,1024]{1,0:T(8,128)(2,1)S(1)} %get-tuple-element.29.refs_2_), channel_id=1, source_target_pairs={{1,0},{2,1},{5,4},{6,5},{9,8},{10,9},{13,12},{14,13},{17,16},{18,1... | collective-permute-start | bytes 1572872 | tf_op jit(solution)/shard_map/ppermute | solution.py:458
  48.4 2.3 %shard_map.77.refs_4_ = f32[256,1024]{1,0:T(8,128)S(1)} custom-call(s32[2,8]{1,0:T(2,128)S(4)} %get-tuple-element.20.facts_ref, bf16[256,1024]{1,0:T(8,128)(2,1)S(1)} %slice_bitcast_fusion.refs_0_, bf16[256,1024]{1,0:T(8,128)(2,1)S(1)} %get-tuple-element.26.refs_1_, bf16[256,1024]{1,0:T(8,128)(2,1)S(1)} %get-tuple-element.27.refs_2_, ...), custom_call_target="tpu_custom_call" | custom-call | flops 1610612736 | bytes 13107200 | tf_op jit(solution)/shard_map/pallas_call | solution.py:218
  50.7 7.0 %collective-permute-done.9.refs_1_ = bf16[256,1024]{1,0:T(8,128)(2,1)S(1)} collective-permute-done((bf16[256,1024]{1,0:T(8,128)(2,1)S(1)}, bf16[256,1024]{1,0:T(8,128)(2,1)S(1)}, u32[]{:S(2)}, u32[]{:S(2)}) %collective-permute-start.9) | collective-permute-done | bytes 524320 | tf_op jit(solution)/shard_map/ppermute | solution.py:458
  57.6 0.9 shard_map.78.refs_2_.refs_0_.refs_1_
  58.6 5.2 %collective-permute-start.10 = (bf16[256,1024]{1,0:T(8,128)(2,1)S(1)}, bf16[256,1024]{1,0:T(8,128)(2,1)S(1)}, u32[]{:S(2)}, u32[]{:S(2)}) collective-permute-start(bf16[256,1024]{1,0:T(8,128)(2,1)S(1)} %shard_map.78.refs_2_.refs_0_.refs_1_), channel_id=1, source_target_pairs={{0,4},{4,0},{8,12},{12,8},{16,20},{20,16},{24,28},{28,24},{1,5},{5... | collective-permute-start | bytes 1572872 | tf_op jit(solution)/shard_map/ppermute | solution.py:427
  63.8 3.1 %collective-permute-start.13 = (bf16[256,1024]{1,0:T(8,128)(2,1)S(1)}, bf16[256,1024]{1,0:T(8,128)(2,1)S(1)}, u32[]{:S(2)}, u32[]{:S(2)}) collective-permute-start(bf16[256,1024]{1,0:T(8,128)(2,1)S(1)} %shard_map.78.refs_2_.refs_0_.refs_1_), channel_id=1, source_target_pairs={{0,8},{4,12},{8,16},{12,20},{16,24},{20,28},{1,9},{5,13},{9,17},{1... | collective-permute-start | bytes 1572872 | tf_op jit(solution)/shard_map/ppermute | solution.py:422
  66.9 2.0 %collective-permute-done.7.refs_1_ = bf16[256,1024]{1,0:T(8,128)(2,1)S(1)} collective-permute-done((bf16[256,1024]{1,0:T(8,128)(2,1)S(1)}, bf16[256,1024]{1,0:T(8,128)(2,1)S(1)}, u32[]{:S(2)}, u32[]{:S(2)}) %collective-permute-start.7) | collective-permute-done | bytes 524320 | tf_op jit(solution)/shard_map/ppermute | solution.py:458
  69.6 1.3 %collective-permute-start.12 = (bf16[256,1024]{1,0:T(8,128)(2,1)S(1)}, bf16[256,1024]{1,0:T(8,128)(2,1)S(1)}, u32[]{:S(2)}, u32[]{:S(2)}) collective-permute-start(bf16[256,1024]{1,0:T(8,128)(2,1)S(1)} %get-tuple-element.33.refs_4_), channel_id=1, source_target_pairs={{1,0},{5,4},{9,8},{13,12},{17,16},{21,20},{25,24},{29,28}} | collective-permute-start | bytes 1572872 | tf_op jit(solution)/shard_map/ppermute | solution.py:458
  70.9 5.8 %collective-permute-start.14 = (bf16[256,1024]{1,0:T(8,128)(2,1)S(1)}, bf16[256,1024]{1,0:T(8,128)(2,1)S(1)}, u32[]{:S(2)}, u32[]{:S(2)}) collective-permute-start(bf16[256,1024]{1,0:T(8,128)(2,1)S(1)} %shard_map.78.refs_2_.refs_0_.refs_1_), channel_id=1, source_target_pairs={{4,16},{12,24},{28,20},{5,17},{13,25},{29,21},{6,18},{14,26},{30,2... | collective-permute-start | bytes 1572872 | tf_op jit(solution)/shard_map/ppermute | solution.py:434
  76.7 2.3 %shard_map.80.refs_4_ = f32[256,1024]{1,0:T(8,128)S(1)} custom-call(s32[2,8]{1,0:T(2,128)S(4)} %get-tuple-element.20.facts_ref, bf16[256,1024]{1,0:T(8,128)(2,1)S(1)} %shard_map.75.refs_0_, bf16[256,1024]{1,0:T(8,128)(2,1)S(1)} %get-tuple-element.28.refs_1_, bf16[256,1024]{1,0:T(8,128)(2,1)S(1)} %get-tuple-element.29.refs_2_, ...), custom_call_target="tpu_custom_call" | custom-call | flops 1610612736 | bytes 13107200 | tf_op jit(solution)/shard_map/pallas_call | solution.py:218
  79.2 2.9 %collective-permute-done.12.refs_1_ = bf16[256,1024]{1,0:T(8,128)(2,1)S(1)} collective-permute-done((bf16[256,1024]{1,0:T(8,128)(2,1)S(1)}, bf16[256,1024]{1,0:T(8,128)(2,1)S(1)}, u32[]{:S(2)}, u32[]{:S(2)}) %collective-permute-start.12) | collective-permute-done | bytes 524320 | tf_op jit(solution)/shard_map/ppermute | solution.py:458
  83.0 2.2 %collective-permute-start.15 = (bf16[256,1024]{1,0:T(8,128)(2,1)S(1)}, bf16[256,1024]{1,0:T(8,128)(2,1)S(1)}, u32[]{:S(2)}, u32[]{:S(2)}) collective-permute-start(bf16[256,1024]{1,0:T(8,128)(2,1)S(1)} %shard_map.81.refs_0_.refs_1_), channel_id=1, source_target_pairs={{8,0},{12,4},{16,8},{20,12},{24,16},{28,20},{9,1},{13,5},{17,9},{2... | collective-permute-start | bytes 1572872 | tf_op jit(solution)/shard_map/ppermute | solution.py:422
  85.2 4.1 %collective-permute-start.18 = (bf16[256,1024]{1,0:T(8,128)(2,1)S(1)}, bf16[256,1024]{1,0:T(8,128)(2,1)S(1)}, u32[]{:S(2)}, u32[]{:S(2)}) collective-permute-start(bf16[256,1024]{1,0:T(8,128)(2,1)S(1)} %collective-permute-done.13.refs_5_.refs_1_.refs_3_), channel_id=1, source_target_pairs={{0,4},{4,0},{8,12},{12,8},{16,20},{20,16},{24,28},{28,24},{1,5},{5... | collective-permute-start | bytes 1572872 | tf_op jit(solution)/shard_map/ppermute | solution.py:427
  89.2 2.1 %collective-permute-start.17 = (bf16[256,1024]{1,0:T(8,128)(2,1)S(1)}, bf16[256,1024]{1,0:T(8,128)(2,1)S(1)}, u32[]{:S(2)}, u32[]{:S(2)}) collective-permute-start(bf16[256,1024]{1,0:T(8,128)(2,1)S(1)} %shard_map.81.refs_0_.refs_1_), channel_id=1, source_target_pairs={{4,0},{12,8},{20,16},{28,24},{16,4},{24,12},{5,1},{13,9},{21,17},{... | collective-permute-start | bytes 1572872 | tf_op jit(solution)/shard_map/ppermute | solution.py:443
  91.3 1.6 %shard_map.83.refs_2_.refs_0_ = f32[256,1024]{1,0:T(8,128)S(1)} custom-call(s32[2,8]{1,0:T(2,128)S(4)} %get-tuple-element.20.facts_ref, bf16[512,256]{1,0:T(8,128)(2,1)S(1)} %get-tuple-element.21.table_ref, bf16[512,512]{1,0:T(8,128)(2,1)S(1)} %get-tuple-element.22.back_ref, f32[4,512,1024]{2,1,0:T(8,128)S(1)} %get-tuple-element.23.spec_ref, ...), custom_call_target="tpu_custom_call" | custom-call | flops 2147483648 | bytes 1048576 | tf_op jit(solution)/shard_map/pallas_call | solution.py:368
  92.9 3.1 %shard_map.82.refs_1_.refs_0_ = f32[256,1024]{1,0:T(8,128)S(1)} custom-call(s32[2,8]{1,0:T(2,128)S(4)} %get-tuple-element.20.facts_ref, bf16[512,256]{1,0:T(8,128)(2,1)S(1)} %get-tuple-element.21.table_ref, bf16[512,512]{1,0:T(8,128)(2,1)S(1)} %get-tuple-element.22.back_ref, f32[4,512,1024]{2,1,0:T(8,128)S(1)} %get-tuple-element.23.spec_ref, ...), custom_call_target="tpu_custom_call" | custom-call | flops 2147483648 | bytes 1048576 | tf_op jit(solution)/shard_map/pallas_call | solution.py:368
  96.1 4.2 %collective-permute-start.16 = (bf16[256,1024]{1,0:T(8,128)(2,1)S(1)}, bf16[256,1024]{1,0:T(8,128)(2,1)S(1)}, u32[]{:S(2)}, u32[]{:S(2)}) collective-permute-start(bf16[256,1024]{1,0:T(8,128)(2,1)S(1)} %shard_map.84.refs_5_), channel_id=1, source_target_pairs={{0,4},{4,0},{8,12},{12,8},{16,20},{20,16},{24,28},{28,24},{1,5},{5... | collective-permute-start | bytes 1572872 | tf_op jit(solution)/shard_map/ppermute | solution.py:427
  100.3 3.6 %shard_map.85 = (f32[1,2,256,1024]{3,2,1,0:T(8,128)}, f32[8,128]{1,0:T(8,128)}) custom-call(s32[2,8]{1,0:T(2,128)S(4)} %get-tuple-element.20.facts_ref, bf16[512,256]{1,0:T(8,128)(2,1)S(1)} %get-tuple-element.21.table_ref, bf16[512,512]{1,0:T(8,128)(2,1)S(1)} %get-tuple-element.22.back_ref, f32[4,512,1024]{2,1,0:T(8,128)S(1)} %get-tuple-element.23.spec_ref, ...), custom_call_target="tpu_custom_call" | custom-call | flops 2147483648 | bytes 1048576 | tf_op jit(solution)/shard_map/pallas_call | solution.py:368
  103.8 1.2 %collective-permute-done.17.refs_7_ = bf16[256,1024]{1,0:T(8,128)(2,1)S(1)} collective-permute-done((bf16[256,1024]{1,0:T(8,128)(2,1)S(1)}, bf16[256,1024]{1,0:T(8,128)(2,1)S(1)}, u32[]{:S(2)}, u32[]{:S(2)}) %collective-permute-start.17) | collective-permute-done | bytes 524320 | tf_op jit(solution)/shard_map/ppermute | solution.py:443
  105.1 4.5 %shard_map.86 = f32[1,2,256,1024]{3,2,1,0:T(8,128)} custom-call(s32[2,8]{1,0:T(2,128)S(4)} %get-tuple-element.20.facts_ref, bf16[512,256]{1,0:T(8,128)(2,1)S(1)} %get-tuple-element.21.table_ref, bf16[512,512]{1,0:T(8,128)(2,1)S(1)} %get-tuple-element.22.back_ref, f32[4,512,1024]{2,1,0:T(8,128)S(1)} %get-tuple-element.23.spec_ref, ...), custom_call_target="tpu_custom_call", output_to_operand_aliasing={{}: (12, {})} | custom-call | flops 2147483648 | bytes 1048576 | tf_op jit(solution)/shard_map/pallas_call | solution.py:368
  (21 shorter events, 3.9 us)
Async XLA Ops:
  1.1 13.8 %collective-permute-start = (bf16[256,1024]{1,0:T(8,128)(2,1)S(1)}, bf16[256,1024]{1,0:T(8,128)(2,1)S(1)}, u32[]{:S(2)}, u32[]{:S(2)}) collective-permute-start(bf16[256,1024]{1,0:T(8,128)(2,1)S(1)} %slice_bitcast_fusion.refs_0_), channel_id=1, source_target_pairs={{0,1},{1,2},{2,3},{4,5},{5,6},{6,7},{8,9},{9,10},{10,11},{12,13},{... | collective-permute-start | bytes 1572872 | tf_op jit(solution)/shard_map/ppermute | solution.py:458
  4.3 14.4 %collective-permute-start.1 = (bf16[256,1024]{1,0:T(8,128)(2,1)S(1)}, bf16[256,1024]{1,0:T(8,128)(2,1)S(1)}, u32[]{:S(2)}, u32[]{:S(2)}) collective-permute-start(bf16[256,1024]{1,0:T(8,128)(2,1)S(1)} %slice_bitcast_fusion.refs_0_), channel_id=1, source_target_pairs={{1,0},{2,1},{3,2},{5,4},{6,5},{7,6},{9,8},{10,9},{11,10},{13,12},{... | collective-permute-start | bytes 1572872 | tf_op jit(solution)/shard_map/ppermute | solution.py:458
  18.7 9.7 %collective-permute-start.4 = (bf16[256,1024]{1,0:T(8,128)(2,1)S(1)}, bf16[256,1024]{1,0:T(8,128)(2,1)S(1)}, u32[]{:S(2)}, u32[]{:S(2)}) collective-permute-start(bf16[256,1024]{1,0:T(8,128)(2,1)S(1)} %get-tuple-element.26.refs_1_), channel_id=1, source_target_pairs={{1,2},{2,3},{5,6},{6,7},{9,10},{10,11},{13,14},{14,15},{17,18},{18... | collective-permute-start | bytes 1572872 | tf_op jit(solution)/shard_map/ppermute | solution.py:458
  19.4 15.8 %collective-permute-start.5 = (bf16[256,1024]{1,0:T(8,128)(2,1)S(1)}, bf16[256,1024]{1,0:T(8,128)(2,1)S(1)}, u32[]{:S(2)}, u32[]{:S(2)}) collective-permute-start(bf16[256,1024]{1,0:T(8,128)(2,1)S(1)} %get-tuple-element.27.refs_2_), channel_id=1, source_target_pairs={{1,0},{2,1},{5,4},{6,5},{9,8},{10,9},{13,12},{14,13},{17,16},{18,1... | collective-permute-start | bytes 1572872 | tf_op jit(solution)/shard_map/ppermute | solution.py:458
  20.7 15.8 %collective-permute-start.2 = (bf16[256,1024]{1,0:T(8,128)(2,1)S(1)}, bf16[256,1024]{1,0:T(8,128)(2,1)S(1)}, u32[]{:S(2)}, u32[]{:S(2)}) collective-permute-start(bf16[256,1024]{1,0:T(8,128)(2,1)S(1)} %shard_map.75.refs_0_), channel_id=1, source_target_pairs={{0,1},{1,2},{2,3},{4,5},{5,6},{6,7},{8,9},{9,10},{10,11},{12,13},{... | collective-permute-start | bytes 1572872 | tf_op jit(solution)/shard_map/ppermute | solution.py:458
  27.1 19.3 %collective-permute-start.3 = (bf16[256,1024]{1,0:T(8,128)(2,1)S(1)}, bf16[256,1024]{1,0:T(8,128)(2,1)S(1)}, u32[]{:S(2)}, u32[]{:S(2)}) collective-permute-start(bf16[256,1024]{1,0:T(8,128)(2,1)S(1)} %shard_map.75.refs_0_), channel_id=1, source_target_pairs={{1,0},{2,1},{3,2},{5,4},{6,5},{7,6},{9,8},{10,9},{11,10},{13,12},{... | collective-permute-start | bytes 1572872 | tf_op jit(solution)/shard_map/ppermute | solution.py:458
  28.4 22.3 %collective-permute-start.8 = (bf16[256,1024]{1,0:T(8,128)(2,1)S(1)}, bf16[256,1024]{1,0:T(8,128)(2,1)S(1)}, u32[]{:S(2)}, u32[]{:S(2)}) collective-permute-start(bf16[256,1024]{1,0:T(8,128)(2,1)S(1)} %collective-permute-done.4.refs_2_.refs_3_), channel_id=1, source_target_pairs={{2,3},{6,7},{10,11},{14,15},{18,19},{22,23},{26,27},{30,31}} | collective-permute-start | bytes 1572872 | tf_op jit(solution)/shard_map/ppermute | solution.py:458
  35.2 22.5 %collective-permute-start.9 = (bf16[256,1024]{1,0:T(8,128)(2,1)S(1)}, bf16[256,1024]{1,0:T(8,128)(2,1)S(1)}, u32[]{:S(2)}, u32[]{:S(2)}) collective-permute-start(bf16[256,1024]{1,0:T(8,128)(2,1)S(1)} %collective-permute-done.5.refs_3_.refs_4_), channel_id=1, source_target_pairs={{1,0},{5,4},{9,8},{13,12},{17,16},{21,20},{25,24},{29,28}} | collective-permute-start | bytes 1572872 | tf_op jit(solution)/shard_map/ppermute | solution.py:458
  46.4 20.5 %collective-permute-start.6 = (bf16[256,1024]{1,0:T(8,128)(2,1)S(1)}, bf16[256,1024]{1,0:T(8,128)(2,1)S(1)}, u32[]{:S(2)}, u32[]{:S(2)}) collective-permute-start(bf16[256,1024]{1,0:T(8,128)(2,1)S(1)} %get-tuple-element.28.refs_1_), channel_id=1, source_target_pairs={{1,2},{2,3},{5,6},{6,7},{9,10},{10,11},{13,14},{14,15},{17,18},{18... | collective-permute-start | bytes 1572872 | tf_op jit(solution)/shard_map/ppermute | solution.py:458
  47.1 21.8 %collective-permute-start.7 = (bf16[256,1024]{1,0:T(8,128)(2,1)S(1)}, bf16[256,1024]{1,0:T(8,128)(2,1)S(1)}, u32[]{:S(2)}, u32[]{:S(2)}) collective-permute-start(bf16[256,1024]{1,0:T(8,128)(2,1)S(1)} %get-tuple-element.29.refs_2_), channel_id=1, source_target_pairs={{1,0},{2,1},{5,4},{6,5},{9,8},{10,9},{13,12},{14,13},{17,16},{18,1... | collective-permute-start | bytes 1572872 | tf_op jit(solution)/shard_map/ppermute | solution.py:458
  58.6 10.3 %collective-permute-start.10 = (bf16[256,1024]{1,0:T(8,128)(2,1)S(1)}, bf16[256,1024]{1,0:T(8,128)(2,1)S(1)}, u32[]{:S(2)}, u32[]{:S(2)}) collective-permute-start(bf16[256,1024]{1,0:T(8,128)(2,1)S(1)} %shard_map.78.refs_2_.refs_0_.refs_1_), channel_id=1, source_target_pairs={{0,4},{4,0},{8,12},{12,8},{16,20},{20,16},{24,28},{28,24},{1,5},{5... | collective-permute-start | bytes 1572872 | tf_op jit(solution)/shard_map/ppermute | solution.py:427
  63.8 15.4 %collective-permute-start.13 = (bf16[256,1024]{1,0:T(8,128)(2,1)S(1)}, bf16[256,1024]{1,0:T(8,128)(2,1)S(1)}, u32[]{:S(2)}, u32[]{:S(2)}) collective-permute-start(bf16[256,1024]{1,0:T(8,128)(2,1)S(1)} %shard_map.78.refs_2_.refs_0_.refs_1_), channel_id=1, source_target_pairs={{0,8},{4,12},{8,16},{12,20},{16,24},{20,28},{1,9},{5,13},{9,17},{1... | collective-permute-start | bytes 1572872 | tf_op jit(solution)/shard_map/ppermute | solution.py:422
  68.9 10.3 %collective-permute-start.11 = (bf16[256,1024]{1,0:T(8,128)(2,1)S(1)}, bf16[256,1024]{1,0:T(8,128)(2,1)S(1)}, u32[]{:S(2)}, u32[]{:S(2)}) collective-permute-start(bf16[256,1024]{1,0:T(8,128)(2,1)S(1)} %get-tuple-element.32.refs_3_), channel_id=1, source_target_pairs={{2,3},{6,7},{10,11},{14,15},{18,19},{22,23},{26,27},{30,31}} | collective-permute-start | bytes 1572872 | tf_op jit(solution)/shard_map/ppermute | solution.py:458
  69.6 12.5 %collective-permute-start.12 = (bf16[256,1024]{1,0:T(8,128)(2,1)S(1)}, bf16[256,1024]{1,0:T(8,128)(2,1)S(1)}, u32[]{:S(2)}, u32[]{:S(2)}) collective-permute-start(bf16[256,1024]{1,0:T(8,128)(2,1)S(1)} %get-tuple-element.33.refs_4_), channel_id=1, source_target_pairs={{1,0},{5,4},{9,8},{13,12},{17,16},{21,20},{25,24},{29,28}} | collective-permute-start | bytes 1572872 | tf_op jit(solution)/shard_map/ppermute | solution.py:458
  70.9 22.0 %collective-permute-start.14 = (bf16[256,1024]{1,0:T(8,128)(2,1)S(1)}, bf16[256,1024]{1,0:T(8,128)(2,1)S(1)}, u32[]{:S(2)}, u32[]{:S(2)}) collective-permute-start(bf16[256,1024]{1,0:T(8,128)(2,1)S(1)} %shard_map.78.refs_2_.refs_0_.refs_1_), channel_id=1, source_target_pairs={{4,16},{12,24},{28,20},{5,17},{13,25},{29,21},{6,18},{14,26},{30,2... | collective-permute-start | bytes 1572872 | tf_op jit(solution)/shard_map/ppermute | solution.py:434
  83.0 13.0 %collective-permute-start.15 = (bf16[256,1024]{1,0:T(8,128)(2,1)S(1)}, bf16[256,1024]{1,0:T(8,128)(2,1)S(1)}, u32[]{:S(2)}, u32[]{:S(2)}) collective-permute-start(bf16[256,1024]{1,0:T(8,128)(2,1)S(1)} %shard_map.81.refs_0_.refs_1_), channel_id=1, source_target_pairs={{8,0},{12,4},{16,8},{20,12},{24,16},{28,20},{9,1},{13,5},{17,9},{2... | collective-permute-start | bytes 1572872 | tf_op jit(solution)/shard_map/ppermute | solution.py:422
  85.2 15.1 %collective-permute-start.18 = (bf16[256,1024]{1,0:T(8,128)(2,1)S(1)}, bf16[256,1024]{1,0:T(8,128)(2,1)S(1)}, u32[]{:S(2)}, u32[]{:S(2)}) collective-permute-start(bf16[256,1024]{1,0:T(8,128)(2,1)S(1)} %collective-permute-done.13.refs_5_.refs_1_.refs_3_), channel_id=1, source_target_pairs={{0,4},{4,0},{8,12},{12,8},{16,20},{20,16},{24,28},{28,24},{1,5},{5... | collective-permute-start | bytes 1572872 | tf_op jit(solution)/shard_map/ppermute | solution.py:427
  89.2 15.8 %collective-permute-start.17 = (bf16[256,1024]{1,0:T(8,128)(2,1)S(1)}, bf16[256,1024]{1,0:T(8,128)(2,1)S(1)}, u32[]{:S(2)}, u32[]{:S(2)}) collective-permute-start(bf16[256,1024]{1,0:T(8,128)(2,1)S(1)} %shard_map.81.refs_0_.refs_1_), channel_id=1, source_target_pairs={{4,0},{12,8},{20,16},{28,24},{16,4},{24,12},{5,1},{13,9},{21,17},{... | collective-permute-start | bytes 1572872 | tf_op jit(solution)/shard_map/ppermute | solution.py:443
  96.1 9.0 %collective-permute-start.16 = (bf16[256,1024]{1,0:T(8,128)(2,1)S(1)}, bf16[256,1024]{1,0:T(8,128)(2,1)S(1)}, u32[]{:S(2)}, u32[]{:S(2)}) collective-permute-start(bf16[256,1024]{1,0:T(8,128)(2,1)S(1)} %shard_map.84.refs_5_), channel_id=1, source_target_pairs={{0,4},{4,0},{8,12},{12,8},{16,20},{20,16},{24,28},{28,24},{1,5},{5... | collective-permute-start | bytes 1572872 | tf_op jit(solution)/shard_map/ppermute | solution.py:427

commit v19 on v18

--- a/solution.py
+++ b/solution.py
@@ -11,7 +11,7 @@
 from jax.sharding import PartitionSpec as P
 
 REACH = 3
-LANES = 512
+LANES = 1024
 VMEM = 20 * 1024 * 1024
 F32 = jnp.float32
 BF16 = jnp.bfloat16
@@ -432,7 +432,7 @@
     far = [(source, source + 3) for source in range(1, count - 3, 2)] + [(count - 1, count - 3)]
     two = shifted(value, 2)
     mate, far = core_swapped(value), lax.ppermute(value, "ctx", far)
-    return [two, core_swapped(two), mate, far]
+    return [two, mate, far]
 
 
 def lower_halo_of(value, *own):
@@ -500,14 +500,16 @@
     partial = partial_of(start, upper_in, 1)
     upper = final_of(upper_in, 1, partial)
     upper_halo = upper_halo_of(upper)
-    two, swapped, mate, fold = upper_halo
+    two, mate, fold = upper_halo
     pass_on(lower_in, upper, mate)
 
     partial = partial_of(own, lower_in, 0)
     lower = final_of(lower_in, 0, partial, [two])
+    near = own_terms(0, tabs, facts, [lower], after=[fold])
+    two = ordered(two, near)
+    upper_halo = [two, core_swapped(two), mate, fold]
     upper_near = own_terms(1, tabs, facts, [upper], after=[lower])
     result, _ = far_terms(1, 1, tabs, facts, [upper_near, *upper_halo])
-    near = own_terms(0, tabs, facts, [lower], after=[fold])
     lower_halo = lower_halo_of(lower, near, upper_near)
     arrays = [near, upper, mate, two, fold, *lower_halo]
     return far_terms(0, 1, tabs, facts, arrays, result)

time: 110 us -> 109 us (level)
  Pallas kernels: 24.7 us -> 23.5 us
    ppermute x1, starting transfers between devices: 2.1 us -> 5.9 us  [lower_halo_of(): mixed = lax.ppermute(value, 'ctx', mixed)]
    ppermute x3, starting transfers between devices: 13.5 us -> 9.76 us  [core_swapped(): lax.ppermute(value, 'ctx', [(source, source ^ 1) for source in range(coun...]
    pallas_call x4, Pallas kernels: 12.8 us -> 11 us  [conv_call(): pl.pallas_call(body, grid=(width // LANES,), out_shape=out_shape, in_spec...]
  transfers between devices with their start and end apart: 19 -> 19, of which waited for: 9 -> 9; matrix products, arithmetic and copies ran while one was open for 0% -> 0% of each run, Pallas kernels for 18% -> 19%
where the time goes in v19:
time: 109 us; the launch traced here: 108 us
  starting transfers between devices  46.9 us (43%)
  waiting for transfers between devices  36.7 us (34%)
  Pallas kernels  23.5 us (22%)
    ppermute x12, waiting for transfers between devices, sent(): return (lax.ppermute(up, 'ch', upward), lax.ppermute(down, 'ch', downward))  34.9 us
    ppermute x12, starting transfers between devices, sent(): return (lax.ppermute(up, 'ch', upward), lax.ppermute(down, 'ch', downward))  20.1 us
    pallas_call x4, Pallas kernels, conv_call(): pl.pallas_call(body, grid=(width // LANES,), out_shape=out_shape, in_spec...  11 us
    ppermute x3, starting transfers between devices, core_swapped(): lax.ppermute(value, 'ctx', [(source, source ^ 1) for source in range(coun...  9.76 us
    pallas_call x4, Pallas kernels, project(): pl.pallas_call(functools.partial(project_kernel, hops, slot, before is No...  6.5 us
    pallas_call x1, Pallas kernels, prepare(): pl.pallas_call(functools.partial(prepare_kernel, pairs), grid=(width // L...  6 us
    ppermute x1, starting transfers between devices, lower_halo_of(): mixed = lax.ppermute(value, 'ctx', mixed)  5.9 us
    ppermute x1, starting transfers between devices, upper_halo_of(): mate, far = (core_swapped(value), lax.ppermute(value, 'ctx', far))  5.85 us
  transfers between devices with their start and end apart: 19, of which 9 were waited for; matrix products, arithmetic and copies ran while one was open for 0% of the time, Pallas kernels for 19%

profile of v19, /device:TPU:3, one launch (start us, length us, event | category | flops | bytes accessed | tf_op | source)
XLA Modules:
  0.0 108.5 jit_solution(14161376796899181028)
XLA Ops:
  0.0 1.1 slice_bitcast_fusion.refs_0_
  1.1 3.2 %collective-permute-start = (bf16[256,1024]{1,0:T(8,128)(2,1)S(1)}, bf16[256,1024]{1,0:T(8,128)(2,1)S(1)}, u32[]{:S(2)}, u32[]{:S(2)}) collective-permute-start(bf16[256,1024]{1,0:T(8,128)(2,1)S(1)} %slice_bitcast_fusion.refs_0_), channel_id=1, source_target_pairs={{0,1},{1,2},{2,3},{4,5},{5,6},{6,7},{8,9},{9,10},{10,11},{12,13},{... | collective-permute-start | bytes 1572872 | tf_op jit(solution)/shard_map/ppermute | solution.py:458
  4.3 1.3 %collective-permute-start.1 = (bf16[256,1024]{1,0:T(8,128)(2,1)S(1)}, bf16[256,1024]{1,0:T(8,128)(2,1)S(1)}, u32[]{:S(2)}, u32[]{:S(2)}) collective-permute-start(bf16[256,1024]{1,0:T(8,128)(2,1)S(1)} %slice_bitcast_fusion.refs_0_), channel_id=1, source_target_pairs={{1,0},{2,1},{3,2},{5,4},{6,5},{7,6},{9,8},{10,9},{11,10},{13,12},{... | collective-permute-start | bytes 1572872 | tf_op jit(solution)/shard_map/ppermute | solution.py:458
  5.6 6.0 %shard_map.73 = (f32[4,512,1024]{2,1,0:T(8,128)S(1)}, bf16[1024,4096]{1,0:T(8,128)(2,1)S(1)}, bf16[1,2,256,1024]{3,2,1,0:T(8,128)(2,1)S(1)}, bf16[256,1024]{1,0:...) custom-call(s32[1]{0:T(128)} %bitcast.refs_0_, ...), custom_call_target="tpu_custom_call" | custom-call | flops 2415919104 | bytes 11534336 | tf_op jit(solution)/shard_map/pallas_call | solution.py:147
  11.6 3.2 %collective-permute-done.refs_0_ = bf16[256,1024]{1,0:T(8,128)(2,1)S(1)} collective-permute-done((bf16[256,1024]{1,0:T(8,128)(2,1)S(1)}, bf16[256,1024]{1,0:T(8,128)(2,1)S(1)}, u32[]{:S(2)}, u32[]{:S(2)}) %collective-permute-start) | collective-permute-done | bytes 524320 | tf_op jit(solution)/shard_map/ppermute | solution.py:458
  14.9 3.8 %collective-permute-done.1.refs_1_ = bf16[256,1024]{1,0:T(8,128)(2,1)S(1)} collective-permute-done((bf16[256,1024]{1,0:T(8,128)(2,1)S(1)}, bf16[256,1024]{1,0:T(8,128)(2,1)S(1)}, u32[]{:S(2)}, u32[]{:S(2)}) %collective-permute-start.1) | collective-permute-done | bytes 524320 | tf_op jit(solution)/shard_map/ppermute | solution.py:458
  19.4 1.3 %collective-permute-start.5 = (bf16[256,1024]{1,0:T(8,128)(2,1)S(1)}, bf16[256,1024]{1,0:T(8,128)(2,1)S(1)}, u32[]{:S(2)}, u32[]{:S(2)}) collective-permute-start(bf16[256,1024]{1,0:T(8,128)(2,1)S(1)} %get-tuple-element.27.refs_2_), channel_id=1, source_target_pairs={{1,0},{2,1},{5,4},{6,5},{9,8},{10,9},{13,12},{14,13},{17,16},{18,1... | collective-permute-start | bytes 1572872 | tf_op jit(solution)/shard_map/ppermute | solution.py:458
  20.7 6.4 %collective-permute-start.2 = (bf16[256,1024]{1,0:T(8,128)(2,1)S(1)}, bf16[256,1024]{1,0:T(8,128)(2,1)S(1)}, u32[]{:S(2)}, u32[]{:S(2)}) collective-permute-start(bf16[256,1024]{1,0:T(8,128)(2,1)S(1)} %shard_map.75.refs_0_), channel_id=1, source_target_pairs={{0,1},{1,2},{2,3},{4,5},{5,6},{6,7},{8,9},{9,10},{10,11},{12,13},{... | collective-permute-start | bytes 1572872 | tf_op jit(solution)/shard_map/ppermute | solution.py:458
  27.1 1.3 %collective-permute-start.3 = (bf16[256,1024]{1,0:T(8,128)(2,1)S(1)}, bf16[256,1024]{1,0:T(8,128)(2,1)S(1)}, u32[]{:S(2)}, u32[]{:S(2)}) collective-permute-start(bf16[256,1024]{1,0:T(8,128)(2,1)S(1)} %shard_map.75.refs_0_), channel_id=1, source_target_pairs={{1,0},{2,1},{3,2},{5,4},{6,5},{7,6},{9,8},{10,9},{11,10},{13,12},{... | collective-permute-start | bytes 1572872 | tf_op jit(solution)/shard_map/ppermute | solution.py:458
  29.1 6.1 %collective-permute-done.5.refs_3_.refs_4_ = bf16[256,1024]{1,0:T(8,128)(2,1)S(1)} collective-permute-done((bf16[256,1024]{1,0:T(8,128)(2,1)S(1)}, bf16[256,1024]{1,0:T(8,128)(2,1)S(1)}, u32[]{:S(2)}, u32[]{:S(2)}) %collective-permute-start.5) | collective-permute-done | bytes 524320 | tf_op jit(solution)/shard_map/ppermute | solution.py:458
  35.2 1.3 %collective-permute-start.9 = (bf16[256,1024]{1,0:T(8,128)(2,1)S(1)}, bf16[256,1024]{1,0:T(8,128)(2,1)S(1)}, u32[]{:S(2)}, u32[]{:S(2)}) collective-permute-start(bf16[256,1024]{1,0:T(8,128)(2,1)S(1)} %collective-permute-done.5.refs_3_.refs_4_), channel_id=1, source_target_pairs={{1,0},{5,4},{9,8},{13,12},{17,16},{21,20},{25,24},{29,28}} | collective-permute-start | bytes 1572872 | tf_op jit(solution)/shard_map/ppermute | solution.py:458
  36.5 9.9 %collective-permute-done.3.refs_1_ = bf16[256,1024]{1,0:T(8,128)(2,1)S(1)} collective-permute-done((bf16[256,1024]{1,0:T(8,128)(2,1)S(1)}, bf16[256,1024]{1,0:T(8,128)(2,1)S(1)}, u32[]{:S(2)}, u32[]{:S(2)}) %collective-permute-start.3) | collective-permute-done | bytes 524320 | tf_op jit(solution)/shard_map/ppermute | solution.py:458
  47.1 1.3 %collective-permute-start.7 = (bf16[256,1024]{1,0:T(8,128)(2,1)S(1)}, bf16[256,1024]{1,0:T(8,128)(2,1)S(1)}, u32[]{:S(2)}, u32[]{:S(2)}) collective-permute-start(bf16[256,1024]{1,0:T(8,128)(2,1)S(1)} %get-tuple-element.29.refs_2_), channel_id=1, source_target_pairs={{1,0},{2,1},{5,4},{6,5},{9,8},{10,9},{13,12},{14,13},{17,16},{18,1... | collective-permute-start | bytes 1572872 | tf_op jit(solution)/shard_map/ppermute | solution.py:458
  48.4 2.3 %shard_map.77.refs_4_ = f32[256,1024]{1,0:T(8,128)S(1)} custom-call(s32[2,8]{1,0:T(2,128)S(4)} %get-tuple-element.20.facts_ref, bf16[256,1024]{1,0:T(8,128)(2,1)S(1)} %slice_bitcast_fusion.refs_0_, bf16[256,1024]{1,0:T(8,128)(2,1)S(1)} %get-tuple-element.26.refs_1_, bf16[256,1024]{1,0:T(8,128)(2,1)S(1)} %get-tuple-element.27.refs_2_, ...), custom_call_target="tpu_custom_call" | custom-call | flops 1610612736 | bytes 13107200 | tf_op jit(solution)/shard_map/pallas_call | solution.py:218
  50.7 7.0 %collective-permute-done.9.refs_1_ = bf16[256,1024]{1,0:T(8,128)(2,1)S(1)} collective-permute-done((bf16[256,1024]{1,0:T(8,128)(2,1)S(1)}, bf16[256,1024]{1,0:T(8,128)(2,1)S(1)}, u32[]{:S(2)}, u32[]{:S(2)}) %collective-permute-start.9) | collective-permute-done | bytes 524320 | tf_op jit(solution)/shard_map/ppermute | solution.py:458
  57.6 0.9 shard_map.78.refs_2_.refs_0_.refs_1_
  58.6 5.2 %collective-permute-start.10 = (bf16[256,1024]{1,0:T(8,128)(2,1)S(1)}, bf16[256,1024]{1,0:T(8,128)(2,1)S(1)}, u32[]{:S(2)}, u32[]{:S(2)}) collective-permute-start(bf16[256,1024]{1,0:T(8,128)(2,1)S(1)} %shard_map.78.refs_2_.refs_0_.refs_1_), channel_id=1, source_target_pairs={{0,4},{4,0},{8,12},{12,8},{16,20},{20,16},{24,28},{28,24},{1,5},{5... | collective-permute-start | bytes 1572872 | tf_op jit(solution)/shard_map/ppermute | solution.py:427
  63.8 3.1 %collective-permute-start.13 = (bf16[256,1024]{1,0:T(8,128)(2,1)S(1)}, bf16[256,1024]{1,0:T(8,128)(2,1)S(1)}, u32[]{:S(2)}, u32[]{:S(2)}) collective-permute-start(bf16[256,1024]{1,0:T(8,128)(2,1)S(1)} %shard_map.78.refs_2_.refs_0_.refs_1_), channel_id=1, source_target_pairs={{0,8},{4,12},{8,16},{12,20},{16,24},{20,28},{1,9},{5,13},{9,17},{1... | collective-permute-start | bytes 1572872 | tf_op jit(solution)/shard_map/ppermute | solution.py:422
  66.9 2.0 %collective-permute-done.7.refs_1_ = bf16[256,1024]{1,0:T(8,128)(2,1)S(1)} collective-permute-done((bf16[256,1024]{1,0:T(8,128)(2,1)S(1)}, bf16[256,1024]{1,0:T(8,128)(2,1)S(1)}, u32[]{:S(2)}, u32[]{:S(2)}) %collective-permute-start.7) | collective-permute-done | bytes 524320 | tf_op jit(solution)/shard_map/ppermute | solution.py:458
  69.6 1.3 %collective-permute-start.12 = (bf16[256,1024]{1,0:T(8,128)(2,1)S(1)}, bf16[256,1024]{1,0:T(8,128)(2,1)S(1)}, u32[]{:S(2)}, u32[]{:S(2)}) collective-permute-start(bf16[256,1024]{1,0:T(8,128)(2,1)S(1)} %get-tuple-element.33.refs_4_), channel_id=1, source_target_pairs={{1,0},{5,4},{9,8},{13,12},{17,16},{21,20},{25,24},{29,28}} | collective-permute-start | bytes 1572872 | tf_op jit(solution)/shard_map/ppermute | solution.py:458
  70.9 5.8 %collective-permute-start.14 = (bf16[256,1024]{1,0:T(8,128)(2,1)S(1)}, bf16[256,1024]{1,0:T(8,128)(2,1)S(1)}, u32[]{:S(2)}, u32[]{:S(2)}) collective-permute-start(bf16[256,1024]{1,0:T(8,128)(2,1)S(1)} %shard_map.78.refs_2_.refs_0_.refs_1_), channel_id=1, source_target_pairs={{4,16},{12,24},{28,20},{5,17},{13,25},{29,21},{6,18},{14,26},{30,2... | collective-permute-start | bytes 1572872 | tf_op jit(solution)/shard_map/ppermute | solution.py:434
  76.7 2.3 %shard_map.80.refs_4_ = f32[256,1024]{1,0:T(8,128)S(1)} custom-call(s32[2,8]{1,0:T(2,128)S(4)} %get-tuple-element.20.facts_ref, bf16[256,1024]{1,0:T(8,128)(2,1)S(1)} %shard_map.75.refs_0_, bf16[256,1024]{1,0:T(8,128)(2,1)S(1)} %get-tuple-element.28.refs_1_, bf16[256,1024]{1,0:T(8,128)(2,1)S(1)} %get-tuple-element.29.refs_2_, ...), custom_call_target="tpu_custom_call" | custom-call | flops 1610612736 | bytes 13107200 | tf_op jit(solution)/shard_map/pallas_call | solution.py:218
  79.2 2.9 %collective-permute-done.12.refs_1_ = bf16[256,1024]{1,0:T(8,128)(2,1)S(1)} collective-permute-done((bf16[256,1024]{1,0:T(8,128)(2,1)S(1)}, bf16[256,1024]{1,0:T(8,128)(2,1)S(1)}, u32[]{:S(2)}, u32[]{:S(2)}) %collective-permute-start.12) | collective-permute-done | bytes 524320 | tf_op jit(solution)/shard_map/ppermute | solution.py:458
  82.1 1.1 shard_map.81.refs_0_.refs_1_
  83.2 2.2 %collective-permute-start.15 = (bf16[256,1024]{1,0:T(8,128)(2,1)S(1)}, bf16[256,1024]{1,0:T(8,128)(2,1)S(1)}, u32[]{:S(2)}, u32[]{:S(2)}) collective-permute-start(bf16[256,1024]{1,0:T(8,128)(2,1)S(1)} %shard_map.81.refs_0_.refs_1_), channel_id=1, source_target_pairs={{8,0},{12,4},{16,8},{20,12},{24,16},{28,20},{9,1},{13,5},{17,9},{2... | collective-permute-start | bytes 1572872 | tf_op jit(solution)/shard_map/ppermute | solution.py:422
  85.4 5.9 %collective-permute-start.17 = (bf16[256,1024]{1,0:T(8,128)(2,1)S(1)}, bf16[256,1024]{1,0:T(8,128)(2,1)S(1)}, u32[]{:S(2)}, u32[]{:S(2)}) collective-permute-start(bf16[256,1024]{1,0:T(8,128)(2,1)S(1)} %shard_map.81.refs_0_.refs_1_), channel_id=1, source_target_pairs={{4,0},{12,8},{20,16},{28,24},{16,4},{24,12},{5,1},{13,9},{21,17},{... | collective-permute-start | bytes 1572872 | tf_op jit(solution)/shard_map/ppermute | solution.py:443
  91.3 2.3 %shard_map.82.refs_1_.refs_0_ = f32[256,1024]{1,0:T(8,128)S(1)} custom-call(s32[2,8]{1,0:T(2,128)S(4)} %get-tuple-element.20.facts_ref, bf16[512,256]{1,0:T(8,128)(2,1)S(1)} %get-tuple-element.21.table_ref, bf16[512,512]{1,0:T(8,128)(2,1)S(1)} %get-tuple-element.22.back_ref, f32[4,512,1024]{2,1,0:T(8,128)S(1)} %get-tuple-element.23.spec_ref, ...), custom_call_target="tpu_custom_call" | custom-call | flops 2147483648 | bytes 1048576 | tf_op jit(solution)/shard_map/pallas_call | solution.py:368
  93.7 2.3 %shard_map.84.refs_2_.refs_0_ = f32[256,1024]{1,0:T(8,128)S(1)} custom-call(s32[2,8]{1,0:T(2,128)S(4)} %get-tuple-element.20.facts_ref, bf16[512,256]{1,0:T(8,128)(2,1)S(1)} %get-tuple-element.21.table_ref, bf16[512,512]{1,0:T(8,128)(2,1)S(1)} %get-tuple-element.22.back_ref, f32[4,512,1024]{2,1,0:T(8,128)S(1)} %get-tuple-element.23.spec_ref, ...), custom_call_target="tpu_custom_call" | custom-call | flops 2147483648 | bytes 1048576 | tf_op jit(solution)/shard_map/pallas_call | solution.py:368
  96.0 4.5 %collective-permute-start.16 = (bf16[256,1024]{1,0:T(8,128)(2,1)S(1)}, bf16[256,1024]{1,0:T(8,128)(2,1)S(1)}, u32[]{:S(2)}, u32[]{:S(2)}) collective-permute-start(bf16[256,1024]{1,0:T(8,128)(2,1)S(1)} %shard_map.85.refs_5_), channel_id=1, source_target_pairs={{0,4},{4,0},{8,12},{12,8},{16,20},{20,16},{24,28},{28,24},{1,5},{5... | collective-permute-start | bytes 1572872 | tf_op jit(solution)/shard_map/ppermute | solution.py:427
  100.4 3.2 %shard_map.86 = (f32[1,2,256,1024]{3,2,1,0:T(8,128)}, f32[8,128]{1,0:T(8,128)}) custom-call(s32[2,8]{1,0:T(2,128)S(4)} %get-tuple-element.20.facts_ref, bf16[512,256]{1,0:T(8,128)(2,1)S(1)} %get-tuple-element.21.table_ref, bf16[512,512]{1,0:T(8,128)(2,1)S(1)} %get-tuple-element.22.back_ref, f32[4,512,1024]{2,1,0:T(8,128)S(1)} %get-tuple-element.23.spec_ref, ...), custom_call_target="tpu_custom_call" | custom-call | flops 2147483648 | bytes 1048576 | tf_op jit(solution)/shard_map/pallas_call | solution.py:368
  103.7 1.6 %collective-permute-done.17.refs_7_ = bf16[256,1024]{1,0:T(8,128)(2,1)S(1)} collective-permute-done((bf16[256,1024]{1,0:T(8,128)(2,1)S(1)}, bf16[256,1024]{1,0:T(8,128)(2,1)S(1)}, u32[]{:S(2)}, u32[]{:S(2)}) %collective-permute-start.17) | collective-permute-done | bytes 524320 | tf_op jit(solution)/shard_map/ppermute | solution.py:443
  105.3 3.2 %shard_map.87 = f32[1,2,256,1024]{3,2,1,0:T(8,128)} custom-call(s32[2,8]{1,0:T(2,128)S(4)} %get-tuple-element.20.facts_ref, bf16[512,256]{1,0:T(8,128)(2,1)S(1)} %get-tuple-element.21.table_ref, bf16[512,512]{1,0:T(8,128)(2,1)S(1)} %get-tuple-element.22.back_ref, f32[4,512,1024]{2,1,0:T(8,128)S(1)} %get-tuple-element.23.spec_ref, ...), custom_call_target="tpu_custom_call", output_to_operand_aliasing={{}: (12, {})} | custom-call | flops 2147483648 | bytes 1048576 | tf_op jit(solution)/shard_map/pallas_call | solution.py:368
  (22 shorter events, 3.0 us)
Async XLA Ops:
  1.1 13.8 %collective-permute-start = (bf16[256,1024]{1,0:T(8,128)(2,1)S(1)}, bf16[256,1024]{1,0:T(8,128)(2,1)S(1)}, u32[]{:S(2)}, u32[]{:S(2)}) collective-permute-start(bf16[256,1024]{1,0:T(8,128)(2,1)S(1)} %slice_bitcast_fusion.refs_0_), channel_id=1, source_target_pairs={{0,1},{1,2},{2,3},{4,5},{5,6},{6,7},{8,9},{9,10},{10,11},{12,13},{... | collective-permute-start | bytes 1572872 | tf_op jit(solution)/shard_map/ppermute | solution.py:458
  4.3 14.4 %collective-permute-start.1 = (bf16[256,1024]{1,0:T(8,128)(2,1)S(1)}, bf16[256,1024]{1,0:T(8,128)(2,1)S(1)}, u32[]{:S(2)}, u32[]{:S(2)}) collective-permute-start(bf16[256,1024]{1,0:T(8,128)(2,1)S(1)} %slice_bitcast_fusion.refs_0_), channel_id=1, source_target_pairs={{1,0},{2,1},{3,2},{5,4},{6,5},{7,6},{9,8},{10,9},{11,10},{13,12},{... | collective-permute-start | bytes 1572872 | tf_op jit(solution)/shard_map/ppermute | solution.py:458
  18.7 9.7 %collective-permute-start.4 = (bf16[256,1024]{1,0:T(8,128)(2,1)S(1)}, bf16[256,1024]{1,0:T(8,128)(2,1)S(1)}, u32[]{:S(2)}, u32[]{:S(2)}) collective-permute-start(bf16[256,1024]{1,0:T(8,128)(2,1)S(1)} %get-tuple-element.26.refs_1_), channel_id=1, source_target_pairs={{1,2},{2,3},{5,6},{6,7},{9,10},{10,11},{13,14},{14,15},{17,18},{18... | collective-permute-start | bytes 1572872 | tf_op jit(solution)/shard_map/ppermute | solution.py:458
  19.4 15.8 %collective-permute-start.5 = (bf16[256,1024]{1,0:T(8,128)(2,1)S(1)}, bf16[256,1024]{1,0:T(8,128)(2,1)S(1)}, u32[]{:S(2)}, u32[]{:S(2)}) collective-permute-start(bf16[256,1024]{1,0:T(8,128)(2,1)S(1)} %get-tuple-element.27.refs_2_), channel_id=1, source_target_pairs={{1,0},{2,1},{5,4},{6,5},{9,8},{10,9},{13,12},{14,13},{17,16},{18,1... | collective-permute-start | bytes 1572872 | tf_op jit(solution)/shard_map/ppermute | solution.py:458
  20.7 15.8 %collective-permute-start.2 = (bf16[256,1024]{1,0:T(8,128)(2,1)S(1)}, bf16[256,1024]{1,0:T(8,128)(2,1)S(1)}, u32[]{:S(2)}, u32[]{:S(2)}) collective-permute-start(bf16[256,1024]{1,0:T(8,128)(2,1)S(1)} %shard_map.75.refs_0_), channel_id=1, source_target_pairs={{0,1},{1,2},{2,3},{4,5},{5,6},{6,7},{8,9},{9,10},{10,11},{12,13},{... | collective-permute-start | bytes 1572872 | tf_op jit(solution)/shard_map/ppermute | solution.py:458
  27.1 19.3 %collective-permute-start.3 = (bf16[256,1024]{1,0:T(8,128)(2,1)S(1)}, bf16[256,1024]{1,0:T(8,128)(2,1)S(1)}, u32[]{:S(2)}, u32[]{:S(2)}) collective-permute-start(bf16[256,1024]{1,0:T(8,128)(2,1)S(1)} %shard_map.75.refs_0_), channel_id=1, source_target_pairs={{1,0},{2,1},{3,2},{5,4},{6,5},{7,6},{9,8},{10,9},{11,10},{13,12},{... | collective-permute-start | bytes 1572872 | tf_op jit(solution)/shard_map/ppermute | solution.py:458
  28.4 22.3 %collective-permute-start.8 = (bf16[256,1024]{1,0:T(8,128)(2,1)S(1)}, bf16[256,1024]{1,0:T(8,128)(2,1)S(1)}, u32[]{:S(2)}, u32[]{:S(2)}) collective-permute-start(bf16[256,1024]{1,0:T(8,128)(2,1)S(1)} %collective-permute-done.4.refs_2_.refs_3_), channel_id=1, source_target_pairs={{2,3},{6,7},{10,11},{14,15},{18,19},{22,23},{26,27},{30,31}} | collective-permute-start | bytes 1572872 | tf_op jit(solution)/shard_map/ppermute | solution.py:458
  35.2 22.5 %collective-permute-start.9 = (bf16[256,1024]{1,0:T(8,128)(2,1)S(1)}, bf16[256,1024]{1,0:T(8,128)(2,1)S(1)}, u32[]{:S(2)}, u32[]{:S(2)}) collective-permute-start(bf16[256,1024]{1,0:T(8,128)(2,1)S(1)} %collective-permute-done.5.refs_3_.refs_4_), channel_id=1, source_target_pairs={{1,0},{5,4},{9,8},{13,12},{17,16},{21,20},{25,24},{29,28}} | collective-permute-start | bytes 1572872 | tf_op jit(solution)/shard_map/ppermute | solution.py:458
  46.4 20.5 %collective-permute-start.6 = (bf16[256,1024]{1,0:T(8,128)(2,1)S(1)}, bf16[256,1024]{1,0:T(8,128)(2,1)S(1)}, u32[]{:S(2)}, u32[]{:S(2)}) collective-permute-start(bf16[256,1024]{1,0:T(8,128)(2,1)S(1)} %get-tuple-element.28.refs_1_), channel_id=1, source_target_pairs={{1,2},{2,3},{5,6},{6,7},{9,10},{10,11},{13,14},{14,15},{17,18},{18... | collective-permute-start | bytes 1572872 | tf_op jit(solution)/shard_map/ppermute | solution.py:458
  47.1 21.8 %collective-permute-start.7 = (bf16[256,1024]{1,0:T(8,128)(2,1)S(1)}, bf16[256,1024]{1,0:T(8,128)(2,1)S(1)}, u32[]{:S(2)}, u32[]{:S(2)}) collective-permute-start(bf16[256,1024]{1,0:T(8,128)(2,1)S(1)} %get-tuple-element.29.refs_2_), channel_id=1, source_target_pairs={{1,0},{2,1},{5,4},{6,5},{9,8},{10,9},{13,12},{14,13},{17,16},{18,1... | collective-permute-start | bytes 1572872 | tf_op jit(solution)/shard_map/ppermute | solution.py:458
  58.6 10.3 %collective-permute-start.10 = (bf16[256,1024]{1,0:T(8,128)(2,1)S(1)}, bf16[256,1024]{1,0:T(8,128)(2,1)S(1)}, u32[]{:S(2)}, u32[]{:S(2)}) collective-permute-start(bf16[256,1024]{1,0:T(8,128)(2,1)S(1)} %shard_map.78.refs_2_.refs_0_.refs_1_), channel_id=1, source_target_pairs={{0,4},{4,0},{8,12},{12,8},{16,20},{20,16},{24,28},{28,24},{1,5},{5... | collective-permute-start | bytes 1572872 | tf_op jit(solution)/shard_map/ppermute | solution.py:427
  63.8 15.4 %collective-permute-start.13 = (bf16[256,1024]{1,0:T(8,128)(2,1)S(1)}, bf16[256,1024]{1,0:T(8,128)(2,1)S(1)}, u32[]{:S(2)}, u32[]{:S(2)}) collective-permute-start(bf16[256,1024]{1,0:T(8,128)(2,1)S(1)} %shard_map.78.refs_2_.refs_0_.refs_1_), channel_id=1, source_target_pairs={{0,8},{4,12},{8,16},{12,20},{16,24},{20,28},{1,9},{5,13},{9,17},{1... | collective-permute-start | bytes 1572872 | tf_op jit(solution)/shard_map/ppermute | solution.py:422
  68.9 10.3 %collective-permute-start.11 = (bf16[256,1024]{1,0:T(8,128)(2,1)S(1)}, bf16[256,1024]{1,0:T(8,128)(2,1)S(1)}, u32[]{:S(2)}, u32[]{:S(2)}) collective-permute-start(bf16[256,1024]{1,0:T(8,128)(2,1)S(1)} %get-tuple-element.32.refs_3_), channel_id=1, source_target_pairs={{2,3},{6,7},{10,11},{14,15},{18,19},{22,23},{26,27},{30,31}} | collective-permute-start | bytes 1572872 | tf_op jit(solution)/shard_map/ppermute | solution.py:458
  69.6 12.5 %collective-permute-start.12 = (bf16[256,1024]{1,0:T(8,128)(2,1)S(1)}, bf16[256,1024]{1,0:T(8,128)(2,1)S(1)}, u32[]{:S(2)}, u32[]{:S(2)}) collective-permute-start(bf16[256,1024]{1,0:T(8,128)(2,1)S(1)} %get-tuple-element.33.refs_4_), channel_id=1, source_target_pairs={{1,0},{5,4},{9,8},{13,12},{17,16},{21,20},{25,24},{29,28}} | collective-permute-start | bytes 1572872 | tf_op jit(solution)/shard_map/ppermute | solution.py:458
  70.9 20.4 %collective-permute-start.14 = (bf16[256,1024]{1,0:T(8,128)(2,1)S(1)}, bf16[256,1024]{1,0:T(8,128)(2,1)S(1)}, u32[]{:S(2)}, u32[]{:S(2)}) collective-permute-start(bf16[256,1024]{1,0:T(8,128)(2,1)S(1)} %shard_map.78.refs_2_.refs_0_.refs_1_), channel_id=1, source_target_pairs={{4,16},{12,24},{28,20},{5,17},{13,25},{29,21},{6,18},{14,26},{30,2... | collective-permute-start | bytes 1572872 | tf_op jit(solution)/shard_map/ppermute | solution.py:434
  83.2 12.8 %collective-permute-start.15 = (bf16[256,1024]{1,0:T(8,128)(2,1)S(1)}, bf16[256,1024]{1,0:T(8,128)(2,1)S(1)}, u32[]{:S(2)}, u32[]{:S(2)}) collective-permute-start(bf16[256,1024]{1,0:T(8,128)(2,1)S(1)} %shard_map.81.refs_0_.refs_1_), channel_id=1, source_target_pairs={{8,0},{12,4},{16,8},{20,12},{24,16},{28,20},{9,1},{13,5},{17,9},{2... | collective-permute-start | bytes 1572872 | tf_op jit(solution)/shard_map/ppermute | solution.py:422
  85.4 19.9 %collective-permute-start.17 = (bf16[256,1024]{1,0:T(8,128)(2,1)S(1)}, bf16[256,1024]{1,0:T(8,128)(2,1)S(1)}, u32[]{:S(2)}, u32[]{:S(2)}) collective-permute-start(bf16[256,1024]{1,0:T(8,128)(2,1)S(1)} %shard_map.81.refs_0_.refs_1_), channel_id=1, source_target_pairs={{4,0},{12,8},{20,16},{28,24},{16,4},{24,12},{5,1},{13,9},{21,17},{... | collective-permute-start | bytes 1572872 | tf_op jit(solution)/shard_map/ppermute | solution.py:443
  93.6 6.9 %collective-permute-start.18 = (bf16[256,1024]{1,0:T(8,128)(2,1)S(1)}, bf16[256,1024]{1,0:T(8,128)(2,1)S(1)}, u32[]{:S(2)}, u32[]{:S(2)}) collective-permute-start(bf16[256,1024]{1,0:T(8,128)(2,1)S(1)} %shard_map.83.refs_1_.refs_3_), channel_id=1, source_target_pairs={{0,4},{4,0},{8,12},{12,8},{16,20},{20,16},{24,28},{28,24},{1,5},{5... | collective-permute-start | bytes 1572872 | tf_op jit(solution)/shard_map/ppermute | solution.py:427
  96.0 9.3 %collective-permute-start.16 = (bf16[256,1024]{1,0:T(8,128)(2,1)S(1)}, bf16[256,1024]{1,0:T(8,128)(2,1)S(1)}, u32[]{:S(2)}, u32[]{:S(2)}) collective-permute-start(bf16[256,1024]{1,0:T(8,128)(2,1)S(1)} %shard_map.85.refs_5_), channel_id=1, source_target_pairs={{0,4},{4,0},{8,12},{12,8},{16,20},{20,16},{24,28},{28,24},{1,5},{5... | collective-permute-start | bytes 1572872 | tf_op jit(solution)/shard_map/ppermute | solution.py:427

commit v20 on v14

--- a/solution.py
+++ b/solution.py
@@ -11,7 +11,7 @@
 from jax.sharding import PartitionSpec as P
 
 REACH = 3
-LANES = 512
+LANES = 1024
 VMEM = 20 * 1024 * 1024
 F32 = jnp.float32
 BF16 = jnp.bfloat16

time: 108 us -> 106 us (0.981); the launches traced: 106 us -> 106 us
  Pallas kernels: 23.1 us -> 20.9 us
  starting transfers between devices: 35.9 us -> 37.3 us
    pallas_call x4, Pallas kernels: 11 us -> 8.45 us  [conv_call(): pl.pallas_call(body, grid=(width // LANES,), out_shape=out_shape, in_spec...]
    ppermute x1, starting transfers between devices: 3.34 us -> 5.11 us  [lower_halo_of(): mixed = lax.ppermute(value, 'ctx', mixed)]
    ppermute x2, starting transfers between devices: 7.05 us -> 5.37 us  [shifted(): lax.ppermute(value, 'ctx', [(source, source + steps) for source in range(...]
    ppermute x3, starting transfers between devices: 6.28 us -> 7.58 us  [core_swapped(): lax.ppermute(value, 'ctx', [(source, source ^ 1) for source in range(coun...]
  transfers between devices with their start and end apart: 19 -> 19, of which waited for: 8 -> 9; matrix products, arithmetic and copies ran while one was open for 0% -> 0% of each run, Pallas kernels for 19% -> 17%
where the time goes in v20:
time: 106 us
  waiting for transfers between devices  46.1 us (43%)
  starting transfers between devices  37.3 us (35%)
  Pallas kernels  20.9 us (20%)
  local copies, waits for them, and re-layouts  1.08 us (1%)
    ppermute x12, waiting for transfers between devices, sent(): return (lax.ppermute(up, 'ch', upward), lax.ppermute(down, 'ch', downward))  39.2 us
    ppermute x12, starting transfers between devices, sent(): return (lax.ppermute(up, 'ch', upward), lax.ppermute(down, 'ch', downward))  17.9 us
    pallas_call x4, Pallas kernels, conv_call(): pl.pallas_call(body, grid=(width // LANES,), out_shape=out_shape, in_spec...  8.45 us
    ppermute x3, starting transfers between devices, core_swapped(): lax.ppermute(value, 'ctx', [(source, source ^ 1) for source in range(coun...  7.58 us
    pallas_call x4, Pallas kernels, project(): pl.pallas_call(functools.partial(project_kernel, hops, slot, before is No...  6.49 us
    pallas_call x1, Pallas kernels, prepare(): pl.pallas_call(functools.partial(prepare_kernel, pairs), grid=(width // L...  6 us
    ppermute x2, starting transfers between devices, shifted(): lax.ppermute(value, 'ctx', [(source, source + steps) for source in range(...  5.37 us
    ppermute x1, starting transfers between devices, lower_halo_of(): mixed = lax.ppermute(value, 'ctx', mixed)  5.11 us
  transfers between devices with their start and end apart: 19, of which 9 were waited for; matrix products, arithmetic and copies ran while one was open for 0% of the time, Pallas kernels for 17%

profile of v20, /device:TPU:3, one launch (start us, length us, event | category | flops | bytes accessed | tf_op | source)
XLA Modules:
  0.0 105.7 jit_solution(11662322257870623426)
XLA Ops:
  0.0 1.1 %slice_bitcast_fusion.refs_0_ = bf16[256,1024]{1,0:T(8,128)(2,1)S(1)} fusion(bf16[1,2,256,1024]{3,2,1,0:T(8,128)(2,1)} %refs_8_.1), kind=kLoop, calls=%fused_computation | loop fusion | bytes 1048576 | tf_op jit(solution)/shard_map/squeeze | solution.py:456
  1.1 3.2 %collective-permute-start = (bf16[256,1024]{1,0:T(8,128)(2,1)S(1)}, bf16[256,1024]{1,0:T(8,128)(2,1)S(1)}, u32[]{:S(2)}, u32[]{:S(2)}) collective-permute-start(bf16[256,1024]{1,0:T(8,128)(2,1)S(1)} %slice_bitcast_fusion.refs_0_), channel_id=1, source_target_pairs={{0,1},{1,2},{2,3},{4,5},{5,6},{6,7},{8,9},{9,10},{10,11},{12,13},{... | collective-permute-start | bytes 1572872 | tf_op jit(solution)/shard_map/ppermute | solution.py:454
  4.3 1.3 %collective-permute-start.1 = (bf16[256,1024]{1,0:T(8,128)(2,1)S(1)}, bf16[256,1024]{1,0:T(8,128)(2,1)S(1)}, u32[]{:S(2)}, u32[]{:S(2)}) collective-permute-start(bf16[256,1024]{1,0:T(8,128)(2,1)S(1)} %slice_bitcast_fusion.refs_0_), channel_id=1, source_target_pairs={{1,0},{2,1},{3,2},{5,4},{6,5},{7,6},{9,8},{10,9},{11,10},{13,12},{... | collective-permute-start | bytes 1572872 | tf_op jit(solution)/shard_map/ppermute | solution.py:454
  5.6 6.0 %shard_map.73 = (f32[4,512,1024]{2,1,0:T(8,128)S(1)}, bf16[1024,4096]{1,0:T(8,128)(2,1)S(1)}, bf16[1,2,256,1024]{3,2,1,0:T(8,128)(2,1)S(1)}, bf16[256,1024]{1,0:...) custom-call(s32[1]{0:T(128)} %bitcast.refs_0_, ...), custom_call_target="tpu_custom_call" | custom-call | flops 2415919104 | bytes 11534336 | tf_op jit(solution)/shard_map/pallas_call | solution.py:147
  11.6 3.2 %collective-permute-done.refs_0_ = bf16[256,1024]{1,0:T(8,128)(2,1)S(1)} collective-permute-done((bf16[256,1024]{1,0:T(8,128)(2,1)S(1)}, bf16[256,1024]{1,0:T(8,128)(2,1)S(1)}, u32[]{:S(2)}, u32[]{:S(2)}) %collective-permute-start) | collective-permute-done | bytes 524320 | tf_op jit(solution)/shard_map/ppermute | solution.py:454
  15.6 3.1 %collective-permute-done.1.refs_0_ = bf16[256,1024]{1,0:T(8,128)(2,1)S(1)} collective-permute-done((bf16[256,1024]{1,0:T(8,128)(2,1)S(1)}, bf16[256,1024]{1,0:T(8,128)(2,1)S(1)}, u32[]{:S(2)}, u32[]{:S(2)}) %collective-permute-start.1) | collective-permute-done | bytes 524320 | tf_op jit(solution)/shard_map/ppermute | solution.py:454
  18.7 1.3 %collective-permute-start.4 = (bf16[256,1024]{1,0:T(8,128)(2,1)S(1)}, bf16[256,1024]{1,0:T(8,128)(2,1)S(1)}, u32[]{:S(2)}, u32[]{:S(2)}) collective-permute-start(bf16[256,1024]{1,0:T(8,128)(2,1)S(1)} %shard_map.75.refs_2_), channel_id=1, source_target_pairs={{1,0},{2,1},{5,4},{6,5},{9,8},{10,9},{13,12},{14,13},{17,16},{18,1... | collective-permute-start | bytes 1572872 | tf_op jit(solution)/shard_map/ppermute | solution.py:454
  20.0 4.2 %collective-permute-start.2 = (bf16[256,1024]{1,0:T(8,128)(2,1)S(1)}, bf16[256,1024]{1,0:T(8,128)(2,1)S(1)}, u32[]{:S(2)}, u32[]{:S(2)}) collective-permute-start(bf16[256,1024]{1,0:T(8,128)(2,1)S(1)} %shard_map.76.refs_0_), channel_id=1, source_target_pairs={{0,1},{1,2},{2,3},{4,5},{5,6},{6,7},{8,9},{9,10},{10,11},{12,13},{... | collective-permute-start | bytes 1572872 | tf_op jit(solution)/shard_map/ppermute | solution.py:454
  24.2 1.3 %collective-permute-start.9 = (bf16[256,1024]{1,0:T(8,128)(2,1)S(1)}, bf16[256,1024]{1,0:T(8,128)(2,1)S(1)}, u32[]{:S(2)}, u32[]{:S(2)}) collective-permute-start(bf16[256,1024]{1,0:T(8,128)(2,1)S(1)} %shard_map.76.refs_0_), channel_id=1, source_target_pairs={{1,0},{2,1},{3,2},{5,4},{6,5},{7,6},{9,8},{10,9},{11,10},{13,12},{... | collective-permute-start | bytes 1572872 | tf_op jit(solution)/shard_map/ppermute | solution.py:454
  26.2 6.3 %collective-permute-done.4.refs_2_.refs_4_ = bf16[256,1024]{1,0:T(8,128)(2,1)S(1)} collective-permute-done((bf16[256,1024]{1,0:T(8,128)(2,1)S(1)}, bf16[256,1024]{1,0:T(8,128)(2,1)S(1)}, u32[]{:S(2)}, u32[]{:S(2)}) %collective-permute-start.4) | collective-permute-done | bytes 524320 | tf_op jit(solution)/shard_map/ppermute | solution.py:454
  32.5 1.3 %collective-permute-start.7 = (bf16[256,1024]{1,0:T(8,128)(2,1)S(1)}, bf16[256,1024]{1,0:T(8,128)(2,1)S(1)}, u32[]{:S(2)}, u32[]{:S(2)}) collective-permute-start(bf16[256,1024]{1,0:T(8,128)(2,1)S(1)} %collective-permute-done.4.refs_2_.refs_4_), channel_id=1, source_target_pairs={{1,0},{5,4},{9,8},{13,12},{17,16},{21,20},{25,24},{29,28}} | collective-permute-start | bytes 1572872 | tf_op jit(solution)/shard_map/ppermute | solution.py:454
  34.5 9.2 %collective-permute-done.9.refs_0_ = bf16[256,1024]{1,0:T(8,128)(2,1)S(1)} collective-permute-done((bf16[256,1024]{1,0:T(8,128)(2,1)S(1)}, bf16[256,1024]{1,0:T(8,128)(2,1)S(1)}, u32[]{:S(2)}, u32[]{:S(2)}) %collective-permute-start.9) | collective-permute-done | bytes 524320 | tf_op jit(solution)/shard_map/ppermute | solution.py:454
  43.7 1.3 %collective-permute-start.10 = (bf16[256,1024]{1,0:T(8,128)(2,1)S(1)}, bf16[256,1024]{1,0:T(8,128)(2,1)S(1)}, u32[]{:S(2)}, u32[]{:S(2)}) collective-permute-start(bf16[256,1024]{1,0:T(8,128)(2,1)S(1)} %shard_map.81.refs_2_), channel_id=1, source_target_pairs={{1,0},{2,1},{5,4},{6,5},{9,8},{10,9},{13,12},{14,13},{17,16},{18,1... | collective-permute-start | bytes 1572872 | tf_op jit(solution)/shard_map/ppermute | solution.py:454
  45.0 2.3 %shard_map.78.refs_4_ = f32[256,1024]{1,0:T(8,128)S(1)} custom-call(s32[2,8]{1,0:T(2,128)S(4)} %get-tuple-element.14.facts_ref, bf16[256,1024]{1,0:T(8,128)(2,1)S(1)} %slice_bitcast_fusion.refs_0_, bf16[256,1024]{1,0:T(8,128)(2,1)S(1)} %shard_map.74.refs_1_, bf16[256,1024]{1,0:T(8,128)(2,1)S(1)} %shard_map.75.refs_2_, ...), custom_call_target="tpu_custom_call" | custom-call | flops 1610612736 | bytes 13107200 | tf_op jit(solution)/shard_map/pallas_call | solution.py:218
  47.3 7.7 %collective-permute-done.7.refs_1_ = bf16[256,1024]{1,0:T(8,128)(2,1)S(1)} collective-permute-done((bf16[256,1024]{1,0:T(8,128)(2,1)S(1)}, bf16[256,1024]{1,0:T(8,128)(2,1)S(1)}, u32[]{:S(2)}, u32[]{:S(2)}) %collective-permute-start.7) | collective-permute-done | bytes 524320 | tf_op jit(solution)/shard_map/ppermute | solution.py:454
  55.0 0.9 shard_map.79.refs_1_.refs_0_
  56.6 9.6 %collective-permute-done.10.refs_0_ = bf16[256,1024]{1,0:T(8,128)(2,1)S(1)} collective-permute-done((bf16[256,1024]{1,0:T(8,128)(2,1)S(1)}, bf16[256,1024]{1,0:T(8,128)(2,1)S(1)}, u32[]{:S(2)}, u32[]{:S(2)}) %collective-permute-start.10) | collective-permute-done | bytes 524320 | tf_op jit(solution)/shard_map/ppermute | solution.py:454
  66.2 1.3 %collective-permute-start.11 = (bf16[256,1024]{1,0:T(8,128)(2,1)S(1)}, bf16[256,1024]{1,0:T(8,128)(2,1)S(1)}, u32[]{:S(2)}, u32[]{:S(2)}) collective-permute-start(bf16[256,1024]{1,0:T(8,128)(2,1)S(1)} %shard_map.82.refs_4_), channel_id=1, source_target_pairs={{1,0},{5,4},{9,8},{13,12},{17,16},{21,20},{25,24},{29,28}} | collective-permute-start | bytes 1572872 | tf_op jit(solution)/shard_map/ppermute | solution.py:454
  67.5 3.1 %collective-permute-start.12 = (bf16[256,1024]{1,0:T(8,128)(2,1)S(1)}, bf16[256,1024]{1,0:T(8,128)(2,1)S(1)}, u32[]{:S(2)}, u32[]{:S(2)}) collective-permute-start(bf16[256,1024]{1,0:T(8,128)(2,1)S(1)} %shard_map.79.refs_1_.refs_0_), channel_id=1, source_target_pairs={{0,8},{4,12},{8,16},{12,20},{16,24},{20,28},{1,9},{5,13},{9,17},{1... | collective-permute-start | bytes 1572872 | tf_op jit(solution)/shard_map/ppermute | solution.py:418
  70.6 3.0 %collective-permute-start.13 = (bf16[256,1024]{1,0:T(8,128)(2,1)S(1)}, bf16[256,1024]{1,0:T(8,128)(2,1)S(1)}, u32[]{:S(2)}, u32[]{:S(2)}) collective-permute-start(bf16[256,1024]{1,0:T(8,128)(2,1)S(1)} %shard_map.79.refs_1_.refs_0_), channel_id=1, source_target_pairs={{0,4},{4,0},{8,12},{12,8},{16,20},{20,16},{24,28},{28,24},{1,5},{5... | collective-permute-start | bytes 1572872 | tf_op jit(solution)/shard_map/ppermute | solution.py:423
  73.6 1.3 %collective-permute-start.14 = (bf16[256,1024]{1,0:T(8,128)(2,1)S(1)}, bf16[256,1024]{1,0:T(8,128)(2,1)S(1)}, u32[]{:S(2)}, u32[]{:S(2)}) collective-permute-start(bf16[256,1024]{1,0:T(8,128)(2,1)S(1)} %shard_map.79.refs_1_.refs_0_), channel_id=1, source_target_pairs={{4,16},{12,24},{28,20},{5,17},{13,25},{29,21},{6,18},{14,26},{30,2... | collective-permute-start | bytes 1572872 | tf_op jit(solution)/shard_map/ppermute | solution.py:430
  74.9 2.3 %shard_map.83.refs_7_.refs_0_ = f32[256,1024]{1,0:T(8,128)S(1)} custom-call(s32[2,8]{1,0:T(2,128)S(4)} %get-tuple-element.14.facts_ref, bf16[512,256]{1,0:T(8,128)(2,1)S(1)} %get-tuple-element.15.table_ref, bf16[512,512]{1,0:T(8,128)(2,1)S(1)} %get-tuple-element.16.back_ref, f32[4,512,1024]{2,1,0:T(8,128)S(1)} %get-tuple-element.17.spec_ref, ...), custom_call_target="tpu_custom_call" | custom-call | flops 2147483648 | bytes 1048576 | tf_op jit(solution)/shard_map/pallas_call | solution.py:368
  77.2 2.4 %shard_map.84.refs_4_ = f32[256,1024]{1,0:T(8,128)S(1)} custom-call(s32[2,8]{1,0:T(2,128)S(4)} %get-tuple-element.14.facts_ref, bf16[256,1024]{1,0:T(8,128)(2,1)S(1)} %shard_map.76.refs_0_, bf16[256,1024]{1,0:T(8,128)(2,1)S(1)} %shard_map.77.refs_1_, bf16[256,1024]{1,0:T(8,128)(2,1)S(1)} %shard_map.81.refs_2_, bf16[256,1024]{1,0:T(8,128)(2,1)S(1)} %shard_map.80.refs_3_, ...), custom_call_target="tpu_custom_call" | custom-call | flops 1610612736 | bytes 13107200 | tf_op jit(solution)/shard_map/pallas_call | solution.py:218
  80.2 0.9 shard_map.85.refs_0_
  81.1 2.3 %collective-permute-start.15 = (bf16[256,1024]{1,0:T(8,128)(2,1)S(1)}, bf16[256,1024]{1,0:T(8,128)(2,1)S(1)}, u32[]{:S(2)}, u32[]{:S(2)}) collective-permute-start(bf16[256,1024]{1,0:T(8,128)(2,1)S(1)} %shard_map.85.refs_0_), channel_id=1, source_target_pairs={{8,0},{12,4},{16,8},{20,12},{24,16},{28,20},{9,1},{13,5},{17,9},{2... | collective-permute-start | bytes 1572872 | tf_op jit(solution)/shard_map/ppermute | solution.py:418
  83.4 5.1 %collective-permute-start.17 = (bf16[256,1024]{1,0:T(8,128)(2,1)S(1)}, bf16[256,1024]{1,0:T(8,128)(2,1)S(1)}, u32[]{:S(2)}, u32[]{:S(2)}) collective-permute-start(bf16[256,1024]{1,0:T(8,128)(2,1)S(1)} %shard_map.85.refs_0_), channel_id=1, source_target_pairs={{4,0},{12,8},{20,16},{28,24},{16,4},{24,12},{5,1},{13,9},{21,17},{... | collective-permute-start | bytes 1572872 | tf_op jit(solution)/shard_map/ppermute | solution.py:439
  88.6 1.1 %shard_map.86.refs_1_.refs_0_ = f32[256,1024]{1,0:T(8,128)S(1)} custom-call(s32[2,8]{1,0:T(2,128)S(4)} %get-tuple-element.14.facts_ref, bf16[512,256]{1,0:T(8,128)(2,1)S(1)} %get-tuple-element.15.table_ref, bf16[512,512]{1,0:T(8,128)(2,1)S(1)} %get-tuple-element.16.back_ref, f32[4,512,1024]{2,1,0:T(8,128)S(1)} %get-tuple-element.17.spec_ref, ...), custom_call_target="tpu_custom_call" | custom-call | flops 2147483648 | bytes 1048576 | tf_op jit(solution)/shard_map/pallas_call | solution.py:368
  89.7 4.1 %collective-permute-done.15.refs_0_ = bf16[256,1024]{1,0:T(8,128)(2,1)S(1)} collective-permute-done((bf16[256,1024]{1,0:T(8,128)(2,1)S(1)}, bf16[256,1024]{1,0:T(8,128)(2,1)S(1)}, u32[]{:S(2)}, u32[]{:S(2)}) %collective-permute-start.15) | collective-permute-done | bytes 524320 | tf_op jit(solution)/shard_map/ppermute | solution.py:418
  93.8 4.6 %collective-permute-start.16 = (bf16[256,1024]{1,0:T(8,128)(2,1)S(1)}, bf16[256,1024]{1,0:T(8,128)(2,1)S(1)}, u32[]{:S(2)}, u32[]{:S(2)}) collective-permute-start(bf16[256,1024]{1,0:T(8,128)(2,1)S(1)} %shard_map.87.refs_5_), channel_id=1, source_target_pairs={{0,4},{4,0},{8,12},{12,8},{16,20},{20,16},{24,28},{28,24},{1,5},{5... | collective-permute-start | bytes 1572872 | tf_op jit(solution)/shard_map/ppermute | solution.py:423
  98.3 2.5 %shard_map.88 = (f32[1,2,256,1024]{3,2,1,0:T(8,128)}, f32[8,128]{1,0:T(8,128)}) custom-call(s32[2,8]{1,0:T(2,128)S(4)} %get-tuple-element.14.facts_ref, bf16[512,256]{1,0:T(8,128)(2,1)S(1)} %get-tuple-element.15.table_ref, bf16[512,512]{1,0:T(8,128)(2,1)S(1)} %get-tuple-element.16.back_ref, f32[4,512,1024]{2,1,0:T(8,128)S(1)} %get-tuple-element.17.spec_ref, ...), custom_call_target="tpu_custom_call" | custom-call | flops 2147483648 | bytes 1048576 | tf_op jit(solution)/shard_map/pallas_call | solution.py:368
  100.9 2.3 %collective-permute-done.17.refs_7_ = bf16[256,1024]{1,0:T(8,128)(2,1)S(1)} collective-permute-done((bf16[256,1024]{1,0:T(8,128)(2,1)S(1)}, bf16[256,1024]{1,0:T(8,128)(2,1)S(1)}, u32[]{:S(2)}, u32[]{:S(2)}) %collective-permute-start.17) | collective-permute-done | bytes 524320 | tf_op jit(solution)/shard_map/ppermute | solution.py:439
  103.2 2.5 %shard_map.89 = f32[1,2,256,1024]{3,2,1,0:T(8,128)} custom-call(s32[2,8]{1,0:T(2,128)S(4)} %get-tuple-element.14.facts_ref, bf16[512,256]{1,0:T(8,128)(2,1)S(1)} %get-tuple-element.15.table_ref, bf16[512,512]{1,0:T(8,128)(2,1)S(1)} %get-tuple-element.16.back_ref, f32[4,512,1024]{2,1,0:T(8,128)S(1)} %get-tuple-element.17.spec_ref, ...), custom_call_target="tpu_custom_call", output_to_operand_aliasing={{}: (12, {})} | custom-call | flops 2147483648 | bytes 1048576 | tf_op jit(solution)/shard_map/pallas_call | solution.py:368
  (24 shorter events, 3.4 us)
Async XLA Ops:
  1.1 13.8 %collective-permute-start = (bf16[256,1024]{1,0:T(8,128)(2,1)S(1)}, bf16[256,1024]{1,0:T(8,128)(2,1)S(1)}, u32[]{:S(2)}, u32[]{:S(2)}) collective-permute-start(bf16[256,1024]{1,0:T(8,128)(2,1)S(1)} %slice_bitcast_fusion.refs_0_), channel_id=1, source_target_pairs={{0,1},{1,2},{2,3},{4,5},{5,6},{6,7},{8,9},{9,10},{10,11},{12,13},{... | collective-permute-start | bytes 1572872 | tf_op jit(solution)/shard_map/ppermute | solution.py:454
  4.3 14.4 %collective-permute-start.1 = (bf16[256,1024]{1,0:T(8,128)(2,1)S(1)}, bf16[256,1024]{1,0:T(8,128)(2,1)S(1)}, u32[]{:S(2)}, u32[]{:S(2)}) collective-permute-start(bf16[256,1024]{1,0:T(8,128)(2,1)S(1)} %slice_bitcast_fusion.refs_0_), channel_id=1, source_target_pairs={{1,0},{2,1},{3,2},{5,4},{6,5},{7,6},{9,8},{10,9},{11,10},{13,12},{... | collective-permute-start | bytes 1572872 | tf_op jit(solution)/shard_map/ppermute | solution.py:454
  14.9 10.6 %collective-permute-start.3 = (bf16[256,1024]{1,0:T(8,128)(2,1)S(1)}, bf16[256,1024]{1,0:T(8,128)(2,1)S(1)}, u32[]{:S(2)}, u32[]{:S(2)}) collective-permute-start(bf16[256,1024]{1,0:T(8,128)(2,1)S(1)} %shard_map.74.refs_1_), channel_id=1, source_target_pairs={{1,2},{2,3},{5,6},{6,7},{9,10},{10,11},{13,14},{14,15},{17,18},{18... | collective-permute-start | bytes 1572872 | tf_op jit(solution)/shard_map/ppermute | solution.py:454
  18.7 13.8 %collective-permute-start.4 = (bf16[256,1024]{1,0:T(8,128)(2,1)S(1)}, bf16[256,1024]{1,0:T(8,128)(2,1)S(1)}, u32[]{:S(2)}, u32[]{:S(2)}) collective-permute-start(bf16[256,1024]{1,0:T(8,128)(2,1)S(1)} %shard_map.75.refs_2_), channel_id=1, source_target_pairs={{1,0},{2,1},{5,4},{6,5},{9,8},{10,9},{13,12},{14,13},{17,16},{18,1... | collective-permute-start | bytes 1572872 | tf_op jit(solution)/shard_map/ppermute | solution.py:454
  20.0 13.8 %collective-permute-start.2 = (bf16[256,1024]{1,0:T(8,128)(2,1)S(1)}, bf16[256,1024]{1,0:T(8,128)(2,1)S(1)}, u32[]{:S(2)}, u32[]{:S(2)}) collective-permute-start(bf16[256,1024]{1,0:T(8,128)(2,1)S(1)} %shard_map.76.refs_0_), channel_id=1, source_target_pairs={{0,1},{1,2},{2,3},{4,5},{5,6},{6,7},{8,9},{9,10},{10,11},{12,13},{... | collective-permute-start | bytes 1572872 | tf_op jit(solution)/shard_map/ppermute | solution.py:454
  24.2 19.5 %collective-permute-start.9 = (bf16[256,1024]{1,0:T(8,128)(2,1)S(1)}, bf16[256,1024]{1,0:T(8,128)(2,1)S(1)}, u32[]{:S(2)}, u32[]{:S(2)}) collective-permute-start(bf16[256,1024]{1,0:T(8,128)(2,1)S(1)} %shard_map.76.refs_0_), channel_id=1, source_target_pairs={{1,0},{2,1},{3,2},{5,4},{6,5},{7,6},{9,8},{10,9},{11,10},{13,12},{... | collective-permute-start | bytes 1572872 | tf_op jit(solution)/shard_map/ppermute | solution.py:454
  25.5 21.8 %collective-permute-start.6 = (bf16[256,1024]{1,0:T(8,128)(2,1)S(1)}, bf16[256,1024]{1,0:T(8,128)(2,1)S(1)}, u32[]{:S(2)}, u32[]{:S(2)}) collective-permute-start(bf16[256,1024]{1,0:T(8,128)(2,1)S(1)} %collective-permute-done.3.refs_1_.refs_3_), channel_id=1, source_target_pairs={{2,3},{6,7},{10,11},{14,15},{18,19},{22,23},{26,27},{30,31}} | collective-permute-start | bytes 1572872 | tf_op jit(solution)/shard_map/ppermute | solution.py:454
  32.5 22.5 %collective-permute-start.7 = (bf16[256,1024]{1,0:T(8,128)(2,1)S(1)}, bf16[256,1024]{1,0:T(8,128)(2,1)S(1)}, u32[]{:S(2)}, u32[]{:S(2)}) collective-permute-start(bf16[256,1024]{1,0:T(8,128)(2,1)S(1)} %collective-permute-done.4.refs_2_.refs_4_), channel_id=1, source_target_pairs={{1,0},{5,4},{9,8},{13,12},{17,16},{21,20},{25,24},{29,28}} | collective-permute-start | bytes 1572872 | tf_op jit(solution)/shard_map/ppermute | solution.py:454
  33.8 22.1 %collective-permute-start.5 = (bf16[256,1024]{1,0:T(8,128)(2,1)S(1)}, bf16[256,1024]{1,0:T(8,128)(2,1)S(1)}, u32[]{:S(2)}, u32[]{:S(2)}) collective-permute-start(bf16[256,1024]{1,0:T(8,128)(2,1)S(1)} %shard_map.77.refs_1_), channel_id=1, source_target_pairs={{1,2},{2,3},{5,6},{6,7},{9,10},{10,11},{13,14},{14,15},{17,18},{18... | collective-permute-start | bytes 1572872 | tf_op jit(solution)/shard_map/ppermute | solution.py:454
  43.7 22.5 %collective-permute-start.10 = (bf16[256,1024]{1,0:T(8,128)(2,1)S(1)}, bf16[256,1024]{1,0:T(8,128)(2,1)S(1)}, u32[]{:S(2)}, u32[]{:S(2)}) collective-permute-start(bf16[256,1024]{1,0:T(8,128)(2,1)S(1)} %shard_map.81.refs_2_), channel_id=1, source_target_pairs={{1,0},{2,1},{5,4},{6,5},{9,8},{10,9},{13,12},{14,13},{17,16},{18,1... | collective-permute-start | bytes 1572872 | tf_op jit(solution)/shard_map/ppermute | solution.py:454
  55.9 23.7 %collective-permute-start.8 = (bf16[256,1024]{1,0:T(8,128)(2,1)S(1)}, bf16[256,1024]{1,0:T(8,128)(2,1)S(1)}, u32[]{:S(2)}, u32[]{:S(2)}) collective-permute-start(bf16[256,1024]{1,0:T(8,128)(2,1)S(1)} %shard_map.80.refs_3_), channel_id=1, source_target_pairs={{2,3},{6,7},{10,11},{14,15},{18,19},{22,23},{26,27},{30,31}} | collective-permute-start | bytes 1572872 | tf_op jit(solution)/shard_map/ppermute | solution.py:454
  66.2 13.4 %collective-permute-start.11 = (bf16[256,1024]{1,0:T(8,128)(2,1)S(1)}, bf16[256,1024]{1,0:T(8,128)(2,1)S(1)}, u32[]{:S(2)}, u32[]{:S(2)}) collective-permute-start(bf16[256,1024]{1,0:T(8,128)(2,1)S(1)} %shard_map.82.refs_4_), channel_id=1, source_target_pairs={{1,0},{5,4},{9,8},{13,12},{17,16},{21,20},{25,24},{29,28}} | collective-permute-start | bytes 1572872 | tf_op jit(solution)/shard_map/ppermute | solution.py:454
  67.5 12.7 %collective-permute-start.12 = (bf16[256,1024]{1,0:T(8,128)(2,1)S(1)}, bf16[256,1024]{1,0:T(8,128)(2,1)S(1)}, u32[]{:S(2)}, u32[]{:S(2)}) collective-permute-start(bf16[256,1024]{1,0:T(8,128)(2,1)S(1)} %shard_map.79.refs_1_.refs_0_), channel_id=1, source_target_pairs={{0,8},{4,12},{8,16},{12,20},{16,24},{20,28},{1,9},{5,13},{9,17},{1... | collective-permute-start | bytes 1572872 | tf_op jit(solution)/shard_map/ppermute | solution.py:418
  70.6 9.6 %collective-permute-start.13 = (bf16[256,1024]{1,0:T(8,128)(2,1)S(1)}, bf16[256,1024]{1,0:T(8,128)(2,1)S(1)}, u32[]{:S(2)}, u32[]{:S(2)}) collective-permute-start(bf16[256,1024]{1,0:T(8,128)(2,1)S(1)} %shard_map.79.refs_1_.refs_0_), channel_id=1, source_target_pairs={{0,4},{4,0},{8,12},{12,8},{16,20},{20,16},{24,28},{28,24},{1,5},{5... | collective-permute-start | bytes 1572872 | tf_op jit(solution)/shard_map/ppermute | solution.py:423
  73.6 15.0 %collective-permute-start.14 = (bf16[256,1024]{1,0:T(8,128)(2,1)S(1)}, bf16[256,1024]{1,0:T(8,128)(2,1)S(1)}, u32[]{:S(2)}, u32[]{:S(2)}) collective-permute-start(bf16[256,1024]{1,0:T(8,128)(2,1)S(1)} %shard_map.79.refs_1_.refs_0_), channel_id=1, source_target_pairs={{4,16},{12,24},{28,20},{5,17},{13,25},{29,21},{6,18},{14,26},{30,2... | collective-permute-start | bytes 1572872 | tf_op jit(solution)/shard_map/ppermute | solution.py:430
  81.1 12.7 %collective-permute-start.15 = (bf16[256,1024]{1,0:T(8,128)(2,1)S(1)}, bf16[256,1024]{1,0:T(8,128)(2,1)S(1)}, u32[]{:S(2)}, u32[]{:S(2)}) collective-permute-start(bf16[256,1024]{1,0:T(8,128)(2,1)S(1)} %shard_map.85.refs_0_), channel_id=1, source_target_pairs={{8,0},{12,4},{16,8},{20,12},{24,16},{28,20},{9,1},{13,5},{17,9},{2... | collective-permute-start | bytes 1572872 | tf_op jit(solution)/shard_map/ppermute | solution.py:418
  83.4 19.8 %collective-permute-start.17 = (bf16[256,1024]{1,0:T(8,128)(2,1)S(1)}, bf16[256,1024]{1,0:T(8,128)(2,1)S(1)}, u32[]{:S(2)}, u32[]{:S(2)}) collective-permute-start(bf16[256,1024]{1,0:T(8,128)(2,1)S(1)} %shard_map.85.refs_0_), channel_id=1, source_target_pairs={{4,0},{12,8},{20,16},{28,24},{16,4},{24,12},{5,1},{13,9},{21,17},{... | collective-permute-start | bytes 1572872 | tf_op jit(solution)/shard_map/ppermute | solution.py:439
  88.5 9.9 %collective-permute-start.18 = (bf16[256,1024]{1,0:T(8,128)(2,1)S(1)}, bf16[256,1024]{1,0:T(8,128)(2,1)S(1)}, u32[]{:S(2)}, u32[]{:S(2)}) collective-permute-start(bf16[256,1024]{1,0:T(8,128)(2,1)S(1)} %collective-permute-done.12.refs_5_.refs_1_.refs_3_), channel_id=1, source_target_pairs={{0,4},{4,0},{8,12},{12,8},{16,20},{20,16},{24,28},{28,24},{1,5},{5... | collective-permute-start | bytes 1572872 | tf_op jit(solution)/shard_map/ppermute | solution.py:423
  93.8 9.4 %collective-permute-start.16 = (bf16[256,1024]{1,0:T(8,128)(2,1)S(1)}, bf16[256,1024]{1,0:T(8,128)(2,1)S(1)}, u32[]{:S(2)}, u32[]{:S(2)}) collective-permute-start(bf16[256,1024]{1,0:T(8,128)(2,1)S(1)} %shard_map.87.refs_5_), channel_id=1, source_target_pairs={{0,4},{4,0},{8,12},{12,8},{16,20},{20,16},{24,28},{28,24},{1,5},{5... | collective-permute-start | bytes 1572872 | tf_op jit(solution)/shard_map/ppermute | solution.py:423
